TPU v7x, 32 devices: a whole 2x2x4 slice. The times are simulated.
32 devices in a mesh: dp: 16 (over z, y, x), tensor: 2 (over core).
Axes of the slice: x: 2, y: 2, z: 4, core: 2. Of those that a mesh axis runs over, the one named last changes fastest.
Arguments:
- tubes: bfloat16 [32, 1568, 1536], P('dp', None, 'tensor'), may hold values from -20 to 20
- tube_order: int32 [32, 1568], P('dp'), may hold values from 0 to 1567, each once within a row
- clip_mask: int32 [32], P('dp'), may hold values from 0 to 1, as said below
- enc_weights: float32 [2, 9984, 768], P('tensor', 'dp')
- dec_weights: float32 [2, 3456, 384], P('tensor', 'dp')
- vec_split: float32 [2, 6528], P('tensor'), may hold values from -2 to 2
- vec_shared: float32 [14976], replicated
- enc_moment: float32 [2, 9984, 768], P('tensor', 'dp'), may hold values from -7.361117e-05 to 7.361117e-05
- dec_moment: float32 [2, 3456, 384], P('tensor', 'dp'), may hold values from -0.024537056 to 0.024537056
- split_moment: float32 [2, 6528], P('tensor'), may hold values from -0.00073611166 to 0.00073611166
- shared_moment: float32 [14976], replicated, may hold values from -0.00073611166 to 0.00073611166
- enc_error: bfloat16 [16, 2, 9984, 768], P('dp', 'tensor'), may hold values from -7.343292e-05 to 7.343292e-05
- dec_error: bfloat16 [16, 2, 3456, 384], P('dp', 'tensor'), may hold values from -7.343292e-05 to 7.343292e-05
- factors: float32 [2, 8, 1152], P('tensor'), may hold values from -5 to 5
Outputs:
- loss_sum: float32 [], replicated
- loss_weight: float32 [], replicated
- enc_weights_new: float32 [2, 9984, 768], P('tensor', 'dp')
- enc_moment_new: float32 [2, 9984, 768], P('tensor', 'dp')
- enc_error_new: bfloat16 [16, 2, 9984, 768], P('dp', 'tensor')
- dec_weights_new: float32 [2, 3456, 384], P('tensor', 'dp')
- dec_moment_new: float32 [2, 3456, 384], P('tensor', 'dp')
- dec_error_new: bfloat16 [16, 2, 3456, 384], P('dp', 'tensor')
- factors_new: float32 [2, 8, 1152], P('tensor')
- vec_split_new: float32 [2, 6528], P('tensor')
- split_moment_new: float32 [2, 6528], P('tensor')
- vec_shared_new: float32 [14976], replicated
- shared_moment_new: float32 [14976], replicated
Inputs may be any that keep to these rules, and one draw needn't show every extreme that they name: `tube_order`: each row is a permutation of the 1568 tubes. `clip_mask`: clip 0 is always counted.
All inputs are finite; a program needn't handle non-finite values.
Results may differ from a plain program's by a relative error of at most 0.014.
Values may be sent and summed in bfloat16 or wider, within the bound.
A program may use at most 384 MiB of HBM per device.

v0:
```python
import math

import jax
import jax.numpy as jnp
from jax import lax
from jax.sharding import PartitionSpec as P

D = 768
HEAD_DIM = 64
FF = 3072
DD = 384
DFF = 1536
PIX = 1536
TUBES = 1568
VIS = 160
MASKED = 1408


highest_precision = lax.Precision.HIGHEST
norm_eps = 1e-06
momentum_keep = 0.9
step_rate = 1000.0


def layer_norm(stream, gain, shift):
    center = stream - jnp.mean(stream, -1, keepdims=True)
    spread = jnp.mean(center * center, -1, keepdims=True)
    return center * lax.rsqrt(spread + norm_eps) * gain + shift


def sinusoid(width):
    place = jnp.arange(TUBES).astype(jnp.float32)[:, None]
    column = jnp.arange(width)
    rate = jnp.exp(-(2 * (column // 2)).astype(jnp.float32) * (math.log(10000.0) / width))
    angle = place * rate[None, :]
    return jnp.where(column % 2 == 0, jnp.sin(angle), jnp.cos(angle))


def project(left, right):
    return jnp.einsum("nsc,ce->nse", left, right, preferred_element_type=jnp.float32)


def project_back(left, right):
    return jnp.einsum("nsc,ec->nse", left, right, preferred_element_type=jnp.float32)


def weight_grad(left, right):
    return jnp.einsum("nsc,nse->ce", left, right, preferred_element_type=jnp.float32)


def bias_grad(grad):
    return jnp.sum(grad.astype(jnp.float32), axis=(0, 1))


def cut(block, widths):
    pieces = []
    start = 0
    for width in widths:
        pieces.append(block[start : start + width])
        start = start + width
    return pieces


def pair_forward(partial_value):
    return lax.psum(partial_value.astype(jnp.bfloat16), "tensor").astype(jnp.float32)


def pair_backward(partial_value):
    return lax.psum(partial_value.astype(jnp.bfloat16), "tensor").astype(jnp.float32)


def split_heads(tensor_in):
    return tensor_in.reshape(tensor_in.shape[0], tensor_in.shape[1] // HEAD_DIM, HEAD_DIM)


def attend_clip(items):
    query, keys, values = items
    query_heads, key_heads, value_heads = (
        split_heads(query),
        split_heads(keys),
        split_heads(values),
    )
    scores = jnp.einsum(
        "qhd,khd->hqk", query_heads, key_heads, preferred_element_type=jnp.float32
    ) * HEAD_DIM ** (-0.5)
    top = jnp.max(scores, -1, keepdims=True)
    expo = jnp.exp(scores - top)
    total = jnp.sum(expo, -1, keepdims=True)
    probs = (expo / total).astype(jnp.bfloat16)
    mixed = jnp.einsum("hqk,khd->qhd", probs, value_heads, preferred_element_type=jnp.float32)
    return (mixed.reshape(query.shape).astype(jnp.bfloat16), (top + jnp.log(total))[..., 0])


def attend_back(items):
    query, keys, values, log_sum_total, grad_mixed = items
    query_heads, key_heads, value_heads = (
        split_heads(query),
        split_heads(keys),
        split_heads(values),
    )
    grad_heads = split_heads(grad_mixed)
    scores = jnp.einsum(
        "qhd,khd->hqk", query_heads, key_heads, preferred_element_type=jnp.float32
    ) * HEAD_DIM ** (-0.5)
    probs = jnp.exp(scores - log_sum_total[..., None])
    grad_probs = jnp.einsum(
        "qhd,khd->hqk", grad_heads, value_heads, preferred_element_type=jnp.float32
    )
    grad_values = jnp.einsum(
        "hqk,qhd->khd", probs.astype(jnp.bfloat16), grad_heads, preferred_element_type=jnp.float32
    )
    row_total = jnp.sum(probs * grad_probs, -1, keepdims=True)
    grad_scores = (probs * (grad_probs - row_total)).astype(jnp.bfloat16)
    grad_query = jnp.einsum(
        "hqk,khd->qhd", grad_scores, key_heads, preferred_element_type=jnp.float32
    ) * HEAD_DIM ** (-0.5)
    grad_keys = jnp.einsum(
        "hqk,qhd->khd", grad_scores, query_heads, preferred_element_type=jnp.float32
    ) * HEAD_DIM ** (-0.5)
    return (
        grad_query.reshape(query.shape).astype(jnp.bfloat16),
        grad_keys.reshape(query.shape).astype(jnp.bfloat16),
        grad_values.reshape(query.shape).astype(jnp.bfloat16),
    )


def layer_forward(stream, mats, vecs):
    w_query, w_key, w_value, w_out, w_up, w_down = mats
    normed = layer_norm(stream, vecs[0], vecs[1]).astype(jnp.bfloat16)
    query = (project_back(normed, w_query) + vecs[2]).astype(jnp.bfloat16)
    keys = project_back(normed, w_key).astype(jnp.bfloat16)
    values = (project_back(normed, w_value) + vecs[3]).astype(jnp.bfloat16)
    mixed, log_sum_total = lax.map(attend_clip, (query, keys, values))
    middle = stream + (pair_forward(project(mixed, w_out)) + vecs[4])
    second = layer_norm(middle, vecs[5], vecs[6]).astype(jnp.bfloat16)
    before = project_back(second, w_up) + vecs[7]
    active = jax.nn.gelu(before, approximate=False).astype(jnp.bfloat16)
    result = middle + (pair_forward(project(active, w_down)) + vecs[8])
    return (
        result,
        (stream, normed, query, keys, values, log_sum_total, mixed, middle, second, before, active),
    )


def layer_backward(grad, kept, mats, vecs):
    stream, normed, query, keys, values, log_sum_total, mixed, middle, second, before, active = kept
    w_query, w_key, w_value, w_out, w_up, w_down = mats
    grad_low = grad.astype(jnp.bfloat16)
    g_down = weight_grad(active, grad_low)
    grad_active = project_back(grad_low, w_down)
    grad_before = jax.vjp(lambda inner: jax.nn.gelu(inner, approximate=False), before)[1](
        grad_active
    )[0].astype(jnp.bfloat16)
    g_up = weight_grad(grad_before, second)
    grad_second = pair_backward(project(grad_before, w_up))
    norm_back = jax.vjp(layer_norm, middle, vecs[5], vecs[6])[1]
    grad_middle, g_gain2, g_shift2 = norm_back(grad_second)
    grad_middle = grad + grad_middle
    middle_low = grad_middle.astype(jnp.bfloat16)
    g_out = weight_grad(mixed, middle_low)
    grad_mixed = project_back(middle_low, w_out).astype(jnp.bfloat16)
    grad_query, grad_keys, grad_values = lax.map(
        attend_back, (query, keys, values, log_sum_total, grad_mixed)
    )
    g_query = weight_grad(grad_query, normed)
    g_key = weight_grad(grad_keys, normed)
    g_value = weight_grad(grad_values, normed)
    normalized_gradient = pair_backward(
        project(grad_query, w_query) + project(grad_keys, w_key) + project(grad_values, w_value)
    )
    norm_back = jax.vjp(layer_norm, stream, vecs[0], vecs[1])[1]
    grad_stream, g_gain1, g_shift1 = norm_back(normalized_gradient)
    vec_grads = (
        g_gain1,
        g_shift1,
        bias_grad(grad_query),
        bias_grad(grad_values),
        bias_grad(middle_low),
        g_gain2,
        g_shift2,
        bias_grad(grad_before),
        bias_grad(grad_low),
    )
    return (grad_middle + grad_stream, (g_query, g_key, g_value, g_out, g_up, g_down), vec_grads)


def gram_of(left):
    return jnp.einsum("rx,sx->rs", left, left, precision=highest_precision)


def lower_solve(gram, left):
    return lax.linalg.triangular_solve(jnp.linalg.cholesky(gram), left, left_side=True, lower=True)


def per_device(
    tubes,
    tube_order,
    clip_mask,
    enc_weights,
    dec_weights,
    vec_split,
    vec_shared,
    enc_moment,
    dec_moment,
    split_moment,
    shared_moment,
    enc_error,
    dec_error,
    factors,
):
    groups = lax.axis_size("tensor")
    workers = lax.axis_size("dp")
    half = lax.axis_index("tensor")
    worker_index = lax.axis_index("dp")
    enc_all, dec_all = (
        lax.all_gather(enc_weights.astype(jnp.bfloat16), "dp", axis=1, tiled=True),
        lax.all_gather(dec_weights.astype(jnp.bfloat16), "dp", axis=1, tiled=True),
    )
    layer_widths = [D // groups, FF // groups, D // groups, D // groups, D // groups, FF // groups]
    enc_pieces = cut(enc_all[0], [PIX // groups] + layer_widths * 2)
    embed = enc_pieces[0]
    proj, d_out, d_down, d_query, d_key, d_value, d_up, head_rows = cut(
        dec_all[0],
        [
            D // groups,
            DD // groups,
            DFF // groups,
            DD // groups,
            DD // groups,
            DD // groups,
            DFF // groups,
            PIX // groups,
        ],
    )
    split_parts = cut(
        vec_split[0],
        [D // groups, D // groups, FF // groups] * 2
        + [DD // groups, DD // groups, DFF // groups, PIX // groups],
    )
    shared = cut(vec_shared, [D] * 15 + [DD] * 9)
    enc_layers = []
    for index in range(2):
        e_out, e_down, e_query, e_key, e_value, e_up = enc_pieces[1 + 6 * index : 7 + 6 * index]
        base = 6 * index
        vecs = (
            shared[1 + base],
            shared[2 + base],
            split_parts[3 * index],
            split_parts[3 * index + 1],
            shared[3 + base],
            shared[4 + base],
            shared[5 + base],
            split_parts[3 * index + 2],
            shared[6 + base],
        )
        enc_layers.append(((e_query, e_key, e_value, e_out, e_up, e_down), vecs))
    dec_mats = (d_query, d_key, d_value, d_out, d_up, d_down)
    dec_vecs = (
        shared[16],
        shared[17],
        split_parts[6],
        split_parts[7],
        shared[18],
        shared[19],
        shared[20],
        split_parts[8],
        shared[21],
    )
    visible = tube_order[:, :VIS]
    masked = tube_order[:, VIS:]
    vis_pixels = jnp.take_along_axis(tubes, visible[:, :, None], axis=1)
    mask_pixels = jnp.take_along_axis(tubes, masked[:, :, None], axis=1).astype(jnp.float32)
    pixel_sum, pixel_square = lax.psum(
        (jnp.sum(mask_pixels, -1), jnp.sum(mask_pixels * mask_pixels, -1)), "tensor"
    )
    center = pixel_sum / PIX
    target = (mask_pixels - center[..., None]) * lax.rsqrt(
        pixel_square / PIX - center * center + norm_eps
    )[..., None]
    pos_enc = jnp.take(sinusoid(D), visible, axis=0)
    pos_dec = sinusoid(DD)
    enc_stream = pair_forward(project(vis_pixels, embed)) + shared[0] + pos_enc
    enc_kept = []
    for mats, vecs in enc_layers:
        enc_stream, kept = layer_forward(enc_stream, mats, vecs)
        enc_kept.append(kept)
    enc_normed = layer_norm(enc_stream, shared[13], shared[14]).astype(jnp.bfloat16)
    quarter = D // groups
    normed_half = lax.dynamic_slice_in_dim(enc_normed, half * quarter, quarter, 2)
    latent = pair_forward(project(normed_half, proj))
    dec_start = jnp.concatenate(
        [
            latent + jnp.take(pos_dec, visible, axis=0),
            shared[15][None, None, :] + jnp.take(pos_dec, masked, axis=0),
        ],
        1,
    )
    dec_stream, dec_kept = layer_forward(dec_start, dec_mats, dec_vecs)
    dec_masked = dec_stream[:, VIS:]
    dec_normed = layer_norm(dec_masked, shared[22], shared[23]).astype(jnp.bfloat16)
    guess = project_back(dec_normed, head_rows) + split_parts[9]
    miss = guess - target
    counted = clip_mask.astype(jnp.float32)
    loss_part = jnp.sum(counted[:, None, None] * miss * miss) / PIX
    count_part = MASKED * jnp.sum(counted) / groups
    loss_sum, loss_weight = lax.psum((loss_part, count_part), ("dp", "tensor"))
    grad_guess = (2.0 * workers / (PIX * loss_weight) * counted[:, None, None] * miss).astype(
        jnp.bfloat16
    )
    g_head = weight_grad(grad_guess, dec_normed)
    g_head_bias = bias_grad(grad_guess)
    normalized_gradient = pair_backward(project(grad_guess, head_rows))
    grad_masked, g_dec_gain, g_dec_shift = jax.vjp(layer_norm, dec_masked, shared[22], shared[23])[
        1
    ](normalized_gradient)
    grad_dec = jnp.concatenate(
        [jnp.zeros((grad_masked.shape[0], VIS, DD), jnp.float32), grad_masked], 1
    )
    grad_start, dec_mat_grads, dec_vec_grads = layer_backward(
        grad_dec, dec_kept, dec_mats, dec_vecs
    )
    grad_latent = grad_start[:, :VIS].astype(jnp.bfloat16)
    g_mask_token = jnp.sum(grad_start[:, VIS:], axis=(0, 1))
    g_proj = weight_grad(normed_half, grad_latent)
    grad_enc_normed = lax.all_gather(
        project_back(grad_latent, proj).astype(jnp.bfloat16), "tensor", axis=2, tiled=True
    ).astype(jnp.float32)
    grad_enc, g_enc_gain, g_enc_shift = jax.vjp(layer_norm, enc_stream, shared[13], shared[14])[1](
        grad_enc_normed
    )
    enc_mat_list = [None, None]
    enc_vec_list = [None, None]
    for index in (1, 0):
        mats, vecs = enc_layers[index]
        grad_enc, enc_mat_list[index], enc_vec_list[index] = layer_backward(
            grad_enc, enc_kept[index], mats, vecs
        )
    embed_low = grad_enc.astype(jnp.bfloat16)
    g_embed = weight_grad(vis_pixels, embed_low)
    enc_blocks = [g_embed]
    partitioned_blocks = []
    shared_blocks = [bias_grad(embed_low)]
    for index in range(2):
        mat_grads = enc_mat_list[index]
        vec_grads = enc_vec_list[index]
        enc_blocks = enc_blocks + [
            mat_grads[3],
            mat_grads[5],
            mat_grads[0],
            mat_grads[1],
            mat_grads[2],
            mat_grads[4],
        ]
        partitioned_blocks = partitioned_blocks + [vec_grads[2], vec_grads[3], vec_grads[7]]
        shared_blocks = shared_blocks + [
            vec_grads[0],
            vec_grads[1],
            vec_grads[4],
            vec_grads[5],
            vec_grads[6],
            vec_grads[8],
        ]
    enc_grad = jnp.concatenate(enc_blocks, 0)
    dec_grad = jnp.concatenate(
        [
            g_proj,
            dec_mat_grads[3],
            dec_mat_grads[5],
            dec_mat_grads[0],
            dec_mat_grads[1],
            dec_mat_grads[2],
            dec_mat_grads[4],
            g_head,
        ],
        0,
    )
    split_grad = jnp.concatenate(
        partitioned_blocks + [dec_vec_grads[2], dec_vec_grads[3], dec_vec_grads[7], g_head_bias]
    )
    shared_grad = jnp.concatenate(
        shared_blocks
        + [
            g_enc_gain,
            g_enc_shift,
            g_mask_token,
            dec_vec_grads[0],
            dec_vec_grads[1],
            dec_vec_grads[4],
            dec_vec_grads[5],
            dec_vec_grads[6],
            dec_vec_grads[8],
            g_dec_gain,
            g_dec_shift,
        ]
    )
    enc_comb = enc_grad + enc_error[0, 0].astype(jnp.float32)
    dec_comb = dec_grad + dec_error[0, 0].astype(jnp.float32)
    enc_left = jnp.einsum("rc,xc->rx", factors[0, :, :D], enc_comb, precision=highest_precision)
    dec_left = jnp.einsum("rc,xc->rx", factors[0, :, D:], dec_comb, precision=highest_precision)
    enc_left, dec_left, split_sum, shared_sum = lax.psum(
        (enc_left, dec_left, split_grad, shared_grad), "dp"
    )
    enc_basis = lower_solve(gram_of(enc_left), enc_left)
    dec_basis = lower_solve(gram_of(dec_left), dec_left)
    enc_rows = enc_basis.shape[1] // workers
    dec_rows = dec_basis.shape[1] // workers
    enc_owned = lax.dynamic_slice_in_dim(enc_basis, worker_index * enc_rows, enc_rows, 1)
    dec_owned = lax.dynamic_slice_in_dim(dec_basis, worker_index * dec_rows, dec_rows, 1)
    enc_right, dec_right = lax.psum(
        (
            jnp.einsum("rx,xc->rc", enc_basis, enc_comb, precision=highest_precision),
            jnp.einsum("rx,xc->rc", dec_basis, dec_comb, precision=highest_precision),
        ),
        "dp",
    )
    enc_right = enc_right / workers
    dec_right = dec_right / workers
    enc_error_new = (
        enc_comb - jnp.einsum("rx,rc->xc", enc_basis, enc_right, precision=highest_precision)
    ).astype(jnp.bfloat16)
    dec_error_new = (
        dec_comb - jnp.einsum("rx,rc->xc", dec_basis, dec_right, precision=highest_precision)
    ).astype(jnp.bfloat16)
    enc_mom = momentum_keep * enc_moment[0] + jnp.einsum(
        "rx,rc->xc", enc_owned, enc_right, precision=highest_precision
    )
    dec_mom = momentum_keep * dec_moment[0] + jnp.einsum(
        "rx,rc->xc", dec_owned, dec_right, precision=highest_precision
    )
    split_mom = momentum_keep * split_moment[0] + split_sum / workers
    shared_mom = momentum_keep * shared_moment + shared_sum / workers
    return (
        loss_sum,
        loss_weight,
        (enc_weights[0] - step_rate * enc_mom)[None],
        enc_mom[None],
        enc_error_new[None, None],
        (dec_weights[0] - step_rate * dec_mom)[None],
        dec_mom[None],
        dec_error_new[None, None],
        jnp.concatenate([enc_right, dec_right], 1)[None],
        (vec_split[0] - step_rate * split_mom)[None],
        split_mom[None],
        vec_shared - step_rate * shared_mom,
        shared_mom,
    )


def solution(mesh):
    placed = (
        P("dp", None, "tensor"),
        P("dp", None),
        P("dp"),
        P("tensor", "dp", None),
        P("tensor", "dp", None),
        P("tensor", None),
        P(),
        P("tensor", "dp", None),
        P("tensor", "dp", None),
        P("tensor", None),
        P(),
        P("dp", "tensor", None, None),
        P("dp", "tensor", None, None),
        P("tensor", None, None),
    )
    return jax.shard_map(
        per_device,
        mesh=mesh,
        in_specs=placed,
        out_specs=(
            P(),
            P(),
            P("tensor", "dp", None),
            P("tensor", "dp", None),
            P("dp", "tensor", None, None),
            P("tensor", "dp", None),
            P("tensor", "dp", None),
            P("dp", "tensor", None, None),
            P("tensor", None, None),
            P("tensor", None),
            P("tensor", None),
            P(),
            P(),
        ),
        check_vma=False,
    )
```

profile of v0, /device:TPU:0, one launch (start us, length us, event | category | flops | bytes accessed | tf_op | source)
XLA Modules:
  0.0 1623.9 jit_solution(1528465759291479771)
XLA Ops:
  11.2 7.4 gather_fusion.3
  18.6 173.5 %all-gather.3.cloned.1.call-done = bf16[1,9984,768]{2,1,0:T(8,128)(2,1)} async-done(((bf16[1,624,768]{2,1,0:T(8,128)(2,1)}), bf16[1,9984,768]{2,1,0:T(8,128)(2,1)}) %all-gather.3.cloned.1.call-update) | async-done | bytes 15335440 | tf_op jit(solution)/shard_map/all_gather | solution.py:216
  194.9 18.3 %fusion.59 = f32[1568,768]{1,0:T(8,128)} fusion(f32[768]{0:T(1024)S(1)} %fusion.169, f32[1568]{0:T(1024)S(1)} %iota_convert_fusion, pred[768]{0:T(1024)(128)(4,1)S(1)} %fusion.163), kind=kLoop, calls=%fused_computation.165 | loop fusion | flops 2408448 | bytes 4827008 | tf_op jit(solution)/shard_map/jit(_where)/select_n | solution.py:36
  230.7 16.7 %all-reduce.25.cloned.1.call-done = bf16[2,160,768]{2,1,0:T(8,128)(2,1)} async-done(((bf16[2,160,768]{2,1,0:T(8,128)(2,1)}), bf16[2,160,768]{2,1,0:T(8,128)(2,1)}) %all-reduce.25.cloned.1.call-update) | async-done | bytes 491536 | tf_op jit(solution)/shard_map/psum | solution.py:65
  253.5 5.3 multiply_convert_fusion.6
  263.2 20.0 %all-reduce.27.cloned.1.call-done = bf16[2,160,768]{2,1,0:T(8,128)(2,1)} async-done(((bf16[2,160,768]{2,1,0:T(8,128)(2,1)}), bf16[2,160,768]{2,1,0:T(8,128)(2,1)}) %all-reduce.27.cloned.1.call-update) | async-done | bytes 491536 | tf_op jit(solution)/shard_map/psum | solution.py:65
  295.1 20.0 %all-reduce.29.cloned.1.call-done = bf16[2,160,768]{2,1,0:T(8,128)(2,1)} async-done(((bf16[2,160,768]{2,1,0:T(8,128)(2,1)}), bf16[2,160,768]{2,1,0:T(8,128)(2,1)}) %all-reduce.29.cloned.1.call-update) | async-done | bytes 491536 | tf_op jit(solution)/shard_map/psum | solution.py:65
  321.8 5.4 multiply_convert_fusion.5
  333.7 8.5 fusion.71
  342.2 7.9 gather_fusion.2
  354.0 66.3 %all-gather.5.cloned.1.call-done = bf16[1,3456,384]{2,1,0:T(8,128)(2,1)} async-done(((bf16[1,216,384]{2,1,0:T(8,128)(2,1)}), bf16[1,3456,384]{2,1,0:T(8,128)(2,1)}) %all-gather.5.cloned.1.call-update) | async-done | bytes 2654224 | tf_op jit(solution)/shard_map/all_gather | solution.py:217
  428.8 11.6 all-reduce.33.cloned.1.call-done
  455.5 80.9 %while.80 = (s32[]{:T(128)}, bf16[2,1568,192]{1,2,0:T(8,128)(2,1)S(1)}, f32[2,3,1568]{2,1,0:T(4,128)S(1)}, bf16[2,1568,192]{1,2,0:T(8,128)(2,1)}, bf16[2,1568,19...) while((s32[]{:T(128)}, bf16[2,1568,192]{1,2,0:T(8,128)(2,1)S(1)}, ...), condition=%wide.region_29.30_spmd, body=%wide.region_26.29_spmd.sunk | while | flops 1954902400 | bytes 95983568 | solution.py:133
  456.7 11.8 multiply_reduce_fusion.17
  468.4 12.7 fusion.410
  482.3 13.5 fusion.411
  497.1 11.8 multiply_reduce_fusion.17
  508.9 12.7 fusion.410
  522.8 13.5 fusion.411
  541.1 22.0 %all-reduce.35.cloned.1.call-done = bf16[2,1568,384]{2,1,0:T(8,128)(2,1)} async-done(((bf16[2,1568,384]{2,1,0:T(8,128)(2,1)}), bf16[2,1568,384]{2,1,0:T(8,128)(2,1)}) %all-reduce.35.cloned.1.call-update) | async-done | bytes 2408464 | tf_op jit(solution)/shard_map/psum | solution.py:65
  568.1 7.5 fusion.73
  575.6 23.5 %multiply_convert_fusion.3 = (bf16[2,1568,768]{2,1,0:T(8,128)(2,1)S(1)}, f32[2,1568,768]{2,1,0:T(8,128)}) fusion(f32[2,1568,768]{2,1,0:T(8,128)S(1)} %get-tuple-element.549, f32[768]{0:T(1024)S(1)} %get-tuple-element.344, u8[1568,768]{1,0:T(8,128)(4,1)S(1)} %get-tuple-element.306, u8[1568,768]{1,0:T(8,128)(4,1)S(1)} %get-tuple-element.305), kind=kLoop, calls=%fused_computation.116 | loop fusion | flops 170999808 | bytes 26496000 | tf_op jit(solution)/shard_map/convert_element_type | solution.py:137
  606.7 39.1 %gather_fusion.4 = bf16[2816,768]{1,0:T(8,128)(2,1)} fusion(bf16[2,1568,768]{2,1,0:T(8,128)(2,1)} %param.27, s32[2816]{0:T(1024)S(1)} %reshape.794), kind=kCustom, calls=%fused_computation.4 | custom fusion | bytes 8673280 | tf_op jit(solution)/shard_map/jit(take_along_axis)/gather | solution.py:272
  659.1 8.8 fusion.44
  668.6 40.6 %all-reduce.1 = (f32[]{:T(128)}, f32[]{:T(128)}) all-reduce(f32[]{:T(128)S(6)} %div.263, f32[]{:T(128)S(6)} %div.264), channel_id=1, replica_groups=mesh['dp'=16,'tensor'=2] {'dp','tensor'}, use_global_device_ids=true, to_apply=%region_41.42 | all-reduce | flops 2 | bytes 16 | tf_op jit(solution)/shard_map/psum | solution.py:306
  710.0 5.3 convert_reduce_fusion.2
  722.4 21.2 %all-reduce.39.cloned.1.call-done = bf16[2,1408,384]{2,1,0:T(8,128)(2,1)} async-done(((bf16[2,1408,384]{2,1,0:T(8,128)(2,1)}), bf16[2,1408,384]{2,1,0:T(8,128)(2,1)}) %all-reduce.39.cloned.1.call-update) | async-done | bytes 2162704 | tf_op jit(solution)/shard_map/psum | solution.py:69
  753.2 11.9 convert_reduce_fusion.1
  765.1 6.6 convolution_convert_fusion.4
  771.8 23.0 %all-reduce.41.cloned.1.call-done = bf16[2,1568,384]{2,1,0:T(8,128)(2,1)} async-done(((bf16[2,1568,384]{2,1,0:T(8,128)(2,1)}), bf16[2,1568,384]{2,1,0:T(8,128)(2,1)}) %all-reduce.41.cloned.1.call-update) | async-done | bytes 2408464 | tf_op jit(solution)/shard_map/psum | solution.py:69
  804.3 7.1 convert_reduce_fusion.7
  817.9 194.7 %while.81 = (s32[]{:T(128)}, bf16[2,1568,192]{1,2,0:T(8,128)(2,1)}, bf16[2,1568,192]{1,2,0:T(8,128)(2,1)}, bf16[2,1568,192]{1,2,0:T(8,128)(2,1)}, bf16[2,1568,19...) while((s32[]{:T(128)}, bf16[2,1568,192]{1,2,0:T(8,128)(2,1)}, ...), condition=%wide.region_52.53_spmd, body=%wide.region_50.52_spmd.sunk | while | flops 4810569216 | bytes 260091296 | solution.py:162
  819.7 11.8 fusion.422
  832.7 23.6 %multiply_reduce_fusion.18 = (f32[3,1568]{1,0:T(4,128)S(1)}, f32[3,1568,1568]{1,2,0:T(8,128)}) fusion(f32[3,1568,1568]{1,2,0:T(8,128)} %fusion.422, f32[3,1568]{1,0:T(4,128)S(1)} %dynamic-slice_bitcast_fusion.6, bf16[1568,3,64]{0,2,1:T(8,128)(2,1)S(1)} %bitcast.659, bf16[1568,3,64]{0,2,1:T(8,128)(2,1)S(1)} %bitcast.669), kind=kOutput, calls=%fused_computation.38.clone.1 | convolution fusion | flops 973610368 | bytes 60248832 | tf_op jit(solution)/shard_map/while/body/eval_jaxpr/qhd,khd->hqk/dot_general | solution.py:106
  856.3 25.4 %multiply_convert_fusion.11 = bf16[3,1568,1568]{1,2,0:T(8,128)(2,1)} fusion(f32[3,1568,1568]{1,2,0:T(8,128)} %get-tuple-element.900, f32[3,1568,1568]{1,2,0:T(8,128)} %fusion.422, f32[3,1568]{1,0:T(4,128)S(1)} %get-tuple-element.901, f32[3,1568]{1,0:T(4,128)S(1)} %dynamic-slice_bitcast_fusion.6), kind=kLoop, calls=%fused_computation.37.clone.1 | loop fusion | flops 36879360 | bytes 73796352 | tf_op jit(solution)/shard_map/while/body/eval_jaxpr/convert_element_type | solution.py:113
  881.7 10.1 fusion.425
  891.8 13.0 fusion.424
  906.0 8.1 fusion.423
  916.8 11.8 fusion.422
  929.8 23.6 %multiply_reduce_fusion.18 = (f32[3,1568]{1,0:T(4,128)S(1)}, f32[3,1568,1568]{1,2,0:T(8,128)}) fusion(f32[3,1568,1568]{1,2,0:T(8,128)} %fusion.422, f32[3,1568]{1,0:T(4,128)S(1)} %dynamic-slice_bitcast_fusion.6, bf16[1568,3,64]{0,2,1:T(8,128)(2,1)S(1)} %bitcast.659, bf16[1568,3,64]{0,2,1:T(8,128)(2,1)S(1)} %bitcast.669), kind=kOutput, calls=%fused_computation.38.clone.1 | convolution fusion | flops 973610368 | bytes 60248832 | tf_op jit(solution)/shard_map/while/body/eval_jaxpr/qhd,khd->hqk/dot_general | solution.py:106
  953.4 25.4 %multiply_convert_fusion.11 = bf16[3,1568,1568]{1,2,0:T(8,128)(2,1)} fusion(f32[3,1568,1568]{1,2,0:T(8,128)} %get-tuple-element.900, f32[3,1568,1568]{1,2,0:T(8,128)} %fusion.422, f32[3,1568]{1,0:T(4,128)S(1)} %get-tuple-element.901, f32[3,1568]{1,0:T(4,128)S(1)} %dynamic-slice_bitcast_fusion.6), kind=kLoop, calls=%fused_computation.37.clone.1 | loop fusion | flops 36879360 | bytes 73796352 | tf_op jit(solution)/shard_map/while/body/eval_jaxpr/convert_element_type | solution.py:113
  978.8 10.1 fusion.425
  988.9 13.0 fusion.424
  1003.1 8.0 fusion.423
  1021.7 21.9 %all-reduce.43.cloned.1.call-done = bf16[2,1568,384]{2,1,0:T(8,128)(2,1)} async-done(((bf16[2,1568,384]{2,1,0:T(8,128)(2,1)}), bf16[2,1568,384]{2,1,0:T(8,128)(2,1)}) %all-reduce.43.cloned.1.call-update) | async-done | bytes 2408464 | tf_op jit(solution)/shard_map/psum | solution.py:69
  1053.1 5.6 add_add_fusion.3
  1081.0 7.8 bitcast_dynamic-update-slice_fusion.15
  1114.2 12.1 while.82
  1135.5 16.8 %all-reduce.47.cloned.1.call-done = bf16[2,160,768]{2,1,0:T(8,128)(2,1)} async-done(((bf16[2,160,768]{2,1,0:T(8,128)(2,1)}), bf16[2,160,768]{2,1,0:T(8,128)(2,1)}) %all-reduce.47.cloned.1.call-update) | async-done | bytes 491536 | tf_op jit(solution)/shard_map/psum | solution.py:69
  1166.1 8.9 fusion.62
  1175.0 9.9 all-reduce.49.cloned.1.call-done
  1195.2 10.6 while.83
  1217.6 13.9 all-reduce.51.cloned.1.call-done
  1241.5 5.1 bitcast_dynamic-update-slice_fusion.6
  1253.6 5.2 bitcast_dynamic-update-slice_fusion.5
  1272.8 5.5 bitcast_dynamic-update-slice_fusion.3
  1280.3 33.6 %fusion.32 = f32[8,9984]{1,0:T(8,128)} fusion(f32[1,1,9984,768]{3,2,1,0:T(8,128)} %get-tuple-element.576, bf16[1,1,9984,768]{3,2,1,0:T(8,128)(2,1)} %param.38, f32[1,8,1152]{2,1,0:T(8,128)S(1)} %copy-done.169), kind=kOutput, calls=%fused_computation.107 | convolution fusion | flops 751435776 | bytes 46350336 | tf_op jit(solution)/shard_map/rc,xc->rx/dot_general | solution.py:398
  1315.1 5.2 bitcast_dynamic-update-slice_fusion.10
  1337.2 86.3 %all-reduce.55.cloned.1.call-done = (f32[8,9984]{1,0:T(8,128)}, f32[8,3456]{1,0:T(8,128)}) async-done(((f32[8,9984]{1,0:T(8,128)}, f32[8,3456]{1,0:T(8,128)}), (f32[8,9984]{1,0:T(8,128)}, f32[8,3456]{1,0:T(8,128)})) %all-reduce.55.cloned.1.call-update) | async-done | bytes 430096 | tf_op jit(solution)/shard_map/psum | solution.py:400
  1435.0 6.0 fusion.67
  1441.0 22.4 %fusion.29 = f32[8,768]{1,0:T(8,128)} fusion(f32[8,9984]{1,0:T(8,128)S(1)} %fusion.172, f32[9984,768]{1,0:T(8,128)} %bitcast_dynamic-update-slice_fusion.7, bf16[1,1,9984,768]{3,2,1,0:T(8,128)(2,1)} %param.38), kind=kOutput, calls=%fused_computation.100 | convolution fusion | flops 751435776 | bytes 46350336 | tf_op jit(solution)/shard_map/rx,xc->rc/dot_general | solution.py:411
  1463.6 104.9 %all-reduce.53.cloned.1.call-done = (f32[8,768]{1,0:T(8,128)}, f32[8,384]{1,0:T(8,128)}, f32[6528]{0:T(1024)}, f32[14976]{0:T(1024)}) async-done(((f32[8,768]{1,0:T(8,128)}, f32[8,384]{1,0:T(8,128)}, f32[6528]{0:T(1024)}, f32[14976]{0:T(1024)}), (f32[8,768]{1,0:T(8,128)}, f32[8,384]{1,0:T(8,128)}, f32[6528]{0:T(1024)}, f32[14976]{0:T(1024)})) %all-reduce.53.cloned.1.call-update) | async-done | bytes 122896 | tf_op jit(solution)/shard_map/psum | solution.py:409
  1569.2 7.7 fusion.54
  1576.9 32.4 %fusion.31 = bf16[1,1,9984,768]{3,2,1,0:T(8,128)(2,1)} fusion(f32[8,9984]{1,0:T(8,128)S(1)} %fusion.172, f32[9984,768]{1,0:T(8,128)} %bitcast_dynamic-update-slice_fusion.7, bf16[1,1,9984,768]{3,2,1,0:T(8,128)(2,1)} %param.38, f32[8,768]{1,0:T(8,128)S(1)} %copy-done.121), kind=kOutput, calls=%fused_computation.101 | convolution fusion | flops 766777344 | bytes 61685760 | tf_op jit(solution)/shard_map/rx,rc->xc/dot_general | solution.py:419
  (941 shorter events, 370.2 us)
Async XLA Ops:
  7.2 185.0 %all-gather.3.cloned.1.call-start = ((), (), s32[]{:S(2)}) async-start(), calls=%async_computation | async-start | bytes 16293888 | tf_op jit(solution)/shard_map/all_gather | solution.py:216
  9.8 208.6 %all-reduce.23.cloned.1.call-start = ((), (), s32[]{:S(2)}) async-start(), calls=%async_computation.1 | async-start | bytes 983040 | tf_op jit(solution)/shard_map/psum | solution.py:65
  18.6 199.6 %copy-start.94 = (bf16[320,768]{1,0:T(8,128)(2,1)}, bf16[320,768]{1,0:T(8,128)(2,1)S(1)}, u32[]{:S(2)}) copy-start(bf16[320,768]{1,0:T(8,128)(2,1)S(1)} %gather_fusion.3) | copy-start | bytes 1474564
  194.9 52.5 %all-reduce.25.cloned.1.call-start = ((), (), s32[]{:S(2)}) async-start(), calls=%async_computation.2 | async-start | bytes 983040 | tf_op jit(solution)/shard_map/psum | solution.py:65
  218.3 30.7 %copy-start.139 = (f32[768]{0:T(1024)}, f32[768]{0:T(1024)S(1)}, u32[]{:S(2)}) copy-start(f32[768]{0:T(1024)S(1)} %get-tuple-element.538) | copy-start | bytes 9220
  218.3 30.7 %copy-start.202 = (f32[768]{0:T(1024)}, f32[768]{0:T(1024)S(1)}, u32[]{:S(2)}) copy-start(f32[768]{0:T(1024)S(1)} %get-tuple-element.537) | copy-start | bytes 9220
  218.3 66.4 %copy-start.143 = (f32[768]{0:T(1024)}, f32[768]{0:T(1024)S(1)}, u32[]{:S(2)}) copy-start(f32[768]{0:T(1024)S(1)} %get-tuple-element.535) | copy-start | bytes 9220
  218.3 98.9 %copy-start.137 = (f32[768]{0:T(1024)}, f32[768]{0:T(1024)S(1)}, u32[]{:S(2)}) copy-start(f32[768]{0:T(1024)S(1)} %get-tuple-element.532) | copy-start | bytes 9220
  218.3 98.9 %copy-start.200 = (f32[768]{0:T(1024)}, f32[768]{0:T(1024)S(1)}, u32[]{:S(2)}) copy-start(f32[768]{0:T(1024)S(1)} %get-tuple-element.531) | copy-start | bytes 9220
  218.4 114.5 %copy-start.128 = (f32[768]{0:T(1024)}, f32[768]{0:T(1024)S(1)}, u32[]{:S(2)}) copy-start(f32[768]{0:T(1024)S(1)} %get-tuple-element.528) | copy-start | bytes 9220
  219.7 27.7 %copy-start.7 = (f32[2,160,768]{2,1,0:T(8,128)}, f32[2,160,768]{2,1,0:T(8,128)S(1)}, u32[]{:S(2)}) copy-start(f32[2,160,768]{2,1,0:T(8,128)S(1)} %get-tuple-element.489) | copy-start | bytes 2949124
  227.6 24.5 %copy-start.102 = (bf16[2,160,384]{1,2,0:T(8,128)(2,1)}, bf16[2,160,384]{1,2,0:T(8,128)(2,1)S(1)}, u32[]{:S(2)}) copy-start(bf16[2,160,384]{1,2,0:T(8,128)(2,1)S(1)} %get-tuple-element.260) | copy-start | bytes 737284
  230.4 52.8 %all-reduce.27.cloned.1.call-start = ((), (), s32[]{:S(2)}) async-start(), calls=%async_computation.3 | async-start | bytes 983040 | tf_op jit(solution)/shard_map/psum | solution.py:65
  248.6 34.6 %copy-start.9 = (f32[2,160,768]{2,1,0:T(8,128)}, f32[2,160,768]{2,1,0:T(8,128)S(1)}, u32[]{:S(2)}) copy-start(f32[2,160,768]{2,1,0:T(8,128)S(1)} %get-tuple-element.487) | copy-start | bytes 2949124
  263.2 51.9 %all-reduce.29.cloned.1.call-start = ((), (), s32[]{:S(2)}) async-start(), calls=%async_computation.4 | async-start | bytes 983040 | tf_op jit(solution)/shard_map/psum | solution.py:65
  284.4 30.7 %copy-start.13 = (f32[2,160,768]{2,1,0:T(8,128)}, f32[2,160,768]{2,1,0:T(8,128)S(1)}, u32[]{:S(2)}) copy-start(f32[2,160,768]{2,1,0:T(8,128)S(1)} %get-tuple-element.483) | copy-start | bytes 2949124
  292.3 28.1 %copy-start.46 = (bf16[2,160,384]{1,2,0:T(8,128)(2,1)}, bf16[2,160,384]{1,2,0:T(8,128)(2,1)S(1)}, u32[]{:S(2)}) copy-start(bf16[2,160,384]{1,2,0:T(8,128)(2,1)S(1)} %get-tuple-element.1119) | copy-start | bytes 737284
  292.3 28.1 %copy-start.48 = (bf16[2,160,384]{1,2,0:T(8,128)(2,1)}, bf16[2,160,384]{1,2,0:T(8,128)(2,1)S(1)}, u32[]{:S(2)}) copy-start(bf16[2,160,384]{1,2,0:T(8,128)(2,1)S(1)} %get-tuple-element.1120) | copy-start | bytes 737284
  292.3 28.1 %copy-start.49 = (bf16[2,160,384]{1,2,0:T(8,128)(2,1)}, bf16[2,160,384]{1,2,0:T(8,128)(2,1)S(1)}, u32[]{:S(2)}) copy-start(bf16[2,160,384]{1,2,0:T(8,128)(2,1)S(1)} %get-tuple-element.1121) | copy-start | bytes 737284
  295.1 56.5 %all-reduce.31.cloned.1.call-start = ((), (), s32[]{:S(2)}) async-start(), calls=%async_computation.5 | async-start | bytes 983040 | tf_op jit(solution)/shard_map/psum | solution.py:65
  316.3 35.3 %copy-start.11 = (f32[2,160,768]{2,1,0:T(8,128)}, f32[2,160,768]{2,1,0:T(8,128)S(1)}, u32[]{:S(2)}) copy-start(f32[2,160,768]{2,1,0:T(8,128)S(1)} %get-tuple-element.481) | copy-start | bytes 2949124
  331.6 88.7 %all-gather.5.cloned.1.call-start = ((), (), s32[]{:S(2)}) async-start(), calls=%async_computation.6 | async-start | bytes 2820096 | tf_op jit(solution)/shard_map/all_gather | solution.py:217
  332.3 108.0 %all-reduce.33.cloned.1.call-start = ((), (), s32[]{:S(2)}) async-start(), calls=%async_computation.7 | async-start | bytes 491520 | tf_op jit(solution)/shard_map/psum | solution.py:65
  332.9 87.4 %copy-start.184 = (f32[384]{0:T(512)}, f32[384]{0:T(512)S(1)}, u32[]{:S(2)}) copy-start(f32[384]{0:T(512)S(1)} %dynamic-slice) | copy-start | bytes 4612
  333.0 87.3 %copy-start.186 = (f32[384]{0:T(512)}, f32[384]{0:T(512)S(1)}, u32[]{:S(2)}) copy-start(f32[384]{0:T(512)S(1)} %dynamic-slice.1) | copy-start | bytes 4612
  333.1 89.5 %copy-start.167 = (pred[2,1408]{1,0:T(4,128)(4,1)}, pred[2,1408]{1,0:T(4,128)(4,1)S(1)}, u32[]{:S(2)}) copy-start(pred[2,1408]{1,0:T(4,128)(4,1)S(1)} %get-tuple-element.492) | copy-start | bytes 8452
  350.7 95.4 %copy-start.165 = (f32[384]{0:T(512)}, f32[384]{0:T(512)S(1)}, u32[]{:S(2)}) copy-start(f32[384]{0:T(512)S(1)} %get-tuple-element.525) | copy-start | bytes 4612
  352.8 73.7 %copy-start.149 = (f32[2,160]{1,0:T(2,128)}, f32[2,160]{1,0:T(2,128)S(1)}, u32[]{:S(2)}) copy-start(f32[2,160]{1,0:T(2,128)S(1)} %broadcast_multiply_fusion.6) | copy-start | bytes 3844
  353.1 73.4 %copy-start.196 = (f32[2,160]{1,0:T(2,128)}, f32[2,160]{1,0:T(2,128)S(1)}, u32[]{:S(2)}) copy-start(f32[2,160]{1,0:T(2,128)S(1)} %multiply_reduce_fusion.7) | copy-start | bytes 3844
  353.8 72.8 %copy-start.159 = (f32[2,160]{1,0:T(2,128)}, f32[2,160]{1,0:T(2,128)S(1)}, u32[]{:S(2)}) copy-start(f32[2,160]{1,0:T(2,128)S(1)} %fusion.195) | copy-start | bytes 3844
  353.9 72.6 %copy-start.75 = (f32[2,160,768]{2,1,0:T(8,128)}, f32[2,160,768]{2,1,0:T(8,128)S(1)}, u32[]{:S(2)}) copy-start(f32[2,160,768]{2,1,0:T(8,128)S(1)} %subtract_multiply_fusion) | copy-start | bytes 2949124
  422.3 140.8 %all-reduce.35.cloned.1.call-start = ((), (), s32[]{:S(2)}) async-start(), calls=%async_computation.8 | async-start | bytes 4816896 | tf_op jit(solution)/shard_map/psum | solution.py:65
  536.4 30.4 %copy-start.33 = (bf16[2,1568,192]{1,2,0:T(8,128)(2,1)}, bf16[2,1568,192]{1,2,0:T(8,128)(2,1)S(1)}, u32[]{:S(2)}) copy-start(bf16[2,1568,192]{1,2,0:T(8,128)(2,1)S(1)} %get-tuple-element.262) | copy-start | bytes 3612676
  536.4 26.7 %copy-start.25 = (f32[2,160,384]{2,1,0:T(8,128)S(1)}, f32[2,160,384]{2,1,0:T(8,128)}, u32[]{:S(2)}) copy-start(f32[2,160,384]{2,1,0:T(8,128)} %copy-done.24) | copy-start | bytes 1474564
  536.4 26.7 %copy-start.217 = (f32[384]{0:T(512)S(1)}, f32[384]{0:T(512)}, u32[]{:S(2)}) copy-start(f32[384]{0:T(512)} %get-tuple-element.523) | copy-start | bytes 4612
  540.1 114.2 %all-reduce.37.cloned.1.call-start = ((), (), s32[]{:S(2)}) async-start(), calls=%async_computation.9 | async-start | bytes 4816896 | tf_op jit(solution)/shard_map/psum | solution.py:65
  566.9 237.5 %copy-start.114 = (f32[2,1568]{1,0:T(2,128)}, f32[2,1568]{1,0:T(2,128)S(1)}, u32[]{:S(2)}) copy-start(f32[2,1568]{1,0:T(2,128)S(1)} %broadcast_multiply_fusion.1) | copy-start | bytes 37636
  568.0 236.3 %copy-start.132 = (f32[2,1568]{1,0:T(2,128)}, f32[2,1568]{1,0:T(2,128)S(1)}, u32[]{:S(2)}) copy-start(f32[2,1568]{1,0:T(2,128)S(1)} %fusion.157) | copy-start | bytes 37636
  606.2 137.5 %all-reduce.39.cloned.1.call-start = ((), (), s32[]{:S(2)}) async-start(), calls=%async_computation.10 | async-start | bytes 4325376 | tf_op jit(solution)/shard_map/psum | solution.py:69
  606.7 39.1 %copy-start.227 = (s32[2]{0:T(128)S(1)}, s32[2]{0:T(128)}, u32[]{:S(2)}) copy-start(s32[2]{0:T(128)} %param.29) | copy-start | bytes 28
  606.7 40.3 %copy-start.168 = (pred[2,1408]{1,0:T(4,128)(4,1)S(1)}, pred[2,1408]{1,0:T(4,128)(4,1)}, u32[]{:S(2)}) copy-start(pred[2,1408]{1,0:T(4,128)(4,1)} %copy-done.167) | copy-start | bytes 8452
  658.1 93.1 %copy-start.119 = (f32[2,1408]{1,0:T(2,128)}, f32[2,1408]{1,0:T(2,128)S(1)}, u32[]{:S(2)}) copy-start(f32[2,1408]{1,0:T(2,128)S(1)} %broadcast_multiply_fusion.5) | copy-start | bytes 33796
  659.1 92.2 %copy-start.145 = (f32[2,1408]{1,0:T(2,128)}, f32[2,1408]{1,0:T(2,128)S(1)}, u32[]{:S(2)}) copy-start(f32[2,1408]{1,0:T(2,128)S(1)} %fusion.160) | copy-start | bytes 33796
  722.2 72.6 %all-reduce.41.cloned.1.call-start = ((), (), s32[]{:S(2)}) async-start(), calls=%async_computation.11 | async-start | bytes 4816896 | tf_op jit(solution)/shard_map/psum | solution.py:69
  771.8 271.9 %all-reduce.43.cloned.1.call-start = ((), (), s32[]{:S(2)}) async-start(), calls=%async_computation.12 | async-start | bytes 4816896 | tf_op jit(solution)/shard_map/psum | solution.py:69
  1020.6 84.1 %all-reduce.45.cloned.1.call-start = ((), (), s32[]{:S(2)}) async-start(), calls=%async_computation.13 | async-start | bytes 983040 | tf_op jit(solution)/shard_map/psum | solution.py:69
  1020.7 27.6 %copy-start.131 = (f32[2,1568]{1,0:T(2,128)S(1)}, f32[2,1568]{1,0:T(2,128)}, u32[]{:S(2)}) copy-start(f32[2,1568]{1,0:T(2,128)} %copy-done.130) | copy-start | bytes 37636
  1020.7 27.6 %copy-start.123 = (f32[2,1568]{1,0:T(2,128)S(1)}, f32[2,1568]{1,0:T(2,128)}, u32[]{:S(2)}) copy-start(f32[2,1568]{1,0:T(2,128)} %copy-done.122) | copy-start | bytes 37636
  1076.3 76.1 %all-reduce.47.cloned.1.call-start = ((), (), s32[]{:S(2)}) async-start(), calls=%async_computation.14 | async-start | bytes 983040 | tf_op jit(solution)/shard_map/psum | solution.py:69
  1110.1 45.5 %copy-start.36 = (f32[2,160,768]{2,1,0:T(8,128)}, f32[2,160,768]{2,1,0:T(8,128)S(1)}, u32[]{:S(2)}) copy-start(f32[2,160,768]{2,1,0:T(8,128)S(1)} %get-tuple-element.461) | copy-start | bytes 2949124
  1128.2 24.2 %copy-start.14 = (f32[2,160,768]{2,1,0:T(8,128)S(1)}, f32[2,160,768]{2,1,0:T(8,128)}, u32[]{:S(2)}) copy-start(f32[2,160,768]{2,1,0:T(8,128)} %copy-done.13) | copy-start | bytes 2949124
  1128.2 24.2 %copy-start.144 = (f32[768]{0:T(1024)S(1)}, f32[768]{0:T(1024)}, u32[]{:S(2)}) copy-start(f32[768]{0:T(1024)} %copy-done.143) | copy-start | bytes 9220
  1128.2 24.2 %copy-start.158 = (f32[2,160]{1,0:T(2,128)S(1)}, f32[2,160]{1,0:T(2,128)}, u32[]{:S(2)}) copy-start(f32[2,160]{1,0:T(2,128)} %copy-done.157) | copy-start | bytes 3844
  1132.4 52.5 %all-reduce.49.cloned.1.call-start = ((), (), s32[]{:S(2)}) async-start(), calls=%async_computation.15 | async-start | bytes 983040 | tf_op jit(solution)/shard_map/psum | solution.py:69
  1164.9 66.6 %all-reduce.51.cloned.1.call-start = ((), (), s32[]{:S(2)}) async-start(), calls=%async_computation.16 | async-start | bytes 983040 | tf_op jit(solution)/shard_map/psum | solution.py:69
  1211.6 212.0 %all-reduce.55.cloned.1.call-start = ((), (), s32[]{:S(2)}) async-start(), calls=%async_computation.18 | async-start | bytes 860160 | tf_op jit(solution)/shard_map/psum | solution.py:400
  1280.2 33.7 %copy-start.66 = (f32[384,768,1]{1,0,2:T(8,128)S(1)}, f32[384,768,1]{1,0,2:T(8,128)}, u32[]{:S(2)}) copy-start(f32[384,768,1]{1,0,2:T(8,128)} %get-tuple-element.555) | copy-start | bytes 3538948
  1313.9 254.6 %all-reduce.53.cloned.1.call-start = ((), (), s32[]{:S(2)}) async-start(), calls=%async_computation.17 | async-start | bytes 253952 | tf_op jit(solution)/shard_map/psum | solution.py:409
  1334.6 100.4 %copy-start.28 = (bf16[1,1,3456,384]{3,2,1,0:T(8,128)(2,1)S(1)}, bf16[1,1,3456,384]{3,2,1,0:T(8,128)(2,1)}, u32[]{:S(2)}) copy-start(bf16[1,1,3456,384]{3,2,1,0:T(8,128)(2,1)} %param.39) | copy-start | bytes 7962628
  1337.2 103.7 %copy-start.164 = (f32[14976]{0:T(1024)}, f32[14976]{0:T(1024)S(1)}, u32[]{:S(2)}) copy-start(f32[14976]{0:T(1024)S(1)} %constant_dynamic-update-slice_fusion.20) | copy-start | bytes 179716
  1576.9 32.4 %copy-start.116 = (f32[1,216,384]{2,1,0:T(8,128)S(1)}, f32[1,216,384]{2,1,0:T(8,128)}, u32[]{:S(2)}) copy-start(f32[1,216,384]{2,1,0:T(8,128)} %param.35) | copy-start | bytes 995332
  1576.9 32.4 %copy-start.134 = (f32[8,384]{1,0:T(8,128)S(1)}, f32[8,384]{1,0:T(8,128)}, u32[]{:S(2)}) copy-start(f32[8,384]{1,0:T(8,128)} %get-tuple-element.445) | copy-start | bytes 36868
  1576.9 33.1 %copy-start.106 = (f32[1,216,384]{2,1,0:T(8,128)S(1)}, f32[1,216,384]{2,1,0:T(8,128)}, u32[]{:S(2)}) copy-start(f32[1,216,384]{2,1,0:T(8,128)} %param.31) | copy-start | bytes 995332
  1576.9 33.9 %copy-start.98 = (f32[1,624,768]{2,1,0:T(8,128)S(1)}, f32[1,624,768]{2,1,0:T(8,128)}, u32[]{:S(2)}) copy-start(f32[1,624,768]{2,1,0:T(8,128)} %param.34) | copy-start | bytes 5750788
  (213 other events, 1450.3 us)
Sparse Core Ops, SparseCore 0:
  11.4 180.7 all-gather.2
  195.1 16.8 all-reduce.22
  230.5 16.8 all-reduce.24
  263.3 19.8 all-reduce.26
  295.2 19.8 all-reduce.28
  331.7 19.8 all-reduce.30
  354.8 65.4 all-gather.4
  423.2 17.1 all-reduce.32
  540.2 22.8 all-reduce.34
  606.3 22.8 all-reduce.36
  722.3 21.2 all-reduce.38
  771.9 22.8 all-reduce.40
  1020.8 22.8 all-reduce.42
  1076.4 19.8 all-reduce.44
  1132.5 19.8 all-reduce.46
  1165.0 19.8 all-reduce.48
  1211.7 19.8 all-reduce.50
  1314.0 109.4 all-reduce.54
  1463.5 104.9 all-reduce.52
where the time goes:
time: 1640 us; the launch traced here: 1620 us
  waiting for transfers between devices  629 us (38%)
  matrix products  514 us (31%)
  other arithmetic  260 us (16%)
  local copies, waits for them, and re-layouts  150 us (9%)
  blocking collectives  46.3 us (3%)
  between operations  19.5 us (1%)
    all_gather x1, waiting for transfers between devices, per_device(): lax.all_gather(enc_weights.astype(jnp.bfloat16), 'dp', axis=1, tiled=True)  174 us
    psum x7, waiting for transfers between devices, pair_backward(): lax.psum(partial_value.astype(jnp.bfloat16), 'tensor').astype(jnp.float32)  107 us
    psum x1, waiting for transfers between devices, per_device(): lax.psum((jnp.einsum('rx,xc->rc', enc_basis, enc_comb, precision=highest_...  105 us
    psum x8, waiting for transfers between devices, pair_forward(): lax.psum(partial_value.astype(jnp.bfloat16), 'tensor').astype(jnp.float32)  91.1 us
    psum x1, waiting for transfers between devices, per_device(): lax.psum((enc_left, dec_left, split_grad, shared_grad), 'dp')  86.3 us
    dot_general x20, matrix products, project_back(): jnp.einsum('nsc,ec->nse', left, right, preferred_element_type=jnp.float32)  70.2 us
    dot_general x21, matrix products, weight_grad(): jnp.einsum('nsc,nse->ce', left, right, preferred_element_type=jnp.float32)  68.4 us
    all_gather x1, waiting for transfers between devices, per_device(): lax.all_gather(dec_weights.astype(jnp.bfloat16), 'dp', axis=1, tiled=True)  66.3 us
  transfers between devices with their start and end apart: 19, of which 16 were waited for; matrix products, arithmetic and copies ran while one was open for 10% of the time, Pallas kernels for 0%

commit v1 on v0

v1 whole, which is shorter than its diff:
```python
import math

import jax
import jax.numpy as jnp
from jax import lax
from jax.experimental import pallas as pl
from jax.experimental.pallas import tpu as pltpu
from jax.sharding import PartitionSpec as P

D = 768
HEAD_DIM = 64
FF = 3072
DD = 384
DFF = 1536
PIX = 1536
TUBES = 1568
VIS = 160
MASKED = 1408
RANK = 8

f32 = jnp.float32
bf16 = jnp.bfloat16
highest_precision = lax.Precision.HIGHEST
norm_eps = 1e-06
momentum_keep = 0.9
step_rate = 1000.0
LOG2E = 1.4426950408889634
SCORE = HEAD_DIM ** (-0.5)
BIG_VMEM = 56 << 20


def nn(left, right):
    return lax.dot_general(left, right, (((1,), (0,)), ((), ())), preferred_element_type=f32)


def nt(left, right):
    return lax.dot_general(left, right, (((1,), (1,)), ((), ())), preferred_element_type=f32)


def tn(left, right):
    return lax.dot_general(left, right, (((0,), (0,)), ((), ())), preferred_element_type=f32)


def col_sum(value):
    return jnp.sum(value, 0, keepdims=True)


def norm_parts(stream):
    center = stream - jnp.mean(stream, -1, keepdims=True)
    rate = lax.rsqrt(jnp.mean(center * center, -1, keepdims=True) + norm_eps)
    return center * rate, rate


def norm_back(grad, gain, unit, rate):
    grad_unit = grad * gain
    return rate * (
        grad_unit
        - jnp.mean(grad_unit, -1, keepdims=True)
        - unit * jnp.mean(grad_unit * unit, -1, keepdims=True)
    )


def gelu_pair(before):
    cdf_tail = jnp.exp(-0.5 * before * before)
    size = jnp.abs(before) * (2.0 ** -0.5)
    t = 1.0 / (1.0 + 0.3275911 * size)
    poly = t * (
        0.254829592 + t * (-0.284496736 + t * (1.421413741 + t * (-1.453152027 + t * 1.061405429)))
    )
    tail = 0.5 * poly * cdf_tail
    cdf = jnp.where(before < 0, tail, 1.0 - tail)
    return before * cdf, cdf + before * cdf_tail * (1.0 / math.sqrt(2.0 * math.pi))


def split3(value):
    high = value.astype(bf16)
    rest = value - high.astype(f32)
    middle = rest.astype(bf16)
    low = (rest - middle.astype(f32)).astype(bf16)
    return jnp.concatenate([high, middle, low], 0)


def fold3(value):
    rows = value.shape[0] // 3
    return value[:rows] + value[rows : 2 * rows] + value[2 * rows :]


def sinusoid_at(place, width):
    column = jnp.arange(width)
    rate = jnp.exp(-(2 * (column // 2)).astype(f32) * (math.log(10000.0) / width))
    angle = place.astype(f32)[:, None] * rate[None, :]
    return jnp.where(column % 2 == 0, jnp.sin(angle), jnp.cos(angle))


def params(**more):
    return pltpu.CompilerParams(vmem_limit_bytes=BIG_VMEM, **more)


def whole(shape):
    return pl.BlockSpec(shape, lambda *_: (0,) * len(shape))


PICK_ROWS = 224


def pick_kernel(order_ref, tubes_ref, out_ref):
    column = lax.broadcasted_iota(jnp.int32, (1, TUBES), 1)
    hot = jnp.where(order_ref[0] == column, 1.0, 0.0).astype(bf16)
    out_ref[0] = nn(hot, tubes_ref[0]).astype(bf16)


def pick(order, tubes):
    clips, _, width = tubes.shape
    return pl.pallas_call(
        pick_kernel,
        grid=(clips, TUBES // PICK_ROWS),
        in_specs=[
            pl.BlockSpec((1, PICK_ROWS, 1), lambda c, i: (c, i, 0)),
            pl.BlockSpec((1, TUBES, width), lambda c, i: (c, 0, 0)),
        ],
        out_specs=pl.BlockSpec((1, PICK_ROWS, width), lambda c, i: (c, i, 0)),
        out_shape=jax.ShapeDtypeStruct(tubes.shape, bf16),
        compiler_params=params(),
        name="pick_tubes",
    )(order[:, :, None], tubes)


QKV_ROWS = 392


def qkv_kernel(x_ref, g_ref, b_ref, w_ref, bias_ref, h_ref, qkv_ref):
    unit, _ = norm_parts(x_ref[...])
    h = (unit * g_ref[...] + b_ref[...]).astype(bf16)
    h_ref[...] = h
    qkv_ref[...] = (nt(h, w_ref[...]) + bias_ref[...]).astype(bf16)


def decoder_qkv(x, gain, shift, weights, bias):
    rows = lambda width: pl.BlockSpec((QKV_ROWS, width), lambda i: (i, 0))
    return pl.pallas_call(
        qkv_kernel,
        grid=(TUBES // QKV_ROWS,),
        in_specs=[
            rows(DD),
            whole((1, DD)),
            whole((1, DD)),
            whole((3 * DD, DD)),
            whole((1, 3 * DD)),
        ],
        out_specs=[rows(DD), rows(3 * DD)],
        out_shape=[
            jax.ShapeDtypeStruct((TUBES, DD), bf16),
            jax.ShapeDtypeStruct((TUBES, 3 * DD), bf16),
        ],
        compiler_params=params(),
        name="decoder_qkv",
    )(x, gain, shift, weights, bias)


FWD_ROWS = 392
BWD_ROWS = 256
PAIRS = DD // 128


def half_lane(index):
    return lax.broadcasted_iota(jnp.int32, (1, 128), 1) // HEAD_DIM == index


def attend_kernel(q_ref, k_ref, v_ref, o_ref, lse_ref):
    q = q_ref[...]
    k = k_ref[...]
    v_one = jnp.concatenate([v_ref[...], jnp.ones((TUBES, 128), bf16)], 1)
    mixed, logs = [], []
    for head in range(2):
        scores = nt(jnp.where(half_lane(head), q, jnp.zeros_like(q)), k)
        top = jnp.max(scores, 1, keepdims=True)
        expo = jnp.exp2((scores - top) * (SCORE * LOG2E)).astype(bf16)
        both = nn(expo, v_one)
        total = both[:, 128:]
        mixed.append(both[:, :128] / total)
        logs.append(top * (SCORE * LOG2E) + jnp.log2(total))
    o_ref[...] = jnp.where(half_lane(0), mixed[0], mixed[1])
    lse_ref[0] = jnp.where(half_lane(0), logs[0], logs[1])


def attend(qkv):
    return pl.pallas_call(
        attend_kernel,
        grid=(PAIRS, TUBES // FWD_ROWS),
        in_specs=[
            pl.BlockSpec((FWD_ROWS, 128), lambda p, i: (i, p)),
            pl.BlockSpec((TUBES, 128), lambda p, i: (0, PAIRS + p)),
            pl.BlockSpec((TUBES, 128), lambda p, i: (0, 2 * PAIRS + p)),
        ],
        out_specs=[
            pl.BlockSpec((FWD_ROWS, 128), lambda p, i: (i, p)),
            pl.BlockSpec((1, FWD_ROWS, 128), lambda p, i: (p, i, 0)),
        ],
        out_shape=[
            jax.ShapeDtypeStruct((TUBES, DD), f32),
            jax.ShapeDtypeStruct((PAIRS, TUBES, 128), f32),
        ],
        compiler_params=params(),
        name="attend",
    )(qkv, qkv, qkv)


def attend_back_kernel(
    q_ref, k_ref, v_ref, o_ref, do_ref, lse_ref, dq_ref, dk_ref, dv_ref, k_turned, dk_sum, dv_sum
):
    step = pl.program_id(1)

    @pl.when(step == 0)
    def _():
        k_turned[...] = k_ref[...].T
        dk_sum[...] = jnp.zeros_like(dk_sum)
        dv_sum[...] = jnp.zeros_like(dv_sum)

    valid = lax.broadcasted_iota(jnp.int32, (BWD_ROWS, 1), 0) + step * BWD_ROWS < TUBES
    zero = jnp.zeros((), bf16)
    q = jnp.where(valid, q_ref[...], zero)
    grad = jnp.where(valid, do_ref[...], zero)
    dots = jnp.where(valid, o_ref[...], 0.0) * grad.astype(f32)
    logs = jnp.where(valid, lse_ref[0], 0.0).T
    select = (
        lax.broadcasted_iota(jnp.int32, (8, 128), 1) // HEAD_DIM
        == lax.broadcasted_iota(jnp.int32, (8, 128), 0)
    ).astype(f32)
    row_total = lax.dot_general(
        select, dots, (((1,), (1,)), ((), ())), precision=highest_precision,
        preferred_element_type=f32,
    )
    k = k_ref[...]
    v = v_ref[...]
    turned = []
    for head in range(2):
        mask = half_lane(head)
        q_head = jnp.where(mask, q, zero)
        grad_head = jnp.where(mask, grad, zero)
        low = head * HEAD_DIM
        probs = jnp.exp2(nt(k, q_head) * (SCORE * LOG2E) - logs[low : low + 1])
        grad_scores = (probs * (nt(v, grad_head) - row_total[head : head + 1])).astype(bf16)
        dv_sum[...] += nn(probs.astype(bf16), grad_head)
        dk_sum[...] += nn(grad_scores, q_head)
        turned.append(nn(k_turned[low : low + HEAD_DIM], grad_scores))
    dq_ref[...] = (jnp.concatenate(turned, 0).T * SCORE).astype(bf16)

    @pl.when(step == pl.num_programs(1) - 1)
    def _():
        dk_ref[...] = (dk_sum[...] * SCORE).astype(bf16)
        dv_ref[...] = dv_sum[...].astype(bf16)


def attend_back(qkv, mixed, grad_mixed, logs):
    some = pl.BlockSpec((BWD_ROWS, 128), lambda p, i: (i, p))
    full = pl.BlockSpec((TUBES, 128), lambda p, i: (0, p))
    return pl.pallas_call(
        attend_back_kernel,
        grid=(PAIRS, pl.cdiv(TUBES, BWD_ROWS)),
        in_specs=[
            some,
            pl.BlockSpec((TUBES, 128), lambda p, i: (0, PAIRS + p)),
            pl.BlockSpec((TUBES, 128), lambda p, i: (0, 2 * PAIRS + p)),
            some,
            some,
            pl.BlockSpec((1, BWD_ROWS, 128), lambda p, i: (p, i, 0)),
        ],
        out_specs=[some, full, full],
        out_shape=[jax.ShapeDtypeStruct((TUBES, DD), bf16)] * 3,
        scratch_shapes=[
            pltpu.VMEM((128, TUBES), bf16),
            pltpu.VMEM((TUBES, 128), f32),
            pltpu.VMEM((TUBES, 128), f32),
        ],
        compiler_params=params(),
        name="attend_back",
    )(qkv, qkv, qkv, mixed, grad_mixed, logs)


TOKEN_ROWS = 224
CHUNK = 384
CHUNKS = DFF // CHUNK


def token_kernel(
    a_ref, x_ref, pix_ref, scal_ref, vec_ref, bu_ref, bh_ref, wo_ref, wd_ref, wu_ref, wh_ref,
    da_ref, dx1_ref,
    g_wo_ref, g_wd_ref, g_wu_ref, g_wh_ref, gvec_ref, gbu_ref, gbh_ref, loss_ref,
    slope,
):
    step = pl.program_id(0)
    sums = (g_wo_ref, g_wd_ref, g_wu_ref, g_wh_ref, gvec_ref, gbu_ref, gbh_ref, loss_ref)

    @pl.when(step == 0)
    def _():
        for ref in sums:
            ref[...] = jnp.zeros_like(ref)

    bo, g2, b2, bd, gf, sf = (vec_ref[index : index + 1] for index in range(6))
    a = a_ref[...].astype(bf16)
    x1 = x_ref[...] + (nn(a, wo_ref[...]) + bo)
    unit2, rate2 = norm_parts(x1)
    h2 = (unit2 * g2 + b2).astype(bf16)
    out = x1 + bd
    active = []
    for chunk in range(CHUNKS):
        part = pl.ds(chunk * CHUNK, CHUNK)
        value, slope_part = gelu_pair(nt(h2, wu_ref[part]) + bu_ref[:, part])
        slope[:, part] = slope_part
        active.append(value.astype(bf16))
        out = out + nn(active[-1], wd_ref[part])
    unit_f, rate_f = norm_parts(out)
    final = (unit_f * gf + sf).astype(bf16)
    pixels = [pix_ref[:, pl.ds(chunk * CHUNK, CHUNK)].astype(f32) for chunk in range(CHUNKS)]
    center = sum(jnp.sum(part, 1, keepdims=True) for part in pixels) * (1.0 / PIX)
    square = sum(jnp.sum(part * part, 1, keepdims=True) for part in pixels) * (1.0 / PIX)
    spread = lax.rsqrt(square - center * center + norm_eps)
    row = lax.broadcasted_iota(jnp.int32, (TOKEN_ROWS, 1), 0) + step * TOKEN_ROWS
    counted = jnp.where(row >= VIS, scal_ref[0:1, 0:1], 0.0)
    rate = jnp.where(row >= VIS, scal_ref[1:2, 0:1], 0.0)
    grad_final = jnp.zeros((TOKEN_ROWS, DD), f32)
    for chunk in range(CHUNKS):
        part = pl.ds(chunk * CHUNK, CHUNK)
        target = (pixels[chunk] - center) * spread
        miss = nt(final, wh_ref[part]) + bh_ref[:, part] - target
        loss_ref[:, part] += col_sum(counted * miss * miss)
        grad_guess = (rate * miss).astype(bf16)
        gbh_ref[:, part] += col_sum(grad_guess.astype(f32))
        g_wh_ref[part] += tn(grad_guess, final)
        grad_final = grad_final + nn(grad_guess, wh_ref[part])
    grad_out = norm_back(grad_final, gf, unit_f, rate_f)
    out_low = grad_out.astype(bf16)
    grad_h2 = jnp.zeros((TOKEN_ROWS, DD), f32)
    for chunk in range(CHUNKS):
        part = pl.ds(chunk * CHUNK, CHUNK)
        g_wd_ref[part] += tn(active[chunk], out_low)
        grad_before = (slope[:, part] * nt(out_low, wd_ref[part])).astype(bf16)
        gbu_ref[:, part] += col_sum(grad_before.astype(f32))
        g_wu_ref[part] += tn(grad_before, h2)
        grad_h2 = grad_h2 + nn(grad_before, wu_ref[part])
    grad_x1 = grad_out + norm_back(grad_h2, g2, unit2, rate2)
    x1_low = grad_x1.astype(bf16)
    g_wo_ref[...] += tn(a, x1_low)
    da_ref[...] = nt(x1_low, wo_ref[...]).astype(bf16)
    dx1_ref[...] = grad_x1
    gvec_ref[0:1] += col_sum(x1_low.astype(f32))
    gvec_ref[1:2] += col_sum(grad_h2 * unit2)
    gvec_ref[2:3] += col_sum(grad_h2)
    gvec_ref[3:4] += col_sum(out_low.astype(f32))
    gvec_ref[4:5] += col_sum(grad_final * unit_f)
    gvec_ref[5:6] += col_sum(grad_final)


def decoder_tokens(mixed, x, pixels, scal, vecs, bu, bh, wo, wd, wu, wh):
    rows = lambda width: pl.BlockSpec((TOKEN_ROWS, width), lambda i: (i, 0))
    sums = [(DD, DD), (DFF, DD), (DFF, DD), (PIX, DD), (8, DD), (1, DFF), (1, PIX), (1, PIX)]
    return pl.pallas_call(
        token_kernel,
        grid=(TUBES // TOKEN_ROWS,),
        in_specs=[
            rows(DD),
            rows(DD),
            rows(PIX),
            whole((8, 128)),
            whole((8, DD)),
            whole((1, DFF)),
            whole((1, PIX)),
            whole((DD, DD)),
            whole((DFF, DD)),
            whole((DFF, DD)),
            whole((PIX, DD)),
        ],
        out_specs=[rows(DD), rows(DD)] + [whole(shape) for shape in sums],
        out_shape=[
            jax.ShapeDtypeStruct((TUBES, DD), bf16),
            jax.ShapeDtypeStruct((TUBES, DD), f32),
        ]
        + [jax.ShapeDtypeStruct(shape, f32) for shape in sums],
        scratch_shapes=[pltpu.VMEM((TOKEN_ROWS, DFF), f32)],
        compiler_params=params(),
        name="decoder_tokens",
    )(mixed, x, pixels, scal, vecs, bu, bh, wo, wd, wu, wh)


def qkv_back_kernel(
    dq_ref, dk_ref, dv_ref, h_ref, x_ref, dx1_ref, g_ref, w_ref,
    dx_ref, gw_ref, gvec_ref,
):
    step = pl.program_id(0)

    @pl.when(step == 0)
    def _():
        gw_ref[...] = jnp.zeros_like(gw_ref)
        gvec_ref[...] = jnp.zeros_like(gvec_ref)

    h = h_ref[...]
    grads = (dq_ref[...], dk_ref[...], dv_ref[...])
    grad_h = jnp.zeros((QKV_ROWS, DD), f32)
    for index, grad in enumerate(grads):
        part = pl.ds(index * DD, DD)
        gw_ref[part] += tn(grad, h)
        grad_h = grad_h + nn(grad, w_ref[part])
    unit, rate = norm_parts(x_ref[...])
    grad_x = dx1_ref[...] + norm_back(grad_h, g_ref[...], unit, rate)
    dx_ref[...] = grad_x
    row = lax.broadcasted_iota(jnp.int32, (QKV_ROWS, 1), 0) + step * QKV_ROWS
    gvec_ref[0:1] += col_sum(grads[0].astype(f32))
    gvec_ref[1:2] += col_sum(grads[2].astype(f32))
    gvec_ref[2:3] += col_sum(grad_h * unit)
    gvec_ref[3:4] += col_sum(grad_h)
    gvec_ref[4:5] += col_sum(jnp.where(row >= VIS, grad_x, 0.0))


def decoder_qkv_back(dq, dk, dv, h, x, dx1, gain, weights):
    rows = lambda width: pl.BlockSpec((QKV_ROWS, width), lambda i: (i, 0))
    return pl.pallas_call(
        qkv_back_kernel,
        grid=(TUBES // QKV_ROWS,),
        in_specs=[rows(DD)] * 6 + [whole((1, DD)), whole((3 * DD, DD))],
        out_specs=[rows(DD), whole((3 * DD, DD)), whole((8, DD))],
        out_shape=[
            jax.ShapeDtypeStruct((TUBES, DD), f32),
            jax.ShapeDtypeStruct((3 * DD, DD), f32),
            jax.ShapeDtypeStruct((8, DD), f32),
        ],
        compiler_params=params(),
        name="decoder_qkv_back",
    )(dq, dk, dv, h, x, dx1, gain, weights)


HALF = D // 2
HALF_FF = FF // 2
LAYER_ROWS = 4 * HALF + 2 * HALF_FF
AT_O, AT_D, AT_Q, AT_U = 0, HALF, HALF + HALF_FF, HALF + HALF_FF + 3 * HALF
STAGES = ((AT_Q, 3 * HALF), (AT_O, HALF), (AT_U, HALF_FF), (AT_D, HALF_FF))


def stage_copies(sources, start, held, sems):
    return [
        [
            pltpu.make_async_copy(
                sources[group].at[pl.ds(start + at, size)],
                held.at[group, pl.ds(at, size)],
                sems.at[group, stage],
            )
            for group in range(2)
        ]
        for stage, (at, size) in enumerate(STAGES)
    ]


def encoder_kernel(
    start, x_ref, vec_ref, bqkv_ref, bu_ref, own_ref, other_ref,
    out_ref, h_ref, qkv_ref, a_ref, x1_ref, h2_ref, u_ref, slope_ref,
    held, sems,
):
    copies = stage_copies((own_ref, other_ref), start, held, sems)
    for stage in copies:
        for copy in stage:
            copy.start()

    def wait(stage):
        for copy in copies[stage]:
            copy.wait()

    g1, b1, bo, g2, b2, bd = (vec_ref[index : index + 1] for index in range(6))
    x = x_ref[...]
    unit, _ = norm_parts(x)
    h = (unit * g1 + b1).astype(bf16)
    h_ref[...] = h
    wait(0)
    for kind in range(3):
        for group in range(2):
            part = pl.ds((2 * kind + group) * HALF, HALF)
            rows = pl.ds(AT_Q + kind * HALF, HALF)
            qkv_ref[:, part] = (nt(h, held[group, rows]) + bqkv_ref[:, part]).astype(bf16)
    for pair in range(D // 128):
        q, k, v = (qkv_ref[:, pl.ds(kind * D + pair * 128, 128)] for kind in range(3))
        v_one = jnp.concatenate([v, jnp.ones((VIS, 128), bf16)], 1)
        mixed = []
        for head in range(2):
            scores = nt(jnp.where(half_lane(head), q, jnp.zeros_like(q)), k)
            top = jnp.max(scores, 1, keepdims=True)
            expo = jnp.exp2((scores - top) * (SCORE * LOG2E)).astype(bf16)
            both = nn(expo, v_one)
            mixed.append(both[:, :128] / both[:, 128:])
        a_ref[:, pl.ds(pair * 128, 128)] = jnp.where(half_lane(0), mixed[0], mixed[1]).astype(bf16)
    wait(1)
    x1 = x + bo
    for group in range(2):
        x1 = x1 + nn(a_ref[:, pl.ds(group * HALF, HALF)], held[group, pl.ds(AT_O, HALF)])
    x1_ref[...] = x1
    unit2, _ = norm_parts(x1)
    h2 = (unit2 * g2 + b2).astype(bf16)
    h2_ref[...] = h2
    wait(2)
    wait(3)
    out = x1 + bd
    for group in range(2):
        for chunk in range(HALF_FF // CHUNK):
            part = pl.ds(group * HALF_FF + chunk * CHUNK, CHUNK)
            before = nt(h2, held[group, pl.ds(AT_U + chunk * CHUNK, CHUNK)]) + bu_ref[:, part]
            value, slope = gelu_pair(before)
            slope_ref[:, part] = slope
            active = value.astype(bf16)
            u_ref[:, part] = active
            out = out + nn(active, held[group, pl.ds(AT_D + chunk * CHUNK, CHUNK)])
    out_ref[...] = out


def any_spec():
    return pl.BlockSpec(memory_space=pl.ANY)


def encoder_layer(start, x, vecs, bqkv, bu, own, other, name):
    shapes = [
        ((VIS, D), f32),
        ((VIS, D), bf16),
        ((VIS, 3 * D), bf16),
        ((VIS, D), bf16),
        ((VIS, D), f32),
        ((VIS, D), bf16),
        ((VIS, FF), bf16),
        ((VIS, FF), f32),
    ]
    return pl.pallas_call(
        lambda *refs: encoder_kernel(start, *refs),
        in_specs=[pl.BlockSpec(memory_space=pltpu.VMEM)] * 4 + [any_spec()] * 2,
        out_specs=[pl.BlockSpec(memory_space=pltpu.VMEM)] * len(shapes),
        out_shape=[jax.ShapeDtypeStruct(shape, kind) for shape, kind in shapes],
        scratch_shapes=[
            pltpu.VMEM((2, LAYER_ROWS, D), bf16),
            pltpu.SemaphoreType.DMA((2, len(STAGES))),
        ],
        compiler_params=params(),
        name=name,
    )(x, vecs, bqkv, bu, own, other)


def encoder_back_kernel(
    start, dout_ref, x_ref, vec_ref, qkv_ref, a_ref, x1_ref, u_ref, slope_ref, own_ref, other_ref,
    dx_ref, left_ref, low_ref, gvec_ref, gbu_ref, gbq_ref,
    held, sems, da, dqkv,
):
    copies = stage_copies((own_ref, other_ref), start, held, sems)
    for stage in (3, 2, 1, 0):
        for copy in copies[stage]:
            copy.start()

    def wait(stage):
        for copy in copies[stage]:
            copy.wait()

    g1, b1, bo, g2, b2, bd = (vec_ref[index : index + 1] for index in range(6))
    grad_out = dout_ref[...]
    out_low = grad_out.astype(bf16)
    low_ref[1] = out_low
    unit2, rate2 = norm_parts(x1_ref[...])
    grad_h2 = jnp.zeros((VIS, D), f32)
    wait(3)
    wait(2)
    for group in range(2):
        for chunk in range(HALF_FF // CHUNK):
            part = pl.ds(group * HALF_FF + chunk * CHUNK, CHUNK)
            grad_active = nt(out_low, held[group, pl.ds(AT_D + chunk * CHUNK, CHUNK)])
            grad_before = (slope_ref[:, part] * grad_active).astype(bf16)
            left_ref[group, :, pl.ds(AT_U + chunk * CHUNK, CHUNK)] = grad_before
            left_ref[group, :, pl.ds(AT_D + chunk * CHUNK, CHUNK)] = u_ref[:, part]
            gbu_ref[:, part] = col_sum(grad_before.astype(f32))
            grad_h2 = grad_h2 + nn(grad_before, held[group, pl.ds(AT_U + chunk * CHUNK, CHUNK)])
    grad_x1 = grad_out + norm_back(grad_h2, g2, unit2, rate2)
    x1_low = grad_x1.astype(bf16)
    low_ref[0] = x1_low
    wait(1)
    for group in range(2):
        part = pl.ds(group * HALF, HALF)
        da[:, part] = nt(x1_low, held[group, pl.ds(AT_O, HALF)]).astype(bf16)
        left_ref[group, :, pl.ds(AT_O, HALF)] = a_ref[:, part]
    zero = jnp.zeros((), bf16)
    for pair in range(D // 128):
        lanes = pl.ds(pair * 128, 128)
        q, k, v = (qkv_ref[:, pl.ds(kind * D + pair * 128, 128)] for kind in range(3))
        grad = da[:, lanes]
        dq = dk = dv = jnp.zeros((VIS, 128), f32)
        for head in range(2):
            mask = half_lane(head)
            q_head = jnp.where(mask, q, zero)
            grad_head = jnp.where(mask, grad, zero)
            scores = nt(q_head, k) * SCORE
            expo = jnp.exp(scores - jnp.max(scores, 1, keepdims=True))
            probs = expo / jnp.sum(expo, 1, keepdims=True)
            grad_probs = nt(grad_head, v)
            row_total = jnp.sum(probs * grad_probs, 1, keepdims=True)
            grad_scores = (probs * (grad_probs - row_total)).astype(bf16)
            dv = dv + tn(probs.astype(bf16), grad_head)
            dk = dk + tn(grad_scores, q_head)
            dq = dq + nn(grad_scores, jnp.where(mask, k, zero))
        dqkv[:, lanes] = (dq * SCORE).astype(bf16)
        dqkv[:, pl.ds(D + pair * 128, 128)] = (dk * SCORE).astype(bf16)
        dqkv[:, pl.ds(2 * D + pair * 128, 128)] = dv.astype(bf16)
    wait(0)
    grad_h = jnp.zeros((VIS, D), f32)
    for kind in range(3):
        for group in range(2):
            grad = dqkv[:, pl.ds((2 * kind + group) * HALF, HALF)]
            rows = pl.ds(AT_Q + kind * HALF, HALF)
            left_ref[group, :, rows] = grad
            grad_h = grad_h + nn(grad, held[group, rows])
    unit, rate = norm_parts(x_ref[...])
    dx_ref[...] = grad_x1 + norm_back(grad_h, g1, unit, rate)
    gbq_ref[0:1] = col_sum(dqkv[:, pl.ds(0, D)].astype(f32))
    gbq_ref[1:2] = col_sum(dqkv[:, pl.ds(2 * D, D)].astype(f32))
    gvec_ref[0:1] = col_sum(grad_h * unit)
    gvec_ref[1:2] = col_sum(grad_h)
    gvec_ref[2:3] = col_sum(x1_low.astype(f32))
    gvec_ref[3:4] = col_sum(grad_h2 * unit2)
    gvec_ref[4:5] = col_sum(grad_h2)
    gvec_ref[5:6] = col_sum(out_low.astype(f32))
    gvec_ref[6:8] = jnp.zeros((2, D), f32)


def encoder_layer_back(start, grad, x, vecs, kept, own, other, name):
    _, h, qkv, a, x1, h2, u, slope = kept
    shapes = [
        ((VIS, D), f32),
        ((2, VIS, LAYER_ROWS), bf16),
        ((2, VIS, D), bf16),
        ((8, D), f32),
        ((1, FF), f32),
        ((2, D), f32),
    ]
    dx, left, low, gvec, gbu, gbq = pl.pallas_call(
        lambda *refs: encoder_back_kernel(start, *refs),
        in_specs=[pl.BlockSpec(memory_space=pltpu.VMEM)] * 8 + [any_spec()] * 2,
        out_specs=[pl.BlockSpec(memory_space=pltpu.VMEM)] * len(shapes),
        out_shape=[jax.ShapeDtypeStruct(shape, kind) for shape, kind in shapes],
        scratch_shapes=[
            pltpu.VMEM((2, LAYER_ROWS, D), bf16),
            pltpu.SemaphoreType.DMA((2, len(STAGES))),
            pltpu.VMEM((VIS, D), bf16),
            pltpu.VMEM((VIS, 3 * D), bf16),
        ],
        compiler_params=params(),
        name=name,
    )(grad, x, vecs, qkv, a, x1, u, slope, own, other)
    right = jnp.concatenate([low, h[None], h2[None]], 0)
    return dx, left, right, gvec, gbu, gbq


ROWS = 384
ENC_BLOCKS = (D + 2 * LAYER_ROWS) // ROWS
PER_LAYER = LAYER_ROWS // ROWS
RIGHTS = 9


def right_of(block):
    inner = lax.rem(jnp.maximum(block - 2, 0), PER_LAYER)
    layer = jnp.maximum(block - 2, 0) // PER_LAYER
    kind = jnp.where(inner < 1, 1, jnp.where(inner < 5, 2, jnp.where(inner < 8, 3, 4)))
    return jnp.where(block < 2, 0, kind + 4 * layer)


def left_factor_kernel(start_ref, left_ref, right_ref, error_part_ref, out_ref):
    start = split3(start_ref[...])
    total = error_part_ref[...]
    for clip in range(2):
        inner = fold3(nt(start, right_ref[clip, 0]))
        total = total + fold3(nn(split3(inner), left_ref[clip]))
    out_ref[...] = total


def left_factor(start, left, right, error_part):
    return pl.pallas_call(
        left_factor_kernel,
        grid=(ENC_BLOCKS,),
        in_specs=[
            whole((RANK, D)),
            pl.BlockSpec((2, VIS, ROWS), lambda j: (0, 0, j)),
            pl.BlockSpec((2, 1, VIS, D), lambda j: (0, right_of(j), 0, 0)),
            pl.BlockSpec((RANK, ROWS), lambda j: (0, j)),
        ],
        out_specs=pl.BlockSpec((RANK, ROWS), lambda j: (0, j)),
        out_shape=jax.ShapeDtypeStruct((RANK, ENC_BLOCKS * ROWS), f32),
        compiler_params=params(),
        name="left_factor",
    )(start, left, right, error_part)


def error_factor_kernel(start_ref, error_ref, out_ref):
    out_ref[...] = fold3(nt(split3(start_ref[...]), error_ref[...]))


def error_factor(start, error):
    rows, width = error.shape
    return pl.pallas_call(
        error_factor_kernel,
        grid=(rows // ROWS,),
        in_specs=[whole((RANK, width)), pl.BlockSpec((ROWS, width), lambda j: (j, 0))],
        out_specs=pl.BlockSpec((RANK, ROWS), lambda j: (0, j)),
        out_shape=jax.ShapeDtypeStruct((RANK, rows), f32),
        compiler_params=params(),
        name="error_factor",
    )(start, error)


def right_factor_kernel(basis_ref, left_ref, right_ref, error_ref, out_ref):
    @pl.when(pl.program_id(0) == 0)
    def _():
        out_ref[...] = jnp.zeros_like(out_ref)

    basis = split3(basis_ref[...])
    total = fold3(nn(basis, error_ref[...]))
    for clip in range(2):
        inner = fold3(nt(basis, left_ref[clip]))
        total = total + fold3(nn(split3(inner), right_ref[clip, 0]))
    out_ref[...] += total


def right_factor(basis, left, right, error):
    return pl.pallas_call(
        right_factor_kernel,
        grid=(ENC_BLOCKS,),
        in_specs=[
            pl.BlockSpec((RANK, ROWS), lambda j: (0, j)),
            pl.BlockSpec((2, VIS, ROWS), lambda j: (0, 0, j)),
            pl.BlockSpec((2, 1, VIS, D), lambda j: (0, right_of(j), 0, 0)),
            pl.BlockSpec((ROWS, D), lambda j: (j, 0)),
        ],
        out_specs=whole((RANK, D)),
        out_shape=jax.ShapeDtypeStruct((RANK, D), f32),
        compiler_params=params(),
        name="right_factor",
    )(basis, left, right, error)


def residue_kernel(basis_ref, factor_ref, left_ref, right_ref, error_ref, out_ref):
    total = error_ref[...].astype(f32)
    total = total - tn(*low_pairs(basis_ref[...], factor_ref[...]))
    for clip in range(2):
        total = total + tn(left_ref[clip], right_ref[clip, 0])
    out_ref[...] = total.astype(bf16)


def low_pairs(basis, factor):
    basis3 = split3(basis)
    factor3 = split3(factor)
    high, middle = basis3[:RANK], basis3[RANK : 2 * RANK]
    return (
        jnp.concatenate([high, high, middle, jnp.zeros_like(high)], 0),
        jnp.concatenate([factor3[: 2 * RANK], factor3[:RANK], jnp.zeros_like(factor3[:RANK])], 0),
    )


def residue(basis, factor, left, right, error):
    return pl.pallas_call(
        residue_kernel,
        grid=(ENC_BLOCKS,),
        in_specs=[
            pl.BlockSpec((RANK, ROWS), lambda j: (0, j)),
            whole((RANK, D)),
            pl.BlockSpec((2, VIS, ROWS), lambda j: (0, 0, j)),
            pl.BlockSpec((2, 1, VIS, D), lambda j: (0, right_of(j), 0, 0)),
            pl.BlockSpec((ROWS, D), lambda j: (j, 0)),
        ],
        out_specs=pl.BlockSpec((ROWS, D), lambda j: (j, 0)),
        out_shape=jax.ShapeDtypeStruct((ENC_BLOCKS * ROWS, D), bf16),
        compiler_params=params(),
        name="residue",
    )(basis, factor, left, right, error)


def basis_kernel(enc_ref, dec_ref, enc_out, dec_out):
    place = lax.broadcasted_iota(jnp.int32, (RANK, 1), 0)
    for ref, out in ((enc_ref, enc_out), (dec_ref, dec_out)):
        left = ref[...]
        gram = lax.dot_general(
            left, left, (((1,), (1,)), ((), ())), precision=highest_precision,
            preferred_element_type=f32,
        )
        for index in range(RANK):
            scale = lax.rsqrt(gram[index : index + 1, index : index + 1])
            column = gram[:, index : index + 1] * scale
            below = jnp.where(place > index, column, 0.0)
            pivot = left[index : index + 1] * scale
            left = jnp.where(place == index, pivot, left - below * pivot)
            gram = gram - below * (gram[index : index + 1] * scale)
        out[...] = left


def orthonormal(enc_left, dec_left):
    return pl.pallas_call(
        basis_kernel,
        in_specs=[pl.BlockSpec(memory_space=pltpu.VMEM)] * 2,
        out_specs=[pl.BlockSpec(memory_space=pltpu.VMEM)] * 2,
        out_shape=[jax.ShapeDtypeStruct(enc_left.shape, f32), jax.ShapeDtypeStruct(dec_left.shape, f32)],
        compiler_params=params(),
        name="orthonormal",
    )(enc_left, dec_left)


def cut(block, widths):
    pieces = []
    start = 0
    for width in widths:
        pieces.append(block[start : start + width])
        start = start + width
    return pieces


def swap(value):
    return lax.ppermute(value, "tensor", [(0, 1), (1, 0)])


def per_device(
    tubes,
    tube_order,
    clip_mask,
    enc_weights,
    dec_weights,
    vec_split,
    vec_shared,
    enc_moment,
    dec_moment,
    split_moment,
    shared_moment,
    enc_error,
    dec_error,
    factors,
):
    workers = lax.axis_size("dp")
    half = lax.axis_index("tensor")
    worker_index = lax.axis_index("dp")
    dec_own = lax.all_gather(dec_weights[0].astype(bf16), "dp", axis=0, tiled=True)
    enc_own = lax.all_gather(enc_weights[0].astype(bf16), "dp", axis=0, tiled=True)
    dec_other = swap(dec_own)
    enc_other = swap(enc_own)
    counted_all = clip_mask.astype(f32)
    loss_weight = MASKED * lax.psum(jnp.sum(counted_all), "dp")

    mine = lambda both: lax.dynamic_index_in_dim(both, half, 0, keepdims=False)
    theirs = lambda both: lax.dynamic_index_in_dim(both, 1 - half, 0, keepdims=False)
    order = mine(tube_order)
    counted = mine(counted_all)
    picked = pick(tube_order, tubes)
    picked_mine = mine(picked)
    picked_theirs = theirs(picked)
    pixels = jnp.concatenate([picked_mine, swap(picked_theirs)], 1)

    split_own = vec_split[0]
    split_other = swap(split_own)
    split_widths = [HALF, HALF, HALF_FF] * 2 + [DD // 2, DD // 2, DFF // 2, PIX // 2]
    split_parts = [
        jnp.concatenate(pair)[None]
        for pair in zip(cut(split_own, split_widths), cut(split_other, split_widths))
    ]
    shared = cut(vec_shared, [D] * 15 + [DD] * 9)
    dec_widths = [D // 2, DD // 2, DFF // 2, 3 * DD // 2, DFF // 2, PIX // 2]
    own_parts = cut(dec_own, dec_widths)
    other_parts = cut(dec_other, dec_widths)
    proj = jnp.where(
        half == 0,
        jnp.concatenate([own_parts[0], other_parts[0]], 0),
        jnp.concatenate([other_parts[0], own_parts[0]], 0),
    )
    d_out, d_down, d_up, head_rows = (
        jnp.concatenate([own_parts[index], other_parts[index]], 0) for index in (1, 2, 4, 5)
    )
    kinds = lambda block: block.reshape(3, DD // 2, DD)
    d_qkv = jnp.concatenate([kinds(own_parts[3]), kinds(other_parts[3])], 1).reshape(3 * DD, DD)

    visible = order[:VIS]
    pos_enc = sinusoid_at(visible, D)
    pos_dec = sinusoid_at(order, DD)

    embed = jnp.concatenate([enc_own[:D], enc_other[:D]], 0)
    stream = nn(pixels[:VIS], embed) + shared[0] + pos_enc
    kept = []
    enc_vecs = []
    for layer in range(2):
        base = 1 + 6 * layer
        vecs = jnp.concatenate(
            [jnp.stack(shared[base : base + 6]), jnp.zeros((2, D), f32)], 0
        )
        bq, bv, bu = split_parts[3 * layer : 3 * layer + 3]
        bqkv = jnp.concatenate([bq, jnp.zeros_like(bq), bv], 1)
        result = encoder_layer(
            D + layer * LAYER_ROWS, stream, vecs, bqkv, bu, enc_own, enc_other, f"encoder_{layer}"
        )
        kept.append((stream, result))
        enc_vecs.append(vecs)
        stream = result[0]
    unit_e, rate_e = norm_parts(stream)
    enc_normed = (unit_e * shared[13] + shared[14]).astype(bf16)
    latent = nn(enc_normed, proj)

    dec_start = pos_dec + jnp.concatenate(
        [latent, jnp.broadcast_to(shared[15][None], (MASKED, DD))], 0
    )
    bq, bv, bu, bh = split_parts[6:]
    h, qkv = decoder_qkv(
        dec_start, shared[16][None], shared[17][None], d_qkv,
        jnp.concatenate([bq, jnp.zeros_like(bq), bv], 1),
    )
    mixed, logs = attend(qkv)
    scal = jnp.broadcast_to(
        jnp.stack([counted, 2.0 * workers / (PIX * loss_weight) * counted] + [counted] * 6)[:, None],
        (8, 128),
    )
    dec_vecs = jnp.stack([shared[index] for index in (18, 19, 20, 21, 22, 23, 22, 23)])
    (
        grad_mixed, grad_middle, g_out, g_down, g_up, g_head, g_vec, g_bu, g_bh, loss_lanes
    ) = decoder_tokens(
        mixed, dec_start, pixels, scal, dec_vecs, bu, bh, d_out, d_down, d_up, head_rows
    )
    dq, dk, dv = attend_back(qkv, mixed, grad_mixed, logs)
    grad_start, g_qkv, g_vec1 = decoder_qkv_back(
        dq, dk, dv, h, dec_start, grad_middle, shared[16][None], d_qkv
    )
    latent_low = grad_start[:VIS].astype(bf16)
    g_proj = tn(enc_normed, latent_low)
    grad_normed = nt(latent_low, proj)
    grad = norm_back(grad_normed, shared[13], unit_e, rate_e)

    proj_parts = g_proj.reshape(2, D // 2, DD)
    halves = lambda block, index: cut(block, [block.shape[0] // 2] * 2)[index]

    def dec_half(index):
        g_kinds = g_qkv.reshape(3, 2, DD // 2, DD)[:, index].reshape(3 * DD // 2, DD)
        first = mine(proj_parts) if index == 0 else theirs(proj_parts)
        return jnp.concatenate(
            [first, halves(g_out, index), halves(g_down, index), g_kinds, halves(g_up, index),
             halves(g_head, index)],
            0,
        )

    dec_comb = dec_half(0) + swap(dec_half(1)) + dec_error[0, 0].astype(f32)

    lefts = [None, None]
    rights = [None, None]
    enc_vec_grads = [None, None]
    for layer in (1, 0):
        source, result = kept[layer]
        grad, lefts[layer], rights[layer], g_vecs, g_hidden, g_qv = encoder_layer_back(
            D + layer * LAYER_ROWS, grad, source, enc_vecs[layer], result, enc_own, enc_other,
            f"encoder_back_{layer}",
        )
        enc_vec_grads[layer] = (g_vecs, g_hidden, g_qv)
    embed_low = grad.astype(bf16)
    left = jnp.stack(
        [
            jnp.concatenate([picked_mine[:VIS], lefts[0][0], lefts[1][0]], 1),
            jnp.concatenate([picked_theirs[:VIS], swap(lefts[0][1]), swap(lefts[1][1])], 1),
        ]
    )
    right_mine = jnp.concatenate([embed_low[None]] + rights, 0)
    right = jnp.stack(
        [
            right_mine,
            jnp.concatenate([swap(embed_low)[None]] + [swap(value) for value in rights], 0),
        ]
    )

    def split_half(index):
        pieces = []
        for layer in range(2):
            _, g_hidden, g_qv = enc_vec_grads[layer]
            pieces += [
                cut(g_qv[0], [HALF] * 2)[index],
                cut(g_qv[1], [HALF] * 2)[index],
                cut(g_hidden[0], [HALF_FF] * 2)[index],
            ]
        pieces += [
            cut(g_vec1[0], [DD // 2] * 2)[index],
            cut(g_vec1[1], [DD // 2] * 2)[index],
            cut(g_bu[0], [DFF // 2] * 2)[index],
            cut(g_bh[0], [PIX // 2] * 2)[index],
        ]
        return jnp.concatenate(pieces)

    shared_grad = jnp.concatenate(
        [jnp.sum(embed_low.astype(f32), 0)]
        + [enc_vec_grads[layer][0][:6].reshape(-1) for layer in range(2)]
        + [jnp.sum(grad_normed * unit_e, 0), jnp.sum(grad_normed, 0)]
        + [g_vec1[4], g_vec1[2], g_vec1[3], g_vec[:6].reshape(-1)]
    )
    loss_part = jnp.sum(loss_lanes) / PIX
    sent = jnp.concatenate([split_half(1), shared_grad, loss_part[None]])
    local = jnp.concatenate([split_half(0), shared_grad, loss_part[None]])
    vec_local = local + swap(sent)

    enc_error_part = error_factor(factors[0, :, :D], enc_error[0, 0])
    enc_left = left_factor(factors[0, :, :D], left, right, enc_error_part)
    dec_left = jnp.einsum("rc,xc->rx", factors[0, :, D:], dec_comb, precision=highest_precision)
    enc_left, dec_left, vec_sum = lax.psum((enc_left, dec_left, vec_local), "dp")
    enc_basis, dec_basis = orthonormal(enc_left, dec_left)
    enc_rows = enc_basis.shape[1] // workers
    dec_rows = dec_basis.shape[1] // workers
    enc_owned = lax.dynamic_slice_in_dim(enc_basis, worker_index * enc_rows, enc_rows, 1)
    dec_owned = lax.dynamic_slice_in_dim(dec_basis, worker_index * dec_rows, dec_rows, 1)
    enc_right, dec_right = lax.psum(
        (
            right_factor(enc_basis, left, right, enc_error[0, 0]),
            jnp.einsum("rx,xc->rc", dec_basis, dec_comb, precision=highest_precision),
        ),
        "dp",
    )
    enc_right = enc_right / workers
    dec_right = dec_right / workers
    enc_error_new = residue(enc_basis, enc_right, left, right, enc_error[0, 0])
    dec_error_new = (
        dec_comb - jnp.einsum("rx,rc->xc", dec_basis, dec_right, precision=highest_precision)
    ).astype(bf16)
    enc_mom = momentum_keep * enc_moment[0] + jnp.einsum(
        "rx,rc->xc", enc_owned, enc_right, precision=highest_precision
    )
    dec_mom = momentum_keep * dec_moment[0] + jnp.einsum(
        "rx,rc->xc", dec_owned, dec_right, precision=highest_precision
    )
    split_len = split_own.shape[0]
    split_mom = momentum_keep * split_moment[0] + vec_sum[:split_len] / workers
    shared_mom = momentum_keep * shared_moment + vec_sum[split_len:-1] / workers
    return (
        vec_sum[-1],
        loss_weight,
        (enc_weights[0] - step_rate * enc_mom)[None],
        enc_mom[None],
        enc_error_new[None, None],
        (dec_weights[0] - step_rate * dec_mom)[None],
        dec_mom[None],
        dec_error_new[None, None],
        jnp.concatenate([enc_right, dec_right], 1)[None],
        (vec_split[0] - step_rate * split_mom)[None],
        split_mom[None],
        vec_shared - step_rate * shared_mom,
        shared_mom,
    )


def solution(mesh):
    placed = (
        P("dp", None, "tensor"),
        P("dp", None),
        P("dp"),
        P("tensor", "dp", None),
        P("tensor", "dp", None),
        P("tensor", None),
        P(),
        P("tensor", "dp", None),
        P("tensor", "dp", None),
        P("tensor", None),
        P(),
        P("dp", "tensor", None, None),
        P("dp", "tensor", None, None),
        P("tensor", None, None),
    )
    return jax.shard_map(
        per_device,
        mesh=mesh,
        in_specs=placed,
        out_specs=(
            P(),
            P(),
            P("tensor", "dp", None),
            P("tensor", "dp", None),
            P("dp", "tensor", None, None),
            P("tensor", "dp", None),
            P("tensor", "dp", None),
            P("dp", "tensor", None, None),
            P("tensor", None, None),
            P("tensor", None),
            P("tensor", None),
            P(),
            P(),
        ),
        check_vma=False,
    )
```

time: 1640 us -> 927 us (0.57)
  matrix products: 514 us -> 30.8 us
  Pallas kernels: 0 us -> 347 us
  waiting for transfers between devices: 629 us -> 288 us
  other arithmetic: 260 us -> 55.9 us
  local copies, waits for them, and re-layouts: 150 us -> 60.8 us
  blocking collectives: 46.3 us -> 116 us
    dot_general x109 -> x4, matrix products: 486 us -> 8.74 us  [the longest x2 5.25 us: nn(): lax.dot_general(left, right, (((1,), (0,)), ((), ())), preferred_element_...]
    pallas_call x0 -> x15, Pallas kernels: none -> 347 us  [the longest x1 62.7 us: decoder_tokens(): pl.pallas_call(token_kernel, grid=(TUBES // TOKEN_ROWS,), in_specs=[rows(...]
    psum x17 -> x1, waiting for transfers between devices: 389 us -> 105 us  [per_device(): lax.psum((enc_left, dec_left, vec_local), 'dp')]
    reduce_sum x51 -> x5, other arithmetic: 118 us -> 4.59 us  [the longest x1 1.23 us: norm_parts(): rate = lax.rsqrt(jnp.mean(center * center, -1, keepdims=True) + norm_eps)]
    convert_element_type x16 -> x5, other arithmetic: 90.6 us -> 3.34 us  [the longest x1 2.61 us: per_device(): enc_weights[0].astype(bf16)]
    psum x2, blocking collectives: 44.1 us -> 116 us  [the longest x1 75.4 us: per_device(): lax.psum((right_factor(enc_basis, left, right, enc_error[0, 0]), jnp.eins...]
    gather x7 -> x0, local copies, waits for them, and re-layouts: 61.6 us -> none  [the longest x2 39.1 us: per_device(): jnp.take_along_axis(tubes, masked[:, :, None], axis=1).astype(jnp.float32)]
    all_gather x2, waiting for transfers between devices: 240 us -> 182 us  [the longest x1 182 us: per_device(): lax.all_gather(enc_weights[0].astype(bf16), 'dp', axis=0, tiled=True)]
  transfers between devices with their start and end apart: 19 -> 14, of which waited for: 16 -> 3; matrix products, arithmetic and copies ran while one was open for 10% -> 9% of each run, Pallas kernels for 0% -> 7%
where the time goes in v1:
time: 927 us; the launch traced here: 920 us
  Pallas kernels  347 us (37%)
  waiting for transfers between devices  288 us (31%)
  blocking collectives  116 us (13%)
  local copies, waits for them, and re-layouts  60.8 us (7%)
  other arithmetic  55.9 us (6%)
  matrix products  30.8 us (3%)
  between operations  19.3 us (2%)
    all_gather x1, waiting for transfers between devices, per_device(): lax.all_gather(enc_weights[0].astype(bf16), 'dp', axis=0, tiled=True)  182 us
    psum x1, waiting for transfers between devices, per_device(): lax.psum((enc_left, dec_left, vec_local), 'dp')  105 us
    psum x1, blocking collectives, per_device(): lax.psum((right_factor(enc_basis, left, right, enc_error[0, 0]), jnp.eins...  75.4 us
    pallas_call x1, Pallas kernels, decoder_tokens(): pl.pallas_call(token_kernel, grid=(TUBES // TOKEN_ROWS,), in_specs=[rows(...  62.7 us
    pallas_call x1, Pallas kernels, attend_back(): pl.pallas_call(attend_back_kernel, grid=(PAIRS, pl.cdiv(TUBES, BWD_ROWS))...  53.8 us
    psum x1, blocking collectives, per_device(): loss_weight = MASKED * lax.psum(jnp.sum(counted_all), 'dp')  40.1 us
    pallas_call x2, Pallas kernels, encoder_layer_back(): pl.pallas_call(lambda *refs: encoder_back_kernel(start, *refs), in_specs=...  35.3 us
    pallas_call x1, Pallas kernels, attend(): pl.pallas_call(attend_kernel, grid=(PAIRS, TUBES // FWD_ROWS), in_specs=[...  32.5 us
  transfers between devices with their start and end apart: 14, of which 3 were waited for; matrix products, arithmetic and copies ran while one was open for 9% of the time, Pallas kernels for 7%

profile of v1, /device:TPU:0, one launch (start us, length us, event | category | flops | bytes accessed | tf_op | source)
XLA Modules:
  0.0 920.2 jit_solution(3220419764818350209)
XLA Ops:
  7.3 2.6 bitcast_convert_fusion
  9.9 182.3 %all-gather.3.cloned.1.call-done.refs_4_.refs_8_ = bf16[9984,768]{1,0:T(8,128)(2,1)} async-done(((bf16[624,768]{1,0:T(8,128)(2,1)}), bf16[9984,768]{1,0:T(8,128)(2,1)}) %all-gather.3.cloned.1.call-update) | async-done | bytes 15335440 | tf_op jit(solution)/shard_map/all_gather | solution.py:834
  193.6 1.7 copy.27.order_ref
  195.3 16.6 %pick_tubes.1 = bf16[2,1568,768]{2,1,0:T(8,128)(2,1)} custom-call(s32[2,1568,1]{2,1,0:T(8,128)} %copy.27.order_ref, bf16[2,1568,768]{2,1,0:T(8,128)(2,1)} %tubes_ref.1), custom_call_target="tpu_custom_call" | custom-call | tf_op jit(solution)/shard_map/pick_tubes/pallas_call | solution.py:114
  212.0 4.2 dynamic-slice_bitcast_fusion
  216.9 1.9 dynamic-slice_bitcast_fusion.3
  219.6 40.1 %psum.42 = f32[]{:T(128)} all-reduce(f32[]{:T(128)} %convert_reduce_fusion.2), channel_id=1, replica_groups=mesh['dp'=16,'tensor'=2] {'dp'}, use_global_device_ids=true, to_apply=%region_3.4 | all-reduce | flops 1 | bytes 8 | tf_op jit(solution)/shard_map/psum | solution.py:838
  261.6 4.6 stack.103
  267.5 19.8 %error_factor.1.error_part_ref = f32[8,9984]{1,0:T(8,128)} custom-call(f32[8,768]{1,0:T(8,128)} %slice_bitcast_fusion.4.start_ref, bf16[9984,768]{1,0:T(8,128)(2,1)} %bitcast.102), custom_call_target="tpu_custom_call" | custom-call | tf_op jit(solution)/shard_map/error_factor/pallas_call | solution.py:695
  292.6 4.4 pad_maximum_fusion.1.pix_ref
  298.1 1.1 pad_maximum_fusion.8
  299.4 1.1 pad_maximum_fusion.5.wh_ref
  300.5 1.7 pad_maximum_fusion.3
  302.2 1.3 slice.589
  303.6 1.3 slice.590
  304.9 3.8 fusion.12.refs_0_.refs_1_
  308.8 12.3 %encoder_0.1 = (f32[160,768]{1,0:T(8,128)}, bf16[160,768]{1,0:T(8,128)(2,1)}, bf16[160,2304]{1,0:T(8,128)(2,1)}, bf16[160,768]{1,0:T(8,128)(2,1)}, f32[160,768]{...) custom-call(f32[160,768]{1,0:T(8,128)} %fusion.12.refs_0_.refs_1_, ...), custom_call_target="tpu_custom_call" | custom-call | tf_op jit(solution)/shard_map/encoder_0/pallas_call | solution.py:526
  321.0 12.3 %encoder_1.1 = (f32[160,768]{1,0:T(8,128)}, bf16[160,768]{1,0:T(8,128)(2,1)}, bf16[160,2304]{1,0:T(8,128)(2,1)}, bf16[160,768]{1,0:T(8,128)(2,1)}, f32[160,768]{...) custom-call(f32[160,768]{1,0:T(8,128)} %get-tuple-element.63.refs_0_.refs_1_, ...), custom_call_target="tpu_custom_call" | custom-call | tf_op jit(solution)/shard_map/encoder_1/pallas_call | solution.py:526
  333.4 1.1 reduce_sum.81
  334.5 1.2 multiply_reduce_fusion.2
  335.8 1.4 fusion.20
  337.4 10.7 %fusion.3.x_ref = f32[1568,384]{1,0:T(8,128)} fusion(f32[1408,384]{1,0:T(8,128)S(1)} %broadcast_in_dim.133, f32[160,384]{1,0:T(8,128)S(1)} %fusion.20, f32[384]{0:T(512)S(1)} %fusion.48, f32[1568]{0:T(1024)S(1)} %convert_reduce_fusion.1, pred[384]{0:T(512)(128)(4,1)S(1)} %fusion.42), kind=kLoop, calls=%fused_computation.15 | loop fusion | flops 2408448 | bytes 4825088 | tf_op jit(solution)/shard_map/add | solution.py:896
  348.0 6.6 decoder_qkv.1
  354.7 32.5 %attend.1 = (f32[1568,384]{1,0:T(8,128)}, f32[3,1568,128]{2,1,0:T(8,128)}) custom-call(bf16[1568,1152]{1,0:T(8,128)(2,1)} %get-tuple-element.65.q_ref.k_ref.v_ref, bf16[1568,1152]{1,0:T(8,128)(2,1)} %get-tuple-element.65.q_ref.k_ref.v_ref, bf16[1568,1152]{1,0:T(8,128)(2,1)} %get-tuple-element.65.q_ref.k_ref.v_ref), custom_call_target="tpu_custom_call" | custom-call | tf_op jit(solution)/shard_map/attend/pallas_call | solution.py:187
  387.8 62.7 %decoder_tokens.1 = (bf16[1568,384]{1,0:T(8,128)(2,1)}, f32[1568,384]{1,0:T(8,128)}, f32[384,384]{1,0:T(8,128)}, f32[1536,384]{1,0:T(8,128)}, f32[1536,384]{1,0:...) custom-call(f32[1568,384]{1,0:T(8,128)} %get-tuple-element.66.a_ref., ...), custom_call_target="tpu_custom_call" | custom-call | tf_op jit(solution)/shard_map/decoder_tokens/pallas_call | solution.py:357
  450.6 53.8 %attend_back.1 = (bf16[1568,384]{1,0:T(8,128)(2,1)}, bf16[1568,384]{1,0:T(8,128)(2,1)}, bf16[1568,384]{1,0:T(8,128)(2,1)}) custom-call(bf16[1568,1152]{1,0:T(8,128)(2,1)} %get-tuple-element.65.q_ref.k_ref.v_ref, bf16[1568,1152]{1,0:T(8,128)(2,1)} %get-tuple-element.65.q_ref.k_ref.v_ref, bf16[1568,1152]{1,0:T(8,128)(2,1)} %get-tuple-element.65.q_ref.k_ref.v_ref, ...), custom_call_target="tpu_custom_call" | custom-call | tf_op jit(solution)/shard_map/attend_back/pallas_call | solution.py:257
  504.4 10.3 %decoder_qkv_back.1 = (f32[1568,384]{1,0:T(8,128)}, f32[1152,384]{1,0:T(8,128)}, f32[8,384]{1,0:T(8,128)}) custom-call(bf16[1568,384]{1,0:T(8,128)(2,1)} %get-tuple-element.69.dq_ref, bf16[1568,384]{1,0:T(8,128)(2,1)} %get-tuple-element.70.dk_ref, bf16[1568,384]{1,0:T(8,128)(2,1)} %get-tuple-element.71.dv_ref, bf16[1568,384]{1,0:T(8,128)(2,1)} %get-tuple-element.72.h_ref, ...), custom_call_target="tpu_custom_call" | custom-call | tf_op jit(solution)/shard_map/decoder_qkv_back/pallas_call | solution.py:416
  514.7 2.1 multiply_reduce_fusion
  516.8 1.4 fusion.22
  520.5 17.5 %encoder_back_1.1 = (f32[160,768]{1,0:T(8,128)}, bf16[2,160,4608]{2,1,0:T(8,128)(2,1)}, bf16[2,160,768]{2,1,0:T(8,128)(2,1)}, f32[8,768]{1,0:T(8,128)}, f32[1,3072]{1,0:T(1,128)}, /*index=5*/f32[2,768]{1,0:T(2,128)}) custom-call(f32[160,768]{1,0:T(8,128)} %subtract_multiply_fusion.refs_0_, f32[160,768]{1,0:T(8,128)} %get-tuple-element.63.refs_0_.refs_1_, ...), custom_call_target="tpu_custom_call" | custom-call | tf_op jit(solution)/shard_map/encoder_back_1/pallas_call | solution.py:632
  538.0 17.8 %encoder_back_0.1 = (f32[160,768]{1,0:T(8,128)}, bf16[2,160,4608]{2,1,0:T(8,128)(2,1)}, bf16[2,160,768]{2,1,0:T(8,128)(2,1)}, f32[8,768]{1,0:T(8,128)}, f32[1,3072]{1,0:T(1,128)}, /*index=5*/f32[2,768]{1,0:T(2,128)}) custom-call(f32[160,768]{1,0:T(8,128)} %get-tuple-element.80.refs_0_, f32[160,768]{1,0:T(8,128)} %fusion.12.refs_0_.refs_1_, ...), custom_call_target="tpu_custom_call" | custom-call | tf_op jit(solution)/shard_map/encoder_back_0/pallas_call | solution.py:632
  555.8 1.9 bitcast_dynamic-update-slice_fusion.2
  559.9 2.5 fusion.61
  563.1 1.4 slice_reduce_fusion.12
  564.5 1.3 slice_reduce_fusion.7
  567.1 1.3 slice_reduce_fusion.1
  568.4 1.3 slice_reduce_fusion
  569.8 1.3 reshape.168
  571.1 1.3 reshape.169
  572.5 1.1 pad_maximum_fusion.7
  573.7 2.1 pad_maximum_fusion.6
  581.0 3.2 slice_bitcast_fusion.3
  584.2 1.1 bitcast_dynamic-update-slice_fusion
  586.3 1.6 slice_dynamic-update-slice_fusion.2
  589.8 1.6 slice_dynamic-update-slice_fusion.1
  592.3 1.6 slice_dynamic-update-slice_fusion
  594.5 1.3 slice_bitcast_fusion.2
  598.9 1.5 add.121
  600.4 1.8 maximum_bitcast_fusion.2
  602.2 4.1 pad_maximum_fusion.2.right_ref
  607.4 3.2 pad_maximum_fusion.left_ref
  610.6 23.7 %left_factor.1 = f32[8,9984]{1,0:T(8,128)} custom-call(f32[8,768]{1,0:T(8,128)} %slice_bitcast_fusion.4.start_ref, bf16[2,160,9984]{2,1,0:T(8,128)(2,1)} %pad_maximum_fusion.left_ref, bf16[2,9,160,768]{3,2,1,0:T(8,128)(2,1)} %pad_maximum_fusion.2.right_ref, f32[8,9984]{1,0:T(8,128)} %error_factor.1.error_part_ref), custom_call_target="tpu_custom_call" | custom-call | tf_op jit(solution)/shard_map/left_factor/pallas_call | solution.py:673
  634.4 4.7 convert_add_fusion
  639.1 2.4 copy-done
  641.5 5.9 convolution_bitcast_fusion
  648.2 104.9 %all-reduce.4.cloned.1.call-done = (f32[21505]{0:T(1024)}, f32[8,9984]{1,0:T(8,128)}, f32[8,3456]{1,0:T(8,128)}) async-done(((f32[21505]{0:T(1024)}, f32[8,9984]{1,0:T(8,128)}, f32[8,3456]{1,0:T(8,128)}), (f32[21505]{0:T(1024)}, f32[8,9984]{1,0:T(8,128)}, f32[8,3456]{1,0:T(8,128)})) %all-reduce.4.cloned.1.call-update) | async-done | bytes 516116 | tf_op jit(solution)/shard_map/psum | solution.py:994
  753.1 3.8 orthonormal.1
  756.9 5.2 fusion.70
  762.1 27.1 %right_factor.1 = f32[8,768]{1,0:T(8,128)} custom-call(f32[8,9984]{1,0:T(8,128)} %get-tuple-element.111.basis_ref, bf16[2,160,9984]{2,1,0:T(8,128)(2,1)} %pad_maximum_fusion.left_ref, bf16[2,9,160,768]{3,2,1,0:T(8,128)(2,1)} %pad_maximum_fusion.2.right_ref, bf16[9984,768]{1,0:T(8,128)(2,1)} %bitcast.103), custom_call_target="tpu_custom_call" | custom-call | tf_op jit(solution)/shard_map/right_factor/pallas_call | solution.py:720
  789.2 75.4 %all-reduce = (f32[8,768]{1,0:T(8,128)S(1)}, f32[8,384]{1,0:T(8,128)S(1)}) all-reduce(f32[8,768]{1,0:T(8,128)} %right_factor.1, f32[8,384]{1,0:T(8,128)S(1)} %fusion.70), channel_id=1, replica_groups=mesh['dp'=16,'tensor'=2] {'dp'}, use_global_device_ids=true, to_apply=%region_13.14 | all-reduce | flops 9216 | bytes 73728 | tf_op jit(solution)/shard_map/psum | solution.py:1000
  864.7 7.6 fusion.1
  874.0 29.9 %residue.1 = bf16[9984,768]{1,0:T(8,128)(2,1)} custom-call(f32[8,9984]{1,0:T(8,128)} %get-tuple-element.111.basis_ref, f32[8,768]{1,0:T(8,128)} %broadcast_multiply_fusion.factor_ref, bf16[2,160,9984]{2,1,0:T(8,128)(2,1)} %pad_maximum_fusion.left_ref, bf16[2,9,160,768]{3,2,1,0:T(8,128)(2,1)} %pad_maximum_fusion.2.right_ref, bf16[9984,768]{1,0:T(8,128)(2,1)} %bitcast.104), custom_call_target="tpu_custom_call" | custom-call | tf_op jit(solution)/shard_map/residue/pallas_call | solution.py:755
  907.3 2.8 bitcast_add_fusion
  910.1 1.6 fusion.8
  (290 shorter events, 36.8 us)
Async XLA Ops:
  7.2 185.0 %copy-start.15 = (f32[1,216,384]{2,1,0:T(8,128)S(1)}, f32[1,216,384]{2,1,0:T(8,128)}, u32[]{:S(2)}) copy-start(f32[1,216,384]{2,1,0:T(8,128)} %param.18) | copy-start | bytes 995332
  7.2 185.8 %copy-start.37 = (f32[1,6528]{1,0:T(1,128)S(1)}, f32[1,6528]{1,0:T(1,128)}, u32[]{:S(2)}) copy-start(f32[1,6528]{1,0:T(1,128)} %param.19) | copy-start | bytes 78340
  7.2 186.4 %copy-start.41 = (s32[2,1568]{1,0:T(2,128)S(1)}, s32[2,1568]{1,0:T(2,128)}, u32[]{:S(2)}) copy-start(s32[2,1568]{1,0:T(2,128)} %param.15) | copy-start | bytes 37636
  7.2 185.0 %all-gather.3.cloned.1.call-start = ((), (), s32[]{:S(2)}) async-start(), calls=%async_computation | async-start | bytes 16293888 | tf_op jit(solution)/shard_map/all_gather | solution.py:834
  9.9 279.4 %all-gather.5.cloned.1.call-start = ((), (), s32[]{:S(2)}) async-start(), calls=%async_computation.1 | async-start | bytes 2820096 | tf_op jit(solution)/shard_map/all_gather | solution.py:833
  192.2 111.4 %collective-permute-start.1 = (bf16[9984,768]{1,0:T(8,128)(2,1)}, bf16[9984,768]{1,0:T(8,128)(2,1)}, u32[]{:S(2)}, u32[]{:S(2)}) collective-permute-start(bf16[9984,768]{1,0:T(8,128)(2,1)} %all-gather.3.cloned.1.call-done.refs_4_.refs_8_), channel_id=1, source_target_pairs={{0,1},{1,0},{2,3},{3,2},{4,5},{5,4},{6,7},{7,6},{8,9},{9,8},{10,11... | collective-permute-start | bytes 46006280 | tf_op jit(solution)/shard_map/ppermute | solution.py:811
  192.9 560.2 %all-reduce.4.cloned.1.call-start = ((), (), s32[]{:S(2)}) async-start(), calls=%async_computation.2 | async-start | bytes 1040384 | tf_op jit(solution)/shard_map/psum | solution.py:994
  193.1 18.9 %copy-start.35 = (f32[6528]{0:T(1024)}, f32[6528]{0:T(1024)S(1)}, u32[]{:S(2)}) copy-start(f32[6528]{0:T(1024)S(1)} %reduce.1) | copy-start | bytes 78340
  193.1 96.1 %collective-permute-start.2 = (f32[6528]{0:T(1024)S(1)}, f32[6528]{0:T(1024)S(1)}, u32[]{:S(2)}, u32[]{:S(2)}) collective-permute-start(f32[6528]{0:T(1024)S(1)} %reduce.1), channel_id=1, source_target_pairs={{0,1},{1,0},{2,3},{3,2},{4,5},{5,4},{6,7},{7,6},{8,9},{9,8},{10,11... | collective-permute-start | bytes 78344 | tf_op jit(solution)/shard_map/ppermute | solution.py:811
  212.0 4.3 copy-start.74
  212.0 7.0 copy-start.28
  212.0 7.0 copy-start.40
  216.1 76.4 %collective-permute-start = (bf16[1568,768]{1,0:T(8,128)(2,1)}, bf16[1568,768]{1,0:T(8,128)(2,1)}, u32[]{:S(2)}, u32[]{:S(2)}) collective-permute-start(bf16[1568,768]{1,0:T(8,128)(2,1)} %get-tuple-element.157), channel_id=1, source_target_pairs={{0,1},{1,0},{2,3},{3,2},{4,5},{5,4},{6,7},{7,6},{8,9},{9,8},{10,11... | collective-permute-start | bytes 7225352 | tf_op jit(solution)/shard_map/ppermute | solution.py:811
  289.3 8.0 collective-permute-start.3
  292.6 4.4 copy-start.7
  504.4 10.3 %copy-start.1 = (f32[160,768]{1,0:T(8,128)S(1)}, f32[160,768]{1,0:T(8,128)}, u32[]{:S(2)}) copy-start(f32[160,768]{1,0:T(8,128)} %get-tuple-element.64) | copy-start | bytes 1474564
  514.7 3.5 copy-start.68
  538.0 21.3 %copy-start.71 = (f32[1,1536]{1,0:T(1,128)S(1)}, f32[1,1536]{1,0:T(1,128)}, u32[]{:S(2)}) copy-start(f32[1,1536]{1,0:T(1,128)} %get-tuple-element.97) | copy-start | bytes 18436
  555.8 10.0 %copy-start.69 = (f32[1,1536]{1,0:T(1,128)S(1)}, f32[1,1536]{1,0:T(1,128)}, u32[]{:S(2)}) copy-start(f32[1,1536]{1,0:T(1,128)} %get-tuple-element.92) | copy-start | bytes 18436
  555.8 16.6 %copy-start.11 = (bf16[2,160,768]{2,1,0:T(8,128)(2,1)S(1)}, bf16[2,160,768]{2,1,0:T(8,128)(2,1)}, u32[]{:S(2)}) copy-start(bf16[2,160,768]{2,1,0:T(8,128)(2,1)} %get-tuple-element.103) | copy-start | bytes 1474564
  555.8 16.6 %copy-start.19 = (bf16[160,768]{1,0:T(8,128)(2,1)S(1)}, bf16[160,768]{1,0:T(8,128)(2,1)}, u32[]{:S(2)}) copy-start(bf16[160,768]{1,0:T(8,128)(2,1)} %get-tuple-element.105) | copy-start | bytes 737284
  555.8 16.6 %copy-start.21 = (bf16[160,768]{1,0:T(8,128)(2,1)S(1)}, bf16[160,768]{1,0:T(8,128)(2,1)}, u32[]{:S(2)}) copy-start(bf16[160,768]{1,0:T(8,128)(2,1)} %get-tuple-element.104) | copy-start | bytes 737284
  558.8 39.4 %collective-permute-start.7 = (bf16[160,768]{1,0:T(8,128)(2,1)}, bf16[160,768]{1,0:T(8,128)(2,1)}, u32[]{:S(2)}, u32[]{:S(2)}) collective-permute-start(bf16[160,768]{1,0:T(8,128)(2,1)} %get-tuple-element.154), channel_id=1, source_target_pairs={{0,1},{1,0},{2,3},{3,2},{4,5},{5,4},{6,7},{7,6},{8,9},{9,8},{10,11... | collective-permute-start | bytes 737288 | tf_op jit(solution)/shard_map/ppermute | solution.py:811
  559.9 13.7 %copy-start.12 = (bf16[2,160,768]{2,1,0:T(8,128)(2,1)S(1)}, bf16[2,160,768]{2,1,0:T(8,128)(2,1)}, u32[]{:S(2)}) copy-start(bf16[2,160,768]{2,1,0:T(8,128)(2,1)} %get-tuple-element.100) | copy-start | bytes 1474564
  572.5 4.7 copy-start.24
  572.5 5.4 copy-start.23
  573.6 26.8 %collective-permute-start.9 = (bf16[4,160,768]{2,1,0:T(8,128)(2,1)}, bf16[4,160,768]{2,1,0:T(8,128)(2,1)}, u32[]{:S(2)}, u32[]{:S(2)}) collective-permute-start(bf16[4,160,768]{2,1,0:T(8,128)(2,1)} %pad_maximum_fusion.7), channel_id=1, source_target_pairs={{0,1},{1,0},{2,3},{3,2},{4,5},{5,4},{6,7},{7,6},{8,9},{9,8},{10,11... | collective-permute-start | bytes 2949128 | tf_op jit(solution)/shard_map/ppermute | solution.py:811
  573.6 6.5 copy-start.31
  573.6 6.5 copy-start.33
  573.6 6.5 copy-start.44
  573.6 6.5 copy-start.45
  573.6 6.5 copy-start.47
  573.6 6.5 copy-start.49
  573.6 6.5 copy-start.51
  573.6 6.5 copy-start.53
  573.7 6.5 copy-start.55
  573.7 6.5 copy-start.59
  573.7 6.5 copy-start.60
  573.7 6.5 copy-start.64
  573.7 6.5 copy-start.65
  573.7 6.5 copy-start.66
  573.7 6.5 copy-start.67
  573.7 6.5 copy-start.72
  573.7 6.5 copy-start.73
  575.9 24.5 %collective-permute-start.8 = (bf16[4,160,768]{2,1,0:T(8,128)(2,1)}, bf16[4,160,768]{2,1,0:T(8,128)(2,1)}, u32[]{:S(2)}, u32[]{:S(2)}) collective-permute-start(bf16[4,160,768]{2,1,0:T(8,128)(2,1)} %pad_maximum_fusion.6), channel_id=1, source_target_pairs={{0,1},{1,0},{2,3},{3,2},{4,5},{5,4},{6,7},{7,6},{8,9},{9,8},{10,11... | collective-permute-start | bytes 2949128 | tf_op jit(solution)/shard_map/ppermute | solution.py:811
  581.0 17.2 %collective-permute-start.4 = (f32[21505]{0:T(1024)}, f32[21505]{0:T(1024)}, u32[]{:S(2)}, u32[]{:S(2)}) collective-permute-start(f32[21505]{0:T(1024)} %concatenate.138), channel_id=1, source_target_pairs={{0,1},{1,0},{2,3},{3,2},{4,5},{5,4},{6,7},{7,6},{8,9},{9,8},{10,11... | collective-permute-start | bytes 258068 | tf_op jit(solution)/shard_map/ppermute | solution.py:811
  581.0 4.3 copy-start.25
  593.9 40.5 %collective-permute-start.10 = (f32[3456,384]{1,0:T(8,128)}, f32[3456,384]{1,0:T(8,128)}, u32[]{:S(2)}, u32[]{:S(2)}) collective-permute-start(f32[3456,384]{1,0:T(8,128)} %get-tuple-element.169), channel_id=1, source_target_pairs={{0,1},{1,0},{2,3},{3,2},{4,5},{5,4},{6,7},{7,6},{8,9},{9,8},{10,11... | collective-permute-start | bytes 15925256 | tf_op jit(solution)/shard_map/ppermute | solution.py:811
  594.5 4.1 copy-start.18
  598.1 8.2 collective-permute-start.5
  598.2 9.0 collective-permute-start.6
  602.2 5.0 copy-start.17
  610.6 23.8 %copy-start.6 = (bf16[1,1,3456,384]{3,2,1,0:T(8,128)(2,1)S(1)}, bf16[1,1,3456,384]{3,2,1,0:T(8,128)(2,1)}, u32[]{:S(2)}) copy-start(bf16[1,1,3456,384]{3,2,1,0:T(8,128)(2,1)} %param.26) | copy-start | bytes 7962628
  641.5 6.6 copy-start.46
  762.1 102.5 %copy-start.26 = (f32[8,3456]{1,0:T(8,128)S(1)}, f32[8,3456]{1,0:T(8,128)}, u32[]{:S(2)}) copy-start(f32[8,3456]{1,0:T(8,128)} %get-tuple-element.112) | copy-start | bytes 331780
  864.7 7.6 copy-start.38
  864.7 8.1 copy-start.36
  874.0 29.9 %copy-start.30 = (f32[8,768]{1,0:T(8,128)S(1)}, f32[8,768]{1,0:T(8,128)}, u32[]{:S(2)}) copy-start(f32[8,768]{1,0:T(8,128)} %broadcast_multiply_fusion.factor_ref) | copy-start | bytes 73732
  874.0 31.2 %copy-start.29 = (f32[14976]{0:T(1024)S(1)}, f32[14976]{0:T(1024)}, u32[]{:S(2)}) copy-start(f32[14976]{0:T(1024)} %param.20) | copy-start | bytes 179716
  874.0 31.2 %copy-start.39 = (f32[14976]{0:T(1024)S(1)}, f32[14976]{0:T(1024)}, u32[]{:S(2)}) copy-start(f32[14976]{0:T(1024)} %param.24) | copy-start | bytes 179716
  874.0 31.8 %copy-start.27 = (f32[1,216,384]{2,1,0:T(8,128)S(1)}, f32[1,216,384]{2,1,0:T(8,128)}, u32[]{:S(2)}) copy-start(f32[1,216,384]{2,1,0:T(8,128)} %param.22) | copy-start | bytes 995332
  874.0 32.5 %copy-start.16 = (f32[1,216,384]{2,1,0:T(8,128)S(1)}, f32[1,216,384]{2,1,0:T(8,128)}, u32[]{:S(2)}) copy-start(f32[1,216,384]{2,1,0:T(8,128)} %param.18) | copy-start | bytes 995332
  906.5 3.6 copy-start.14
  906.5 3.6 copy-start.3
  (25 other events, 65.1 us)
Sparse Core Ops, SparseCore 0:
  11.4 180.7 all-gather.2
  195.5 62.7 all-gather.4
  647.6 105.4 all-reduce.3

commit v2 on v1

--- a/solution.py
+++ b/solution.py
@@ -100,6 +100,14 @@
     return pl.BlockSpec(shape, lambda *_: (0,) * len(shape))
 
 
+def any_spec():
+    return pl.BlockSpec(memory_space=pl.ANY)
+
+
+def vmem_spec():
+    return pl.BlockSpec(memory_space=pltpu.VMEM)
+
+
 PICK_ROWS = 224
 
 
@@ -128,33 +136,39 @@
 QKV_ROWS = 392
 
 
-def qkv_kernel(x_ref, g_ref, b_ref, w_ref, bias_ref, h_ref, qkv_ref):
-    unit, _ = norm_parts(x_ref[...])
-    h = (unit * g_ref[...] + b_ref[...]).astype(bf16)
+def qkv_kernel(pos_ref, latent_ref, vec_ref, w_ref, bias_ref, x_ref, h_ref, qkv_ref):
+    token, gain, shift = (vec_ref[index : index + 1] for index in range(3))
+    hidden = jnp.broadcast_to(token, (QKV_ROWS, DD))
+    shown = jnp.concatenate([latent_ref[...], hidden[VIS:]], 0)
+    x = pos_ref[...] + jnp.where(pl.program_id(0) == 0, shown, hidden)
+    x_ref[...] = x
+    unit, _ = norm_parts(x)
+    h = (unit * gain + shift).astype(bf16)
     h_ref[...] = h
     qkv_ref[...] = (nt(h, w_ref[...]) + bias_ref[...]).astype(bf16)
 
 
-def decoder_qkv(x, gain, shift, weights, bias):
+def decoder_qkv(pos, latent, vecs, weights, bias):
     rows = lambda width: pl.BlockSpec((QKV_ROWS, width), lambda i: (i, 0))
     return pl.pallas_call(
         qkv_kernel,
         grid=(TUBES // QKV_ROWS,),
         in_specs=[
             rows(DD),
-            whole((1, DD)),
-            whole((1, DD)),
+            whole((VIS, DD)),
+            whole((8, DD)),
             whole((3 * DD, DD)),
             whole((1, 3 * DD)),
         ],
-        out_specs=[rows(DD), rows(3 * DD)],
+        out_specs=[rows(DD), rows(DD), rows(3 * DD)],
         out_shape=[
+            jax.ShapeDtypeStruct((TUBES, DD), f32),
             jax.ShapeDtypeStruct((TUBES, DD), bf16),
             jax.ShapeDtypeStruct((TUBES, 3 * DD), bf16),
         ],
         compiler_params=params(),
         name="decoder_qkv",
-    )(x, gain, shift, weights, bias)
+    )(pos, latent, vecs, weights, bias)
 
 
 FWD_ROWS = 392
@@ -279,17 +293,23 @@
 
 TOKEN_ROWS = 224
 CHUNK = 384
+DEC_O = D // 2
+DEC_D = DEC_O + DD // 2
+DEC_Q = DEC_D + DFF // 2
+DEC_U = DEC_Q + 3 * DD // 2
+DEC_H = DEC_U + DFF // 2
+DEC_ROWS = DEC_H + PIX // 2
 CHUNKS = DFF // CHUNK
 
 
 def token_kernel(
     a_ref, x_ref, pix_ref, scal_ref, vec_ref, bu_ref, bh_ref, wo_ref, wd_ref, wu_ref, wh_ref,
     da_ref, dx1_ref,
-    g_wo_ref, g_wd_ref, g_wu_ref, g_wh_ref, gvec_ref, gbu_ref, gbh_ref, loss_ref,
+    grads_ref, gvec_ref, gbu_ref, gbh_ref, loss_ref,
     slope,
 ):
     step = pl.program_id(0)
-    sums = (g_wo_ref, g_wd_ref, g_wu_ref, g_wh_ref, gvec_ref, gbu_ref, gbh_ref, loss_ref)
+    sums = (grads_ref, gvec_ref, gbu_ref, gbh_ref, loss_ref)
 
     @pl.when(step == 0)
     def _():
@@ -326,21 +346,25 @@
         loss_ref[:, part] += col_sum(counted * miss * miss)
         grad_guess = (rate * miss).astype(bf16)
         gbh_ref[:, part] += col_sum(grad_guess.astype(f32))
-        g_wh_ref[part] += tn(grad_guess, final)
+        grads_ref[chunk // 2, pl.ds(DEC_H + (chunk % 2) * CHUNK, CHUNK)] += tn(grad_guess, final)
         grad_final = grad_final + nn(grad_guess, wh_ref[part])
     grad_out = norm_back(grad_final, gf, unit_f, rate_f)
     out_low = grad_out.astype(bf16)
     grad_h2 = jnp.zeros((TOKEN_ROWS, DD), f32)
     for chunk in range(CHUNKS):
         part = pl.ds(chunk * CHUNK, CHUNK)
-        g_wd_ref[part] += tn(active[chunk], out_low)
+        grads_ref[chunk // 2, pl.ds(DEC_D + (chunk % 2) * CHUNK, CHUNK)] += tn(
+            active[chunk], out_low
+        )
         grad_before = (slope[:, part] * nt(out_low, wd_ref[part])).astype(bf16)
         gbu_ref[:, part] += col_sum(grad_before.astype(f32))
-        g_wu_ref[part] += tn(grad_before, h2)
+        grads_ref[chunk // 2, pl.ds(DEC_U + (chunk % 2) * CHUNK, CHUNK)] += tn(grad_before, h2)
         grad_h2 = grad_h2 + nn(grad_before, wu_ref[part])
     grad_x1 = grad_out + norm_back(grad_h2, g2, unit2, rate2)
     x1_low = grad_x1.astype(bf16)
-    g_wo_ref[...] += tn(a, x1_low)
+    g_out = tn(a, x1_low)
+    for group in range(2):
+        grads_ref[group, pl.ds(DEC_O, DD // 2)] += g_out[group * DD // 2 : (group + 1) * DD // 2]
     da_ref[...] = nt(x1_low, wo_ref[...]).astype(bf16)
     dx1_ref[...] = grad_x1
     gvec_ref[0:1] += col_sum(x1_low.astype(f32))
@@ -353,7 +377,7 @@
 
 def decoder_tokens(mixed, x, pixels, scal, vecs, bu, bh, wo, wd, wu, wh):
     rows = lambda width: pl.BlockSpec((TOKEN_ROWS, width), lambda i: (i, 0))
-    sums = [(DD, DD), (DFF, DD), (DFF, DD), (PIX, DD), (8, DD), (1, DFF), (1, PIX), (1, PIX)]
+    sums = [(2, DEC_ROWS, DD), (8, DD), (1, DFF), (1, PIX), (1, PIX)]
     return pl.pallas_call(
         token_kernel,
         grid=(TUBES // TOKEN_ROWS,),
@@ -383,26 +407,28 @@
 
 
 def qkv_back_kernel(
-    dq_ref, dk_ref, dv_ref, h_ref, x_ref, dx1_ref, g_ref, w_ref,
-    dx_ref, gw_ref, gvec_ref,
+    half_ref, dq_ref, dk_ref, dv_ref, h_ref, x_ref, dx1_ref, vec_ref, w_ref, normed_ref, _,
+    latent_ref, grads_ref, gvec_ref,
+    g_qkv, g_proj, sems,
 ):
     step = pl.program_id(0)
 
     @pl.when(step == 0)
     def _():
-        gw_ref[...] = jnp.zeros_like(gw_ref)
+        g_qkv[...] = jnp.zeros_like(g_qkv)
         gvec_ref[...] = jnp.zeros_like(gvec_ref)
 
     h = h_ref[...]
     grads = (dq_ref[...], dk_ref[...], dv_ref[...])
     grad_h = jnp.zeros((QKV_ROWS, DD), f32)
     for index, grad in enumerate(grads):
-        part = pl.ds(index * DD, DD)
-        gw_ref[part] += tn(grad, h)
-        grad_h = grad_h + nn(grad, w_ref[part])
+        g_both = tn(grad, h)
+        for group in range(2):
+            rows = pl.ds(index * DD // 2, DD // 2)
+            g_qkv[group, rows] += g_both[group * DD // 2 : (group + 1) * DD // 2]
+        grad_h = grad_h + nn(grad, w_ref[pl.ds(index * DD, DD)])
     unit, rate = norm_parts(x_ref[...])
-    grad_x = dx1_ref[...] + norm_back(grad_h, g_ref[...], unit, rate)
-    dx_ref[...] = grad_x
+    grad_x = dx1_ref[...] + norm_back(grad_h, vec_ref[1:2], unit, rate)
     row = lax.broadcasted_iota(jnp.int32, (QKV_ROWS, 1), 0) + step * QKV_ROWS
     gvec_ref[0:1] += col_sum(grads[0].astype(f32))
     gvec_ref[1:2] += col_sum(grads[2].astype(f32))
@@ -410,22 +436,55 @@
     gvec_ref[3:4] += col_sum(grad_h)
     gvec_ref[4:5] += col_sum(jnp.where(row >= VIS, grad_x, 0.0))
 
-
-def decoder_qkv_back(dq, dk, dv, h, x, dx1, gain, weights):
+    @pl.when(step == 0)
+    def _():
+        latent = grad_x[:VIS].astype(bf16)
+        latent_ref[...] = latent
+        both = tn(normed_ref[...], latent)
+        g_proj[0] = both[: D // 2]
+        g_proj[1] = both[D // 2 :]
+
+    @pl.when(step == pl.num_programs(0) - 1)
+    def _():
+        half = half_ref[0]
+        copies = [
+            pltpu.make_async_copy(g_qkv, grads_ref.at[:, pl.ds(DEC_Q, 3 * DD // 2)], sems.at[0]),
+            pltpu.make_async_copy(
+                g_proj.at[half], grads_ref.at[0, pl.ds(0, D // 2)], sems.at[1]
+            ),
+            pltpu.make_async_copy(
+                g_proj.at[1 - half], grads_ref.at[1, pl.ds(0, D // 2)], sems.at[2]
+            ),
+        ]
+        for copy in copies:
+            copy.start()
+        for copy in copies:
+            copy.wait()
+
+
+def decoder_qkv_back(half, dq, dk, dv, h, x, dx1, vecs, weights, normed, grads):
     rows = lambda width: pl.BlockSpec((QKV_ROWS, width), lambda i: (i, 0))
     return pl.pallas_call(
         qkv_back_kernel,
         grid=(TUBES // QKV_ROWS,),
-        in_specs=[rows(DD)] * 6 + [whole((1, DD)), whole((3 * DD, DD))],
-        out_specs=[rows(DD), whole((3 * DD, DD)), whole((8, DD))],
+        in_specs=[pl.BlockSpec(memory_space=pltpu.SMEM)]
+        + [rows(DD)] * 6
+        + [whole((8, DD)), whole((3 * DD, DD)), whole((VIS, D)), any_spec()],
+        out_specs=[whole((VIS, DD)), any_spec(), whole((8, DD))],
         out_shape=[
-            jax.ShapeDtypeStruct((TUBES, DD), f32),
-            jax.ShapeDtypeStruct((3 * DD, DD), f32),
+            jax.ShapeDtypeStruct((VIS, DD), bf16),
+            jax.ShapeDtypeStruct((2, DEC_ROWS, DD), f32),
             jax.ShapeDtypeStruct((8, DD), f32),
         ],
+        scratch_shapes=[
+            pltpu.VMEM((2, 3 * DD // 2, DD), f32),
+            pltpu.VMEM((2, D // 2, DD), f32),
+            pltpu.SemaphoreType.DMA((3,)),
+        ],
+        input_output_aliases={10: 1},
         compiler_params=params(),
         name="decoder_qkv_back",
-    )(dq, dk, dv, h, x, dx1, gain, weights)
+    )(half, dq, dk, dv, h, x, dx1, vecs, weights, normed, grads)
 
 
 HALF = D // 2
@@ -449,11 +508,12 @@
     ]
 
 
-def encoder_kernel(
-    start, x_ref, vec_ref, bqkv_ref, bu_ref, own_ref, other_ref,
-    out_ref, h_ref, qkv_ref, a_ref, x1_ref, h2_ref, u_ref, slope_ref,
-    held, sems,
-):
+def encoder_kernel(start, last, x_ref, vec_ref, bqkv_ref, bu_ref, own_ref, other_ref, *refs):
+    if last:
+        proj_ref, *refs = refs
+        normed_ref, latent_ref = refs[8:10]
+    out_ref, h_ref, qkv_ref, a_ref, x1_ref, h2_ref, u_ref, slope_ref = refs[:8]
+    held, sems = refs[-2:]
     copies = stage_copies((own_ref, other_ref), start, held, sems)
     for stage in copies:
         for copy in stage:
@@ -506,13 +566,14 @@
             u_ref[:, part] = active
             out = out + nn(active, held[group, pl.ds(AT_D + chunk * CHUNK, CHUNK)])
     out_ref[...] = out
-
-
-def any_spec():
-    return pl.BlockSpec(memory_space=pl.ANY)
-
-
-def encoder_layer(start, x, vecs, bqkv, bu, own, other, name):
+    if last:
+        unit3, _ = norm_parts(out)
+        normed = (unit3 * vec_ref[6:7] + vec_ref[7:8]).astype(bf16)
+        normed_ref[...] = normed
+        latent_ref[...] = nn(normed, proj_ref[...])
+
+
+def encoder_layer(start, x, vecs, bqkv, bu, own, other, name, proj=None):
     shapes = [
         ((VIS, D), f32),
         ((VIS, D), bf16),
@@ -523,10 +584,15 @@
         ((VIS, FF), bf16),
         ((VIS, FF), f32),
     ]
-    return pl.pallas_call(
-        lambda *refs: encoder_kernel(start, *refs),
-        in_specs=[pl.BlockSpec(memory_space=pltpu.VMEM)] * 4 + [any_spec()] * 2,
-        out_specs=[pl.BlockSpec(memory_space=pltpu.VMEM)] * len(shapes),
+    last = proj is not None
+    more = ()
+    if last:
+        more = (proj,)
+        shapes += [((VIS, D), bf16), ((VIS, DD), f32)]
+    return pl.pallas_call(
+        lambda *refs: encoder_kernel(start, last, *refs),
+        in_specs=[vmem_spec()] * 4 + [any_spec()] * 2 + [vmem_spec()] * len(more),
+        out_specs=[vmem_spec()] * len(shapes),
         out_shape=[jax.ShapeDtypeStruct(shape, kind) for shape, kind in shapes],
         scratch_shapes=[
             pltpu.VMEM((2, LAYER_ROWS, D), bf16),
@@ -534,14 +600,23 @@
         ],
         compiler_params=params(),
         name=name,
-    )(x, vecs, bqkv, bu, own, other)
-
-
-def encoder_back_kernel(
-    start, dout_ref, x_ref, vec_ref, qkv_ref, a_ref, x1_ref, u_ref, slope_ref, own_ref, other_ref,
-    dx_ref, left_ref, low_ref, gvec_ref, gbu_ref, gbq_ref,
-    held, sems, da, dqkv,
-):
+    )(x, vecs, bqkv, bu, own, other, *more)
+
+
+RIGHT_AT = LAYER_ROWS
+
+
+def encoder_back_kernel(start, last, *refs):
+    (
+        grad_ref, x_ref, vec_ref, h_ref, qkv_ref, a_ref, x1_ref, h2_ref, u_ref, slope_ref,
+        start_ref, own_ref, other_ref, extra_ref,
+    ) = refs[:14]
+    refs = refs[14:]
+    if last:
+        out_ref, proj_ref, *refs = refs
+    dx_ref, mine_ref, other_pack_ref, left_ref, gvec_ref, gbu_ref, gbq_ref = refs[:7]
+    held, sems, da, dqkv = refs[7:]
+    packs = (mine_ref, other_pack_ref)
     copies = stage_copies((own_ref, other_ref), start, held, sems)
     for stage in (3, 2, 1, 0):
         for copy in copies[stage]:
@@ -552,9 +627,16 @@
             copy.wait()
 
     g1, b1, bo, g2, b2, bd = (vec_ref[index : index + 1] for index in range(6))
-    grad_out = dout_ref[...]
+    gvec_ref[6:8] = jnp.zeros((2, D), f32)
+    if last:
+        unit3, rate3 = norm_parts(out_ref[...])
+        grad_normed = nt(grad_ref[...], proj_ref[...])
+        grad_out = norm_back(grad_normed, vec_ref[6:7], unit3, rate3)
+        gvec_ref[6:7] = col_sum(grad_normed * unit3)
+        gvec_ref[7:8] = col_sum(grad_normed)
+    else:
+        grad_out = grad_ref[...]
     out_low = grad_out.astype(bf16)
-    low_ref[1] = out_low
     unit2, rate2 = norm_parts(x1_ref[...])
     grad_h2 = jnp.zeros((VIS, D), f32)
     wait(3)
@@ -564,18 +646,17 @@
             part = pl.ds(group * HALF_FF + chunk * CHUNK, CHUNK)
             grad_active = nt(out_low, held[group, pl.ds(AT_D + chunk * CHUNK, CHUNK)])
             grad_before = (slope_ref[:, part] * grad_active).astype(bf16)
-            left_ref[group, :, pl.ds(AT_U + chunk * CHUNK, CHUNK)] = grad_before
-            left_ref[group, :, pl.ds(AT_D + chunk * CHUNK, CHUNK)] = u_ref[:, part]
+            packs[group][:, pl.ds(AT_U + chunk * CHUNK, CHUNK)] = grad_before
+            packs[group][:, pl.ds(AT_D + chunk * CHUNK, CHUNK)] = u_ref[:, part]
             gbu_ref[:, part] = col_sum(grad_before.astype(f32))
             grad_h2 = grad_h2 + nn(grad_before, held[group, pl.ds(AT_U + chunk * CHUNK, CHUNK)])
     grad_x1 = grad_out + norm_back(grad_h2, g2, unit2, rate2)
     x1_low = grad_x1.astype(bf16)
-    low_ref[0] = x1_low
     wait(1)
     for group in range(2):
         part = pl.ds(group * HALF, HALF)
         da[:, part] = nt(x1_low, held[group, pl.ds(AT_O, HALF)]).astype(bf16)
-        left_ref[group, :, pl.ds(AT_O, HALF)] = a_ref[:, part]
+        packs[group][:, pl.ds(AT_O, HALF)] = a_ref[:, part]
     zero = jnp.zeros((), bf16)
     for pair in range(D // 128):
         lanes = pl.ds(pair * 128, 128)
@@ -604,10 +685,11 @@
         for group in range(2):
             grad = dqkv[:, pl.ds((2 * kind + group) * HALF, HALF)]
             rows = pl.ds(AT_Q + kind * HALF, HALF)
-            left_ref[group, :, rows] = grad
+            packs[group][:, rows] = grad
             grad_h = grad_h + nn(grad, held[group, rows])
     unit, rate = norm_parts(x_ref[...])
-    dx_ref[...] = grad_x1 + norm_back(grad_h, g1, unit, rate)
+    grad_x = grad_x1 + norm_back(grad_h, g1, unit, rate)
+    dx_ref[...] = grad_x
     gbq_ref[0:1] = col_sum(dqkv[:, pl.ds(0, D)].astype(f32))
     gbq_ref[1:2] = col_sum(dqkv[:, pl.ds(2 * D, D)].astype(f32))
     gvec_ref[0:1] = col_sum(grad_h * unit)
@@ -616,23 +698,45 @@
     gvec_ref[3:4] = col_sum(grad_h2 * unit2)
     gvec_ref[4:5] = col_sum(grad_h2)
     gvec_ref[5:6] = col_sum(out_low.astype(f32))
-    gvec_ref[6:8] = jnp.zeros((2, D), f32)
-
-
-def encoder_layer_back(start, grad, x, vecs, kept, own, other, name):
-    _, h, qkv, a, x1, h2, u, slope = kept
+    rights = [x1_low, out_low, h_ref[...], h2_ref[...]]
+    spans = [(AT_O, HALF, 0), (AT_D, HALF_FF, 0), (AT_Q, 3 * HALF, 0), (AT_U, HALF_FF, 0)]
+    if not last:
+        embed_low = grad_x.astype(bf16)
+        rights.append(embed_low)
+        gvec_ref[6:7] = col_sum(embed_low.astype(f32))
+    starts = jnp.concatenate([split3(start_ref[0]), split3(start_ref[1])], 0)
+    before = 0 if last else D
+    for index, right in enumerate(rights):
+        for pack in packs:
+            pack[:, pl.ds(RIGHT_AT + index * D, D)] = right
+        inner = nt(starts, right)
+        for group in range(2):
+            parts = split3(fold3(inner[3 * RANK * group : 3 * RANK * (group + 1)]))
+            if index == 4:
+                value = fold3(nn(parts, extra_ref[:, pl.ds(group * D, D)]))
+                left_ref[group, :, pl.ds(0, D)] = value
+            else:
+                at, size, _ = spans[index]
+                value = fold3(nn(parts, packs[group][:, pl.ds(at, size)]))
+                left_ref[group, :, pl.ds(before + at, size)] = value
+
+
+def encoder_layer_back(start, grad, source, vecs, kept, starts, own, other, extra, name, last=()):
+    width = RIGHT_AT + (4 if last else 5) * D
     shapes = [
         ((VIS, D), f32),
-        ((2, VIS, LAYER_ROWS), bf16),
-        ((2, VIS, D), bf16),
+        ((VIS, width), bf16),
+        ((VIS, width), bf16),
+        ((2, RANK, LAYER_ROWS if last else D + LAYER_ROWS), f32),
         ((8, D), f32),
         ((1, FF), f32),
         ((2, D), f32),
     ]
-    dx, left, low, gvec, gbu, gbq = pl.pallas_call(
-        lambda *refs: encoder_back_kernel(start, *refs),
-        in_specs=[pl.BlockSpec(memory_space=pltpu.VMEM)] * 8 + [any_spec()] * 2,
-        out_specs=[pl.BlockSpec(memory_space=pltpu.VMEM)] * len(shapes),
+    _, h, qkv, a, x1, h2, u, slope = kept[:8]
+    return pl.pallas_call(
+        lambda *refs: encoder_back_kernel(start, bool(last), *refs),
+        in_specs=[vmem_spec()] * 11 + [any_spec()] * 2 + [vmem_spec()] * (1 + len(last)),
+        out_specs=[vmem_spec()] * len(shapes),
         out_shape=[jax.ShapeDtypeStruct(shape, kind) for shape, kind in shapes],
         scratch_shapes=[
             pltpu.VMEM((2, LAYER_ROWS, D), bf16),
@@ -642,103 +746,117 @@
         ],
         compiler_params=params(),
         name=name,
-    )(grad, x, vecs, qkv, a, x1, u, slope, own, other)
-    right = jnp.concatenate([low, h[None], h2[None]], 0)
-    return dx, left, right, gvec, gbu, gbq
-
-
-ROWS = 384
-ENC_BLOCKS = (D + 2 * LAYER_ROWS) // ROWS
+    )(grad, source, vecs, h, qkv, a, x1, h2, u, slope, starts, own, other, extra, *last)
+
+
+ROWS = 768
+HALF_ROWS = ROWS // 2
+ENC_ROWS = D + 2 * LAYER_ROWS
+ENC_BLOCKS = ENC_ROWS // ROWS
 PER_LAYER = LAYER_ROWS // ROWS
-RIGHTS = 9
-
-
-def right_of(block):
-    inner = lax.rem(jnp.maximum(block - 2, 0), PER_LAYER)
-    layer = jnp.maximum(block - 2, 0) // PER_LAYER
-    kind = jnp.where(inner < 1, 1, jnp.where(inner < 5, 2, jnp.where(inner < 8, 3, 4)))
-    return jnp.where(block < 2, 0, kind + 4 * layer)
-
-
-def left_factor_kernel(start_ref, left_ref, right_ref, error_part_ref, out_ref):
-    start = split3(start_ref[...])
-    total = error_part_ref[...]
-    for clip in range(2):
-        inner = fold3(nt(start, right_ref[clip, 0]))
-        total = total + fold3(nn(split3(inner), left_ref[clip]))
-    out_ref[...] = total
-
-
-def left_factor(start, left, right, error_part):
-    return pl.pallas_call(
-        left_factor_kernel,
-        grid=(ENC_BLOCKS,),
-        in_specs=[
-            whole((RANK, D)),
-            pl.BlockSpec((2, VIS, ROWS), lambda j: (0, 0, j)),
-            pl.BlockSpec((2, 1, VIS, D), lambda j: (0, right_of(j), 0, 0)),
-            pl.BlockSpec((RANK, ROWS), lambda j: (0, j)),
-        ],
-        out_specs=pl.BlockSpec((RANK, ROWS), lambda j: (0, j)),
-        out_shape=jax.ShapeDtypeStruct((RANK, ENC_BLOCKS * ROWS), f32),
-        compiler_params=params(),
-        name="left_factor",
-    )(start, left, right, error_part)
+
+
+def kinds_of(inner):
+    first = jnp.where(inner < 1, 0, jnp.where(inner < 3, 1, jnp.where(inner < 4, 2, 3)))
+    first = jnp.where(inner == 2, 1, first)
+    second = jnp.where(inner < 2, 1, jnp.where(inner < 4, 2, 3))
+    return jnp.where(inner == 3, 2, first), second
+
+
+def pack_specs():
+    pixel = pl.BlockSpec((VIS, D), lambda j: (0, 0))
+    specs = []
+    for layer in range(2):
+        inner = lambda j, layer=layer: jnp.clip(j - 1 - layer * PER_LAYER, 0, PER_LAYER - 1)
+        at = RIGHT_AT // D
+        specs.append(pl.BlockSpec((VIS, ROWS), lambda j, inner=inner: (0, inner(j))))
+        for side in range(2):
+            specs.append(
+                pl.BlockSpec(
+                    (VIS, D), lambda j, inner=inner, side=side: (0, at + kinds_of(inner(j))[side])
+                )
+            )
+    embed = pl.BlockSpec((VIS, D), lambda j: (0, RIGHT_AT // D + 4))
+    return [pixel, embed] + specs
+
+
+def by_segment(refs, run):
+    step = pl.program_id(0)
+    count = len(refs) // 2
+    mine, theirs = refs[:count], refs[count:]
+
+    @pl.when(step == 0)
+    def _():
+        run((mine[0], theirs[0]), (mine[1], theirs[1]), (mine[1], theirs[1]))
+
+    for layer in range(2):
+        low = 1 + layer * PER_LAYER
+
+        @pl.when(jnp.logical_and(step >= low, step < low + PER_LAYER))
+        def _(at=2 + 3 * layer):
+            run(*((mine[at + index], theirs[at + index]) for index in range(3)))
 
 
 def error_factor_kernel(start_ref, error_ref, out_ref):
-    out_ref[...] = fold3(nt(split3(start_ref[...]), error_ref[...]))
+    turned = nt(error_ref[...], split3(start_ref[...]))
+    out_ref[...] = fold3(turned.T)
 
 
 def error_factor(start, error):
     rows, width = error.shape
     return pl.pallas_call(
         error_factor_kernel,
-        grid=(rows // ROWS,),
-        in_specs=[whole((RANK, width)), pl.BlockSpec((ROWS, width), lambda j: (j, 0))],
-        out_specs=pl.BlockSpec((RANK, ROWS), lambda j: (0, j)),
+        grid=(rows // HALF_ROWS,),
+        in_specs=[whole((RANK, width)), pl.BlockSpec((HALF_ROWS, width), lambda j: (j, 0))],
+        out_specs=pl.BlockSpec((RANK, HALF_ROWS), lambda j: (0, j)),
         out_shape=jax.ShapeDtypeStruct((RANK, rows), f32),
         compiler_params=params(),
         name="error_factor",
     )(start, error)
 
 
-def right_factor_kernel(basis_ref, left_ref, right_ref, error_ref, out_ref):
+def right_factor_kernel(basis_ref, error_ref, *refs):
+    out_ref = refs[-1]
+
     @pl.when(pl.program_id(0) == 0)
     def _():
         out_ref[...] = jnp.zeros_like(out_ref)
 
     basis = split3(basis_ref[...])
-    total = fold3(nn(basis, error_ref[...]))
-    for clip in range(2):
-        inner = fold3(nt(basis, left_ref[clip]))
-        total = total + fold3(nn(split3(inner), right_ref[clip, 0]))
-    out_ref[...] += total
-
-
-def right_factor(basis, left, right, error):
+    out_ref[...] += fold3(nn(basis, error_ref[...]))
+
+    def run(left, first, second):
+        total = jnp.zeros((3 * RANK, D), f32)
+        for clip in range(2):
+            for side, right in ((0, first), (1, second)):
+                lanes = pl.ds(side * HALF_ROWS, HALF_ROWS)
+                inner = fold3(nt(basis[:, side * HALF_ROWS : (side + 1) * HALF_ROWS],
+                                 left[clip][:, lanes]))
+                total = total + nn(split3(inner), right[clip][...])
+        out_ref[...] += fold3(total)
+
+    by_segment(refs[:-1], run)
+
+
+def right_factor(basis, error, mine, theirs):
     return pl.pallas_call(
         right_factor_kernel,
         grid=(ENC_BLOCKS,),
         in_specs=[
             pl.BlockSpec((RANK, ROWS), lambda j: (0, j)),
-            pl.BlockSpec((2, VIS, ROWS), lambda j: (0, 0, j)),
-            pl.BlockSpec((2, 1, VIS, D), lambda j: (0, right_of(j), 0, 0)),
             pl.BlockSpec((ROWS, D), lambda j: (j, 0)),
-        ],
+        ]
+        + pack_specs() * 2,
         out_specs=whole((RANK, D)),
         out_shape=jax.ShapeDtypeStruct((RANK, D), f32),
         compiler_params=params(),
         name="right_factor",
-    )(basis, left, right, error)
-
-
-def residue_kernel(basis_ref, factor_ref, left_ref, right_ref, error_ref, out_ref):
-    total = error_ref[...].astype(f32)
-    total = total - tn(*low_pairs(basis_ref[...], factor_ref[...]))
-    for clip in range(2):
-        total = total + tn(left_ref[clip], right_ref[clip, 0])
-    out_ref[...] = total.astype(bf16)
+    )(basis, error, *pack_args(mine), *pack_args(theirs))
+
+
+def pack_args(packs):
+    pixels, first, second = packs
+    return (pixels, first, first, first, first, second, second, second)
 
 
 def low_pairs(basis, factor):
@@ -751,28 +869,197 @@
     )
 
 
-def residue(basis, factor, left, right, error):
+def residue_kernel(basis_ref, factor_ref, error_ref, *refs):
+    out_ref = refs[-1]
+    basis, factor = low_pairs(basis_ref[...], -factor_ref[...])
+
+    def run(left, first, second):
+        for side, right in ((0, first), (1, second)):
+            rows = pl.ds(side * HALF_ROWS, HALF_ROWS)
+            low = basis[:, side * HALF_ROWS : (side + 1) * HALF_ROWS]
+            lefts = jnp.concatenate([left[0][:, rows], left[1][:, rows], low], 0)
+            rights = jnp.concatenate([right[0][...], right[1][...], factor], 0)
+            out_ref[rows] = (tn(lefts, rights) + error_ref[rows].astype(f32)).astype(bf16)
+
+    by_segment(refs[:-1], run)
+
+
+def residue(basis, factor, error, mine, theirs):
     return pl.pallas_call(
         residue_kernel,
         grid=(ENC_BLOCKS,),
         in_specs=[
             pl.BlockSpec((RANK, ROWS), lambda j: (0, j)),
             whole((RANK, D)),
-            pl.BlockSpec((2, VIS, ROWS), lambda j: (0, 0, j)),
-            pl.BlockSpec((2, 1, VIS, D), lambda j: (0, right_of(j), 0, 0)),
             pl.BlockSpec((ROWS, D), lambda j: (j, 0)),
-        ],
+        ]
+        + pack_specs() * 2,
         out_specs=pl.BlockSpec((ROWS, D), lambda j: (j, 0)),
-        out_shape=jax.ShapeDtypeStruct((ENC_BLOCKS * ROWS, D), bf16),
+        out_shape=jax.ShapeDtypeStruct((ENC_ROWS, D), bf16),
         compiler_params=params(),
         name="residue",
-    )(basis, factor, left, right, error)
-
-
-def basis_kernel(enc_ref, dec_ref, enc_out, dec_out):
+    )(basis, factor, error, *pack_args(mine), *pack_args(theirs))
+
+
+DEC_BLOCK = 1152
+
+
+def dec_right_kernel(basis_ref, comb_ref, out_ref):
+    @pl.when(pl.program_id(0) == 0)
+    def _():
+        out_ref[...] = jnp.zeros_like(out_ref)
+
+    basis = split3(basis_ref[...])
+    comb = comb_ref[...]
+    high = comb.astype(bf16)
+    rest = (comb - high.astype(f32)).astype(bf16)
+    out_ref[...] += fold3(nn(basis, high) + nn(basis, rest))
+
+
+def dec_right_factor(basis, comb):
+    return pl.pallas_call(
+        dec_right_kernel,
+        grid=(DEC_ROWS // DEC_BLOCK,),
+        in_specs=[
+            pl.BlockSpec((RANK, DEC_BLOCK), lambda j: (0, j)),
+            pl.BlockSpec((DEC_BLOCK, DD), lambda j: (j, 0)),
+        ],
+        out_specs=whole((RANK, DD)),
+        out_shape=jax.ShapeDtypeStruct((RANK, DD), f32),
+        compiler_params=params(),
+        name="dec_right_factor",
+    )(basis, comb)
+
+
+def dec_residue_kernel(basis_ref, factor_ref, comb_ref, out_ref):
+    out_ref[...] = (
+        comb_ref[...] + tn(*low_pairs(basis_ref[...], -factor_ref[...]))
+    ).astype(bf16)
+
+
+def dec_residue(basis, factor, comb):
+    return pl.pallas_call(
+        dec_residue_kernel,
+        grid=(DEC_ROWS // DEC_BLOCK,),
+        in_specs=[
+            pl.BlockSpec((RANK, DEC_BLOCK), lambda j: (0, j)),
+            whole((RANK, DD)),
+            pl.BlockSpec((DEC_BLOCK, DD), lambda j: (j, 0)),
+        ],
+        out_specs=pl.BlockSpec((DEC_BLOCK, DD), lambda j: (j, 0)),
+        out_shape=jax.ShapeDtypeStruct((DEC_ROWS, DD), bf16),
+        compiler_params=params(),
+        name="dec_residue",
+    )(basis, factor, comb)
+
+
+def dec_left_kernel(start_ref, grad_ref, out_ref):
+    start = split3(start_ref[0])
+    grad = grad_ref[0]
+    high = grad.astype(bf16)
+    rest = (grad - high.astype(f32)).astype(bf16)
+    out_ref[0] = fold3((nt(high, start) + nt(rest, start)).T)
+
+
+def dec_left_factor(starts, grads):
+    return pl.pallas_call(
+        dec_left_kernel,
+        grid=(2, DEC_ROWS // DEC_BLOCK),
+        in_specs=[
+            pl.BlockSpec((1, RANK, DD), lambda g, j: (g, 0, 0)),
+            pl.BlockSpec((1, DEC_BLOCK, DD), lambda g, j: (g, j, 0)),
+        ],
+        out_specs=pl.BlockSpec((1, RANK, DEC_BLOCK), lambda g, j: (g, 0, j)),
+        out_shape=jax.ShapeDtypeStruct((2, RANK, DEC_ROWS), f32),
+        compiler_params=params(),
+        name="dec_left_factor",
+    )(starts, grads)
+
+
+MESH_ID = pl.DeviceIdType.MESH
+
+
+def greet(workers, me, partner):
+    barrier = pltpu.get_barrier_semaphore()
+    for distance in range(1, workers):
+        pl.semaphore_signal(
+            barrier, 1, device_id={"dp": lax.rem(me + distance, workers)}, device_id_type=MESH_ID
+        )
+    if partner is not None:
+        pl.semaphore_signal(barrier, 1, device_id={"tensor": partner}, device_id_type=MESH_ID)
+    pl.semaphore_wait(barrier, workers - 1 + (partner is not None))
+
+
+def sum_workers(workers, me, lanes, local, slots, sums, sems):
+    def share(index):
+        return pl.ds(pl.multiple_of(index * lanes, 128), lanes)
+
+    def to_all(turn, source, target):
+        copies = []
+        for distance in range(1, workers):
+            peer = lax.rem(me + distance, workers)
+            copy = pltpu.make_async_remote_copy(
+                src_ref=source(peer),
+                dst_ref=target(distance),
+                send_sem=sems.at[2 * turn, distance],
+                recv_sem=sems.at[2 * turn + 1, distance],
+                device_id={"dp": peer},
+                device_id_type=MESH_ID,
+            )
+            copy.start()
+            copies.append(copy)
+        return copies
+
+    copies = to_all(0, lambda peer: local.at[:, share(peer)], lambda distance: slots.at[distance])
+    total = local[:, share(me)]
+    for distance, copy in enumerate(copies, 1):
+        copy.wait_recv()
+        total = total + slots[distance]
+    sums[:, share(me)] = total
+    more = to_all(1, lambda peer: sums.at[:, share(me)], lambda distance: sums.at[:, share(me)])
+    for copy in copies:
+        copy.wait_send()
+    for copy in more:
+        copy.wait()
+
+
+def basis_kernel(
+    workers, lanes, enc_width, first_ref, second_ref, dec_ref, error_ref, dec_error_ref,
+    enc_out, dec_out,
+    send, came, local, slots, sums, sems, pair_sems,
+):
+    me = lax.axis_index("dp")
+    half = lax.axis_index("tensor")
+    first = first_ref.shape[2]
+    second = second_ref.shape[2]
+    width = enc_width + dec_ref.shape[2]
+    spans = ((first_ref, 0, first), (second_ref, first, second), (dec_ref, enc_width, width - enc_width))
+    for ref, at, size in spans:
+        send[:, at : at + size] = ref[1]
+    if width < workers * lanes:
+        tail = jnp.zeros((RANK, workers * lanes - width), f32)
+        send[:, width:] = tail
+    greet(workers, me, 1 - half)
+    copy = pltpu.make_async_remote_copy(
+        src_ref=send,
+        dst_ref=came,
+        send_sem=pair_sems.at[0],
+        recv_sem=pair_sems.at[1],
+        device_id={"tensor": 1 - half},
+        device_id_type=MESH_ID,
+    )
+    copy.start()
+    for ref, at, size in spans[:2]:
+        local[:, at : at + size] = ref[0] + error_ref[:, at : at + size]
+    local[:, enc_width:width] = dec_ref[0] + dec_error_ref[...]
+    if width < workers * lanes:
+        local[:, width:] = tail
+    copy.wait()
+    local[...] += came[...]
+    sum_workers(workers, me, lanes, local, slots, sums, sems)
     place = lax.broadcasted_iota(jnp.int32, (RANK, 1), 0)
-    for ref, out in ((enc_ref, enc_out), (dec_ref, dec_out)):
-        left = ref[...]
+    for at, out in ((0, enc_out), (enc_width, dec_out)):
+        left = sums[:, at : at + out.shape[1]]
         gram = lax.dot_general(
             left, left, (((1,), (1,)), ((), ())), precision=highest_precision,
             preferred_element_type=f32,
@@ -787,15 +1074,77 @@
         out[...] = left
 
 
-def orthonormal(enc_left, dec_left):
-    return pl.pallas_call(
-        basis_kernel,
-        in_specs=[pl.BlockSpec(memory_space=pltpu.VMEM)] * 2,
-        out_specs=[pl.BlockSpec(memory_space=pltpu.VMEM)] * 2,
-        out_shape=[jax.ShapeDtypeStruct(enc_left.shape, f32), jax.ShapeDtypeStruct(dec_left.shape, f32)],
-        compiler_params=params(),
-        name="orthonormal",
-    )(enc_left, dec_left)
+def lanes_for(width, workers):
+    return pl.cdiv(width, 128 * workers) * 128
+
+
+def summed_basis(workers, first, second, dec, error_part, dec_error_part):
+    enc_width = first.shape[2] + second.shape[2]
+    width = enc_width + dec.shape[2]
+    lanes = lanes_for(width, workers)
+    wide = pltpu.VMEM((RANK, workers * lanes), f32)
+    return pl.pallas_call(
+        lambda *refs: basis_kernel(workers, lanes, enc_width, *refs),
+        in_specs=[vmem_spec()] * 5,
+        out_specs=[vmem_spec()] * 2,
+        out_shape=[
+            jax.ShapeDtypeStruct((RANK, enc_width), f32),
+            jax.ShapeDtypeStruct((RANK, width - enc_width), f32),
+        ],
+        scratch_shapes=[
+            wide,
+            wide,
+            wide,
+            pltpu.VMEM((workers, RANK, lanes), f32),
+            wide,
+            pltpu.SemaphoreType.DMA((4, workers)),
+            pltpu.SemaphoreType.DMA((2,)),
+        ],
+        compiler_params=pltpu.CompilerParams(
+            collective_id=1, has_side_effects=True, vmem_limit_bytes=BIG_VMEM
+        ),
+        name="summed_basis",
+    )(first, second, dec, error_part, dec_error_part)
+
+
+def sum_kernel(workers, lanes, *refs):
+    count = (len(refs) - 4) // 2
+    parts, outs = refs[:count], refs[count : 2 * count]
+    local, slots, sums, sems = refs[2 * count :]
+    me = lax.axis_index("dp")
+    at = 0
+    for part in parts:
+        local[:, at : at + part.shape[1]] = part[...]
+        at += part.shape[1]
+    if at < workers * lanes:
+        local[:, at:] = jnp.zeros((RANK, workers * lanes - at), f32)
+    greet(workers, me, None)
+    sum_workers(workers, me, lanes, local, slots, sums, sems)
+    at = 0
+    for out in outs:
+        out[...] = sums[:, at : at + out.shape[1]] * (1.0 / workers)
+        at += out.shape[1]
+
+
+def mean_over_workers(workers, parts):
+    lanes = lanes_for(sum(part.shape[1] for part in parts), workers)
+    wide = pltpu.VMEM((RANK, workers * lanes), f32)
+    return pl.pallas_call(
+        lambda *refs: sum_kernel(workers, lanes, *refs),
+        in_specs=[vmem_spec()] * len(parts),
+        out_specs=[vmem_spec()] * len(parts),
+        out_shape=[jax.ShapeDtypeStruct(part.shape, f32) for part in parts],
+        scratch_shapes=[
+            wide,
+            pltpu.VMEM((workers, RANK, lanes), f32),
+            wide,
+            pltpu.SemaphoreType.DMA((4, workers)),
+        ],
+        compiler_params=pltpu.CompilerParams(
+            collective_id=2, has_side_effects=True, vmem_limit_bytes=BIG_VMEM
+        ),
+        name="mean_over_workers",
+    )(*parts)
 
 
 def cut(block, widths):
@@ -868,38 +1217,38 @@
     kinds = lambda block: block.reshape(3, DD // 2, DD)
     d_qkv = jnp.concatenate([kinds(own_parts[3]), kinds(other_parts[3])], 1).reshape(3 * DD, DD)
 
-    visible = order[:VIS]
-    pos_enc = sinusoid_at(visible, D)
+    pos_enc = sinusoid_at(order[:VIS], D)
     pos_dec = sinusoid_at(order, DD)
+    start_own = factors[0]
+    start_other = swap(start_own)
+    enc_starts = jnp.stack([start_own[:, :D], start_other[:, :D]])
+    dec_starts = jnp.stack([start_own[:, D:], start_other[:, D:]])
+    enc_error_part = error_factor(start_own[:, :D], enc_error[0, 0])
+    dec_error_part = error_factor(start_own[:, D:], dec_error[0, 0])
 
     embed = jnp.concatenate([enc_own[:D], enc_other[:D]], 0)
-    stream = nn(pixels[:VIS], embed) + shared[0] + pos_enc
+    pixels_vis = pixels[:VIS]
+    stream = nn(pixels_vis, embed) + shared[0] + pos_enc
     kept = []
     enc_vecs = []
     for layer in range(2):
         base = 1 + 6 * layer
-        vecs = jnp.concatenate(
-            [jnp.stack(shared[base : base + 6]), jnp.zeros((2, D), f32)], 0
-        )
+        vecs = jnp.stack(shared[base : base + 6] + shared[13:15])
         bq, bv, bu = split_parts[3 * layer : 3 * layer + 3]
         bqkv = jnp.concatenate([bq, jnp.zeros_like(bq), bv], 1)
         result = encoder_layer(
-            D + layer * LAYER_ROWS, stream, vecs, bqkv, bu, enc_own, enc_other, f"encoder_{layer}"
+            D + layer * LAYER_ROWS, stream, vecs, bqkv, bu, enc_own, enc_other,
+            f"encoder_{layer}", proj if layer == 1 else None,
         )
         kept.append((stream, result))
         enc_vecs.append(vecs)
         stream = result[0]
-    unit_e, rate_e = norm_parts(stream)
-    enc_normed = (unit_e * shared[13] + shared[14]).astype(bf16)
-    latent = nn(enc_normed, proj)
-
-    dec_start = pos_dec + jnp.concatenate(
-        [latent, jnp.broadcast_to(shared[15][None], (MASKED, DD))], 0
-    )
+    enc_normed, latent = result[8:]
+
     bq, bv, bu, bh = split_parts[6:]
-    h, qkv = decoder_qkv(
-        dec_start, shared[16][None], shared[17][None], d_qkv,
-        jnp.concatenate([bq, jnp.zeros_like(bq), bv], 1),
+    qkv_vecs = jnp.stack([shared[index] for index in (15, 16, 17, 15, 16, 17, 15, 16)])
+    dec_start, h, qkv = decoder_qkv(
+        pos_dec, latent, qkv_vecs, d_qkv, jnp.concatenate([bq, jnp.zeros_like(bq), bv], 1)
     )
     mixed, logs = attend(qkv)
     scal = jnp.broadcast_to(
@@ -907,57 +1256,35 @@
         (8, 128),
     )
     dec_vecs = jnp.stack([shared[index] for index in (18, 19, 20, 21, 22, 23, 22, 23)])
-    (
-        grad_mixed, grad_middle, g_out, g_down, g_up, g_head, g_vec, g_bu, g_bh, loss_lanes
-    ) = decoder_tokens(
+    grad_mixed, grad_middle, dec_grads, g_vec, g_bu, g_bh, loss_lanes = decoder_tokens(
         mixed, dec_start, pixels, scal, dec_vecs, bu, bh, d_out, d_down, d_up, head_rows
     )
     dq, dk, dv = attend_back(qkv, mixed, grad_mixed, logs)
-    grad_start, g_qkv, g_vec1 = decoder_qkv_back(
-        dq, dk, dv, h, dec_start, grad_middle, shared[16][None], d_qkv
-    )
-    latent_low = grad_start[:VIS].astype(bf16)
-    g_proj = tn(enc_normed, latent_low)
-    grad_normed = nt(latent_low, proj)
-    grad = norm_back(grad_normed, shared[13], unit_e, rate_e)
-
-    proj_parts = g_proj.reshape(2, D // 2, DD)
-    halves = lambda block, index: cut(block, [block.shape[0] // 2] * 2)[index]
-
-    def dec_half(index):
-        g_kinds = g_qkv.reshape(3, 2, DD // 2, DD)[:, index].reshape(3 * DD // 2, DD)
-        first = mine(proj_parts) if index == 0 else theirs(proj_parts)
-        return jnp.concatenate(
-            [first, halves(g_out, index), halves(g_down, index), g_kinds, halves(g_up, index),
-             halves(g_head, index)],
-            0,
-        )
-
-    dec_comb = dec_half(0) + swap(dec_half(1)) + dec_error[0, 0].astype(f32)
-
-    lefts = [None, None]
-    rights = [None, None]
+    latent_low, dec_grads, g_vec1 = decoder_qkv_back(
+        half.astype(jnp.int32)[None], dq, dk, dv, h, dec_start, grad_middle, qkv_vecs, d_qkv,
+        enc_normed, dec_grads,
+    )
+    dec_left = dec_left_factor(dec_starts, dec_grads)
+    dec_comb = dec_grads[0] + swap(dec_grads[1]) + dec_error[0, 0].astype(f32)
+
+    grad = latent_low
+    packs = [None, None]
+    came = [None, None]
+    enc_lefts = [None, None]
     enc_vec_grads = [None, None]
     for layer in (1, 0):
         source, result = kept[layer]
-        grad, lefts[layer], rights[layer], g_vecs, g_hidden, g_qv = encoder_layer_back(
-            D + layer * LAYER_ROWS, grad, source, enc_vecs[layer], result, enc_own, enc_other,
-            f"encoder_back_{layer}",
+        grad, packs[layer], sent, enc_lefts[layer], *enc_vec_grads[layer] = encoder_layer_back(
+            D + layer * LAYER_ROWS, grad, source, enc_vecs[layer], result, enc_starts,
+            enc_own, enc_other, pixels_vis, f"encoder_back_{layer}",
+            (result[0], proj) if layer == 1 else (),
         )
-        enc_vec_grads[layer] = (g_vecs, g_hidden, g_qv)
-    embed_low = grad.astype(bf16)
-    left = jnp.stack(
-        [
-            jnp.concatenate([picked_mine[:VIS], lefts[0][0], lefts[1][0]], 1),
-            jnp.concatenate([picked_theirs[:VIS], swap(lefts[0][1]), swap(lefts[1][1])], 1),
-        ]
-    )
-    right_mine = jnp.concatenate([embed_low[None]] + rights, 0)
-    right = jnp.stack(
-        [
-            right_mine,
-            jnp.concatenate([swap(embed_low)[None]] + [swap(value) for value in rights], 0),
-        ]
+        came[layer] = swap(sent)
+    mine_packs = (picked_mine, packs[0], packs[1])
+    their_packs = (picked_theirs, came[0], came[1])
+
+    enc_basis, dec_basis = summed_basis(
+        workers, enc_lefts[0], enc_lefts[1], dec_left, enc_error_part, dec_error_part
     )
 
     def split_half(index):
@@ -977,50 +1304,45 @@
         ]
         return jnp.concatenate(pieces)
 
+    g_vec_enc = [grads[0] for grads in enc_vec_grads]
     shared_grad = jnp.concatenate(
-        [jnp.sum(embed_low.astype(f32), 0)]
-        + [enc_vec_grads[layer][0][:6].reshape(-1) for layer in range(2)]
-        + [jnp.sum(grad_normed * unit_e, 0), jnp.sum(grad_normed, 0)]
+        [g_vec_enc[0][6], g_vec_enc[0][:6].reshape(-1), g_vec_enc[1].reshape(-1)]
         + [g_vec1[4], g_vec1[2], g_vec1[3], g_vec[:6].reshape(-1)]
     )
     loss_part = jnp.sum(loss_lanes) / PIX
-    sent = jnp.concatenate([split_half(1), shared_grad, loss_part[None]])
-    local = jnp.concatenate([split_half(0), shared_grad, loss_part[None]])
-    vec_local = local + swap(sent)
-
-    enc_error_part = error_factor(factors[0, :, :D], enc_error[0, 0])
-    enc_left = left_factor(factors[0, :, :D], left, right, enc_error_part)
-    dec_left = jnp.einsum("rc,xc->rx", factors[0, :, D:], dec_comb, precision=highest_precision)
-    enc_left, dec_left, vec_sum = lax.psum((enc_left, dec_left, vec_local), "dp")
-    enc_basis, dec_basis = orthonormal(enc_left, dec_left)
+    split_len = split_own.shape[0]
+    length = split_len + shared_grad.shape[0] + 1
+    vec_lanes = pl.cdiv(length, RANK * 128) * 128
+    fill = jnp.zeros((RANK * vec_lanes - length,), f32)
+    sent = jnp.concatenate([split_half(1), shared_grad, loss_part[None], fill])
+    local = jnp.concatenate([split_half(0), shared_grad, loss_part[None], fill])
+    vec_local = (local + swap(sent)).reshape(RANK, vec_lanes)
+
     enc_rows = enc_basis.shape[1] // workers
     dec_rows = dec_basis.shape[1] // workers
     enc_owned = lax.dynamic_slice_in_dim(enc_basis, worker_index * enc_rows, enc_rows, 1)
     dec_owned = lax.dynamic_slice_in_dim(dec_basis, worker_index * dec_rows, dec_rows, 1)
-    enc_right, dec_right = lax.psum(
+    enc_right, dec_right, vec_mean = mean_over_workers(
+        workers,
         (
-            right_factor(enc_basis, left, right, enc_error[0, 0]),
-            jnp.einsum("rx,xc->rc", dec_basis, dec_comb, precision=highest_precision),
+            right_factor(enc_basis, enc_error[0, 0], mine_packs, their_packs),
+            dec_right_factor(dec_basis, dec_comb),
+            vec_local,
         ),
-        "dp",
-    )
-    enc_right = enc_right / workers
-    dec_right = dec_right / workers
-    enc_error_new = residue(enc_basis, enc_right, left, right, enc_error[0, 0])
-    dec_error_new = (
-        dec_comb - jnp.einsum("rx,rc->xc", dec_basis, dec_right, precision=highest_precision)
-    ).astype(bf16)
+    )
+    vec_mean = vec_mean.reshape(-1)
+    enc_error_new = residue(enc_basis, enc_right, enc_error[0, 0], mine_packs, their_packs)
+    dec_error_new = dec_residue(dec_basis, dec_right, dec_comb)
     enc_mom = momentum_keep * enc_moment[0] + jnp.einsum(
         "rx,rc->xc", enc_owned, enc_right, precision=highest_precision
     )
     dec_mom = momentum_keep * dec_moment[0] + jnp.einsum(
         "rx,rc->xc", dec_owned, dec_right, precision=highest_precision
     )
-    split_len = split_own.shape[0]
-    split_mom = momentum_keep * split_moment[0] + vec_sum[:split_len] / workers
-    shared_mom = momentum_keep * shared_moment + vec_sum[split_len:-1] / workers
+    split_mom = momentum_keep * split_moment[0] + vec_mean[:split_len]
+    shared_mom = momentum_keep * shared_moment + vec_mean[split_len : length - 1]
     return (
-        vec_sum[-1],
+        vec_mean[length - 1] * workers,
         loss_weight,
         (enc_weights[0] - step_rate * enc_mom)[None],
         enc_mom[None],

time: 927 us -> 728 us (0.79)
  waiting for transfers between devices: 288 us -> 187 us
  blocking collectives: 116 us -> 39.9 us
  Pallas kernels: 347 us -> 390 us
  local copies, waits for them, and re-layouts: 60.8 us -> 31.9 us
  matrix products: 30.8 us -> 7.54 us
  other arithmetic: 55.9 us -> 40 us
    psum x1 -> x0, waiting for transfers between devices: 105 us -> none  [per_device(): lax.psum((enc_left, dec_left, vec_local), 'dp')]
    psum x1 -> x0, blocking collectives: 75.4 us -> none  [per_device(): lax.psum((right_factor(enc_basis, left, right, enc_error[0, 0]), jnp.eins...]
    pallas_call x8 -> x12, Pallas kernels: 118 us -> 171 us  [the longest x2 40.3 us: encoder_layer_back(): pl.pallas_call(lambda *refs: encoder_back_kernel(start, bool(last), *refs...]
    dot_general x5 -> x0, matrix products: 22.2 us -> none  [the longest x1 7.55 us: per_device(): jnp.einsum('rx,rc->xc', dec_basis, dec_right, precision=highest_precision)]
    unnamed x161 -> x74, local copies, waits for them, and re-layouts: 14.8 us -> 1.86 us
    select_n x0 -> x2, other arithmetic: none -> 10.8 us  [the longest x1 9.81 us: sinusoid_at(): return jnp.where(column % 2 == 0, jnp.sin(angle), jnp.cos(angle))]
    add x3 -> x2, other arithmetic: 16.9 us -> 7.04 us  [the longest x1 7.03 us: per_device(): dec_comb = dec_grads[0] + swap(dec_grads[1]) + dec_error[0, 0].astype(f32)]
  transfers between devices with their start and end apart: 14 -> 11, of which waited for: 3 -> 2; matrix products, arithmetic and copies ran while one was open for 9% -> 7% of each run, Pallas kernels for 7% -> 20%
where the time goes in v2:
time: 728 us; the launch traced here: 719 us
  Pallas kernels  390 us (54%)
  waiting for transfers between devices  187 us (26%)
  other arithmetic  40 us (5%)
  blocking collectives  39.9 us (5%)
  local copies, waits for them, and re-layouts  31.9 us (4%)
  between operations  20.9 us (3%)
  matrix products  7.54 us (1%)
    all_gather x1, waiting for transfers between devices, per_device(): lax.all_gather(enc_weights[0].astype(bf16), 'dp', axis=0, tiled=True)  182 us
    pallas_call x1, Pallas kernels, decoder_tokens(): pl.pallas_call(token_kernel, grid=(TUBES // TOKEN_ROWS,), in_specs=[rows(...  65 us
    pallas_call x1, Pallas kernels, attend_back(): pl.pallas_call(attend_back_kernel, grid=(PAIRS, pl.cdiv(TUBES, BWD_ROWS))...  53.8 us
    pallas_call x2, Pallas kernels, encoder_layer_back(): pl.pallas_call(lambda *refs: encoder_back_kernel(start, bool(last), *refs...  40.3 us
    psum x1, blocking collectives, per_device(): loss_weight = MASKED * lax.psum(jnp.sum(counted_all), 'dp')  39.9 us
    pallas_call x1, Pallas kernels, attend(): pl.pallas_call(attend_kernel, grid=(PAIRS, TUBES // FWD_ROWS), in_specs=[...  32.5 us
    pallas_call x1, Pallas kernels, summed_basis(): pl.pallas_call(lambda *refs: basis_kernel(workers, lanes, enc_width, *ref...  28.7 us
    pallas_call x2, Pallas kernels, error_factor(): pl.pallas_call(error_factor_kernel, grid=(rows // HALF_ROWS,), in_specs=[...  27 us
  transfers between devices with their start and end apart: 11, of which 2 were waited for; matrix products, arithmetic and copies ran while one was open for 7% of the time, Pallas kernels for 20%

profile of v2, /device:TPU:0, one launch (start us, length us, event | category | flops | bytes accessed | tf_op | source)
XLA Modules:
  0.0 719.5 jit_solution(14162457304913545596)
XLA Ops:
  7.2 2.6 bitcast_convert_fusion
  9.9 182.3 %all-gather.3.cloned.1.call-done.refs_4_.refs_11_ = bf16[9984,768]{1,0:T(8,128)(2,1)} async-done(((bf16[624,768]{1,0:T(8,128)(2,1)}), bf16[9984,768]{1,0:T(8,128)(2,1)}) %all-gather.3.cloned.1.call-update) | async-done | bytes 15335440 | tf_op jit(solution)/shard_map/all_gather | solution.py:1183
  192.2 0.7 bitcast_convert_fusion.1
  192.9 1.7 copy.28.order_ref
  194.6 16.7 %pick_tubes.1 = bf16[2,1568,768]{2,1,0:T(8,128)(2,1)} custom-call(s32[2,1568,1]{2,1,0:T(8,128)} %copy.28.order_ref, bf16[2,1568,768]{2,1,0:T(8,128)(2,1)} %tubes_ref.1), custom_call_target="tpu_custom_call" | custom-call | tf_op jit(solution)/shard_map/pick_tubes/pallas_call | solution.py:122
  211.3 4.2 dynamic-slice_bitcast_fusion
  216.9 9.8 %fusion.1.pos_ref = f32[1568,384]{1,0:T(8,128)} fusion(f32[384]{0:T(512)S(1)} %fusion.36, f32[1568]{0:T(1024)S(1)} %convert_reduce_fusion, pred[384]{0:T(512)(128)(4,1)S(1)} %fusion.30), kind=kLoop, calls=%fused_computation.8 | loop fusion | flops 1204224 | bytes 2416640 | tf_op jit(solution)/shard_map/jit(_where)/select_n | solution.py:92
  226.8 39.9 %psum.7 = f32[]{:T(128)} all-reduce(f32[]{:T(128)} %convert_reduce_fusion.1), channel_id=1, replica_groups=mesh['dp'=16,'tensor'=2] {'dp'}, use_global_device_ids=true, to_apply=%region_1.0 | all-reduce | flops 1 | bytes 8 | tf_op jit(solution)/shard_map/psum | solution.py:1187
  268.8 4.6 stack.142
  273.5 0.6 stack.140.vec_ref
  274.1 0.6 stack.129.refs_1_.refs_2_
  274.8 0.6 stack.136.refs_1_.refs_2_
  275.4 0.6 stack.149.vec_ref
  277.5 0.6 pad_maximum_fusion.8
  278.1 0.6 pad_maximum_fusion.9
  279.3 0.6 pad_maximum_fusion.11
  280.0 1.0 fusion.13.refs_13_
  281.0 4.4 pad_maximum_fusion.pix_ref
  285.8 0.7 pad_maximum_fusion.5.wo_ref
  286.5 1.0 maximum_select_fusion.refs_6_.refs_15_
  287.5 1.0 pad_maximum_fusion.4
  288.7 1.2 pad_maximum_fusion.3.wh_ref
  289.9 1.7 pad_maximum_fusion.1
  291.6 1.3 slice.529
  293.0 1.3 slice.530
  294.3 3.4 fusion.10.refs_0_.refs_1_
  297.7 12.4 %encoder_0.1 = (f32[160,768]{1,0:T(8,128)}, bf16[160,768]{1,0:T(8,128)(2,1)}, bf16[160,2304]{1,0:T(8,128)(2,1)}, bf16[160,768]{1,0:T(8,128)(2,1)}, f32[160,768]{...) custom-call(f32[160,768]{1,0:T(8,128)} %fusion.10.refs_0_.refs_1_, ...), custom_call_target="tpu_custom_call" | custom-call | tf_op jit(solution)/shard_map/encoder_0/pallas_call | solution.py:592
  310.1 12.9 %encoder_1.1 = (f32[160,768]{1,0:T(8,128)}, bf16[160,768]{1,0:T(8,128)(2,1)}, bf16[160,2304]{1,0:T(8,128)(2,1)}, bf16[160,768]{1,0:T(8,128)(2,1)}, f32[160,768]{...) custom-call(f32[160,768]{1,0:T(8,128)} %get-tuple-element.67.refs_0_, ...), custom_call_target="tpu_custom_call" | custom-call | tf_op jit(solution)/shard_map/encoder_1/pallas_call | solution.py:592
  323.0 7.2 %decoder_qkv.1 = (f32[1568,384]{1,0:T(8,128)}, bf16[1568,384]{1,0:T(8,128)(2,1)}, bf16[1568,1152]{1,0:T(8,128)(2,1)}) custom-call(f32[1568,384]{1,0:T(8,128)} %fusion.1.pos_ref, f32[160,384]{1,0:T(8,128)} %get-tuple-element.68.latent_ref, f32[8,384]{1,0:T(8,128)} %stack.140.vec_ref, bf16[1152,384]{1,0:T(8,128)(2,1)} %bitcast.74, f32[1,1152]{1,0:T(1,128)} %fusion.18.bias_ref), custom_call_target="tpu_custom_call" | custom-call | tf_op jit(solution)/shard_map/decoder_qkv/pallas_call | solution.py:153
  330.3 32.5 %attend.1 = (f32[1568,384]{1,0:T(8,128)}, f32[3,1568,128]{2,1,0:T(8,128)}) custom-call(bf16[1568,1152]{1,0:T(8,128)(2,1)} %get-tuple-element.69.q_ref.k_ref.v_ref, bf16[1568,1152]{1,0:T(8,128)(2,1)} %get-tuple-element.69.q_ref.k_ref.v_ref, bf16[1568,1152]{1,0:T(8,128)(2,1)} %get-tuple-element.69.q_ref.k_ref.v_ref), custom_call_target="tpu_custom_call" | custom-call | tf_op jit(solution)/shard_map/attend/pallas_call | solution.py:201
  362.7 0.7 broadcast_in_dim.105.scal_ref
  363.4 65.0 %decoder_tokens.1 = (bf16[1568,384]{1,0:T(8,128)(2,1)}, f32[1568,384]{1,0:T(8,128)}, f32[2,3456,384]{2,1,0:T(8,128)}, f32[8,384]{1,0:T(8,128)}, f32[1,1536]{1,0:...) custom-call(f32[1568,384]{1,0:T(8,128)} %get-tuple-element.70.a_ref.o_ref, f32[1568,384]{1,0:T(8,128)} %get-tuple-element.71.x_ref, ...), custom_call_target="tpu_custom_call" | custom-call | tf_op jit(solution)/shard_map/decoder_tokens/pallas_call | solution.py:381
  428.4 53.8 %attend_back.1 = (bf16[1568,384]{1,0:T(8,128)(2,1)}, bf16[1568,384]{1,0:T(8,128)(2,1)}, bf16[1568,384]{1,0:T(8,128)(2,1)}) custom-call(bf16[1568,1152]{1,0:T(8,128)(2,1)} %get-tuple-element.69.q_ref.k_ref.v_ref, bf16[1568,1152]{1,0:T(8,128)(2,1)} %get-tuple-element.69.q_ref.k_ref.v_ref, bf16[1568,1152]{1,0:T(8,128)(2,1)} %get-tuple-element.69.q_ref.k_ref.v_ref, ...), custom_call_target="tpu_custom_call" | custom-call | tf_op jit(solution)/shard_map/attend_back/pallas_call | solution.py:271
  482.2 11.9 %decoder_qkv_back.1 = (bf16[160,384]{1,0:T(8,128)(2,1)}, f32[2,3456,384]{2,1,0:T(8,128)}, f32[8,384]{1,0:T(8,128)}) custom-call(s32[1]{0:T(128)} %bitcast.half_ref, bf16[1568,384]{1,0:T(8,128)(2,1)} %get-tuple-element.74.dq_ref, bf16[1568,384]{1,0:T(8,128)(2,1)} %get-tuple-element.75.dk_ref, ...), custom_call_target="tpu_custom_call", output_to_operand_aliasing={{1}: (10, {})} | custom-call | tf_op jit(solution)/shard_map/decoder_qkv_back/pallas_call | solution.py:467
  494.1 5.2 slice_bitcast_fusion
  499.8 0.6 fusion.50
  500.4 5.0 collective-permute-done.4
  505.4 0.6 pad_maximum_fusion.6.refs_10_
  506.1 20.0 %encoder_back_1.1 = (f32[160,768]{1,0:T(8,128)}, bf16[160,7680]{1,0:T(8,128)(2,1)}, bf16[160,7680]{1,0:T(8,128)(2,1)}, f32[2,8,4608]{2,1,0:T(8,128)}, f32[8,768]...) custom-call(bf16[160,384]{1,0:T(8,128)(2,1)} %get-tuple-element.81.refs_0_, ...), custom_call_target="tpu_custom_call" | custom-call | tf_op jit(solution)/shard_map/encoder_back_1/pallas_call | solution.py:736
  526.0 20.3 %encoder_back_0.1 = (f32[160,768]{1,0:T(8,128)}, bf16[160,8448]{1,0:T(8,128)(2,1)}, bf16[160,8448]{1,0:T(8,128)(2,1)}, f32[2,8,5376]{2,1,0:T(8,128)}, f32[8,768]...) custom-call(f32[160,768]{1,0:T(8,128)} %get-tuple-element.90.refs_0_, f32[160,768]{1,0:T(8,128)} %fusion.10.refs_0_.refs_1_, ...), custom_call_target="tpu_custom_call" | custom-call | tf_op jit(solution)/shard_map/encoder_back_0/pallas_call | solution.py:736
  547.6 20.0 %error_factor.2.refs_3_ = f32[8,9984]{1,0:T(8,128)} custom-call(f32[8,768]{1,0:T(8,128)} %get-tuple-element.186.start_ref, bf16[9984,768]{1,0:T(8,128)(2,1)} %bitcast.69), custom_call_target="tpu_custom_call" | custom-call | tf_op jit(solution)/shard_map/error_factor/pallas_call | solution.py:807
  568.3 6.9 error_factor.3.refs_4_
  575.4 0.6 reduce_sum.19
  576.8 0.6 slice_reduce_fusion.15
  577.4 0.6 slice_reduce_fusion.13
  579.0 0.6 pad_maximum_fusion.7.start_ref
  579.6 8.2 %dec_left_factor.1.refs_2_ = f32[2,8,3456]{2,1,0:T(8,128)} custom-call(f32[2,8,384]{2,1,0:T(8,128)} %pad_maximum_fusion.7.start_ref, f32[2,3456,384]{2,1,0:T(8,128)} %get-tuple-element.100.grad_ref), custom_call_target="tpu_custom_call" | custom-call | tf_op jit(solution)/shard_map/dec_left_factor/pallas_call | solution.py:965
  587.7 28.7 %summed_basis.1 = (f32[8,9984]{1,0:T(8,128)}, f32[8,3456]{1,0:T(8,128)}) custom-call(f32[2,8,5376]{2,1,0:T(8,128)} %get-tuple-element.98.refs_0_, f32[2,8,4608]{2,1,0:T(8,128)} %get-tuple-element.99.refs_1_, f32[2,8,3456]{2,1,0:T(8,128)} %dec_left_factor.1.refs_2_, f32[8,9984]{1,0:T(8,128)} %error_factor.2.refs_3_, f32[8,3456]{1,0:T(8,128)} %error_factor.3.refs_4_), custom_call_target="tpu_custom_call" | custom-call | tf_op jit(solution)/shard_map/summed_basis/pallas_call | solution.py:1086
  616.6 0.7 reshape.145.refs_2_
  617.2 1.5 copy-done
  618.8 21.9 %right_factor.1.refs_0_ = f32[8,768]{1,0:T(8,128)} custom-call(f32[8,9984]{1,0:T(8,128)} %get-tuple-element.101.basis_ref, bf16[9984,768]{1,0:T(8,128)(2,1)} %bitcast.70, bf16[1568,768]{1,0:T(8,128)(2,1)} %copy-done.1, bf16[160,8448]{1,0:T(8,128)(2,1)} %get-tuple-element.102.refs_1_.refs_2_.refs_3_.refs_4_, ...), custom_call_target="tpu_custom_call" | custom-call | tf_op jit(solution)/shard_map/right_factor/pallas_call | solution.py:842
  640.7 7.0 fusion.comb_ref
  647.7 4.5 dec_right_factor.1.refs_1_
  652.2 19.4 %mean_over_workers.1 = (f32[8,768]{1,0:T(8,128)}, f32[8,384]{1,0:T(8,128)}, f32[8,2816]{1,0:T(8,128)}) custom-call(f32[8,768]{1,0:T(8,128)} %right_factor.1.refs_0_, f32[8,384]{1,0:T(8,128)} %dec_right_factor.1.refs_1_, f32[8,2816]{1,0:T(8,128)} %reshape.145.refs_2_), custom_call_target="tpu_custom_call" | custom-call | tf_op jit(solution)/shard_map/mean_over_workers/pallas_call | solution.py:1132
  671.6 6.0 dec_residue.1
  677.7 0.6 maximum_bitcast_fusion
  678.3 1.3 convolution_add_fusion
  679.6 0.8 fusion.15
  680.4 2.8 bitcast_add_fusion.1
  683.3 1.7 fusion.6
  685.7 0.6 broadcast_in_dim.117
  686.3 0.6 broadcast_in_dim.118
  686.9 0.7 multiply_subtract_fusion
  688.2 21.7 %residue.1 = bf16[9984,768]{1,0:T(8,128)(2,1)} custom-call(f32[8,9984]{1,0:T(8,128)} %get-tuple-element.101.basis_ref, f32[8,768]{1,0:T(8,128)} %get-tuple-element.119.factor_ref, bf16[9984,768]{1,0:T(8,128)(2,1)} %bitcast.71, bf16[1568,768]{1,0:T(8,128)(2,1)} %copy-done.1, bf16[160,8448]{1,0:T(8,128)(2,1)} %get-tuple-element.102.refs_1_.refs_2_.refs_3_.refs_4_, ...), custom_call_target="tpu_custom_call" | custom-call | tf_op jit(solution)/shard_map/residue/pallas_call | solution.py:888
  (184 shorter events, 8.7 us)
Async XLA Ops:
  7.2 185.0 %copy-start.9 = (f32[1,216,384]{2,1,0:T(8,128)S(1)}, f32[1,216,384]{2,1,0:T(8,128)}, u32[]{:S(2)}) copy-start(f32[1,216,384]{2,1,0:T(8,128)} %param.18) | copy-start | bytes 995332
  7.2 185.7 %copy-start.18 = (s32[2,1568]{1,0:T(2,128)S(1)}, s32[2,1568]{1,0:T(2,128)}, u32[]{:S(2)}) copy-start(s32[2,1568]{1,0:T(2,128)} %param.15) | copy-start | bytes 37636
  7.2 185.0 %all-gather.3.cloned.1.call-start = ((), (), s32[]{:S(2)}) async-start(), calls=%async_computation | async-start | bytes 16293888 | tf_op jit(solution)/shard_map/all_gather | solution.py:1183
  9.9 266.2 %all-gather.5.cloned.1.call-start = ((), (), s32[]{:S(2)}) async-start(), calls=%async_computation.1 | async-start | bytes 2820096 | tf_op jit(solution)/shard_map/all_gather | solution.py:1182
  192.2 100.8 %collective-permute-start.1 = (bf16[9984,768]{1,0:T(8,128)(2,1)}, bf16[9984,768]{1,0:T(8,128)(2,1)}, u32[]{:S(2)}, u32[]{:S(2)}) collective-permute-start(bf16[9984,768]{1,0:T(8,128)(2,1)} %all-gather.3.cloned.1.call-done.refs_4_.refs_11_), channel_id=1, source_target_pairs={{0,1},{1,0},{2,3},{3,2},{4,5},{5,4},{6,7},{7,6},{8,9},{9,8},{10,11... | collective-permute-start | bytes 46006280 | tf_op jit(solution)/shard_map/ppermute | solution.py:1160
  211.3 4.7 copy-start.14
  211.3 4.9 copy-start.36
  211.3 5.6 copy-start.11
  215.5 65.5 %copy-start.1 = (bf16[1568,768]{1,0:T(8,128)(2,1)}, bf16[1568,768]{1,0:T(8,128)(2,1)S(1)}, u32[]{:S(2)}) copy-start(bf16[1568,768]{1,0:T(8,128)(2,1)S(1)} %get-tuple-element.153.refs_0_) | copy-start | bytes 7225348
  215.5 64.5 %collective-permute-start = (bf16[1568,768]{1,0:T(8,128)(2,1)}, bf16[1568,768]{1,0:T(8,128)(2,1)}, u32[]{:S(2)}, u32[]{:S(2)}) collective-permute-start(bf16[1568,768]{1,0:T(8,128)(2,1)} %get-tuple-element.152.refs_8_), channel_id=1, source_target_pairs={{0,1},{1,0},{2,3},{3,2},{4,5},{5,4},{6,7},{7,6},{8,9},{9,8},{10,11... | collective-permute-start | bytes 7225352 | tf_op jit(solution)/shard_map/ppermute | solution.py:1160
  216.0 60.0 %collective-permute-start.2 = (f32[6528]{0:T(1024)S(1)}, f32[6528]{0:T(1024)S(1)}, u32[]{:S(2)}, u32[]{:S(2)}) collective-permute-start(f32[6528]{0:T(1024)S(1)} %reduce.2), channel_id=1, source_target_pairs={{0,1},{1,0},{2,3},{3,2},{4,5},{5,4},{6,7},{7,6},{8,9},{9,8},{10,11... | collective-permute-start | bytes 78344 | tf_op jit(solution)/shard_map/ppermute | solution.py:1160
  276.1 9.5 %collective-permute-start.3 = (bf16[3456,384]{1,0:T(8,128)(2,1)}, bf16[3456,384]{1,0:T(8,128)(2,1)S(1)}, u32[]{:S(2)}, u32[]{:S(2)}) collective-permute-start(bf16[3456,384]{1,0:T(8,128)(2,1)} %all-gather.5.cloned.1.call-done), channel_id=1, source_target_pairs={{0,1},{1,0},{2,3},{3,2},{4,5},{5,4},{6,7},{7,6},{8,9},{9,8},{10,11... | collective-permute-start | bytes 7962632 | tf_op jit(solution)/shard_map/ppermute | solution.py:1160
  281.0 13.4 %copy-start.5 = (bf16[160,1536]{1,0:T(8,128)(2,1)}, bf16[160,1536]{1,0:T(8,128)(2,1)S(1)}, u32[]{:S(2)}) copy-start(bf16[160,1536]{1,0:T(8,128)(2,1)S(1)} %fusion.13.refs_13_) | copy-start | bytes 1474564
  281.0 4.4 copy-start.6
  494.1 5.7 copy-start.17
  499.3 141.4 %collective-permute-start.7 = (f32[3456,384]{1,0:T(8,128)}, f32[3456,384]{1,0:T(8,128)}, u32[]{:S(2)}, u32[]{:S(2)}) collective-permute-start(f32[3456,384]{1,0:T(8,128)} %slice_bitcast_fusion), channel_id=1, source_target_pairs={{0,1},{1,0},{2,3},{3,2},{4,5},{5,4},{6,7},{7,6},{8,9},{9,8},{10,11... | collective-permute-start | bytes 15925256 | tf_op jit(solution)/shard_map/ppermute | solution.py:1160
  499.8 5.7 collective-permute-start.4
  546.4 70.9 %collective-permute-start.5 = (bf16[160,8448]{1,0:T(8,128)(2,1)}, bf16[160,8448]{1,0:T(8,128)(2,1)S(1)}, u32[]{:S(2)}, u32[]{:S(2)}) collective-permute-start(bf16[160,8448]{1,0:T(8,128)(2,1)} %get-tuple-element.104), channel_id=1, source_target_pairs={{0,1},{1,0},{2,3},{3,2},{4,5},{5,4},{6,7},{7,6},{8,9},{9,8},{10,11... | collective-permute-start | bytes 8110088 | tf_op jit(solution)/shard_map/ppermute | solution.py:1160
  546.6 70.7 %collective-permute-start.6 = (bf16[160,7680]{1,0:T(8,128)(2,1)}, bf16[160,7680]{1,0:T(8,128)(2,1)}, u32[]{:S(2)}, u32[]{:S(2)}) collective-permute-start(bf16[160,7680]{1,0:T(8,128)(2,1)} %get-tuple-element.105), channel_id=1, source_target_pairs={{0,1},{1,0},{2,3},{3,2},{4,5},{5,4},{6,7},{7,6},{8,9},{9,8},{10,11... | collective-permute-start | bytes 7372808 | tf_op jit(solution)/shard_map/ppermute | solution.py:1160
  567.6 7.6 %copy-start.20 = (f32[1,6528]{1,0:T(1,128)S(1)}, f32[1,6528]{1,0:T(1,128)}, u32[]{:S(2)}) copy-start(f32[1,6528]{1,0:T(1,128)} %param.23) | copy-start | bytes 78340
  567.6 7.7 %copy-start.19 = (f32[8,768]{1,0:T(8,128)S(1)}, f32[8,768]{1,0:T(8,128)}, u32[]{:S(2)}) copy-start(f32[8,768]{1,0:T(8,128)} %get-tuple-element.114) | copy-start | bytes 73732
  567.6 7.7 %copy-start.21 = (f32[8,768]{1,0:T(8,128)S(1)}, f32[8,768]{1,0:T(8,128)}, u32[]{:S(2)}) copy-start(f32[8,768]{1,0:T(8,128)} %get-tuple-element.115) | copy-start | bytes 73732
  567.6 7.8 %copy-start.24 = (f32[8,384]{1,0:T(8,128)S(1)}, f32[8,384]{1,0:T(8,128)}, u32[]{:S(2)}) copy-start(f32[8,384]{1,0:T(8,128)} %get-tuple-element.116) | copy-start | bytes 36868
  567.6 7.8 %copy-start.33 = (f32[1,1536]{1,0:T(1,128)S(1)}, f32[1,1536]{1,0:T(1,128)}, u32[]{:S(2)}) copy-start(f32[1,1536]{1,0:T(1,128)} %get-tuple-element.117) | copy-start | bytes 18436
  567.6 9.0 %copy-start.30 = (f32[1,1536]{1,0:T(1,128)S(1)}, f32[1,1536]{1,0:T(1,128)}, u32[]{:S(2)}) copy-start(f32[1,1536]{1,0:T(1,128)} %get-tuple-element.113) | copy-start | bytes 18436
  567.6 9.1 %copy-start.29 = (f32[1,1536]{1,0:T(1,128)S(1)}, f32[1,1536]{1,0:T(1,128)}, u32[]{:S(2)}) copy-start(f32[1,1536]{1,0:T(1,128)} %get-tuple-element.112) | copy-start | bytes 18436
  567.7 9.1 %copy-start.32 = (f32[2,768]{1,0:T(2,128)S(1)}, f32[2,768]{1,0:T(2,128)}, u32[]{:S(2)}) copy-start(f32[2,768]{1,0:T(2,128)} %get-tuple-element.107) | copy-start | bytes 18436
  567.7 9.7 %copy-start.31 = (f32[2,768]{1,0:T(2,128)S(1)}, f32[2,768]{1,0:T(2,128)}, u32[]{:S(2)}) copy-start(f32[2,768]{1,0:T(2,128)} %get-tuple-element.109) | copy-start | bytes 18436
  567.7 10.3 %copy-start.23 = (f32[1,3072]{1,0:T(1,128)S(1)}, f32[1,3072]{1,0:T(1,128)}, u32[]{:S(2)}) copy-start(f32[1,3072]{1,0:T(1,128)} %get-tuple-element.108) | copy-start | bytes 36868
  567.7 10.3 %copy-start.22 = (f32[1,3072]{1,0:T(1,128)S(1)}, f32[1,3072]{1,0:T(1,128)}, u32[]{:S(2)}) copy-start(f32[1,3072]{1,0:T(1,128)} %get-tuple-element.110) | copy-start | bytes 36868
  567.7 10.4 %copy-start.28 = (f32[8,384]{1,0:T(8,128)S(1)}, f32[8,384]{1,0:T(8,128)}, u32[]{:S(2)}) copy-start(f32[8,384]{1,0:T(8,128)} %get-tuple-element.111) | copy-start | bytes 36868
  578.8 37.8 %collective-permute-start.8 = (f32[22528]{0:T(1024)S(1)}, f32[22528]{0:T(1024)S(1)}, u32[]{:S(2)}, u32[]{:S(2)}) collective-permute-start(f32[22528]{0:T(1024)S(1)} %concatenate.101), channel_id=1, source_target_pairs={{0,1},{1,0},{2,3},{3,2},{4,5},{5,4},{6,7},{7,6},{8,9},{9,8},{10,11... | collective-permute-start | bytes 270344 | tf_op jit(solution)/shard_map/ppermute | solution.py:1160
  579.6 36.9 %copy-start.25 = (f32[384]{0:T(512)S(1)}, f32[384]{0:T(512)}, u32[]{:S(2)}) copy-start(f32[384]{0:T(512)} %get-tuple-element.147) | copy-start | bytes 4612
  579.6 36.9 %copy-start.26 = (f32[384]{0:T(512)S(1)}, f32[384]{0:T(512)}, u32[]{:S(2)}) copy-start(f32[384]{0:T(512)} %get-tuple-element.142) | copy-start | bytes 4612
  579.6 36.9 %copy-start.27 = (f32[384]{0:T(512)S(1)}, f32[384]{0:T(512)}, u32[]{:S(2)}) copy-start(f32[384]{0:T(512)} %get-tuple-element.143) | copy-start | bytes 4612
  579.6 36.9 %copy-start.34 = (f32[1,192]{1,0:T(1,128)S(1)}, f32[1,192]{1,0:T(1,128)}, u32[]{:S(2)}) copy-start(f32[1,192]{1,0:T(1,128)} %get-tuple-element.202) | copy-start | bytes 2308
  579.6 36.9 %copy-start.35 = (f32[1,192]{1,0:T(1,128)S(1)}, f32[1,192]{1,0:T(1,128)}, u32[]{:S(2)}) copy-start(f32[1,192]{1,0:T(1,128)} %get-tuple-element.203) | copy-start | bytes 2308
  617.2 1.5 copy-start
  618.8 21.9 %copy-start.2 = (bf16[1,1,3456,384]{3,2,1,0:T(8,128)(2,1)S(1)}, bf16[1,1,3456,384]{3,2,1,0:T(8,128)(2,1)}, u32[]{:S(2)}) copy-start(bf16[1,1,3456,384]{3,2,1,0:T(8,128)(2,1)} %param.26) | copy-start | bytes 7962628
  671.6 6.1 copy-start.12
  671.6 6.1 copy-start.13
  671.6 6.7 copy-start.10
  671.6 8.8 %copy-start.7 = (f32[1,624,768]{2,1,0:T(8,128)S(1)}, f32[1,624,768]{2,1,0:T(8,128)}, u32[]{:S(2)}) copy-start(f32[1,624,768]{2,1,0:T(8,128)} %param.21) | copy-start | bytes 5750788
  679.6 3.6 copy-start.8
  679.6 3.6 copy-start.4
  683.2 1.9 copy-start.3
  683.2 1.9 copy-start.15
  683.3 3.7 copy-start.16
Sparse Core Ops, SparseCore 0:
  11.4 180.7 all-gather.2
  195.5 63.5 all-gather.4

commit v3 on v2

--- a/solution.py
+++ b/solution.py
@@ -92,6 +92,18 @@
     return jnp.where(column % 2 == 0, jnp.sin(angle), jnp.cos(angle))
 
 
+def sinusoid_table(width):
+    column = jnp.arange(width)
+    rate = jnp.exp(-(2 * (column // 2)).astype(f32) * (math.log(10000.0) / width))[None, :]
+    first = (32 * jnp.arange(TUBES // 32)).astype(f32)[:, None] * rate
+    second = jnp.arange(32).astype(f32)[:, None] * rate
+    even = column % 2 == 0
+    ahead = jnp.where(even, jnp.sin(first), jnp.cos(first))[:, None]
+    turned = jnp.where(even, jnp.cos(first), -jnp.sin(first))[:, None]
+    table = ahead * jnp.cos(second)[None] + turned * jnp.sin(second)[None]
+    return table.reshape(TUBES, width)
+
+
 def params(**more):
     return pltpu.CompilerParams(vmem_limit_bytes=BIG_VMEM, **more)
 
@@ -108,39 +120,49 @@
     return pl.BlockSpec(memory_space=pltpu.VMEM)
 
 
-PICK_ROWS = 224
-
-
-def pick_kernel(order_ref, tubes_ref, out_ref):
+def pick_kernel(half_ref, order_ref, tubes_ref, out_ref):
     column = lax.broadcasted_iota(jnp.int32, (1, TUBES), 1)
     hot = jnp.where(order_ref[0] == column, 1.0, 0.0).astype(bf16)
     out_ref[0] = nn(hot, tubes_ref[0]).astype(bf16)
 
 
-def pick(order, tubes):
+def pick_visible(half, order, tubes):
     clips, _, width = tubes.shape
+    which = lambda c, half_ref: jnp.where(c == 0, half_ref[0], 1 - half_ref[0])
     return pl.pallas_call(
         pick_kernel,
-        grid=(clips, TUBES // PICK_ROWS),
-        in_specs=[
-            pl.BlockSpec((1, PICK_ROWS, 1), lambda c, i: (c, i, 0)),
-            pl.BlockSpec((1, TUBES, width), lambda c, i: (c, 0, 0)),
-        ],
-        out_specs=pl.BlockSpec((1, PICK_ROWS, width), lambda c, i: (c, i, 0)),
-        out_shape=jax.ShapeDtypeStruct(tubes.shape, bf16),
+        grid_spec=pltpu.PrefetchScalarGridSpec(
+            num_scalar_prefetch=1,
+            grid=(clips,),
+            in_specs=[
+                pl.BlockSpec((1, VIS, 1), lambda c, half_ref: (which(c, half_ref), 0, 0)),
+                pl.BlockSpec((1, TUBES, width), lambda c, half_ref: (which(c, half_ref), 0, 0)),
+            ],
+            out_specs=pl.BlockSpec((1, VIS, width), lambda c, half_ref: (c, 0, 0)),
+        ),
+        out_shape=jax.ShapeDtypeStruct((clips, VIS, width), bf16),
         compiler_params=params(),
-        name="pick_tubes",
-    )(order[:, :, None], tubes)
+        name="pick_visible",
+    )(half, order[:, :VIS, None], tubes)
 
 
 QKV_ROWS = 392
 
 
-def qkv_kernel(pos_ref, latent_ref, vec_ref, w_ref, bias_ref, x_ref, h_ref, qkv_ref):
+def place_matrix(order, rows):
+    place = lax.broadcasted_iota(jnp.int32, (rows, 1), 0) + pl.program_id(0) * rows
+    return jnp.where(order == place, 1.0, 0.0)
+
+
+def qkv_kernel(order_ref, pos_ref, latent_ref, vec_ref, w_ref, bias_ref, x_ref, h_ref, qkv_ref, hidden_ref):
     token, gain, shift = (vec_ref[index : index + 1] for index in range(3))
-    hidden = jnp.broadcast_to(token, (QKV_ROWS, DD))
-    shown = jnp.concatenate([latent_ref[...], hidden[VIS:]], 0)
-    x = pos_ref[...] + jnp.where(pl.program_id(0) == 0, shown, hidden)
+    places = place_matrix(order_ref[...], QKV_ROWS)
+    hidden = 1.0 - jnp.sum(places, 1, keepdims=True)
+    hidden_ref[...] = hidden
+    latent = split3(latent_ref[...])
+    places = places.astype(bf16)
+    shown = sum(nn(places, latent[VIS * part : VIS * (part + 1)]) for part in (2, 1, 0))
+    x = pos_ref[...] + (shown + hidden * token)
     x_ref[...] = x
     unit, _ = norm_parts(x)
     h = (unit * gain + shift).astype(bf16)
@@ -148,27 +170,29 @@
     qkv_ref[...] = (nt(h, w_ref[...]) + bias_ref[...]).astype(bf16)
 
 
-def decoder_qkv(pos, latent, vecs, weights, bias):
+def decoder_qkv(order, pos, latent, vecs, weights, bias):
     rows = lambda width: pl.BlockSpec((QKV_ROWS, width), lambda i: (i, 0))
     return pl.pallas_call(
         qkv_kernel,
         grid=(TUBES // QKV_ROWS,),
         in_specs=[
+            whole((1, VIS)),
             rows(DD),
             whole((VIS, DD)),
-            whole((8, DD)),
+            whole(vecs.shape),
             whole((3 * DD, DD)),
             whole((1, 3 * DD)),
         ],
-        out_specs=[rows(DD), rows(DD), rows(3 * DD)],
+        out_specs=[rows(DD), rows(DD), rows(3 * DD), rows(1)],
         out_shape=[
             jax.ShapeDtypeStruct((TUBES, DD), f32),
             jax.ShapeDtypeStruct((TUBES, DD), bf16),
             jax.ShapeDtypeStruct((TUBES, 3 * DD), bf16),
+            jax.ShapeDtypeStruct((TUBES, 1), f32),
         ],
         compiler_params=params(),
         name="decoder_qkv",
-    )(pos, latent, vecs, weights, bias)
+    )(order, pos, latent, vecs, weights, bias)
 
 
 FWD_ROWS = 392
@@ -303,20 +327,22 @@
 
 
 def token_kernel(
-    a_ref, x_ref, pix_ref, scal_ref, vec_ref, bu_ref, bh_ref, wo_ref, wd_ref, wu_ref, wh_ref,
+    _, a_ref, x_ref, pix_ref, pix_other_ref, hidden_ref, scal_ref, vec_ref, bu_ref, bh_ref,
+    wo_ref, wd_ref, wu_ref, wh_ref,
     da_ref, dx1_ref,
-    grads_ref, gvec_ref, gbu_ref, gbh_ref, loss_ref,
+    own_ref, other_ref, gvec_ref, gbu_ref, gbh_ref, loss_ref,
     slope,
 ):
     step = pl.program_id(0)
-    sums = (grads_ref, gvec_ref, gbu_ref, gbh_ref, loss_ref)
+    sums = (own_ref, other_ref, gvec_ref, gbu_ref, gbh_ref, loss_ref)
+    grads = (own_ref, other_ref)
 
     @pl.when(step == 0)
     def _():
         for ref in sums:
             ref[...] = jnp.zeros_like(ref)
 
-    bo, g2, b2, bd, gf, sf = (vec_ref[index : index + 1] for index in range(6))
+    bo, g2, b2, bd, gf, sf = (vec_ref[index : index + 1] for index in range(3, 9))
     a = a_ref[...].astype(bf16)
     x1 = x_ref[...] + (nn(a, wo_ref[...]) + bo)
     unit2, rate2 = norm_parts(x1)
@@ -331,13 +357,16 @@
         out = out + nn(active[-1], wd_ref[part])
     unit_f, rate_f = norm_parts(out)
     final = (unit_f * gf + sf).astype(bf16)
-    pixels = [pix_ref[:, pl.ds(chunk * CHUNK, CHUNK)].astype(f32) for chunk in range(CHUNKS)]
+    pixels = [
+        ref[:, pl.ds(side * CHUNK, CHUNK)].astype(f32)
+        for ref in (pix_ref.at[0], pix_other_ref)
+        for side in range(2)
+    ]
     center = sum(jnp.sum(part, 1, keepdims=True) for part in pixels) * (1.0 / PIX)
     square = sum(jnp.sum(part * part, 1, keepdims=True) for part in pixels) * (1.0 / PIX)
     spread = lax.rsqrt(square - center * center + norm_eps)
-    row = lax.broadcasted_iota(jnp.int32, (TOKEN_ROWS, 1), 0) + step * TOKEN_ROWS
-    counted = jnp.where(row >= VIS, scal_ref[0:1, 0:1], 0.0)
-    rate = jnp.where(row >= VIS, scal_ref[1:2, 0:1], 0.0)
+    counted = hidden_ref[...] * scal_ref[0:1, 0:1]
+    rate = hidden_ref[...] * scal_ref[1:2, 0:1]
     grad_final = jnp.zeros((TOKEN_ROWS, DD), f32)
     for chunk in range(CHUNKS):
         part = pl.ds(chunk * CHUNK, CHUNK)
@@ -346,25 +375,23 @@
         loss_ref[:, part] += col_sum(counted * miss * miss)
         grad_guess = (rate * miss).astype(bf16)
         gbh_ref[:, part] += col_sum(grad_guess.astype(f32))
-        grads_ref[chunk // 2, pl.ds(DEC_H + (chunk % 2) * CHUNK, CHUNK)] += tn(grad_guess, final)
+        grads[chunk // 2][pl.ds(DEC_H + (chunk % 2) * CHUNK, CHUNK)] += tn(grad_guess, final)
         grad_final = grad_final + nn(grad_guess, wh_ref[part])
     grad_out = norm_back(grad_final, gf, unit_f, rate_f)
     out_low = grad_out.astype(bf16)
     grad_h2 = jnp.zeros((TOKEN_ROWS, DD), f32)
     for chunk in range(CHUNKS):
         part = pl.ds(chunk * CHUNK, CHUNK)
-        grads_ref[chunk // 2, pl.ds(DEC_D + (chunk % 2) * CHUNK, CHUNK)] += tn(
-            active[chunk], out_low
-        )
+        grads[chunk // 2][pl.ds(DEC_D + (chunk % 2) * CHUNK, CHUNK)] += tn(active[chunk], out_low)
         grad_before = (slope[:, part] * nt(out_low, wd_ref[part])).astype(bf16)
         gbu_ref[:, part] += col_sum(grad_before.astype(f32))
-        grads_ref[chunk // 2, pl.ds(DEC_U + (chunk % 2) * CHUNK, CHUNK)] += tn(grad_before, h2)
+        grads[chunk // 2][pl.ds(DEC_U + (chunk % 2) * CHUNK, CHUNK)] += tn(grad_before, h2)
         grad_h2 = grad_h2 + nn(grad_before, wu_ref[part])
     grad_x1 = grad_out + norm_back(grad_h2, g2, unit2, rate2)
     x1_low = grad_x1.astype(bf16)
     g_out = tn(a, x1_low)
     for group in range(2):
-        grads_ref[group, pl.ds(DEC_O, DD // 2)] += g_out[group * DD // 2 : (group + 1) * DD // 2]
+        grads[group][pl.ds(DEC_O, DD // 2)] += g_out[group * DD // 2 : (group + 1) * DD // 2]
     da_ref[...] = nt(x1_low, wo_ref[...]).astype(bf16)
     dx1_ref[...] = grad_x1
     gvec_ref[0:1] += col_sum(x1_low.astype(f32))
@@ -375,41 +402,47 @@
     gvec_ref[5:6] += col_sum(grad_final)
 
 
-def decoder_tokens(mixed, x, pixels, scal, vecs, bu, bh, wo, wd, wu, wh):
-    rows = lambda width: pl.BlockSpec((TOKEN_ROWS, width), lambda i: (i, 0))
-    sums = [(2, DEC_ROWS, DD), (8, DD), (1, DFF), (1, PIX), (1, PIX)]
+def decoder_tokens(half, mixed, x, tubes, pixels, hidden, scal, vecs, bu, bh, wo, wd, wu, wh):
+    rows = lambda width: pl.BlockSpec((TOKEN_ROWS, width), lambda i, _: (i, 0))
+    sums = [(DEC_ROWS, DD), (DEC_ROWS, DD), (8, DD), (1, DFF), (1, PIX), (1, PIX)]
     return pl.pallas_call(
         token_kernel,
-        grid=(TUBES // TOKEN_ROWS,),
-        in_specs=[
-            rows(DD),
-            rows(DD),
-            rows(PIX),
-            whole((8, 128)),
-            whole((8, DD)),
-            whole((1, DFF)),
-            whole((1, PIX)),
-            whole((DD, DD)),
-            whole((DFF, DD)),
-            whole((DFF, DD)),
-            whole((PIX, DD)),
-        ],
-        out_specs=[rows(DD), rows(DD)] + [whole(shape) for shape in sums],
+        grid_spec=pltpu.PrefetchScalarGridSpec(
+            num_scalar_prefetch=1,
+            grid=(TUBES // TOKEN_ROWS,),
+            in_specs=[
+                rows(DD),
+                rows(DD),
+                pl.BlockSpec((1, TOKEN_ROWS, PIX // 2), lambda i, half_ref: (half_ref[0], i, 0)),
+                rows(PIX // 2),
+                rows(1),
+                whole((8, 128)),
+                whole(vecs.shape),
+                whole((1, DFF)),
+                whole((1, PIX)),
+                whole((DD, DD)),
+                whole((DFF, DD)),
+                whole((DFF, DD)),
+                whole((PIX, DD)),
+            ],
+            out_specs=[rows(DD), rows(DD)] + [whole(shape) for shape in sums],
+            scratch_shapes=[pltpu.VMEM((TOKEN_ROWS, DFF), f32)],
+        ),
         out_shape=[
             jax.ShapeDtypeStruct((TUBES, DD), bf16),
             jax.ShapeDtypeStruct((TUBES, DD), f32),
         ]
         + [jax.ShapeDtypeStruct(shape, f32) for shape in sums],
-        scratch_shapes=[pltpu.VMEM((TOKEN_ROWS, DFF), f32)],
         compiler_params=params(),
         name="decoder_tokens",
-    )(mixed, x, pixels, scal, vecs, bu, bh, wo, wd, wu, wh)
+    )(half, mixed, x, tubes, pixels, hidden, scal, vecs, bu, bh, wo, wd, wu, wh)
 
 
 def qkv_back_kernel(
-    half_ref, dq_ref, dk_ref, dv_ref, h_ref, x_ref, dx1_ref, vec_ref, w_ref, normed_ref, _,
-    latent_ref, grads_ref, gvec_ref,
-    g_qkv, g_proj, sems,
+    half_ref, order_ref, dq_ref, dk_ref, dv_ref, h_ref, x_ref, dx1_ref, vec_ref, w_ref, normed_ref,
+    _own, _other,
+    latent_ref, own_ref, other_ref, gvec_ref,
+    g_qkv, g_proj, latent_sum, sems,
 ):
     step = pl.program_id(0)
 
@@ -417,6 +450,7 @@
     def _():
         g_qkv[...] = jnp.zeros_like(g_qkv)
         gvec_ref[...] = jnp.zeros_like(gvec_ref)
+        latent_sum[...] = jnp.zeros_like(latent_sum)
 
     h = h_ref[...]
     grads = (dq_ref[...], dk_ref[...], dv_ref[...])
@@ -429,32 +463,29 @@
         grad_h = grad_h + nn(grad, w_ref[pl.ds(index * DD, DD)])
     unit, rate = norm_parts(x_ref[...])
     grad_x = dx1_ref[...] + norm_back(grad_h, vec_ref[1:2], unit, rate)
-    row = lax.broadcasted_iota(jnp.int32, (QKV_ROWS, 1), 0) + step * QKV_ROWS
+    places = place_matrix(order_ref[...], QKV_ROWS)
+    hidden = 1.0 - jnp.sum(places, 1, keepdims=True)
+    latent_sum[...] += tn(places.astype(bf16), grad_x.astype(bf16))
     gvec_ref[0:1] += col_sum(grads[0].astype(f32))
     gvec_ref[1:2] += col_sum(grads[2].astype(f32))
     gvec_ref[2:3] += col_sum(grad_h * unit)
     gvec_ref[3:4] += col_sum(grad_h)
-    gvec_ref[4:5] += col_sum(jnp.where(row >= VIS, grad_x, 0.0))
-
-    @pl.when(step == 0)
+    gvec_ref[4:5] += col_sum(hidden * grad_x)
+
+    @pl.when(step == pl.num_programs(0) - 1)
     def _():
-        latent = grad_x[:VIS].astype(bf16)
+        latent = latent_sum[...].astype(bf16)
         latent_ref[...] = latent
         both = tn(normed_ref[...], latent)
         g_proj[0] = both[: D // 2]
         g_proj[1] = both[D // 2 :]
-
-    @pl.when(step == pl.num_programs(0) - 1)
-    def _():
         half = half_ref[0]
+        kinds = pl.ds(DEC_Q, 3 * DD // 2)
         copies = [
-            pltpu.make_async_copy(g_qkv, grads_ref.at[:, pl.ds(DEC_Q, 3 * DD // 2)], sems.at[0]),
-            pltpu.make_async_copy(
-                g_proj.at[half], grads_ref.at[0, pl.ds(0, D // 2)], sems.at[1]
-            ),
-            pltpu.make_async_copy(
-                g_proj.at[1 - half], grads_ref.at[1, pl.ds(0, D // 2)], sems.at[2]
-            ),
+            pltpu.make_async_copy(g_qkv.at[0], own_ref.at[kinds], sems.at[0]),
+            pltpu.make_async_copy(g_qkv.at[1], other_ref.at[kinds], sems.at[1]),
+            pltpu.make_async_copy(g_proj.at[half], own_ref.at[pl.ds(0, D // 2)], sems.at[2]),
+            pltpu.make_async_copy(g_proj.at[1 - half], other_ref.at[pl.ds(0, D // 2)], sems.at[3]),
         ]
         for copy in copies:
             copy.start()
@@ -462,29 +493,31 @@
             copy.wait()
 
 
-def decoder_qkv_back(half, dq, dk, dv, h, x, dx1, vecs, weights, normed, grads):
+def decoder_qkv_back(half, order, dq, dk, dv, h, x, dx1, vecs, weights, normed, own, other):
     rows = lambda width: pl.BlockSpec((QKV_ROWS, width), lambda i: (i, 0))
     return pl.pallas_call(
         qkv_back_kernel,
         grid=(TUBES // QKV_ROWS,),
-        in_specs=[pl.BlockSpec(memory_space=pltpu.SMEM)]
+        in_specs=[pl.BlockSpec(memory_space=pltpu.SMEM), whole((1, VIS))]
         + [rows(DD)] * 6
-        + [whole((8, DD)), whole((3 * DD, DD)), whole((VIS, D)), any_spec()],
-        out_specs=[whole((VIS, DD)), any_spec(), whole((8, DD))],
+        + [whole(vecs.shape), whole((3 * DD, DD)), whole((VIS, D)), any_spec(), any_spec()],
+        out_specs=[whole((VIS, DD)), any_spec(), any_spec(), whole((8, DD))],
         out_shape=[
             jax.ShapeDtypeStruct((VIS, DD), bf16),
-            jax.ShapeDtypeStruct((2, DEC_ROWS, DD), f32),
+            jax.ShapeDtypeStruct((DEC_ROWS, DD), f32),
+            jax.ShapeDtypeStruct((DEC_ROWS, DD), f32),
             jax.ShapeDtypeStruct((8, DD), f32),
         ],
         scratch_shapes=[
             pltpu.VMEM((2, 3 * DD // 2, DD), f32),
             pltpu.VMEM((2, D // 2, DD), f32),
-            pltpu.SemaphoreType.DMA((3,)),
-        ],
-        input_output_aliases={10: 1},
+            pltpu.VMEM((VIS, DD), f32),
+            pltpu.SemaphoreType.DMA((4,)),
+        ],
+        input_output_aliases={11: 1, 12: 2},
         compiler_params=params(),
         name="decoder_qkv_back",
-    )(half, dq, dk, dv, h, x, dx1, vecs, weights, normed, grads)
+    )(half, order, dq, dk, dv, h, x, dx1, vecs, weights, normed, own, other)
 
 
 HALF = D // 2
@@ -494,37 +527,81 @@
 STAGES = ((AT_Q, 3 * HALF), (AT_O, HALF), (AT_U, HALF_FF), (AT_D, HALF_FF))
 
 
-def stage_copies(sources, start, held, sems):
-    return [
-        [
-            pltpu.make_async_copy(
-                sources[group].at[pl.ds(start + at, size)],
-                held.at[group, pl.ds(at, size)],
-                sems.at[group, stage],
-            )
-            for group in range(2)
-        ]
-        for stage, (at, size) in enumerate(STAGES)
-    ]
-
-
-def encoder_kernel(start, last, x_ref, vec_ref, bqkv_ref, bu_ref, own_ref, other_ref, *refs):
-    if last:
-        proj_ref, *refs = refs
-        normed_ref, latent_ref = refs[8:10]
-    out_ref, h_ref, qkv_ref, a_ref, x1_ref, h2_ref, u_ref, slope_ref = refs[:8]
-    held, sems = refs[-2:]
-    copies = stage_copies((own_ref, other_ref), start, held, sems)
-    for stage in copies:
-        for copy in stage:
+def pieces_of(start, size, per):
+    pieces = []
+    at = start
+    while at < start + size:
+        many = min(start + size, (at // per + 1) * per) - at
+        pieces.append((at // per, at % per, many, at - start))
+        at += many
+    return pieces
+
+
+def stage_copies(sources, start, per, held, sems, stages):
+    copies = []
+    count = 0
+    for at, size in stages:
+        stage = []
+        for shard, row, many, before in pieces_of(start + at, size, per):
+            for group in range(2):
+                stage.append(
+                    pltpu.make_async_copy(
+                        sources[group].at[shard, pl.ds(row, many)],
+                        held.at[group, pl.ds(at + before, many)],
+                        sems.at[count],
+                    )
+                )
+                count += 1
+        copies.append(stage)
+    return copies
+
+
+MOST_COPIES = 48
+
+
+def encoder_kernel(layer, per, *refs):
+    if layer == 0:
+        pix_ref, pix_other_ref, pos_ref, *refs = refs
+    else:
+        x_ref, proj_ref, *refs = refs
+    vec_ref, split_ref, own_ref, other_ref, *refs = refs
+    if layer == 0:
+        x_out_ref, *refs = refs
+    else:
+        normed_ref, latent_ref, *refs = refs
+    out_ref, h_ref, qkv_ref, a_ref, x1_ref, h2_ref, u_ref, slope_ref, held, sems = refs
+    base = 1 + 6 * layer
+    biases = layer * (2 * HALF + HALF_FF)
+    if layer == 0:
+        copies = stage_copies(
+            (own_ref, other_ref), 0, per, held.at[:, pl.ds(LAYER_ROWS, D)], sems, ((0, D),)
+        )
+        used = sum(len(stage) for stage in copies)
+        copies = copies + stage_copies(
+            (own_ref, other_ref), D, per, held, sems.at[pl.ds(used, MOST_COPIES - used)], STAGES
+        )
+        copies = copies[1:] + copies[:1]
+        order = (4, 0, 1, 2, 3)
+    else:
+        copies = stage_copies((own_ref, other_ref), D + LAYER_ROWS, per, held, sems, STAGES)
+        order = (0, 1, 2, 3)
+    for stage in order:
+        for copy in copies[stage]:
             copy.start()
 
     def wait(stage):
         for copy in copies[stage]:
             copy.wait()
 
-    g1, b1, bo, g2, b2, bd = (vec_ref[index : index + 1] for index in range(6))
-    x = x_ref[...]
+    g1, b1, bo, g2, b2, bd = (vec_ref[base + index : base + index + 1] for index in range(6))
+    if layer == 0:
+        wait(4)
+        x = pos_ref[...] + vec_ref[0:1]
+        for group, pixels in enumerate((pix_ref, pix_other_ref)):
+            x = x + nn(pixels[...], held[group, pl.ds(LAYER_ROWS, D)])
+        x_out_ref[...] = x
+    else:
+        x = x_ref[...]
     unit, _ = norm_parts(x)
     h = (unit * g1 + b1).astype(bf16)
     h_ref[...] = h
@@ -533,7 +610,11 @@
         for group in range(2):
             part = pl.ds((2 * kind + group) * HALF, HALF)
             rows = pl.ds(AT_Q + kind * HALF, HALF)
-            qkv_ref[:, part] = (nt(h, held[group, rows]) + bqkv_ref[:, part]).astype(bf16)
+            value = nt(h, held[group, rows])
+            if kind != 1:
+                at = biases + kind // 2 * HALF
+                value = value + split_ref[group : group + 1, at : at + HALF]
+            qkv_ref[:, part] = value.astype(bf16)
     for pair in range(D // 128):
         q, k, v = (qkv_ref[:, pl.ds(kind * D + pair * 128, 128)] for kind in range(3))
         v_one = jnp.concatenate([v, jnp.ones((VIS, 128), bf16)], 1)
@@ -559,21 +640,22 @@
     for group in range(2):
         for chunk in range(HALF_FF // CHUNK):
             part = pl.ds(group * HALF_FF + chunk * CHUNK, CHUNK)
-            before = nt(h2, held[group, pl.ds(AT_U + chunk * CHUNK, CHUNK)]) + bu_ref[:, part]
-            value, slope = gelu_pair(before)
+            before = nt(h2, held[group, pl.ds(AT_U + chunk * CHUNK, CHUNK)])
+            at = biases + 2 * HALF + chunk * CHUNK
+            value, slope = gelu_pair(before + split_ref[group : group + 1, at : at + CHUNK])
             slope_ref[:, part] = slope
             active = value.astype(bf16)
             u_ref[:, part] = active
             out = out + nn(active, held[group, pl.ds(AT_D + chunk * CHUNK, CHUNK)])
     out_ref[...] = out
-    if last:
+    if layer == 1:
         unit3, _ = norm_parts(out)
-        normed = (unit3 * vec_ref[6:7] + vec_ref[7:8]).astype(bf16)
+        normed = (unit3 * vec_ref[13:14] + vec_ref[14:15]).astype(bf16)
         normed_ref[...] = normed
         latent_ref[...] = nn(normed, proj_ref[...])
 
 
-def encoder_layer(start, x, vecs, bqkv, bu, own, other, name, proj=None):
+def encoder_layer(layer, per, first, vecs, split2, own, other):
     shapes = [
         ((VIS, D), f32),
         ((VIS, D), bf16),
@@ -584,40 +666,41 @@
         ((VIS, FF), bf16),
         ((VIS, FF), f32),
     ]
-    last = proj is not None
-    more = ()
-    if last:
-        more = (proj,)
-        shapes += [((VIS, D), bf16), ((VIS, DD), f32)]
+    before = [((VIS, D), f32)] if layer == 0 else [((VIS, D), bf16), ((VIS, DD), f32)]
+    shapes = before + shapes
     return pl.pallas_call(
-        lambda *refs: encoder_kernel(start, last, *refs),
-        in_specs=[vmem_spec()] * 4 + [any_spec()] * 2 + [vmem_spec()] * len(more),
+        lambda *refs: encoder_kernel(layer, per, *refs),
+        in_specs=[vmem_spec()] * (len(first) + 2) + [any_spec()] * 2,
         out_specs=[vmem_spec()] * len(shapes),
         out_shape=[jax.ShapeDtypeStruct(shape, kind) for shape, kind in shapes],
         scratch_shapes=[
-            pltpu.VMEM((2, LAYER_ROWS, D), bf16),
-            pltpu.SemaphoreType.DMA((2, len(STAGES))),
+            pltpu.VMEM((2, LAYER_ROWS + (D if layer == 0 else 0), D), bf16),
+            pltpu.SemaphoreType.DMA((MOST_COPIES,)),
         ],
         compiler_params=params(),
-        name=name,
-    )(x, vecs, bqkv, bu, own, other, *more)
+        name=f"encoder_{layer}",
+    )(*first, vecs, split2, own, other)
 
 
 RIGHT_AT = LAYER_ROWS
 
 
-def encoder_back_kernel(start, last, *refs):
+def encoder_back_kernel(layer, per, *refs):
+    last = layer == 1
+    start = D + layer * LAYER_ROWS
+    base = 1 + 6 * layer
     (
         grad_ref, x_ref, vec_ref, h_ref, qkv_ref, a_ref, x1_ref, h2_ref, u_ref, slope_ref,
-        start_ref, own_ref, other_ref, extra_ref,
-    ) = refs[:14]
-    refs = refs[14:]
+        start_ref, own_ref, other_ref, pix_ref, pix_other_ref,
+    ) = refs[:15]
+    pixels = (pix_ref, pix_other_ref)
+    refs = refs[15:]
     if last:
         out_ref, proj_ref, *refs = refs
     dx_ref, mine_ref, other_pack_ref, left_ref, gvec_ref, gbu_ref, gbq_ref = refs[:7]
     held, sems, da, dqkv = refs[7:]
     packs = (mine_ref, other_pack_ref)
-    copies = stage_copies((own_ref, other_ref), start, held, sems)
+    copies = stage_copies((own_ref, other_ref), start, per, held, sems, STAGES)
     for stage in (3, 2, 1, 0):
         for copy in copies[stage]:
             copy.start()
@@ -626,12 +709,12 @@
         for copy in copies[stage]:
             copy.wait()
 
-    g1, b1, bo, g2, b2, bd = (vec_ref[index : index + 1] for index in range(6))
+    g1, b1, bo, g2, b2, bd = (vec_ref[base + index : base + index + 1] for index in range(6))
     gvec_ref[6:8] = jnp.zeros((2, D), f32)
     if last:
         unit3, rate3 = norm_parts(out_ref[...])
         grad_normed = nt(grad_ref[...], proj_ref[...])
-        grad_out = norm_back(grad_normed, vec_ref[6:7], unit3, rate3)
+        grad_out = norm_back(grad_normed, vec_ref[13:14], unit3, rate3)
         gvec_ref[6:7] = col_sum(grad_normed * unit3)
         gvec_ref[7:8] = col_sum(grad_normed)
     else:
@@ -713,7 +796,7 @@
         for group in range(2):
             parts = split3(fold3(inner[3 * RANK * group : 3 * RANK * (group + 1)]))
             if index == 4:
-                value = fold3(nn(parts, extra_ref[:, pl.ds(group * D, D)]))
+                value = fold3(nn(parts, pixels[group][...]))
                 left_ref[group, :, pl.ds(0, D)] = value
             else:
                 at, size, _ = spans[index]
@@ -721,32 +804,32 @@
                 left_ref[group, :, pl.ds(before + at, size)] = value
 
 
-def encoder_layer_back(start, grad, source, vecs, kept, starts, own, other, extra, name, last=()):
-    width = RIGHT_AT + (4 if last else 5) * D
+def encoder_layer_back(layer, per, grad, source, vecs, kept, starts, own, other, pixels, last=()):
+    width = RIGHT_AT + (5 - layer) * D
     shapes = [
         ((VIS, D), f32),
         ((VIS, width), bf16),
         ((VIS, width), bf16),
-        ((2, RANK, LAYER_ROWS if last else D + LAYER_ROWS), f32),
+        ((2, RANK, LAYER_ROWS + (1 - layer) * D), f32),
         ((8, D), f32),
         ((1, FF), f32),
         ((2, D), f32),
     ]
-    _, h, qkv, a, x1, h2, u, slope = kept[:8]
+    _, h, qkv, a, x1, h2, u, slope = kept
     return pl.pallas_call(
-        lambda *refs: encoder_back_kernel(start, bool(last), *refs),
-        in_specs=[vmem_spec()] * 11 + [any_spec()] * 2 + [vmem_spec()] * (1 + len(last)),
+        lambda *refs: encoder_back_kernel(layer, per, *refs),
+        in_specs=[vmem_spec()] * 11 + [any_spec()] * 2 + [vmem_spec()] * (2 + len(last)),
         out_specs=[vmem_spec()] * len(shapes),
         out_shape=[jax.ShapeDtypeStruct(shape, kind) for shape, kind in shapes],
         scratch_shapes=[
             pltpu.VMEM((2, LAYER_ROWS, D), bf16),
-            pltpu.SemaphoreType.DMA((2, len(STAGES))),
+            pltpu.SemaphoreType.DMA((MOST_COPIES,)),
             pltpu.VMEM((VIS, D), bf16),
             pltpu.VMEM((VIS, 3 * D), bf16),
         ],
         compiler_params=params(),
-        name=name,
-    )(grad, source, vecs, h, qkv, a, x1, h2, u, slope, starts, own, other, extra, *last)
+        name=f"encoder_back_{layer}",
+    )(grad, source, vecs, h, qkv, a, x1, h2, u, slope, starts, own, other, *pixels, *last)
 
 
 ROWS = 768
@@ -904,31 +987,33 @@
 DEC_BLOCK = 1152
 
 
-def dec_right_kernel(basis_ref, comb_ref, out_ref):
+def dec_right_kernel(basis_ref, own_ref, came_ref, error_ref, out_ref, comb_ref):
     @pl.when(pl.program_id(0) == 0)
     def _():
         out_ref[...] = jnp.zeros_like(out_ref)
 
     basis = split3(basis_ref[...])
-    comb = comb_ref[...]
+    comb = own_ref[...] + came_ref[...] + error_ref[...].astype(f32)
+    comb_ref[...] = comb
     high = comb.astype(bf16)
     rest = (comb - high.astype(f32)).astype(bf16)
     out_ref[...] += fold3(nn(basis, high) + nn(basis, rest))
 
 
-def dec_right_factor(basis, comb):
+def dec_right_factor(basis, own, came, error):
+    rows = pl.BlockSpec((DEC_BLOCK, DD), lambda j: (j, 0))
     return pl.pallas_call(
         dec_right_kernel,
         grid=(DEC_ROWS // DEC_BLOCK,),
-        in_specs=[
-            pl.BlockSpec((RANK, DEC_BLOCK), lambda j: (0, j)),
-            pl.BlockSpec((DEC_BLOCK, DD), lambda j: (j, 0)),
-        ],
-        out_specs=whole((RANK, DD)),
-        out_shape=jax.ShapeDtypeStruct((RANK, DD), f32),
+        in_specs=[pl.BlockSpec((RANK, DEC_BLOCK), lambda j: (0, j)), rows, rows, rows],
+        out_specs=[whole((RANK, DD)), rows],
+        out_shape=[
+            jax.ShapeDtypeStruct((RANK, DD), f32),
+            jax.ShapeDtypeStruct((DEC_ROWS, DD), f32),
+        ],
         compiler_params=params(),
         name="dec_right_factor",
-    )(basis, comb)
+    )(basis, own, came, error)
 
 
 def dec_residue_kernel(basis_ref, factor_ref, comb_ref, out_ref):
@@ -953,27 +1038,26 @@
     )(basis, factor, comb)
 
 
-def dec_left_kernel(start_ref, grad_ref, out_ref):
-    start = split3(start_ref[0])
-    grad = grad_ref[0]
-    high = grad.astype(bf16)
-    rest = (grad - high.astype(f32)).astype(bf16)
-    out_ref[0] = fold3((nt(high, start) + nt(rest, start)).T)
-
-
-def dec_left_factor(starts, grads):
+def dec_left_kernel(start_ref, own_ref, other_ref, out_ref):
+    for group, ref in enumerate((own_ref, other_ref)):
+        start = split3(start_ref[group])
+        grad = ref[...]
+        high = grad.astype(bf16)
+        rest = (grad - high.astype(f32)).astype(bf16)
+        out_ref[group] = fold3((nt(high, start) + nt(rest, start)).T)
+
+
+def dec_left_factor(starts, own, other):
+    rows = pl.BlockSpec((DEC_BLOCK, DD), lambda j: (j, 0))
     return pl.pallas_call(
         dec_left_kernel,
-        grid=(2, DEC_ROWS // DEC_BLOCK),
-        in_specs=[
-            pl.BlockSpec((1, RANK, DD), lambda g, j: (g, 0, 0)),
-            pl.BlockSpec((1, DEC_BLOCK, DD), lambda g, j: (g, j, 0)),
-        ],
-        out_specs=pl.BlockSpec((1, RANK, DEC_BLOCK), lambda g, j: (g, 0, j)),
+        grid=(DEC_ROWS // DEC_BLOCK,),
+        in_specs=[whole((2, RANK, DD)), rows, rows],
+        out_specs=pl.BlockSpec((2, RANK, DEC_BLOCK), lambda j: (0, 0, j)),
         out_shape=jax.ShapeDtypeStruct((2, RANK, DEC_ROWS), f32),
         compiler_params=params(),
         name="dec_left_factor",
-    )(starts, grads)
+    )(starts, own, other)
 
 
 MESH_ID = pl.DeviceIdType.MESH
@@ -1147,6 +1231,285 @@
     )(*parts)
 
 
+PLANE = 4
+PART_Z_X_Y, PART_Z_Y_X, PART_X_Y_Z = range(3)
+WAY_X, WAY_Y, WAY_UP, WAY_DOWN = range(4)
+ERROR_ROWS = 1248
+
+
+def gather_kernel(
+    parts, planes, shard_ref, tubes_ref, error_ref, dec_error_ref, start_ref,
+    own_ref, other_ref, pixels_ref, part_ref, dec_part_ref,
+    held, dec_held, send_sems, recv_sems, pair_sems, sems,
+):
+    me = lax.axis_index("dp")
+    half = lax.axis_index("tensor")
+    z = me // PLANE
+    column = lax.rem(me, PLANE)
+    column_x = column + 1 - 2 * lax.rem(column, 2)
+    column_y = lax.rem(column + 2, PLANE)
+    column_xy = lax.rem(column_x + 2, PLANE)
+    up = z < planes - 1
+    down = z > 0
+    peers = (
+        z * PLANE + column_x,
+        z * PLANE + column_y,
+        jnp.minimum(me + PLANE, PLANE * planes - 1),
+        jnp.maximum(me - PLANE, 0),
+    )
+    rows = [pl.ds(at, size) for at, size in parts]
+
+    def copy(way, part, slot, mine=False):
+        return pltpu.make_async_remote_copy(
+            src_ref=shard_ref.at[rows[part]] if mine else own_ref.at[slot, rows[part]],
+            dst_ref=own_ref.at[slot, rows[part]],
+            send_sem=send_sems.at[way, part, slot],
+            recv_sem=recv_sems.at[part, slot],
+            device_id={"dp": peers[way]},
+            device_id_type=MESH_ID,
+        )
+
+    def send(way, part, slot, mine=False):
+        copy(way, part, slot, mine).start()
+
+    def recv(part, slot):
+        copy(WAY_X, part, slot).wait_recv()
+
+    def pair(part, plane):
+        block = pl.ds(plane * PLANE, PLANE)
+        return pltpu.make_async_remote_copy(
+            src_ref=own_ref.at[block, rows[part]],
+            dst_ref=other_ref.at[block, rows[part]],
+            send_sem=pair_sems.at[0, part, plane],
+            recv_sem=pair_sems.at[1, part, plane],
+            device_id={"tensor": 1 - half},
+            device_id_type=MESH_ID,
+        )
+
+    def load(index):
+        return pltpu.make_async_copy(
+            error_ref.at[pl.ds(index * ERROR_ROWS, ERROR_ROWS)], held.at[index % 2], sems.at[index % 2]
+        )
+
+    load(0).start()
+    load(1).start()
+    dec_load = pltpu.make_async_copy(dec_error_ref, dec_held, sems.at[2])
+    dec_load.start()
+
+    barrier = pltpu.get_barrier_semaphore()
+    for way in (WAY_X, WAY_Y):
+        pl.semaphore_signal(barrier, 1, device_id={"dp": peers[way]}, device_id_type=MESH_ID)
+    pl.semaphore_signal(barrier, 1, device_id={"tensor": 1 - half}, device_id_type=MESH_ID)
+    for ok, way in ((up, WAY_UP), (down, WAY_DOWN)):
+
+        @pl.when(ok)
+        def _(way=way):
+            pl.semaphore_signal(barrier, 1, device_id={"dp": peers[way]}, device_id_type=MESH_ID)
+
+    pl.semaphore_wait(barrier, 3 + up.astype(jnp.int32) + down.astype(jnp.int32))
+
+    def both_z(part, slot, mine=False):
+        @pl.when(up)
+        def _():
+            send(WAY_UP, part, slot, mine)
+
+        @pl.when(down)
+        def _():
+            send(WAY_DOWN, part, slot, mine)
+
+    def sides(distance):
+        return [
+            ((z + side * distance >= 0) & (z + side * distance < planes), z + side * distance, on, way)
+            for side, on, way in ((-1, up, WAY_UP), (1, down, WAY_DOWN))
+        ]
+
+    def along(distance):
+        for there, plane, on, way in sides(distance):
+
+            @pl.when(there)
+            def _(slot=plane * PLANE + column, on=on, way=way):
+                for part in (PART_Z_X_Y, PART_Z_Y_X):
+                    recv(part, slot)
+
+                    @pl.when(on)
+                    def _():
+                        send(way, part, slot)
+
+                    send(WAY_X if part == PART_Z_X_Y else WAY_Y, part, slot)
+                send(WAY_Y, PART_Z_X_Y, slot)
+                send(WAY_X, PART_Z_Y_X, slot)
+
+    def cross(distance):
+        for there, plane, _, _ in sides(distance):
+
+            @pl.when(there)
+            def _(base=plane * PLANE):
+                recv(PART_Z_X_Y, base + column_x)
+                send(WAY_Y, PART_Z_X_Y, base + column_x)
+                recv(PART_Z_Y_X, base + column_y)
+                send(WAY_X, PART_Z_Y_X, base + column_y)
+
+    def finish(distance):
+        for there, plane, _, _ in sides(distance)[: 2 if distance else 1]:
+
+            @pl.when(there)
+            def _(plane=plane, base=plane * PLANE):
+                recv(PART_Z_X_Y, base + column_y)
+                recv(PART_Z_X_Y, base + column_xy)
+                pair(PART_Z_X_Y, plane).start()
+                recv(PART_Z_Y_X, base + column_x)
+                recv(PART_Z_Y_X, base + column_xy)
+                pair(PART_Z_Y_X, plane).start()
+
+    def whole_plane(distance):
+        for there, plane, on, way in sides(distance):
+
+            @pl.when(there)
+            def _(plane=plane, on=on, way=way):
+                for index in range(PLANE):
+                    slot = plane * PLANE + index
+                    recv(PART_X_Y_Z, slot)
+
+                    @pl.when(on)
+                    def _(slot=slot):
+                        send(way, PART_X_Y_Z, slot)
+
+                pair(PART_X_Y_Z, plane).start()
+
+    start3 = split3(start_ref[:, :D])
+    chunks = error_ref.shape[0] // ERROR_ROWS
+
+    def work(index):
+        load(index).wait()
+        lanes = pl.ds(index * ERROR_ROWS, ERROR_ROWS)
+        part_ref[:, lanes] = fold3(nt(start3, held[index % 2]))
+        if index + 2 < chunks:
+            load(index + 2).start()
+
+    send(WAY_X, PART_X_Y_Z, me, True)
+    send(WAY_Y, PART_X_Y_Z, me, True)
+    both_z(PART_Z_X_Y, me, True)
+    both_z(PART_Z_Y_X, me, True)
+    send(WAY_X, PART_Z_X_Y, me, True)
+    send(WAY_Y, PART_Z_Y_X, me, True)
+    send(WAY_X, PART_Z_Y_X, me, True)
+    send(WAY_Y, PART_Z_X_Y, me, True)
+    keep = pltpu.make_async_copy(shard_ref, own_ref.at[me], sems.at[3])
+    keep.start()
+    swap_pixels = pltpu.make_async_remote_copy(
+        src_ref=tubes_ref.at[1 - half],
+        dst_ref=pixels_ref,
+        send_sem=sems.at[4],
+        recv_sem=sems.at[5],
+        device_id={"tensor": 1 - half},
+        device_id_type=MESH_ID,
+    )
+    swap_pixels.start()
+    work(0)
+    near = z * PLANE
+    recv(PART_X_Y_Z, near + column_x)
+    send(WAY_Y, PART_X_Y_Z, near + column_x)
+    recv(PART_Z_X_Y, near + column_x)
+    send(WAY_Y, PART_Z_X_Y, near + column_x)
+    recv(PART_Z_Y_X, near + column_y)
+    send(WAY_X, PART_Z_Y_X, near + column_y)
+    keep.wait()
+    work(1)
+    along(1)
+    recv(PART_X_Y_Z, near + column_y)
+    recv(PART_X_Y_Z, near + column_xy)
+    for index in range(PLANE):
+        both_z(PART_X_Y_Z, near + index)
+    pair(PART_X_Y_Z, z).start()
+    work(2)
+    cross(1)
+    finish(0)
+    work(3)
+    along(2)
+    work(4)
+    whole_plane(1)
+    cross(2)
+    work(5)
+    finish(1)
+    along(3)
+    work(6)
+    whole_plane(2)
+    cross(3)
+    work(7)
+    finish(2)
+    dec_load.wait()
+    dec_part_ref[...] = fold3(nt(split3(start_ref[:, D:]), dec_held[...]))
+    whole_plane(3)
+    finish(3)
+    swap_pixels.wait()
+    for plane in range(planes):
+        for part in range(3):
+            pair(part, plane).wait()
+        for index in range(PLANE):
+            slot = plane * PLANE + index
+
+            @pl.when(column == index)
+            def _():
+                for part in (PART_Z_X_Y, PART_Z_Y_X):
+                    copy(WAY_X, part, slot).wait_send()
+                    copy(WAY_Y, part, slot).wait_send()
+
+            @pl.when(column_x == index)
+            def _():
+                copy(WAY_Y, PART_Z_X_Y, slot).wait_send()
+
+            @pl.when(column_y == index)
+            def _():
+                copy(WAY_X, PART_Z_Y_X, slot).wait_send()
+
+            for part in range(3):
+                sent = True if part == PART_X_Y_Z else column == index
+
+                @pl.when(up & (plane <= z) & sent)
+                def _():
+                    copy(WAY_UP, part, slot).wait_send()
+
+                @pl.when(down & (plane >= z) & sent)
+                def _():
+                    copy(WAY_DOWN, part, slot).wait_send()
+
+    copy(WAY_X, PART_X_Y_Z, me).wait_send()
+    copy(WAY_Y, PART_X_Y_Z, me).wait_send()
+    copy(WAY_Y, PART_X_Y_Z, near + column_x).wait_send()
+
+
+def gather_weights(planes, shard, tubes, error, dec_error, start):
+    workers = planes * PLANE
+    size = shard.shape[0]
+    long = (size * 2 // 5 + 15) // 16 * 16
+    parts = ((0, long), (long, long), (2 * long, size - 2 * long))
+    shards = jax.ShapeDtypeStruct((workers,) + shard.shape, shard.dtype)
+    return pl.pallas_call(
+        lambda *refs: gather_kernel(parts, planes, *refs),
+        in_specs=[any_spec()] * 4 + [vmem_spec()],
+        out_specs=[any_spec()] * 3 + [vmem_spec()] * 2,
+        out_shape=[
+            shards,
+            shards,
+            jax.ShapeDtypeStruct(tubes.shape[1:], tubes.dtype),
+            jax.ShapeDtypeStruct((RANK, error.shape[0]), f32),
+            jax.ShapeDtypeStruct((RANK, dec_error.shape[0]), f32),
+        ],
+        scratch_shapes=[
+            pltpu.VMEM((2, ERROR_ROWS, D), bf16),
+            pltpu.VMEM(dec_error.shape, bf16),
+            pltpu.SemaphoreType.DMA((4, 3, workers)),
+            pltpu.SemaphoreType.DMA((3, workers)),
+            pltpu.SemaphoreType.DMA((2, 3, planes)),
+            pltpu.SemaphoreType.DMA((6,)),
+        ],
+        compiler_params=pltpu.CompilerParams(
+            collective_id=3, has_side_effects=True, vmem_limit_bytes=BIG_VMEM
+        ),
+        name="gather_weights",
+    )(shard, tubes, error, dec_error, start)
+
+
 def cut(block, widths):
     pieces = []
     start = 0
@@ -1179,30 +1542,58 @@
     workers = lax.axis_size("dp")
     half = lax.axis_index("tensor")
     worker_index = lax.axis_index("dp")
-    dec_own = lax.all_gather(dec_weights[0].astype(bf16), "dp", axis=0, tiled=True)
-    enc_own = lax.all_gather(enc_weights[0].astype(bf16), "dp", axis=0, tiled=True)
-    dec_other = swap(dec_own)
-    enc_other = swap(enc_own)
+    mine = lambda both: lax.dynamic_index_in_dim(both, half, 0, keepdims=False)
+    which = half.astype(jnp.int32)[None]
     counted_all = clip_mask.astype(f32)
-    loss_weight = MASKED * lax.psum(jnp.sum(counted_all), "dp")
-
-    mine = lambda both: lax.dynamic_index_in_dim(both, half, 0, keepdims=False)
-    theirs = lambda both: lax.dynamic_index_in_dim(both, 1 - half, 0, keepdims=False)
-    order = mine(tube_order)
     counted = mine(counted_all)
-    picked = pick(tube_order, tubes)
-    picked_mine = mine(picked)
-    picked_theirs = theirs(picked)
-    pixels = jnp.concatenate([picked_mine, swap(picked_theirs)], 1)
+    enc_per = enc_weights.shape[1]
+    dec_per = dec_weights.shape[1] * DD // D
+    spare = -(enc_per + dec_per + 1) % 16 + 1
+    shard = jnp.concatenate(
+        [
+            enc_weights[0].astype(bf16),
+            dec_weights[0].astype(bf16).reshape(dec_per, D),
+            jnp.broadcast_to(jnp.sum(counted_all).astype(bf16), (spare, D)),
+        ],
+        0,
+    )
+    start_own = factors[0]
+    picked = pick_visible(which, tube_order, tubes)
+    pix_vis = picked[0]
+    pix_vis_other = swap(picked[1])
+    if workers == 4 * PLANE:
+        per = enc_per
+        own, other, pixels, enc_error_part, dec_error_part = gather_weights(
+            workers // PLANE, shard, tubes, enc_error[0, 0], dec_error[0, 0], start_own
+        )
+        enc_own, enc_other = own, other
+    else:
+        own = lax.all_gather(shard, "dp", axis=0)
+        other = swap(own)
+        pixels = swap(lax.dynamic_index_in_dim(tubes, 1 - half, 0, keepdims=False))
+        per = enc_per * workers
+        enc_own, enc_other = (shards[:, :enc_per].reshape(1, per, D) for shards in (own, other))
+        enc_error_part = error_factor(start_own[:, :D], enc_error[0, 0])
+        dec_error_part = error_factor(start_own[:, D:], dec_error[0, 0])
+    dec_own, dec_other = (
+        shards[:, enc_per : enc_per + dec_per].reshape(DEC_ROWS, DD) for shards in (own, other)
+    )
+    loss_weight = MASKED * jnp.sum(own[:, enc_per + dec_per, 0].astype(f32))
 
     split_own = vec_split[0]
-    split_other = swap(split_own)
-    split_widths = [HALF, HALF, HALF_FF] * 2 + [DD // 2, DD // 2, DFF // 2, PIX // 2]
-    split_parts = [
-        jnp.concatenate(pair)[None]
-        for pair in zip(cut(split_own, split_widths), cut(split_other, split_widths))
-    ]
-    shared = cut(vec_shared, [D] * 15 + [DD] * 9)
+    split2 = jnp.stack([split_own, swap(split_own)])
+    dec_at = 2 * (2 * HALF + HALF_FF)
+    bq, bv, bu, bh = (
+        split2[:, at : at + size].reshape(1, 2 * size)
+        for at, size in (
+            (dec_at, DD // 2),
+            (dec_at + DD // 2, DD // 2),
+            (dec_at + DD, DFF // 2),
+            (dec_at + DD + DFF // 2, PIX // 2),
+        )
+    )
+    wide = vec_shared[: 15 * D].reshape(15, D)
+    narrow = vec_shared[15 * D :].reshape(9, DD)
     dec_widths = [D // 2, DD // 2, DFF // 2, 3 * DD // 2, DFF // 2, PIX // 2]
     own_parts = cut(dec_own, dec_widths)
     other_parts = cut(dec_other, dec_widths)
@@ -1217,55 +1608,42 @@
     kinds = lambda block: block.reshape(3, DD // 2, DD)
     d_qkv = jnp.concatenate([kinds(own_parts[3]), kinds(other_parts[3])], 1).reshape(3 * DD, DD)
 
-    pos_enc = sinusoid_at(order[:VIS], D)
-    pos_dec = sinusoid_at(order, DD)
-    start_own = factors[0]
+    visible = mine(tube_order)[:VIS]
+    pos_enc = sinusoid_at(visible, D)
+    pos_dec = sinusoid_table(DD)
     start_other = swap(start_own)
     enc_starts = jnp.stack([start_own[:, :D], start_other[:, :D]])
     dec_starts = jnp.stack([start_own[:, D:], start_other[:, D:]])
-    enc_error_part = error_factor(start_own[:, :D], enc_error[0, 0])
-    dec_error_part = error_factor(start_own[:, D:], dec_error[0, 0])
-
-    embed = jnp.concatenate([enc_own[:D], enc_other[:D]], 0)
-    pixels_vis = pixels[:VIS]
-    stream = nn(pixels_vis, embed) + shared[0] + pos_enc
-    kept = []
-    enc_vecs = []
-    for layer in range(2):
-        base = 1 + 6 * layer
-        vecs = jnp.stack(shared[base : base + 6] + shared[13:15])
-        bq, bv, bu = split_parts[3 * layer : 3 * layer + 3]
-        bqkv = jnp.concatenate([bq, jnp.zeros_like(bq), bv], 1)
-        result = encoder_layer(
-            D + layer * LAYER_ROWS, stream, vecs, bqkv, bu, enc_own, enc_other,
-            f"encoder_{layer}", proj if layer == 1 else None,
-        )
-        kept.append((stream, result))
-        enc_vecs.append(vecs)
-        stream = result[0]
-    enc_normed, latent = result[8:]
-
-    bq, bv, bu, bh = split_parts[6:]
-    qkv_vecs = jnp.stack([shared[index] for index in (15, 16, 17, 15, 16, 17, 15, 16)])
-    dec_start, h, qkv = decoder_qkv(
-        pos_dec, latent, qkv_vecs, d_qkv, jnp.concatenate([bq, jnp.zeros_like(bq), bv], 1)
+
+    stream0, *kept0 = encoder_layer(
+        0, per, (pix_vis, pix_vis_other, pos_enc), wide, split2, enc_own, enc_other
+    )
+    stream1 = kept0[0]
+    enc_normed, latent, *kept1 = encoder_layer(
+        1, per, (stream1, proj), wide, split2, enc_own, enc_other
+    )
+    kept = [(stream0, kept0), (stream1, kept1)]
+
+    dec_start, h, qkv, hidden = decoder_qkv(
+        visible[None], pos_dec, latent, narrow, d_qkv,
+        jnp.concatenate([bq, jnp.zeros_like(bq), bv], 1),
     )
     mixed, logs = attend(qkv)
     scal = jnp.broadcast_to(
         jnp.stack([counted, 2.0 * workers / (PIX * loss_weight) * counted] + [counted] * 6)[:, None],
         (8, 128),
     )
-    dec_vecs = jnp.stack([shared[index] for index in (18, 19, 20, 21, 22, 23, 22, 23)])
-    grad_mixed, grad_middle, dec_grads, g_vec, g_bu, g_bh, loss_lanes = decoder_tokens(
-        mixed, dec_start, pixels, scal, dec_vecs, bu, bh, d_out, d_down, d_up, head_rows
+    grad_mixed, grad_middle, dec_grads, dec_sent, g_vec, g_bu, g_bh, loss_lanes = decoder_tokens(
+        which, mixed, dec_start, tubes, pixels, hidden, scal, narrow, bu, bh, d_out, d_down, d_up,
+        head_rows,
     )
     dq, dk, dv = attend_back(qkv, mixed, grad_mixed, logs)
-    latent_low, dec_grads, g_vec1 = decoder_qkv_back(
-        half.astype(jnp.int32)[None], dq, dk, dv, h, dec_start, grad_middle, qkv_vecs, d_qkv,
-        enc_normed, dec_grads,
-    )
-    dec_left = dec_left_factor(dec_starts, dec_grads)
-    dec_comb = dec_grads[0] + swap(dec_grads[1]) + dec_error[0, 0].astype(f32)
+    latent_low, dec_grads, dec_sent, g_vec1 = decoder_qkv_back(
+        which, visible[None], dq, dk, dv, h, dec_start, grad_middle, narrow, d_qkv, enc_normed,
+        dec_grads, dec_sent,
+    )
+    dec_left = dec_left_factor(dec_starts, dec_grads, dec_sent)
+    dec_came = swap(dec_sent)
 
     grad = latent_low
     packs = [None, None]
@@ -1275,13 +1653,12 @@
     for layer in (1, 0):
         source, result = kept[layer]
         grad, packs[layer], sent, enc_lefts[layer], *enc_vec_grads[layer] = encoder_layer_back(
-            D + layer * LAYER_ROWS, grad, source, enc_vecs[layer], result, enc_starts,
-            enc_own, enc_other, pixels_vis, f"encoder_back_{layer}",
-            (result[0], proj) if layer == 1 else (),
+            layer, per, grad, source, wide, result, enc_starts, enc_own, enc_other,
+            (pix_vis, pix_vis_other), (result[0], proj) if layer == 1 else (),
         )
         came[layer] = swap(sent)
-    mine_packs = (picked_mine, packs[0], packs[1])
-    their_packs = (picked_theirs, came[0], came[1])
+    mine_packs = (pix_vis, packs[0], packs[1])
+    their_packs = (picked[1], came[0], came[1])
 
     enc_basis, dec_basis = summed_basis(
         workers, enc_lefts[0], enc_lefts[1], dec_left, enc_error_part, dec_error_part
@@ -1322,11 +1699,12 @@
     dec_rows = dec_basis.shape[1] // workers
     enc_owned = lax.dynamic_slice_in_dim(enc_basis, worker_index * enc_rows, enc_rows, 1)
     dec_owned = lax.dynamic_slice_in_dim(dec_basis, worker_index * dec_rows, dec_rows, 1)
+    dec_right_part, dec_comb = dec_right_factor(dec_basis, dec_grads, dec_came, dec_error[0, 0])
     enc_right, dec_right, vec_mean = mean_over_workers(
         workers,
         (
             right_factor(enc_basis, enc_error[0, 0], mine_packs, their_packs),
-            dec_right_factor(dec_basis, dec_comb),
+            dec_right_part,
             vec_local,
         ),
     )

time: 728 us -> 600 us (0.82)
  waiting for transfers between devices: 187 us -> 4.38 us
  Pallas kernels: 390 us -> 516 us
  blocking collectives: 39.9 us -> 0 us
  between operations: 20.9 us -> 7.05 us
  other arithmetic: 40 us -> 28.2 us
    all_gather x2 -> x0, waiting for transfers between devices: 182 us -> none  [the longest x1 182 us: per_device(): lax.all_gather(enc_weights[0].astype(bf16), 'dp', axis=0, tiled=True)]
    pallas_call x10 -> x9, Pallas kernels: 190 us -> 311 us  [the longest x1 146 us: gather_weights(): pl.pallas_call(lambda *refs: gather_kernel(parts, planes, *refs), in_spec...]
    psum x1 -> x0, blocking collectives: 39.9 us -> none  [per_device(): loss_weight = MASKED * lax.psum(jnp.sum(counted_all), 'dp')]
    squeeze x2 -> x1, local copies, waits for them, and re-layouts: 9.33 us -> 1.83 us  [per_device(): pix_vis_other = swap(picked[1])]
  transfers between devices with their start and end apart: 11 -> 7, of which waited for: 2 -> 1; matrix products, arithmetic and copies ran while one was open for 7% -> 9% of each run, Pallas kernels for 20% -> 41%
where the time goes in v3:
time: 600 us; the launch traced here: 597 us
  Pallas kernels  516 us (86%)
  local copies, waits for them, and re-layouts  35.5 us (6%)
  other arithmetic  28.2 us (5%)
  between operations  7.05 us (1%)
    pallas_call x1, Pallas kernels, gather_weights(): pl.pallas_call(lambda *refs: gather_kernel(parts, planes, *refs), in_spec...  146 us
    pallas_call x1, Pallas kernels, decoder_tokens(): pl.pallas_call(token_kernel, grid_spec=pltpu.PrefetchScalarGridSpec(num_s...  65 us
    pallas_call x1, Pallas kernels, attend_back(): pl.pallas_call(attend_back_kernel, grid=(PAIRS, pl.cdiv(TUBES, BWD_ROWS))...  53.9 us
    pallas_call x2, Pallas kernels, encoder_layer_back(): pl.pallas_call(lambda *refs: encoder_back_kernel(layer, per, *refs), in_s...  41 us
    pallas_call x2, Pallas kernels, encoder_layer(): pl.pallas_call(lambda *refs: encoder_kernel(layer, per, *refs), in_specs=...  39.3 us
    pallas_call x1, Pallas kernels, attend(): pl.pallas_call(attend_kernel, grid=(PAIRS, TUBES // FWD_ROWS), in_specs=[...  32.5 us
    pallas_call x1, Pallas kernels, summed_basis(): pl.pallas_call(lambda *refs: basis_kernel(workers, lanes, enc_width, *ref...  29.2 us
    pallas_call x1, Pallas kernels, right_factor(): pl.pallas_call(right_factor_kernel, grid=(ENC_BLOCKS,), in_specs=[pl.Bloc...  21.8 us
  transfers between devices with their start and end apart: 7, of which 1 were waited for; matrix products, arithmetic and copies ran while one was open for 9% of the time, Pallas kernels for 41%

profile of v3, /device:TPU:0, one launch (start us, length us, event | category | flops | bytes accessed | tf_op | source)
XLA Modules:
  0.0 597.2 jit_solution(1394657817956508317)
XLA Ops:
  0.6 0.7 slice_bitcast_fusion.6
  1.3 0.8 copy.29.order_ref
  2.2 4.0 pick_visible.1
  6.2 1.8 slice_bitcast_fusion
  10.1 0.6 broadcast_in_dim.76
  10.8 1.3 maximum_maximum_fusion.refs_0_
  12.1 146.0 %gather_weights.1 = (bf16[16,736,768]{2,1,0:T(8,128)(2,1)}, bf16[16,736,768]{2,1,0:T(8,128)(2,1)}, bf16[1568,768]{1,0:T(8,128)(2,1)}, f32[8,9984]{1,0:T(8,128)}, f32[8,3456]{1,0:T(8,128)}) custom-call(bf16[736,768]{1,0:T(8,128)(2,1)} %maximum_maximum_fusion.refs_0_, bf16[2,1568,768]{2,1,0:T(8,128)(2,1)} %pix_ref.1, bf16[9984,768]{1,0:T(8,128)(2,1)} %bitcast.66, ...), custom_call_target="tpu_custom_call" | custom-call | tf_op jit(solution)/shard_map/gather_weights/pallas_call | solution.py:1487
  158.1 2.0 slice.275
  160.1 2.4 reshape.298
  162.4 2.0 slice.277
  164.4 2.4 reshape.299
  166.8 2.0 slice.354
  170.3 2.7 fusion.40
  173.0 1.3 fusion.41
  174.3 1.4 fusion.39
  175.7 2.0 pad_maximum_fusion.3
  177.7 1.0 multiply_cosine_fusion.2
  178.7 1.1 fusion.4
  179.8 1.2 pad_maximum_fusion.2.wh_ref
  181.0 0.7 pad_maximum_fusion.4.wo_ref
  181.7 2.8 fusion.1.refs_2_
  184.6 1.0 maximum_select_fusion.refs_1_.refs_16_
  185.6 1.8 multiply_add_fusion
  187.5 1.6 pad_maximum_fusion
  189.1 1.4 convert_reduce_fusion
  190.6 0.6 reshape.297.refs_3_.refs_2_
  191.2 0.6 slice.280.vec_ref
  193.7 4.6 stack.40
  198.3 0.8 stack.37
  199.1 0.7 pad_maximum_fusion.5.refs_4_.refs_3_
  201.8 13.7 %encoder_0.1 = (f32[160,768]{1,0:T(8,128)}, f32[160,768]{1,0:T(8,128)}, bf16[160,768]{1,0:T(8,128)(2,1)}, bf16[160,2304]{1,0:T(8,128)(2,1)}, bf16[160,768]{1,0:T...) custom-call(bf16[160,768]{1,0:T(8,128)(2,1)} %get-tuple-element.175., ...), custom_call_target="tpu_custom_call" | custom-call | tf_op jit(solution)/shard_map/encoder_0/pallas_call | solution.py:671
  215.6 25.6 %encoder_1.1 = (bf16[160,768]{1,0:T(8,128)(2,1)}, f32[160,384]{1,0:T(8,128)}, f32[160,768]{1,0:T(8,128)}, bf16[160,768]{1,0:T(8,128)(2,1)}, bf16[160,2304]{1,0:T...) custom-call(f32[160,768]{1,0:T(8,128)} %get-tuple-element.80.refs_0_, ...), custom_call_target="tpu_custom_call" | custom-call | tf_op jit(solution)/shard_map/encoder_1/pallas_call | solution.py:671
  241.2 8.5 %decoder_qkv.1 = (f32[1568,384]{1,0:T(8,128)}, bf16[1568,384]{1,0:T(8,128)(2,1)}, bf16[1568,1152]{1,0:T(8,128)(2,1)}, f32[1568,1]{1,0:T(8,128)}) custom-call(s32[1,160]{1,0:T(1,128)} %get-tuple-element.167.order_ref, f32[1568,384]{1,0:T(8,128)} %bitcast.73, f32[160,384]{1,0:T(8,128)} %get-tuple-element.81.latent_ref, f32[9,384]{1,0:T(8,128)} %slice.280.vec_ref, ...), custom_call_target="tpu_custom_call" | custom-call | tf_op jit(solution)/shard_map/decoder_qkv/pallas_call | solution.py:175
  249.7 32.5 %attend.1 = (f32[1568,384]{1,0:T(8,128)}, f32[3,1568,128]{2,1,0:T(8,128)}) custom-call(bf16[1568,1152]{1,0:T(8,128)(2,1)} %get-tuple-element.82.q_ref.k_ref.v_ref, bf16[1568,1152]{1,0:T(8,128)(2,1)} %get-tuple-element.82.q_ref.k_ref.v_ref, bf16[1568,1152]{1,0:T(8,128)(2,1)} %get-tuple-element.82.q_ref.k_ref.v_ref), custom_call_target="tpu_custom_call" | custom-call | tf_op jit(solution)/shard_map/attend/pallas_call | solution.py:225
  282.2 0.7 broadcast_in_dim.78.scal_ref
  282.8 65.0 %decoder_tokens.1 = (bf16[1568,384]{1,0:T(8,128)(2,1)}, f32[1568,384]{1,0:T(8,128)}, f32[3456,384]{1,0:T(8,128)}, f32[3456,384]{1,0:T(8,128)}, f32[8,384]{1,0:T(...) custom-call(s32[1]{0:T(128)} %bitcast.half_ref._, f32[1568,384]{1,0:T(8,128)} %get-tuple-element.83.a_ref.o_ref, ...), custom_call_target="tpu_custom_call" | custom-call | tf_op jit(solution)/shard_map/decoder_tokens/pallas_call | solution.py:408
  347.9 53.9 %attend_back.1 = (bf16[1568,384]{1,0:T(8,128)(2,1)}, bf16[1568,384]{1,0:T(8,128)(2,1)}, bf16[1568,384]{1,0:T(8,128)(2,1)}) custom-call(bf16[1568,1152]{1,0:T(8,128)(2,1)} %get-tuple-element.82.q_ref.k_ref.v_ref, bf16[1568,1152]{1,0:T(8,128)(2,1)} %get-tuple-element.82.q_ref.k_ref.v_ref, bf16[1568,1152]{1,0:T(8,128)(2,1)} %get-tuple-element.82.q_ref.k_ref.v_ref, ...), custom_call_target="tpu_custom_call" | custom-call | tf_op jit(solution)/shard_map/attend_back/pallas_call | solution.py:295
  401.7 12.5 %decoder_qkv_back.1 = (bf16[160,384]{1,0:T(8,128)(2,1)}, f32[3456,384]{1,0:T(8,128)}, f32[3456,384]{1,0:T(8,128)}, f32[8,384]{1,0:T(8,128)}) custom-call(s32[1]{0:T(128)} %bitcast.half_ref._, s32[1,160]{1,0:T(1,128)} %get-tuple-element.167.order_ref, bf16[1568,384]{1,0:T(8,128)(2,1)} %get-tuple-element.89.dq_ref, ...), custom_call_target="tpu_custom_call", output_to_operand_aliasing={{1}: (11, {}), {2}: (12, {})} | custom-call | tf_op jit(solution)/shard_map/decoder_qkv_back/pallas_call | solution.py:498
  414.8 4.4 collective-permute-done.2
  419.2 0.6 pad_maximum_fusion.6.refs_10_
  419.8 20.3 %encoder_back_1.1 = (f32[160,768]{1,0:T(8,128)}, bf16[160,7680]{1,0:T(8,128)(2,1)}, bf16[160,7680]{1,0:T(8,128)(2,1)}, f32[2,8,4608]{2,1,0:T(8,128)}, f32[8,768]...) custom-call(bf16[160,384]{1,0:T(8,128)(2,1)} %get-tuple-element.97.refs_0_, ...), custom_call_target="tpu_custom_call" | custom-call | tf_op jit(solution)/shard_map/encoder_back_1/pallas_call | solution.py:819
  440.2 20.7 %encoder_back_0.1 = (f32[160,768]{1,0:T(8,128)}, bf16[160,8448]{1,0:T(8,128)(2,1)}, bf16[160,8448]{1,0:T(8,128)(2,1)}, f32[2,8,5376]{2,1,0:T(8,128)}, f32[8,768]...) custom-call(f32[160,768]{1,0:T(8,128)} %get-tuple-element.106.refs_0_, f32[160,768]{1,0:T(8,128)} %get-tuple-element.107.refs_1_, ...), custom_call_target="tpu_custom_call" | custom-call | tf_op jit(solution)/shard_map/encoder_back_0/pallas_call | solution.py:819
  462.3 0.7 reshape.307
  463.1 0.6 reduce_sum.29
  464.4 0.8 slice_reduce_fusion.11
  465.2 0.7 slice_reduce_fusion.1
  466.1 0.8 slice_reduce_fusion.6
  467.7 7.0 %dec_left_factor.1.refs_2_ = f32[2,8,3456]{2,1,0:T(8,128)} custom-call(f32[2,8,384]{2,1,0:T(8,128)} %pad_maximum_fusion.7.start_ref, f32[3456,384]{1,0:T(8,128)} %get-tuple-element.117.own_ref, f32[3456,384]{1,0:T(8,128)} %get-tuple-element.118.other_ref), custom_call_target="tpu_custom_call" | custom-call | tf_op jit(solution)/shard_map/dec_left_factor/pallas_call | solution.py:1052
  474.7 29.2 %summed_basis.1 = (f32[8,9984]{1,0:T(8,128)}, f32[8,3456]{1,0:T(8,128)}) custom-call(f32[2,8,5376]{2,1,0:T(8,128)} %get-tuple-element.115.refs_0_, f32[2,8,4608]{2,1,0:T(8,128)} %get-tuple-element.116.refs_1_, f32[2,8,3456]{2,1,0:T(8,128)} %dec_left_factor.1.refs_2_, f32[8,9984]{1,0:T(8,128)} %get-tuple-element.119.refs_3_, f32[8,3456]{1,0:T(8,128)} %get-tuple-element.120.refs_4_), custom_call_target="tpu_custom_call" | custom-call | tf_op jit(solution)/shard_map/summed_basis/pallas_call | solution.py:1170
  504.1 0.7 reshape.310.refs_2_
  504.7 1.5 copy-done
  506.2 21.8 %right_factor.1.refs_0_ = f32[8,768]{1,0:T(8,128)} custom-call(f32[8,9984]{1,0:T(8,128)} %get-tuple-element.121.basis_ref, bf16[9984,768]{1,0:T(8,128)(2,1)} %bitcast.67, bf16[160,768]{1,0:T(8,128)(2,1)} %get-tuple-element.175.refs_0_.refs_13_, bf16[160,8448]{1,0:T(8,128)(2,1)} %get-tuple-element.122.refs_1_.refs_2_.refs_3_.refs_4_, ...), custom_call_target="tpu_custom_call" | custom-call | tf_op jit(solution)/shard_map/right_factor/pallas_call | solution.py:925
  528.0 7.9 %dec_right_factor.1 = (f32[8,384]{1,0:T(8,128)}, f32[3456,384]{1,0:T(8,128)}) custom-call(f32[8,3456]{1,0:T(8,128)} %get-tuple-element.126.basis_ref, f32[3456,384]{1,0:T(8,128)} %get-tuple-element.117.own_ref, f32[3456,384]{1,0:T(8,128)} %collective-permute-done.5.came_ref, bf16[3456,384]{1,0:T(8,128)(2,1)} %bitcast.72), custom_call_target="tpu_custom_call" | custom-call | tf_op jit(solution)/shard_map/dec_right_factor/pallas_call | solution.py:1005
  535.9 20.0 %mean_over_workers.1 = (f32[8,768]{1,0:T(8,128)}, f32[8,384]{1,0:T(8,128)}, f32[8,2816]{1,0:T(8,128)}) custom-call(f32[8,768]{1,0:T(8,128)} %right_factor.1.refs_0_, f32[8,384]{1,0:T(8,128)} %get-tuple-element.127.refs_1_, f32[8,2816]{1,0:T(8,128)} %reshape.310.refs_2_), custom_call_target="tpu_custom_call" | custom-call | tf_op jit(solution)/shard_map/mean_over_workers/pallas_call | solution.py:1216
  555.9 1.4 maximum_bitcast_fusion
  557.3 5.8 dec_residue.1
  563.1 1.3 convolution_add_fusion
  564.5 0.8 fusion.2
  565.3 2.8 bitcast_add_fusion
  568.1 1.9 fusion
  570.5 0.6 broadcast_in_dim.88
  571.1 0.6 broadcast_in_dim.89
  571.8 0.7 multiply_subtract_fusion
  573.1 21.7 %residue.1 = bf16[9984,768]{1,0:T(8,128)(2,1)} custom-call(f32[8,9984]{1,0:T(8,128)} %get-tuple-element.121.basis_ref, f32[8,768]{1,0:T(8,128)} %get-tuple-element.140.factor_ref, bf16[9984,768]{1,0:T(8,128)(2,1)} %bitcast.68, bf16[160,768]{1,0:T(8,128)(2,1)} %get-tuple-element.175.refs_0_.refs_13_, ...), custom_call_target="tpu_custom_call" | custom-call | tf_op jit(solution)/shard_map/residue/pallas_call | solution.py:971
  (141 shorter events, 9.4 us)
Async XLA Ops:
  2.2 6.3 %copy-start.16 = (f32[1,6528]{1,0:T(1,128)S(1)}, f32[1,6528]{1,0:T(1,128)}, u32[]{:S(2)}) copy-start(f32[1,6528]{1,0:T(1,128)} %param.19) | copy-start | bytes 78340
  2.2 7.1 %copy-start.3 = (f32[1,624,768]{2,1,0:T(8,128)S(1)}, f32[1,624,768]{2,1,0:T(8,128)}, u32[]{:S(2)}) copy-start(f32[1,624,768]{2,1,0:T(8,128)} %param.17) | copy-start | bytes 5750788
  6.2 3.2 copy-start.14
  6.2 3.3 copy-start.34
  8.0 4.0 copy-start.11
  8.0 193.8 %collective-permute-start = (bf16[160,768]{1,0:T(8,128)(2,1)S(1)}, bf16[160,768]{1,0:T(8,128)(2,1)}, u32[]{:S(2)}, u32[]{:S(2)}) collective-permute-start(bf16[160,768]{1,0:T(8,128)(2,1)S(1)} %get-tuple-element.174.refs_8_), channel_id=1, source_target_pairs={{0,1},{1,0},{2,3},{3,2},{4,5},{5,4},{6,7},{7,6},{8,9},{9,8},{10,11... | collective-permute-start | bytes 737288 | tf_op jit(solution)/shard_map/ppermute | solution.py:1523
  8.5 189.8 %collective-permute-start.1 = (f32[6528]{0:T(1024)S(1)}, f32[6528]{0:T(1024)}, u32[]{:S(2)}, u32[]{:S(2)}) collective-permute-start(f32[6528]{0:T(1024)S(1)} %reduce.1), channel_id=1, source_target_pairs={{0,1},{1,0},{2,3},{3,2},{4,5},{5,4},{6,7},{7,6},{8,9},{9,8},{10,11... | collective-permute-start | bytes 78344 | tf_op jit(solution)/shard_map/ppermute | solution.py:1523
  166.7 6.3 %copy-start.1 = (bf16[3456,384]{1,0:T(8,128)(2,1)S(1)}, bf16[3456,384]{1,0:T(8,128)(2,1)}, u32[]{:S(2)}) copy-start(bf16[3456,384]{1,0:T(8,128)(2,1)} %reshape.299) | copy-start | bytes 7962628
  173.0 2.7 slice-start.1
  174.3 5.5 copy-start.9
  174.3 5.5 copy-start.10
  174.3 6.7 %slice-start.2 = ((bf16[3456,384]{1,0:T(8,128)(2,1)}), bf16[192,384]{1,0:T(8,128)(2,1)S(1)}, s32[]{:S(2)}) async-start(bf16[3456,384]{1,0:T(8,128)(2,1)} %reshape.298), calls=%async_computation.2 | async-start | bytes 294912 | tf_op jit(solution)/shard_map/slice | solution.py:1517
  174.3 6.7 %slice-start.4 = ((bf16[3456,384]{1,0:T(8,128)(2,1)}), bf16[192,384]{1,0:T(8,128)(2,1)S(1)}, s32[]{:S(2)}) async-start(bf16[3456,384]{1,0:T(8,128)(2,1)} %reshape.299), calls=%async_computation.4 | async-start | bytes 294912 | tf_op jit(solution)/shard_map/slice | solution.py:1517
  175.7 6.0 %copy-start.33 = (pred[768]{0:T(1024)(128)(4,1)S(1)}, pred[768]{0:T(1024)(128)(4,1)}, u32[]{:S(2)}) copy-start(pred[768]{0:T(1024)(128)(4,1)} %fusion.13) | copy-start | bytes 2308
  177.7 6.8 %slice-start = ((bf16[3456,384]{1,0:T(8,128)(2,1)}), bf16[384,384]{1,0:T(8,128)(2,1)S(1)}, s32[]{:S(2)}) async-start(bf16[3456,384]{1,0:T(8,128)(2,1)} %reshape.298), calls=%async_computation | async-start | bytes 589824 | tf_op jit(solution)/shard_map/slice | solution.py:1517
  177.7 6.9 %slice-start.3 = ((bf16[3456,384]{1,0:T(8,128)(2,1)}), bf16[384,384]{1,0:T(8,128)(2,1)S(1)}, s32[]{:S(2)}) async-start(bf16[3456,384]{1,0:T(8,128)(2,1)} %reshape.299), calls=%async_computation.3 | async-start | bytes 589824 | tf_op jit(solution)/shard_map/slice | solution.py:1517
  181.7 5.7 copy-start.5
  181.7 5.7 copy-start.6
  181.7 5.7 copy-start.7
  181.7 5.7 copy-start.8
  187.4 3.1 copy-start.18
  187.4 3.1 copy-start.35
  187.5 3.1 slice-start.5
  401.7 12.9 %copy-start.20 = (f32[1,8,1152]{2,1,0:T(8,128)S(1)}, f32[1,8,1152]{2,1,0:T(8,128)}, u32[]{:S(2)}) copy-start(f32[1,8,1152]{2,1,0:T(8,128)} %param.27) | copy-start | bytes 110596
  414.2 113.8 %collective-permute-start.5 = (f32[3456,384]{1,0:T(8,128)}, f32[3456,384]{1,0:T(8,128)}, u32[]{:S(2)}, u32[]{:S(2)}) collective-permute-start(f32[3456,384]{1,0:T(8,128)} %get-tuple-element.118.other_ref), channel_id=1, source_target_pairs={{0,1},{1,0},{2,3},{3,2},{4,5},{5,4},{6,7},{7,6},{8,9},{9,8},{10,11... | collective-permute-start | bytes 15925256 | tf_op jit(solution)/shard_map/ppermute | solution.py:1523
  414.6 4.5 collective-permute-start.2
  440.1 22.0 %copy-start.24 = (f32[1,6528]{1,0:T(1,128)S(1)}, f32[1,6528]{1,0:T(1,128)}, u32[]{:S(2)}) copy-start(f32[1,6528]{1,0:T(1,128)} %param.23) | copy-start | bytes 78340
  440.2 22.9 %copy-start.25 = (f32[8,768]{1,0:T(8,128)S(1)}, f32[8,768]{1,0:T(8,128)}, u32[]{:S(2)}) copy-start(f32[8,768]{1,0:T(8,128)} %get-tuple-element.136) | copy-start | bytes 73732
  440.2 22.9 %copy-start.27 = (f32[8,384]{1,0:T(8,128)S(1)}, f32[8,384]{1,0:T(8,128)}, u32[]{:S(2)}) copy-start(f32[8,384]{1,0:T(8,128)} %get-tuple-element.137) | copy-start | bytes 36868
  440.2 22.9 %copy-start.32 = (f32[1,1536]{1,0:T(1,128)S(1)}, f32[1,1536]{1,0:T(1,128)}, u32[]{:S(2)}) copy-start(f32[1,1536]{1,0:T(1,128)} %get-tuple-element.138) | copy-start | bytes 18436
  440.2 24.1 %copy-start.30 = (f32[1,1536]{1,0:T(1,128)S(1)}, f32[1,1536]{1,0:T(1,128)}, u32[]{:S(2)}) copy-start(f32[1,1536]{1,0:T(1,128)} %get-tuple-element.134) | copy-start | bytes 18436
  440.2 24.2 %copy-start.29 = (f32[1,1536]{1,0:T(1,128)S(1)}, f32[1,1536]{1,0:T(1,128)}, u32[]{:S(2)}) copy-start(f32[1,1536]{1,0:T(1,128)} %get-tuple-element.133) | copy-start | bytes 18436
  440.2 25.0 %copy-start.31 = (f32[2,768]{1,0:T(2,128)S(1)}, f32[2,768]{1,0:T(2,128)}, u32[]{:S(2)}) copy-start(f32[2,768]{1,0:T(2,128)} %get-tuple-element.130) | copy-start | bytes 18436
  440.2 25.8 %copy-start.26 = (f32[1,3072]{1,0:T(1,128)S(1)}, f32[1,3072]{1,0:T(1,128)}, u32[]{:S(2)}) copy-start(f32[1,3072]{1,0:T(1,128)} %get-tuple-element.131) | copy-start | bytes 36868
  440.2 25.8 %copy-start.28 = (f32[8,384]{1,0:T(8,128)S(1)}, f32[8,384]{1,0:T(8,128)}, u32[]{:S(2)}) copy-start(f32[8,384]{1,0:T(8,128)} %get-tuple-element.132) | copy-start | bytes 36868
  460.9 43.8 %collective-permute-start.3 = (bf16[160,8448]{1,0:T(8,128)(2,1)}, bf16[160,8448]{1,0:T(8,128)(2,1)S(1)}, u32[]{:S(2)}, u32[]{:S(2)}) collective-permute-start(bf16[160,8448]{1,0:T(8,128)(2,1)} %get-tuple-element.124), channel_id=1, source_target_pairs={{0,1},{1,0},{2,3},{3,2},{4,5},{5,4},{6,7},{7,6},{8,9},{9,8},{10,11... | collective-permute-start | bytes 8110088 | tf_op jit(solution)/shard_map/ppermute | solution.py:1523
  461.1 43.6 %collective-permute-start.4 = (bf16[160,7680]{1,0:T(8,128)(2,1)}, bf16[160,7680]{1,0:T(8,128)(2,1)}, u32[]{:S(2)}, u32[]{:S(2)}) collective-permute-start(bf16[160,7680]{1,0:T(8,128)(2,1)} %get-tuple-element.125), channel_id=1, source_target_pairs={{0,1},{1,0},{2,3},{3,2},{4,5},{5,4},{6,7},{7,6},{8,9},{9,8},{10,11... | collective-permute-start | bytes 7372808 | tf_op jit(solution)/shard_map/ppermute | solution.py:1523
  467.0 37.1 %collective-permute-start.6 = (f32[22528]{0:T(1024)S(1)}, f32[22528]{0:T(1024)S(1)}, u32[]{:S(2)}, u32[]{:S(2)}) collective-permute-start(f32[22528]{0:T(1024)S(1)} %concatenate.49), channel_id=1, source_target_pairs={{0,1},{1,0},{2,3},{3,2},{4,5},{5,4},{6,7},{7,6},{8,9},{9,8},{10,11... | collective-permute-start | bytes 270344 | tf_op jit(solution)/shard_map/ppermute | solution.py:1523
  504.7 1.5 copy-start
  557.3 5.8 copy-start.17
  557.3 5.8 copy-start.21
  557.3 7.2 %copy-start.15 = (f32[1,216,384]{2,1,0:T(8,128)S(1)}, f32[1,216,384]{2,1,0:T(8,128)}, u32[]{:S(2)}) copy-start(f32[1,216,384]{2,1,0:T(8,128)} %param.18) | copy-start | bytes 995332
  557.3 8.0 %copy-start.12 = (f32[1,624,768]{2,1,0:T(8,128)S(1)}, f32[1,624,768]{2,1,0:T(8,128)}, u32[]{:S(2)}) copy-start(f32[1,624,768]{2,1,0:T(8,128)} %param.21) | copy-start | bytes 5750788
  557.3 8.0 %copy-start.19 = (f32[8,768]{1,0:T(8,128)S(1)}, f32[8,768]{1,0:T(8,128)}, u32[]{:S(2)}) copy-start(f32[8,768]{1,0:T(8,128)} %get-tuple-element.140.factor_ref) | copy-start | bytes 73732
  564.5 3.6 copy-start.13
  564.5 3.6 copy-start.4
  568.1 1.9 copy-start.2
  568.1 1.9 copy-start.22
  568.1 3.7 copy-start.23

commit v4 on v3

--- a/solution.py
+++ b/solution.py
@@ -85,23 +85,17 @@
     return value[:rows] + value[rows : 2 * rows] + value[2 * rows :]
 
 
-def sinusoid_at(place, width):
-    column = jnp.arange(width)
-    rate = jnp.exp(-(2 * (column // 2)).astype(f32) * (math.log(10000.0) / width))
-    angle = place.astype(f32)[:, None] * rate[None, :]
-    return jnp.where(column % 2 == 0, jnp.sin(angle), jnp.cos(angle))
-
-
-def sinusoid_table(width):
-    column = jnp.arange(width)
-    rate = jnp.exp(-(2 * (column // 2)).astype(f32) * (math.log(10000.0) / width))[None, :]
-    first = (32 * jnp.arange(TUBES // 32)).astype(f32)[:, None] * rate
-    second = jnp.arange(32).astype(f32)[:, None] * rate
-    even = column % 2 == 0
-    ahead = jnp.where(even, jnp.sin(first), jnp.cos(first))[:, None]
-    turned = jnp.where(even, jnp.cos(first), -jnp.sin(first))[:, None]
-    table = ahead * jnp.cos(second)[None] + turned * jnp.sin(second)[None]
-    return table.reshape(TUBES, width)
+def rates(width):
+    column = lax.broadcasted_iota(jnp.int32, (1, width), 1)
+    low_bit = lax.rem(column, 2)
+    rate = jnp.exp((column - low_bit).astype(f32) * (-math.log(10000.0) / width))
+    return rate, low_bit == 0
+
+
+def sinusoid_of(place, width):
+    rate, even = rates(width)
+    angle = place * rate
+    return jnp.where(even, jnp.sin(angle), jnp.cos(angle))
 
 
 def params(**more):
@@ -195,8 +189,6 @@
     )(order, pos, latent, vecs, weights, bias)
 
 
-FWD_ROWS = 392
-BWD_ROWS = 256
 PAIRS = DD // 128
 
 
@@ -224,15 +216,15 @@
 def attend(qkv):
     return pl.pallas_call(
         attend_kernel,
-        grid=(PAIRS, TUBES // FWD_ROWS),
+        grid=(PAIRS, TUBES // TUBES),
         in_specs=[
-            pl.BlockSpec((FWD_ROWS, 128), lambda p, i: (i, p)),
+            pl.BlockSpec((TUBES, 128), lambda p, i: (i, p)),
             pl.BlockSpec((TUBES, 128), lambda p, i: (0, PAIRS + p)),
             pl.BlockSpec((TUBES, 128), lambda p, i: (0, 2 * PAIRS + p)),
         ],
         out_specs=[
-            pl.BlockSpec((FWD_ROWS, 128), lambda p, i: (i, p)),
-            pl.BlockSpec((1, FWD_ROWS, 128), lambda p, i: (p, i, 0)),
+            pl.BlockSpec((TUBES, 128), lambda p, i: (i, p)),
+            pl.BlockSpec((1, TUBES, 128), lambda p, i: (p, i, 0)),
         ],
         out_shape=[
             jax.ShapeDtypeStruct((TUBES, DD), f32),
@@ -243,23 +235,11 @@
     )(qkv, qkv, qkv)
 
 
-def attend_back_kernel(
-    q_ref, k_ref, v_ref, o_ref, do_ref, lse_ref, dq_ref, dk_ref, dv_ref, k_turned, dk_sum, dv_sum
-):
-    step = pl.program_id(1)
-
-    @pl.when(step == 0)
-    def _():
-        k_turned[...] = k_ref[...].T
-        dk_sum[...] = jnp.zeros_like(dk_sum)
-        dv_sum[...] = jnp.zeros_like(dv_sum)
-
-    valid = lax.broadcasted_iota(jnp.int32, (BWD_ROWS, 1), 0) + step * BWD_ROWS < TUBES
-    zero = jnp.zeros((), bf16)
-    q = jnp.where(valid, q_ref[...], zero)
-    grad = jnp.where(valid, do_ref[...], zero)
-    dots = jnp.where(valid, o_ref[...], 0.0) * grad.astype(f32)
-    logs = jnp.where(valid, lse_ref[0], 0.0).T
+def attend_back_kernel(q_ref, k_ref, v_ref, o_ref, do_ref, lse_ref, dq_ref, dk_ref, dv_ref):
+    q, k, v, grad = q_ref[...], k_ref[...], v_ref[...], do_ref[...]
+    k_turned = k.T
+    dots = o_ref[...] * grad.astype(f32)
+    logs = lse_ref[0].T
     select = (
         lax.broadcasted_iota(jnp.int32, (8, 128), 1) // HEAD_DIM
         == lax.broadcasted_iota(jnp.int32, (8, 128), 0)
@@ -268,8 +248,8 @@
         select, dots, (((1,), (1,)), ((), ())), precision=highest_precision,
         preferred_element_type=f32,
     )
-    k = k_ref[...]
-    v = v_ref[...]
+    zero = jnp.zeros((), bf16)
+    dk = dv = jnp.zeros((TUBES, 128), f32)
     turned = []
     for head in range(2):
         mask = half_lane(head)
@@ -278,44 +258,35 @@
         low = head * HEAD_DIM
         probs = jnp.exp2(nt(k, q_head) * (SCORE * LOG2E) - logs[low : low + 1])
         grad_scores = (probs * (nt(v, grad_head) - row_total[head : head + 1])).astype(bf16)
-        dv_sum[...] += nn(probs.astype(bf16), grad_head)
-        dk_sum[...] += nn(grad_scores, q_head)
+        dv = dv + nn(probs.astype(bf16), grad_head)
+        dk = dk + nn(grad_scores, q_head)
         turned.append(nn(k_turned[low : low + HEAD_DIM], grad_scores))
     dq_ref[...] = (jnp.concatenate(turned, 0).T * SCORE).astype(bf16)
-
-    @pl.when(step == pl.num_programs(1) - 1)
-    def _():
-        dk_ref[...] = (dk_sum[...] * SCORE).astype(bf16)
-        dv_ref[...] = dv_sum[...].astype(bf16)
+    dk_ref[...] = (dk * SCORE).astype(bf16)
+    dv_ref[...] = dv.astype(bf16)
 
 
 def attend_back(qkv, mixed, grad_mixed, logs):
-    some = pl.BlockSpec((BWD_ROWS, 128), lambda p, i: (i, p))
-    full = pl.BlockSpec((TUBES, 128), lambda p, i: (0, p))
+    pair = lambda kind: pl.BlockSpec((TUBES, 128), lambda p: (0, kind * PAIRS + p))
     return pl.pallas_call(
         attend_back_kernel,
-        grid=(PAIRS, pl.cdiv(TUBES, BWD_ROWS)),
+        grid=(PAIRS,),
         in_specs=[
-            some,
-            pl.BlockSpec((TUBES, 128), lambda p, i: (0, PAIRS + p)),
-            pl.BlockSpec((TUBES, 128), lambda p, i: (0, 2 * PAIRS + p)),
-            some,
-            some,
-            pl.BlockSpec((1, BWD_ROWS, 128), lambda p, i: (p, i, 0)),
+            pair(0),
+            pair(1),
+            pair(2),
+            pair(0),
+            pair(0),
+            pl.BlockSpec((1, TUBES, 128), lambda p: (p, 0, 0)),
         ],
-        out_specs=[some, full, full],
+        out_specs=[pair(0)] * 3,
         out_shape=[jax.ShapeDtypeStruct((TUBES, DD), bf16)] * 3,
-        scratch_shapes=[
-            pltpu.VMEM((128, TUBES), bf16),
-            pltpu.VMEM((TUBES, 128), f32),
-            pltpu.VMEM((TUBES, 128), f32),
-        ],
         compiler_params=params(),
         name="attend_back",
     )(qkv, qkv, qkv, mixed, grad_mixed, logs)
 
 
-TOKEN_ROWS = 224
+TOKEN_ROWS = 784
 CHUNK = 384
 DEC_O = D // 2
 DEC_D = DEC_O + DD // 2
@@ -564,7 +535,8 @@
         pix_ref, pix_other_ref, pos_ref, *refs = refs
     else:
         x_ref, proj_ref, *refs = refs
-    vec_ref, split_ref, own_ref, other_ref, *refs = refs
+    vec_ref, split_own_ref, split_other_ref, own_ref, other_ref, *refs = refs
+    splits = (split_own_ref, split_other_ref)
     if layer == 0:
         x_out_ref, *refs = refs
     else:
@@ -613,7 +585,7 @@
             value = nt(h, held[group, rows])
             if kind != 1:
                 at = biases + kind // 2 * HALF
-                value = value + split_ref[group : group + 1, at : at + HALF]
+                value = value + splits[group][:, at : at + HALF]
             qkv_ref[:, part] = value.astype(bf16)
     for pair in range(D // 128):
         q, k, v = (qkv_ref[:, pl.ds(kind * D + pair * 128, 128)] for kind in range(3))
@@ -642,7 +614,7 @@
             part = pl.ds(group * HALF_FF + chunk * CHUNK, CHUNK)
             before = nt(h2, held[group, pl.ds(AT_U + chunk * CHUNK, CHUNK)])
             at = biases + 2 * HALF + chunk * CHUNK
-            value, slope = gelu_pair(before + split_ref[group : group + 1, at : at + CHUNK])
+            value, slope = gelu_pair(before + splits[group][:, at : at + CHUNK])
             slope_ref[:, part] = slope
             active = value.astype(bf16)
             u_ref[:, part] = active
@@ -655,7 +627,7 @@
         latent_ref[...] = nn(normed, proj_ref[...])
 
 
-def encoder_layer(layer, per, first, vecs, split2, own, other):
+def encoder_layer(layer, per, first, vecs, splits, own, other):
     shapes = [
         ((VIS, D), f32),
         ((VIS, D), bf16),
@@ -670,7 +642,7 @@
     shapes = before + shapes
     return pl.pallas_call(
         lambda *refs: encoder_kernel(layer, per, *refs),
-        in_specs=[vmem_spec()] * (len(first) + 2) + [any_spec()] * 2,
+        in_specs=[vmem_spec()] * (len(first) + 3) + [any_spec()] * 2,
         out_specs=[vmem_spec()] * len(shapes),
         out_shape=[jax.ShapeDtypeStruct(shape, kind) for shape, kind in shapes],
         scratch_shapes=[
@@ -679,7 +651,7 @@
         ],
         compiler_params=params(),
         name=f"encoder_{layer}",
-    )(*first, vecs, split2, own, other)
+    )(*first, vecs, *splits, own, other)
 
 
 RIGHT_AT = LAYER_ROWS
@@ -691,10 +663,10 @@
     base = 1 + 6 * layer
     (
         grad_ref, x_ref, vec_ref, h_ref, qkv_ref, a_ref, x1_ref, h2_ref, u_ref, slope_ref,
-        start_ref, own_ref, other_ref, pix_ref, pix_other_ref,
-    ) = refs[:15]
+        start_ref, start_other_ref, own_ref, other_ref, pix_ref, pix_other_ref,
+    ) = refs[:16]
     pixels = (pix_ref, pix_other_ref)
-    refs = refs[15:]
+    refs = refs[16:]
     if last:
         out_ref, proj_ref, *refs = refs
     dx_ref, mine_ref, other_pack_ref, left_ref, gvec_ref, gbu_ref, gbq_ref = refs[:7]
@@ -787,7 +759,7 @@
         embed_low = grad_x.astype(bf16)
         rights.append(embed_low)
         gvec_ref[6:7] = col_sum(embed_low.astype(f32))
-    starts = jnp.concatenate([split3(start_ref[0]), split3(start_ref[1])], 0)
+    starts = jnp.concatenate([split3(ref[:, :D]) for ref in (start_ref, start_other_ref)], 0)
     before = 0 if last else D
     for index, right in enumerate(rights):
         for pack in packs:
@@ -818,7 +790,7 @@
     _, h, qkv, a, x1, h2, u, slope = kept
     return pl.pallas_call(
         lambda *refs: encoder_back_kernel(layer, per, *refs),
-        in_specs=[vmem_spec()] * 11 + [any_spec()] * 2 + [vmem_spec()] * (2 + len(last)),
+        in_specs=[vmem_spec()] * 12 + [any_spec()] * 2 + [vmem_spec()] * (2 + len(last)),
         out_specs=[vmem_spec()] * len(shapes),
         out_shape=[jax.ShapeDtypeStruct(shape, kind) for shape, kind in shapes],
         scratch_shapes=[
@@ -829,7 +801,7 @@
         ],
         compiler_params=params(),
         name=f"encoder_back_{layer}",
-    )(grad, source, vecs, h, qkv, a, x1, h2, u, slope, starts, own, other, *pixels, *last)
+    )(grad, source, vecs, h, qkv, a, x1, h2, u, slope, *starts, own, other, *pixels, *last)
 
 
 ROWS = 768
@@ -1038,9 +1010,9 @@
     )(basis, factor, comb)
 
 
-def dec_left_kernel(start_ref, own_ref, other_ref, out_ref):
-    for group, ref in enumerate((own_ref, other_ref)):
-        start = split3(start_ref[group])
+def dec_left_kernel(start_ref, start_other_ref, own_ref, other_ref, out_ref):
+    for group, (begin_ref, ref) in enumerate(((start_ref, own_ref), (start_other_ref, other_ref))):
+        start = split3(begin_ref[:, D:])
         grad = ref[...]
         high = grad.astype(bf16)
         rest = (grad - high.astype(f32)).astype(bf16)
@@ -1052,12 +1024,12 @@
     return pl.pallas_call(
         dec_left_kernel,
         grid=(DEC_ROWS // DEC_BLOCK,),
-        in_specs=[whole((2, RANK, DD)), rows, rows],
+        in_specs=[whole((RANK, D + DD))] * 2 + [rows, rows],
         out_specs=pl.BlockSpec((2, RANK, DEC_BLOCK), lambda j: (0, 0, j)),
         out_shape=jax.ShapeDtypeStruct((2, RANK, DEC_ROWS), f32),
         compiler_params=params(),
         name="dec_left_factor",
-    )(starts, own, other)
+    )(*starts, own, other)
 
 
 MESH_ID = pl.DeviceIdType.MESH
@@ -1232,15 +1204,19 @@
 
 
 PLANE = 4
-PART_Z_X_Y, PART_Z_Y_X, PART_X_Y_Z = range(3)
+PART_Z_X_Y, PART_Z_Y_X, PART_X_Y_Z, PART_DEC = range(4)
+Z_X_Y_PARTS = (PART_DEC, PART_Z_X_Y)
 WAY_X, WAY_Y, WAY_UP, WAY_DOWN = range(4)
 ERROR_ROWS = 1248
 
 
 def gather_kernel(
-    parts, planes, shard_ref, tubes_ref, error_ref, dec_error_ref, start_ref,
-    own_ref, other_ref, pixels_ref, part_ref, dec_part_ref,
-    held, dec_held, send_sems, recv_sems, pair_sems, sems,
+    parts, planes, shard_ref, dec_shard_ref, tubes_ref, error_ref, dec_error_ref, start_ref, order_ref,
+    counted_ref,
+    own_ref, other_ref, pixels_ref, part_ref, dec_part_ref, picked_ref, pix_other_ref,
+    pos_enc_ref, pos_dec_ref, scal_ref, proj_ref, wqkv_ref, wo_ref, wd_ref, wu_ref, wh_ref,
+    held, dec_held, dec_own, dec_other, joined, pix_held,
+    send_sems, recv_sems, pair_sems, sems,
 ):
     me = lax.axis_index("dp")
     half = lax.axis_index("tensor")
@@ -1259,10 +1235,16 @@
     )
     rows = [pl.ds(at, size) for at, size in parts]
 
+    def place(part, slot):
+        return dec_own.at[slot] if part == PART_DEC else own_ref.at[slot, rows[part]]
+
     def copy(way, part, slot, mine=False):
+        source = place(part, slot)
+        if mine:
+            source = dec_shard_ref if part == PART_DEC else shard_ref.at[rows[part]]
         return pltpu.make_async_remote_copy(
-            src_ref=shard_ref.at[rows[part]] if mine else own_ref.at[slot, rows[part]],
-            dst_ref=own_ref.at[slot, rows[part]],
+            src_ref=source,
+            dst_ref=place(part, slot),
             send_sem=send_sems.at[way, part, slot],
             recv_sem=recv_sems.at[part, slot],
             device_id={"dp": peers[way]},
@@ -1277,9 +1259,13 @@
 
     def pair(part, plane):
         block = pl.ds(plane * PLANE, PLANE)
+        if part == PART_DEC:
+            source, target = dec_own.at[block], dec_other.at[block]
+        else:
+            source, target = own_ref.at[block, rows[part]], other_ref.at[block, rows[part]]
         return pltpu.make_async_remote_copy(
-            src_ref=own_ref.at[block, rows[part]],
-            dst_ref=other_ref.at[block, rows[part]],
+            src_ref=source,
+            dst_ref=target,
             send_sem=pair_sems.at[0, part, plane],
             recv_sem=pair_sems.at[1, part, plane],
             device_id={"tensor": 1 - half},
@@ -1328,15 +1314,16 @@
 
             @pl.when(there)
             def _(slot=plane * PLANE + column, on=on, way=way):
-                for part in (PART_Z_X_Y, PART_Z_Y_X):
+                for part in Z_X_Y_PARTS + (PART_Z_Y_X,):
                     recv(part, slot)
 
                     @pl.when(on)
                     def _():
                         send(way, part, slot)
 
-                    send(WAY_X if part == PART_Z_X_Y else WAY_Y, part, slot)
-                send(WAY_Y, PART_Z_X_Y, slot)
+                    send(WAY_Y if part == PART_Z_Y_X else WAY_X, part, slot)
+                for part in Z_X_Y_PARTS:
+                    send(WAY_Y, part, slot)
                 send(WAY_X, PART_Z_Y_X, slot)
 
     def cross(distance):
@@ -1344,8 +1331,9 @@
 
             @pl.when(there)
             def _(base=plane * PLANE):
-                recv(PART_Z_X_Y, base + column_x)
-                send(WAY_Y, PART_Z_X_Y, base + column_x)
+                for part in Z_X_Y_PARTS:
+                    recv(part, base + column_x)
+                    send(WAY_Y, part, base + column_x)
                 recv(PART_Z_Y_X, base + column_y)
                 send(WAY_X, PART_Z_Y_X, base + column_y)
 
@@ -1354,9 +1342,10 @@
 
             @pl.when(there)
             def _(plane=plane, base=plane * PLANE):
-                recv(PART_Z_X_Y, base + column_y)
-                recv(PART_Z_X_Y, base + column_xy)
-                pair(PART_Z_X_Y, plane).start()
+                for part in Z_X_Y_PARTS:
+                    recv(part, base + column_y)
+                    recv(part, base + column_xy)
+                    pair(part, plane).start()
                 recv(PART_Z_Y_X, base + column_x)
                 recv(PART_Z_Y_X, base + column_xy)
                 pair(PART_Z_Y_X, plane).start()
@@ -1376,6 +1365,7 @@
 
                 pair(PART_X_Y_Z, plane).start()
 
+    workers = planes * PLANE
     start3 = split3(start_ref[:, :D])
     chunks = error_ref.shape[0] // ERROR_ROWS
 
@@ -1388,14 +1378,20 @@
 
     send(WAY_X, PART_X_Y_Z, me, True)
     send(WAY_Y, PART_X_Y_Z, me, True)
-    both_z(PART_Z_X_Y, me, True)
-    both_z(PART_Z_Y_X, me, True)
-    send(WAY_X, PART_Z_X_Y, me, True)
+    for part in (PART_DEC, PART_Z_X_Y, PART_Z_Y_X):
+        both_z(part, me, True)
+    for part in Z_X_Y_PARTS:
+        send(WAY_X, part, me, True)
     send(WAY_Y, PART_Z_Y_X, me, True)
     send(WAY_X, PART_Z_Y_X, me, True)
-    send(WAY_Y, PART_Z_X_Y, me, True)
-    keep = pltpu.make_async_copy(shard_ref, own_ref.at[me], sems.at[3])
-    keep.start()
+    for part in Z_X_Y_PARTS:
+        send(WAY_Y, part, me, True)
+    keeps = [
+        pltpu.make_async_copy(shard_ref, own_ref.at[me], sems.at[3]),
+        pltpu.make_async_copy(dec_shard_ref, dec_own.at[me], sems.at[6]),
+    ]
+    for keep in keeps:
+        keep.start()
     swap_pixels = pltpu.make_async_remote_copy(
         src_ref=tubes_ref.at[1 - half],
         dst_ref=pixels_ref,
@@ -1405,15 +1401,37 @@
         device_id_type=MESH_ID,
     )
     swap_pixels.start()
+    loads = [
+        pltpu.make_async_copy(tubes_ref.at[index], pix_held.at[clip], sems.at[7 + clip])
+        for clip, index in ((0, half), (1, 1 - half))
+    ]
+    for get in loads:
+        get.start()
     work(0)
     near = z * PLANE
     recv(PART_X_Y_Z, near + column_x)
     send(WAY_Y, PART_X_Y_Z, near + column_x)
-    recv(PART_Z_X_Y, near + column_x)
-    send(WAY_Y, PART_Z_X_Y, near + column_x)
+    for part in Z_X_Y_PARTS:
+        recv(part, near + column_x)
+        send(WAY_Y, part, near + column_x)
     recv(PART_Z_Y_X, near + column_y)
     send(WAY_X, PART_Z_Y_X, near + column_y)
-    keep.wait()
+    for keep in keeps:
+        keep.wait()
+    place_index = lax.broadcasted_iota(jnp.int32, (1, TUBES), 1)
+    for clip, index in ((0, half), (1, 1 - half)):
+        loads[clip].wait()
+        hot = jnp.where(order_ref[index] == place_index, 1.0, 0.0).astype(bf16)
+        picked_ref[clip] = nn(hot, pix_held[clip]).astype(bf16)
+    swap_picked = pltpu.make_async_remote_copy(
+        src_ref=picked_ref.at[1],
+        dst_ref=pix_other_ref,
+        send_sem=sems.at[9],
+        recv_sem=sems.at[10],
+        device_id={"tensor": 1 - half},
+        device_id_type=MESH_ID,
+    )
+    swap_picked.start()
     work(1)
     along(1)
     recv(PART_X_Y_Z, near + column_y)
@@ -1424,8 +1442,21 @@
     work(2)
     cross(1)
     finish(0)
+    pos_enc_ref[...] = sinusoid_of(order_ref[half].astype(f32), D)
     work(3)
     along(2)
+    first_place = lax.broadcasted_iota(jnp.int32, (TUBES // 32, 1), 0).astype(f32) * 32.0
+    second_place = lax.broadcasted_iota(jnp.int32, (32, 1), 0).astype(f32)
+    rate, even = rates(DD)
+    first = first_place * rate
+    second = second_place * rate
+    ahead = jnp.where(even, jnp.sin(first), jnp.cos(first))
+    turned = jnp.where(even, jnp.cos(first), -jnp.sin(first))
+    cos2, sin2 = jnp.cos(second), jnp.sin(second)
+    for index in range(TUBES // 32):
+        pos_dec_ref[pl.ds(32 * index, 32)] = (
+            ahead[index : index + 1] * cos2 + turned[index : index + 1] * sin2
+        )
     work(4)
     whole_plane(1)
     cross(2)
@@ -1441,7 +1472,36 @@
     dec_part_ref[...] = fold3(nt(split3(start_ref[:, D:]), dec_held[...]))
     whole_plane(3)
     finish(3)
+    for plane in range(planes):
+        pair(PART_DEC, plane).wait()
+    total = jnp.zeros((1, 128), f32)
+    per = joined.shape[1] // workers
+    for index in range(workers):
+        for group, ref in enumerate((dec_own, dec_other)):
+            block = ref[index].astype(f32)
+            joined[group, pl.ds(index * per, per)] = block[:per]
+            if group == 0:
+                total = total + block[per : per + 1, :128]
+    for group in range(2):
+
+        def matrix(at, size):
+            return joined[group, pl.ds(at, size)].astype(bf16)
+
+        wo_ref[pl.ds(group * DD // 2, DD // 2)] = matrix(DEC_O, DD // 2)
+        for kind in range(3):
+            wqkv_ref[pl.ds((2 * kind + group) * DD // 2, DD // 2)] = matrix(
+                DEC_Q + kind * DD // 2, DD // 2
+            )
+        for ref, at in ((wd_ref, DEC_D), (wu_ref, DEC_U), (wh_ref, DEC_H)):
+            ref[pl.ds(group * DFF // 2, DFF // 2)] = matrix(at, DFF // 2)
+        proj_ref[half if group == 0 else 1 - half] = matrix(0, D // 2)
+    counted = counted_ref[half]
+    scal_ref[0:1] = jnp.zeros((1, 128), f32) + counted
+    scal_ref[1:2] = counted * (2.0 * workers / PIX) / (MASKED * total)
+    scal_ref[2:3] = MASKED * total
+    scal_ref[3:8] = jnp.zeros((5, 128), f32)
     swap_pixels.wait()
+    swap_picked.wait()
     for plane in range(planes):
         for part in range(3):
             pair(part, plane).wait()
@@ -1450,19 +1510,20 @@
 
             @pl.when(column == index)
             def _():
-                for part in (PART_Z_X_Y, PART_Z_Y_X):
+                for part in (PART_DEC, PART_Z_X_Y, PART_Z_Y_X):
                     copy(WAY_X, part, slot).wait_send()
                     copy(WAY_Y, part, slot).wait_send()
 
             @pl.when(column_x == index)
             def _():
-                copy(WAY_Y, PART_Z_X_Y, slot).wait_send()
+                for part in Z_X_Y_PARTS:
+                    copy(WAY_Y, part, slot).wait_send()
 
             @pl.when(column_y == index)
             def _():
                 copy(WAY_X, PART_Z_Y_X, slot).wait_send()
 
-            for part in range(3):
+            for part in range(4):
                 sent = True if part == PART_X_Y_Z else column == index
 
                 @pl.when(up & (plane <= z) & sent)
@@ -1478,36 +1539,57 @@
     copy(WAY_Y, PART_X_Y_Z, near + column_x).wait_send()
 
 
-def gather_weights(planes, shard, tubes, error, dec_error, start):
+def gather_weights(planes, shard, dec_shard, tubes, error, dec_error, start, order, counted):
     workers = planes * PLANE
     size = shard.shape[0]
-    long = (size * 2 // 5 + 15) // 16 * 16
-    parts = ((0, long), (long, long), (2 * long, size - 2 * long))
+    same = dec_shard.shape[0] * DD // D
+    long = (size + same) * 2 // 5 // 16 * 16 + 16
+    parts = ((0, long - same), (long - same, long), (2 * long - same, size - 2 * long + same))
     shards = jax.ShapeDtypeStruct((workers,) + shard.shape, shard.dtype)
+    low = lambda *shape: jax.ShapeDtypeStruct(shape, bf16)
+    wide = lambda *shape: jax.ShapeDtypeStruct(shape, f32)
+    dec_shards = pltpu.VMEM((workers,) + dec_shard.shape, bf16)
     return pl.pallas_call(
         lambda *refs: gather_kernel(parts, planes, *refs),
-        in_specs=[any_spec()] * 4 + [vmem_spec()],
-        out_specs=[any_spec()] * 3 + [vmem_spec()] * 2,
+        in_specs=[any_spec()] * 5
+        + [vmem_spec()] * 2
+        + [pl.BlockSpec(memory_space=pltpu.SMEM)],
+        out_specs=[any_spec()] * 3 + [vmem_spec()] * 13,
         out_shape=[
             shards,
             shards,
             jax.ShapeDtypeStruct(tubes.shape[1:], tubes.dtype),
-            jax.ShapeDtypeStruct((RANK, error.shape[0]), f32),
-            jax.ShapeDtypeStruct((RANK, dec_error.shape[0]), f32),
+            wide(RANK, error.shape[0]),
+            wide(RANK, dec_error.shape[0]),
+            low(2, VIS, D),
+            low(VIS, D),
+            wide(VIS, D),
+            wide(TUBES, DD),
+            wide(8, 128),
+            low(2, D // 2, DD),
+            low(3 * DD, DD),
+            low(DD, DD),
+            low(DFF, DD),
+            low(DFF, DD),
+            low(PIX, DD),
         ],
         scratch_shapes=[
             pltpu.VMEM((2, ERROR_ROWS, D), bf16),
             pltpu.VMEM(dec_error.shape, bf16),
-            pltpu.SemaphoreType.DMA((4, 3, workers)),
-            pltpu.SemaphoreType.DMA((3, workers)),
-            pltpu.SemaphoreType.DMA((2, 3, planes)),
-            pltpu.SemaphoreType.DMA((6,)),
+            dec_shards,
+            dec_shards,
+            pltpu.VMEM((2, DEC_ROWS, DD), f32),
+            pltpu.VMEM((2, TUBES, D), bf16),
+            pltpu.SemaphoreType.DMA((4, 4, workers)),
+            pltpu.SemaphoreType.DMA((4, workers)),
+            pltpu.SemaphoreType.DMA((2, 4, planes)),
+            pltpu.SemaphoreType.DMA((11,)),
         ],
         compiler_params=pltpu.CompilerParams(
             collective_id=3, has_side_effects=True, vmem_limit_bytes=BIG_VMEM
         ),
         name="gather_weights",
-    )(shard, tubes, error, dec_error, start)
+    )(shard, dec_shard, tubes, error, dec_error, start, order, counted)
 
 
 def cut(block, widths):
@@ -1547,44 +1629,23 @@
     counted_all = clip_mask.astype(f32)
     counted = mine(counted_all)
     enc_per = enc_weights.shape[1]
-    dec_per = dec_weights.shape[1] * DD // D
-    spare = -(enc_per + dec_per + 1) % 16 + 1
-    shard = jnp.concatenate(
+    dec_per = dec_weights.shape[1]
+    spare = -(dec_per + 1) % 16 + 1
+    shard = enc_weights[0].astype(bf16)
+    dec_shard = jnp.concatenate(
         [
-            enc_weights[0].astype(bf16),
-            dec_weights[0].astype(bf16).reshape(dec_per, D),
-            jnp.broadcast_to(jnp.sum(counted_all).astype(bf16), (spare, D)),
+            dec_weights[0].astype(bf16),
+            jnp.broadcast_to(jnp.sum(counted_all).astype(bf16), (spare, DD)),
         ],
         0,
     )
     start_own = factors[0]
-    picked = pick_visible(which, tube_order, tubes)
-    pix_vis = picked[0]
-    pix_vis_other = swap(picked[1])
-    if workers == 4 * PLANE:
-        per = enc_per
-        own, other, pixels, enc_error_part, dec_error_part = gather_weights(
-            workers // PLANE, shard, tubes, enc_error[0, 0], dec_error[0, 0], start_own
-        )
-        enc_own, enc_other = own, other
-    else:
-        own = lax.all_gather(shard, "dp", axis=0)
-        other = swap(own)
-        pixels = swap(lax.dynamic_index_in_dim(tubes, 1 - half, 0, keepdims=False))
-        per = enc_per * workers
-        enc_own, enc_other = (shards[:, :enc_per].reshape(1, per, D) for shards in (own, other))
-        enc_error_part = error_factor(start_own[:, :D], enc_error[0, 0])
-        dec_error_part = error_factor(start_own[:, D:], dec_error[0, 0])
-    dec_own, dec_other = (
-        shards[:, enc_per : enc_per + dec_per].reshape(DEC_ROWS, DD) for shards in (own, other)
-    )
-    loss_weight = MASKED * jnp.sum(own[:, enc_per + dec_per, 0].astype(f32))
-
-    split_own = vec_split[0]
-    split2 = jnp.stack([split_own, swap(split_own)])
+    start_other = swap(start_own)
+    starts = (start_own, start_other)
+    splits = (vec_split, swap(vec_split))
     dec_at = 2 * (2 * HALF + HALF_FF)
     bq, bv, bu, bh = (
-        split2[:, at : at + size].reshape(1, 2 * size)
+        jnp.concatenate([split[:, at : at + size] for split in splits], 1)
         for at, size in (
             (dec_at, DD // 2),
             (dec_at + DD // 2, DD // 2),
@@ -1592,57 +1653,82 @@
             (dec_at + DD + DFF // 2, PIX // 2),
         )
     )
+    bqkv = jnp.concatenate([bq, jnp.zeros_like(bq), bv], 1)
     wide = vec_shared[: 15 * D].reshape(15, D)
     narrow = vec_shared[15 * D :].reshape(9, DD)
-    dec_widths = [D // 2, DD // 2, DFF // 2, 3 * DD // 2, DFF // 2, PIX // 2]
-    own_parts = cut(dec_own, dec_widths)
-    other_parts = cut(dec_other, dec_widths)
-    proj = jnp.where(
-        half == 0,
-        jnp.concatenate([own_parts[0], other_parts[0]], 0),
-        jnp.concatenate([other_parts[0], own_parts[0]], 0),
-    )
-    d_out, d_down, d_up, head_rows = (
-        jnp.concatenate([own_parts[index], other_parts[index]], 0) for index in (1, 2, 4, 5)
-    )
-    kinds = lambda block: block.reshape(3, DD // 2, DD)
-    d_qkv = jnp.concatenate([kinds(own_parts[3]), kinds(other_parts[3])], 1).reshape(3 * DD, DD)
-
-    visible = mine(tube_order)[:VIS]
-    pos_enc = sinusoid_at(visible, D)
-    pos_dec = sinusoid_table(DD)
-    start_other = swap(start_own)
-    enc_starts = jnp.stack([start_own[:, :D], start_other[:, :D]])
-    dec_starts = jnp.stack([start_own[:, D:], start_other[:, D:]])
+    visible = mine(tube_order)[None, :VIS]
+    if workers == 4 * PLANE:
+        per = enc_per
+        (
+            enc_own, enc_other, pixels, enc_error_part, dec_error_part, picked, pix_vis_other,
+            pos_enc, pos_dec, scal, proj, d_qkv, d_out, d_down, d_up, head_rows,
+        ) = gather_weights(
+            workers // PLANE, shard, dec_shard, tubes, enc_error[0, 0], dec_error[0, 0], start_own,
+            tube_order[:, :VIS, None], counted_all,
+        )
+        proj = proj.reshape(D, DD)
+        loss_weight = scal[2, 0]
+    else:
+        picked = pick_visible(which, tube_order, tubes)
+        pix_vis_other = swap(picked[1])
+        own = lax.all_gather(shard, "dp", axis=0)
+        dec_all = lax.all_gather(dec_shard, "dp", axis=0)
+        pixels = swap(lax.dynamic_index_in_dim(tubes, 1 - half, 0, keepdims=False))
+        per = enc_per * workers
+        enc_own = own.reshape(1, per, D)
+        enc_other = swap(enc_own)
+        enc_error_part = error_factor(start_own[:, :D], enc_error[0, 0])
+        dec_error_part = error_factor(start_own[:, D:], dec_error[0, 0])
+        dec_own = dec_all[:, :dec_per].reshape(DEC_ROWS, DD)
+        dec_other = swap(dec_own)
+        loss_weight = MASKED * jnp.sum(dec_all[:, dec_per, 0].astype(f32))
+        dec_widths = [D // 2, DD // 2, DFF // 2, 3 * DD // 2, DFF // 2, PIX // 2]
+        own_parts = cut(dec_own, dec_widths)
+        other_parts = cut(dec_other, dec_widths)
+        proj = jnp.where(
+            half == 0,
+            jnp.concatenate([own_parts[0], other_parts[0]], 0),
+            jnp.concatenate([other_parts[0], own_parts[0]], 0),
+        )
+        d_out, d_down, d_up, head_rows = (
+            jnp.concatenate([own_parts[index], other_parts[index]], 0) for index in (1, 2, 4, 5)
+        )
+        kinds = lambda block: block.reshape(3, DD // 2, DD)
+        d_qkv = jnp.concatenate([kinds(own_parts[3]), kinds(other_parts[3])], 1)
+        d_qkv = d_qkv.reshape(3 * DD, DD)
+        pos_enc = sinusoid_of(visible.reshape(VIS, 1).astype(f32), D)
+        pos_dec = sinusoid_of(jnp.arange(TUBES).astype(f32)[:, None], DD)
+        scal = jnp.broadcast_to(
+            jnp.stack([counted, 2.0 * workers / (PIX * loss_weight) * counted] + [counted] * 6)[
+                :, None
+            ],
+            (8, 128),
+        )
+    pix_vis = picked[0]
 
     stream0, *kept0 = encoder_layer(
-        0, per, (pix_vis, pix_vis_other, pos_enc), wide, split2, enc_own, enc_other
+        0, per, (pix_vis, pix_vis_other, pos_enc), wide, splits, enc_own, enc_other
     )
     stream1 = kept0[0]
     enc_normed, latent, *kept1 = encoder_layer(
-        1, per, (stream1, proj), wide, split2, enc_own, enc_other
+        1, per, (stream1, proj), wide, splits, enc_own, enc_other
     )
     kept = [(stream0, kept0), (stream1, kept1)]
 
     dec_start, h, qkv, hidden = decoder_qkv(
-        visible[None], pos_dec, latent, narrow, d_qkv,
-        jnp.concatenate([bq, jnp.zeros_like(bq), bv], 1),
+        visible, pos_dec, latent, narrow, d_qkv, bqkv
     )
     mixed, logs = attend(qkv)
-    scal = jnp.broadcast_to(
-        jnp.stack([counted, 2.0 * workers / (PIX * loss_weight) * counted] + [counted] * 6)[:, None],
-        (8, 128),
-    )
     grad_mixed, grad_middle, dec_grads, dec_sent, g_vec, g_bu, g_bh, loss_lanes = decoder_tokens(
         which, mixed, dec_start, tubes, pixels, hidden, scal, narrow, bu, bh, d_out, d_down, d_up,
         head_rows,
     )
     dq, dk, dv = attend_back(qkv, mixed, grad_mixed, logs)
     latent_low, dec_grads, dec_sent, g_vec1 = decoder_qkv_back(
-        which, visible[None], dq, dk, dv, h, dec_start, grad_middle, narrow, d_qkv, enc_normed,
+        which, visible, dq, dk, dv, h, dec_start, grad_middle, narrow, d_qkv, enc_normed,
         dec_grads, dec_sent,
     )
-    dec_left = dec_left_factor(dec_starts, dec_grads, dec_sent)
+    dec_left = dec_left_factor(starts, dec_grads, dec_sent)
     dec_came = swap(dec_sent)
 
     grad = latent_low
@@ -1653,7 +1739,7 @@
     for layer in (1, 0):
         source, result = kept[layer]
         grad, packs[layer], sent, enc_lefts[layer], *enc_vec_grads[layer] = encoder_layer_back(
-            layer, per, grad, source, wide, result, enc_starts, enc_own, enc_other,
+            layer, per, grad, source, wide, result, starts, enc_own, enc_other,
             (pix_vis, pix_vis_other), (result[0], proj) if layer == 1 else (),
         )
         came[layer] = swap(sent)
@@ -1687,7 +1773,7 @@
         + [g_vec1[4], g_vec1[2], g_vec1[3], g_vec[:6].reshape(-1)]
     )
     loss_part = jnp.sum(loss_lanes) / PIX
-    split_len = split_own.shape[0]
+    split_len = vec_split.shape[1]
     length = split_len + shared_grad.shape[0] + 1
     vec_lanes = pl.cdiv(length, RANK * 128) * 128
     fill = jnp.zeros((RANK * vec_lanes - length,), f32)

time: 600 us -> 533 us (0.89); the launches traced: 597 us -> 523 us
  Pallas kernels: 516 us -> 477 us
  other arithmetic: 28.2 us -> 11 us
  local copies, waits for them, and re-layouts: 35.5 us -> 20 us
    pallas_call x3 -> x2, Pallas kernels: 90.4 us -> 72.8 us  [the longest x1 43.8 us: attend_back(): pl.pallas_call(attend_back_kernel, grid=(PAIRS,), in_specs=[pair(0), pair...]
    pallas_call x1, Pallas kernels: 65 us -> 51.4 us  [decoder_tokens(): pl.pallas_call(token_kernel, grid_spec=pltpu.PrefetchScalarGridSpec(num_s...]
    pallas_call x2, Pallas kernels: 39.3 us -> 26.9 us  [encoder_layer(): pl.pallas_call(lambda *refs: encoder_kernel(layer, per, *refs), in_specs=...]
    concatenate x6 -> x1, other arithmetic: 7.41 us -> 0.61 us  [per_device(): jnp.concatenate([split[:, at:at + size] for split in splits], 1)]
  transfers between devices with their start and end apart: 7 -> 6, of which waited for: 1 -> 1; matrix products, arithmetic and copies ran while one was open for 9% -> 4% of each run, Pallas kernels for 41% -> 48%
where the time goes in v4:
time: 533 us; the launch traced here: 523 us
  Pallas kernels  477 us (89%)
  local copies, waits for them, and re-layouts  20 us (4%)
  other arithmetic  11 us (2%)
    pallas_call x1, Pallas kernels, gather_weights(): pl.pallas_call(lambda *refs: gather_kernel(parts, planes, *refs), in_spec...  151 us
    pallas_call x1, Pallas kernels, decoder_tokens(): pl.pallas_call(token_kernel, grid_spec=pltpu.PrefetchScalarGridSpec(num_s...  51.4 us
    pallas_call x1, Pallas kernels, attend_back(): pl.pallas_call(attend_back_kernel, grid=(PAIRS,), in_specs=[pair(0), pair...  43.8 us
    pallas_call x2, Pallas kernels, encoder_layer_back(): pl.pallas_call(lambda *refs: encoder_back_kernel(layer, per, *refs), in_s...  40.9 us
    pallas_call x1, Pallas kernels, summed_basis(): pl.pallas_call(lambda *refs: basis_kernel(workers, lanes, enc_width, *ref...  29.4 us
    pallas_call x1, Pallas kernels, attend(): pl.pallas_call(attend_kernel, grid=(PAIRS, TUBES // TUBES), in_specs=[pl....  29 us
    pallas_call x2, Pallas kernels, encoder_layer(): pl.pallas_call(lambda *refs: encoder_kernel(layer, per, *refs), in_specs=...  26.9 us
    pallas_call x1, Pallas kernels, right_factor(): pl.pallas_call(right_factor_kernel, grid=(ENC_BLOCKS,), in_specs=[pl.Bloc...  21.8 us
  transfers between devices with their start and end apart: 6, of which 1 were waited for; matrix products, arithmetic and copies ran while one was open for 4% of the time, Pallas kernels for 48%

profile of v4, /device:TPU:0, one launch (start us, length us, event | category | flops | bytes accessed | tf_op | source)
XLA Modules:
  0.0 522.7 jit_solution(8109411903896144695)
XLA Ops:
  0.7 0.5 collective-permute-start
  1.2 1.3 convert_reduce_fusion
  2.4 1.2 convert_element_type.14.refs_7_
  3.6 0.8 fusion.9
  4.4 0.7 fusion.6
  5.1 2.6 bitcast_convert_fusion.refs_0_
  7.7 0.7 slice_bitcast_fusion.2
  8.4 0.8 copy.29.refs_6_
  9.2 1.3 concatenate.24.refs_1_
  10.6 150.5 %gather_weights.1 = (bf16[16,624,768]{2,1,0:T(8,128)(2,1)}, bf16[16,624,768]{2,1,0:T(8,128)(2,1)}, bf16[1568,768]{1,0:T(8,128)(2,1)}, f32[8,9984]{1,0:T(8,128)},...) custom-call(bf16[624,768]{1,0:T(8,128)(2,1)} %bitcast_convert_fusion, ...), custom_call_target="tpu_custom_call" | custom-call | tf_op jit(solution)/shard_map/gather_weights/pallas_call | solution.py:1552
  161.1 1.9 slice_bitcast_fusion
  163.0 1.3 constant_dynamic-slice_fusion.order_ref
  164.3 0.6 reshape.86.refs_3_.refs_2_
  164.9 0.6 slice.232.vec_ref
  165.5 0.1 fusion.8
  165.6 0.7 concatenate.25.bias_ref
  166.3 13.7 %encoder_0.1 = (f32[160,768]{1,0:T(8,128)}, f32[160,768]{1,0:T(8,128)}, bf16[160,768]{1,0:T(8,128)(2,1)}, bf16[160,2304]{1,0:T(8,128)(2,1)}, bf16[160,768]{1,0:T...) custom-call(bf16[160,768]{1,0:T(8,128)(2,1)} %get-tuple-element.189., ...), custom_call_target="tpu_custom_call" | custom-call | tf_op jit(solution)/shard_map/encoder_0/pallas_call | solution.py:643
  180.0 13.2 %encoder_1.1 = (bf16[160,768]{1,0:T(8,128)(2,1)}, f32[160,384]{1,0:T(8,128)}, f32[160,768]{1,0:T(8,128)}, bf16[160,768]{1,0:T(8,128)(2,1)}, bf16[160,2304]{1,0:T...) custom-call(f32[160,768]{1,0:T(8,128)} %get-tuple-element.95.refs_0_, ...), custom_call_target="tpu_custom_call" | custom-call | tf_op jit(solution)/shard_map/encoder_1/pallas_call | solution.py:643
  193.2 9.0 %decoder_qkv.1 = (f32[1568,384]{1,0:T(8,128)}, bf16[1568,384]{1,0:T(8,128)(2,1)}, bf16[1568,1152]{1,0:T(8,128)(2,1)}, f32[1568,1]{1,0:T(8,128)}) custom-call(s32[1,160]{1,0:T(1,128)} %constant_dynamic-slice_fusion.order_ref, f32[1568,384]{1,0:T(8,128)} %get-tuple-element.89.pos_ref, f32[160,384]{1,0:T(8,128)} %get-tuple-element.97.latent_ref, ...), custom_call_target="tpu_custom_call" | custom-call | tf_op jit(solution)/shard_map/decoder_qkv/pallas_call | solution.py:169
  202.2 29.0 %attend.1 = (f32[1568,384]{1,0:T(8,128)}, f32[3,1568,128]{2,1,0:T(8,128)}) custom-call(bf16[1568,1152]{1,0:T(8,128)(2,1)} %get-tuple-element.99.q_ref.k_ref.v_ref, bf16[1568,1152]{1,0:T(8,128)(2,1)} %get-tuple-element.99.q_ref.k_ref.v_ref, bf16[1568,1152]{1,0:T(8,128)(2,1)} %get-tuple-element.99.q_ref.k_ref.v_ref), custom_call_target="tpu_custom_call" | custom-call | tf_op jit(solution)/shard_map/attend/pallas_call | solution.py:217
  231.3 0.7 fusion.7
  232.0 0.6 pad_maximum_fusion
  232.6 51.4 %decoder_tokens.1 = (bf16[1568,384]{1,0:T(8,128)(2,1)}, f32[1568,384]{1,0:T(8,128)}, f32[3456,384]{1,0:T(8,128)}, f32[3456,384]{1,0:T(8,128)}, f32[8,384]{1,0:T(...) custom-call(s32[1]{0:T(128)} %bitcast._.half_ref, f32[1568,384]{1,0:T(8,128)} %get-tuple-element.100.a_ref.o_ref, ...), custom_call_target="tpu_custom_call" | custom-call | tf_op jit(solution)/shard_map/decoder_tokens/pallas_call | solution.py:379
  283.9 43.8 %attend_back.1 = (bf16[1568,384]{1,0:T(8,128)(2,1)}, bf16[1568,384]{1,0:T(8,128)(2,1)}, bf16[1568,384]{1,0:T(8,128)(2,1)}) custom-call(bf16[1568,1152]{1,0:T(8,128)(2,1)} %get-tuple-element.99.q_ref.k_ref.v_ref, bf16[1568,1152]{1,0:T(8,128)(2,1)} %get-tuple-element.99.q_ref.k_ref.v_ref, bf16[1568,1152]{1,0:T(8,128)(2,1)} %get-tuple-element.99.q_ref.k_ref.v_ref, ...), custom_call_target="tpu_custom_call" | custom-call | tf_op jit(solution)/shard_map/attend_back/pallas_call | solution.py:271
  327.7 12.1 %decoder_qkv_back.1 = (bf16[160,384]{1,0:T(8,128)(2,1)}, f32[3456,384]{1,0:T(8,128)}, f32[3456,384]{1,0:T(8,128)}, f32[8,384]{1,0:T(8,128)}) custom-call(s32[1]{0:T(128)} %bitcast._.half_ref, s32[1,160]{1,0:T(1,128)} %constant_dynamic-slice_fusion.order_ref, ...), custom_call_target="tpu_custom_call", output_to_operand_aliasing={{1}: (11, {}), {2}: (12, {})} | custom-call | tf_op jit(solution)/shard_map/decoder_qkv_back/pallas_call | solution.py:469
  339.8 0.4 collective-permute-start.4
  340.3 0.2 collective-permute-start.1
  340.4 4.3 collective-permute-done.1.refs_11_.start_other_ref
  344.7 0.6 copy-done.7
  345.3 20.3 %encoder_back_1.1 = (f32[160,768]{1,0:T(8,128)}, bf16[160,7680]{1,0:T(8,128)(2,1)}, bf16[160,7680]{1,0:T(8,128)(2,1)}, f32[2,8,4608]{2,1,0:T(8,128)}, f32[8,768]...) custom-call(bf16[160,384]{1,0:T(8,128)(2,1)} %get-tuple-element.119.refs_0_, ...), custom_call_target="tpu_custom_call" | custom-call | tf_op jit(solution)/shard_map/encoder_back_1/pallas_call | solution.py:791
  365.6 0.0 copy-start.9
  365.7 20.6 %encoder_back_0.1 = (f32[160,768]{1,0:T(8,128)}, bf16[160,8448]{1,0:T(8,128)(2,1)}, bf16[160,8448]{1,0:T(8,128)(2,1)}, f32[2,8,5376]{2,1,0:T(8,128)}, f32[8,768]...) custom-call(f32[160,768]{1,0:T(8,128)} %get-tuple-element.128.refs_0_, f32[160,768]{1,0:T(8,128)} %get-tuple-element.129.refs_1_, ...), custom_call_target="tpu_custom_call" | custom-call | tf_op jit(solution)/shard_map/encoder_back_0/pallas_call | solution.py:791
  386.4 0.2 collective-permute-start.2
  386.6 0.4 collective-permute-start.3
  387.0 1.2 slice.289
  388.2 0.1 reduce.20
  388.3 0.6 reduce_sum.19
  389.6 0.6 fusion.10
  390.2 0.7 reshape.88
  391.0 0.8 slice_reduce_fusion.11
  391.8 0.7 slice_reduce_fusion.1
  392.6 0.8 slice_reduce_fusion.6
  393.3 0.1 concatenate.29
  393.4 0.1 collective-permute-start.5
  393.6 0.1 multiply_reduce_fusion
  393.7 7.0 %dec_left_factor.1.refs_2_ = f32[2,8,3456]{2,1,0:T(8,128)} custom-call(f32[8,1152]{1,0:T(8,128)} %bitcast.60, f32[8,1152]{1,0:T(8,128)} %copy-done.7, f32[3456,384]{1,0:T(8,128)} %get-tuple-element.139.own_ref, f32[3456,384]{1,0:T(8,128)} %get-tuple-element.140.other_ref), custom_call_target="tpu_custom_call" | custom-call | tf_op jit(solution)/shard_map/dec_left_factor/pallas_call | solution.py:1024
  400.7 29.4 %summed_basis.1 = (f32[8,9984]{1,0:T(8,128)}, f32[8,3456]{1,0:T(8,128)}) custom-call(f32[2,8,5376]{2,1,0:T(8,128)} %get-tuple-element.137.refs_0_, f32[2,8,4608]{2,1,0:T(8,128)} %get-tuple-element.138.refs_1_, f32[2,8,3456]{2,1,0:T(8,128)} %dec_left_factor.1.refs_2_, f32[8,9984]{1,0:T(8,128)} %get-tuple-element.141.refs_3_, f32[8,3456]{1,0:T(8,128)} %get-tuple-element.142.refs_4_), custom_call_target="tpu_custom_call" | custom-call | tf_op jit(solution)/shard_map/summed_basis/pallas_call | solution.py:1142
  430.1 0.1 concatenate.28
  430.2 0.7 reshape.91.refs_2_
  430.9 1.5 copy-done
  432.4 21.8 %right_factor.1.refs_0_ = f32[8,768]{1,0:T(8,128)} custom-call(f32[8,9984]{1,0:T(8,128)} %get-tuple-element.143.basis_ref, bf16[9984,768]{1,0:T(8,128)(2,1)} %bitcast.47, bf16[160,768]{1,0:T(8,128)(2,1)} %get-tuple-element.189.refs_0_.refs_14_, bf16[160,8448]{1,0:T(8,128)(2,1)} %get-tuple-element.144.refs_1_.refs_2_.refs_3_.refs_4_, ...), custom_call_target="tpu_custom_call" | custom-call | tf_op jit(solution)/shard_map/right_factor/pallas_call | solution.py:897
  454.2 7.9 %dec_right_factor.1 = (f32[8,384]{1,0:T(8,128)}, f32[3456,384]{1,0:T(8,128)}) custom-call(f32[8,3456]{1,0:T(8,128)} %get-tuple-element.148.basis_ref, f32[3456,384]{1,0:T(8,128)} %get-tuple-element.139.own_ref, f32[3456,384]{1,0:T(8,128)} %collective-permute-done.4.came_ref, bf16[3456,384]{1,0:T(8,128)(2,1)} %bitcast.51), custom_call_target="tpu_custom_call" | custom-call | tf_op jit(solution)/shard_map/dec_right_factor/pallas_call | solution.py:977
  462.2 20.0 %mean_over_workers.1 = (f32[8,768]{1,0:T(8,128)}, f32[8,384]{1,0:T(8,128)}, f32[8,2816]{1,0:T(8,128)}) custom-call(f32[8,768]{1,0:T(8,128)} %right_factor.1.refs_0_, f32[8,384]{1,0:T(8,128)} %get-tuple-element.149.refs_1_, f32[8,2816]{1,0:T(8,128)} %reshape.91.refs_2_), custom_call_target="tpu_custom_call" | custom-call | tf_op jit(solution)/shard_map/mean_over_workers/pallas_call | solution.py:1188
  482.2 1.4 maximum_bitcast_fusion
  483.6 5.8 %dec_residue.1 = bf16[3456,384]{1,0:T(8,128)(2,1)} custom-call(f32[8,3456]{1,0:T(8,128)} %get-tuple-element.148.basis_ref, f32[8,384]{1,0:T(8,128)} %get-tuple-element.163.factor_ref, f32[3456,384]{1,0:T(8,128)} %get-tuple-element.164.comb_ref), custom_call_target="tpu_custom_call" | custom-call | tf_op jit(solution)/shard_map/dec_residue/pallas_call | solution.py:998
  489.5 1.3 convolution_add_fusion
  490.8 0.8 fusion.1
  491.6 2.8 bitcast_add_fusion
  494.4 1.9 fusion
  496.3 0.5 slice.296
  496.8 0.6 broadcast_in_dim.57
  497.4 0.6 broadcast_in_dim.58
  498.1 0.7 multiply_subtract_fusion
  499.4 21.7 %residue.1 = bf16[9984,768]{1,0:T(8,128)(2,1)} custom-call(f32[8,9984]{1,0:T(8,128)} %get-tuple-element.143.basis_ref, f32[8,768]{1,0:T(8,128)} %get-tuple-element.162.factor_ref, bf16[9984,768]{1,0:T(8,128)(2,1)} %bitcast.48, bf16[160,768]{1,0:T(8,128)(2,1)} %get-tuple-element.189.refs_0_.refs_14_, ...), custom_call_target="tpu_custom_call" | custom-call | tf_op jit(solution)/shard_map/residue/pallas_call | solution.py:943
  (70 shorter events, 0.3 us)
Async XLA Ops:
  0.6 7.0 %copy-start.5 = (f32[1,216,384]{2,1,0:T(8,128)S(1)}, f32[1,216,384]{2,1,0:T(8,128)}, u32[]{:S(2)}) copy-start(f32[1,216,384]{2,1,0:T(8,128)} %param.18) | copy-start | bytes 995332
  0.7 164.8 %collective-permute-start = (f32[1,6528]{1,0:T(1,128)}, f32[1,6528]{1,0:T(1,128)S(1)}, u32[]{:S(2)}, u32[]{:S(2)}) collective-permute-start(f32[1,6528]{1,0:T(1,128)} %refs_3_.1), channel_id=1, source_target_pairs={{0,1},{1,0},{2,3},{3,2},{4,5},{5,4},{6,7},{7,6},{8,9},{9,8},{10,11... | collective-permute-start | bytes 78344 | tf_op jit(solution)/shard_map/ppermute | solution.py:1605
  10.6 153.7 %copy-start.10 = (f32[14976]{0:T(1024)S(1)}, f32[14976]{0:T(1024)}, u32[]{:S(2)}) copy-start(f32[14976]{0:T(1024)} %param.20) | copy-start | bytes 179716
  10.6 153.7 %slice-start = ((f32[14976]{0:T(1024)}), f32[11520]{0:T(1024)S(1)}, s32[]{:S(2)}) async-start(f32[14976]{0:T(1024)} %param.20), calls=%async_computation | async-start | bytes 98304 | tf_op jit(solution)/shard_map/slice | solution.py:1657
  165.5 0.8 copy-start.12
  327.7 12.5 %copy-start.6 = (f32[1,8,1152]{2,1,0:T(8,128)S(1)}, f32[1,8,1152]{2,1,0:T(8,128)}, u32[]{:S(2)}) copy-start(f32[1,8,1152]{2,1,0:T(8,128)} %param.27) | copy-start | bytes 110596
  339.8 114.4 %collective-permute-start.4 = (f32[3456,384]{1,0:T(8,128)}, f32[3456,384]{1,0:T(8,128)}, u32[]{:S(2)}, u32[]{:S(2)}) collective-permute-start(f32[3456,384]{1,0:T(8,128)} %get-tuple-element.140.other_ref), channel_id=1, source_target_pairs={{0,1},{1,0},{2,3},{3,2},{4,5},{5,4},{6,7},{7,6},{8,9},{9,8},{10,11... | collective-permute-start | bytes 15925256 | tf_op jit(solution)/shard_map/ppermute | solution.py:1605
  340.3 4.4 collective-permute-start.1
  344.7 0.6 copy-start.7
  365.6 22.5 %copy-start.9 = (f32[1,6528]{1,0:T(1,128)S(1)}, f32[1,6528]{1,0:T(1,128)}, u32[]{:S(2)}) copy-start(f32[1,6528]{1,0:T(1,128)} %refs_3_.1) | copy-start | bytes 78340
  365.6 22.6 %copy-start.19 = (f32[8,384]{1,0:T(8,128)S(1)}, f32[8,384]{1,0:T(8,128)}, u32[]{:S(2)}) copy-start(f32[8,384]{1,0:T(8,128)} %get-tuple-element.159) | copy-start | bytes 36868
  365.7 22.6 %copy-start.24 = (f32[1,1536]{1,0:T(1,128)S(1)}, f32[1,1536]{1,0:T(1,128)}, u32[]{:S(2)}) copy-start(f32[1,1536]{1,0:T(1,128)} %get-tuple-element.160) | copy-start | bytes 18436
  365.7 23.9 %copy-start.22 = (f32[1,1536]{1,0:T(1,128)S(1)}, f32[1,1536]{1,0:T(1,128)}, u32[]{:S(2)}) copy-start(f32[1,1536]{1,0:T(1,128)} %get-tuple-element.156) | copy-start | bytes 18436
  365.7 23.9 %copy-start.21 = (f32[1,1536]{1,0:T(1,128)S(1)}, f32[1,1536]{1,0:T(1,128)}, u32[]{:S(2)}) copy-start(f32[1,1536]{1,0:T(1,128)} %get-tuple-element.155) | copy-start | bytes 18436
  365.7 23.9 %copy-start.20 = (f32[8,384]{1,0:T(8,128)S(1)}, f32[8,384]{1,0:T(8,128)}, u32[]{:S(2)}) copy-start(f32[8,384]{1,0:T(8,128)} %get-tuple-element.154) | copy-start | bytes 36868
  365.7 25.3 %copy-start.17 = (f32[8,768]{1,0:T(8,128)S(1)}, f32[8,768]{1,0:T(8,128)}, u32[]{:S(2)}) copy-start(f32[8,768]{1,0:T(8,128)} %get-tuple-element.158) | copy-start | bytes 73732
  365.7 26.0 %copy-start.23 = (f32[2,768]{1,0:T(2,128)S(1)}, f32[2,768]{1,0:T(2,128)}, u32[]{:S(2)}) copy-start(f32[2,768]{1,0:T(2,128)} %get-tuple-element.152) | copy-start | bytes 18436
  365.7 26.8 %copy-start.18 = (f32[1,3072]{1,0:T(1,128)S(1)}, f32[1,3072]{1,0:T(1,128)}, u32[]{:S(2)}) copy-start(f32[1,3072]{1,0:T(1,128)} %get-tuple-element.153) | copy-start | bytes 36868
  365.7 27.9 %copy-start.16 = (f32[1,6528]{1,0:T(1,128)S(1)}, f32[1,6528]{1,0:T(1,128)}, u32[]{:S(2)}) copy-start(f32[1,6528]{1,0:T(1,128)} %param.23) | copy-start | bytes 78340
  386.4 44.5 %collective-permute-start.2 = (bf16[160,8448]{1,0:T(8,128)(2,1)}, bf16[160,8448]{1,0:T(8,128)(2,1)S(1)}, u32[]{:S(2)}, u32[]{:S(2)}) collective-permute-start(bf16[160,8448]{1,0:T(8,128)(2,1)} %get-tuple-element.146), channel_id=1, source_target_pairs={{0,1},{1,0},{2,3},{3,2},{4,5},{5,4},{6,7},{7,6},{8,9},{9,8},{10,11... | collective-permute-start | bytes 8110088 | tf_op jit(solution)/shard_map/ppermute | solution.py:1605
  386.6 44.3 %collective-permute-start.3 = (bf16[160,7680]{1,0:T(8,128)(2,1)}, bf16[160,7680]{1,0:T(8,128)(2,1)}, u32[]{:S(2)}, u32[]{:S(2)}) collective-permute-start(bf16[160,7680]{1,0:T(8,128)(2,1)} %get-tuple-element.147), channel_id=1, source_target_pairs={{0,1},{1,0},{2,3},{3,2},{4,5},{5,4},{6,7},{7,6},{8,9},{9,8},{10,11... | collective-permute-start | bytes 7372808 | tf_op jit(solution)/shard_map/ppermute | solution.py:1605
  393.4 36.7 %collective-permute-start.5 = (f32[22528]{0:T(1024)S(1)}, f32[22528]{0:T(1024)S(1)}, u32[]{:S(2)}, u32[]{:S(2)}) collective-permute-start(f32[22528]{0:T(1024)S(1)} %concatenate.29), channel_id=1, source_target_pairs={{0,1},{1,0},{2,3},{3,2},{4,5},{5,4},{6,7},{7,6},{8,9},{9,8},{10,11... | collective-permute-start | bytes 270344 | tf_op jit(solution)/shard_map/ppermute | solution.py:1605
  393.7 36.4 %copy-start.25 = (f32[1,192]{1,0:T(1,128)S(1)}, f32[1,192]{1,0:T(1,128)}, u32[]{:S(2)}) copy-start(f32[1,192]{1,0:T(1,128)} %get-tuple-element.201) | copy-start | bytes 2308
  430.9 1.5 copy-start
  483.6 5.9 %copy-start.8 = (f32[1,216,384]{2,1,0:T(8,128)S(1)}, f32[1,216,384]{2,1,0:T(8,128)}, u32[]{:S(2)}) copy-start(f32[1,216,384]{2,1,0:T(8,128)} %param.22) | copy-start | bytes 995332
  483.6 5.9 %copy-start.13 = (f32[8,384]{1,0:T(8,128)S(1)}, f32[8,384]{1,0:T(8,128)}, u32[]{:S(2)}) copy-start(f32[8,384]{1,0:T(8,128)} %get-tuple-element.163.factor_ref) | copy-start | bytes 36868
  483.6 8.0 %copy-start.3 = (f32[1,624,768]{2,1,0:T(8,128)S(1)}, f32[1,624,768]{2,1,0:T(8,128)}, u32[]{:S(2)}) copy-start(f32[1,624,768]{2,1,0:T(8,128)} %param.21) | copy-start | bytes 5750788
  483.6 8.0 %copy-start.11 = (f32[8,768]{1,0:T(8,128)S(1)}, f32[8,768]{1,0:T(8,128)}, u32[]{:S(2)}) copy-start(f32[8,768]{1,0:T(8,128)} %get-tuple-element.162.factor_ref) | copy-start | bytes 73732
  490.8 3.6 copy-start.4
  490.8 3.6 copy-start.2
  494.4 1.9 copy-start.1
  494.4 1.9 copy-start.14
  494.4 3.7 copy-start.15

commit v5 on v4

--- a/solution.py
+++ b/solution.py
@@ -39,6 +39,14 @@
 
 def tn(left, right):
     return lax.dot_general(left, right, (((0,), (0,)), ((), ())), preferred_element_type=f32)
+
+
+def ahead(count, product):
+    value = product(0)
+    for index in range(count):
+        later = product(index + 1) if index + 1 < count else None
+        yield index, value
+        value = later
 
 
 def col_sum(value):
@@ -196,36 +204,43 @@
     return lax.broadcasted_iota(jnp.int32, (1, 128), 1) // HEAD_DIM == index
 
 
+ATTEND_ROWS = 784
+
+
 def attend_kernel(q_ref, k_ref, v_ref, o_ref, lse_ref):
-    q = q_ref[...]
     k = k_ref[...]
     v_one = jnp.concatenate([v_ref[...], jnp.ones((TUBES, 128), bf16)], 1)
+    turns = [(at, head) for at in range(0, TUBES, ATTEND_ROWS) for head in range(2)]
+
+    def scores_of(turn):
+        at, head = turn
+        q = q_ref[pl.ds(at, ATTEND_ROWS)]
+        return nt(jnp.where(half_lane(head), q, jnp.zeros_like(q)), k)
+
     mixed, logs = [], []
-    for head in range(2):
-        scores = nt(jnp.where(half_lane(head), q, jnp.zeros_like(q)), k)
+    scores = scores_of(turns[0])
+    for index, (at, head) in enumerate(turns):
+        later = scores_of(turns[index + 1]) if index + 1 < len(turns) else None
         top = jnp.max(scores, 1, keepdims=True)
         expo = jnp.exp2((scores - top) * (SCORE * LOG2E)).astype(bf16)
         both = nn(expo, v_one)
         total = both[:, 128:]
         mixed.append(both[:, :128] / total)
         logs.append(top * (SCORE * LOG2E) + jnp.log2(total))
-    o_ref[...] = jnp.where(half_lane(0), mixed[0], mixed[1])
-    lse_ref[0] = jnp.where(half_lane(0), logs[0], logs[1])
+        if head == 1:
+            rows = pl.ds(at, ATTEND_ROWS)
+            o_ref[rows] = jnp.where(half_lane(0), mixed[-2], mixed[-1])
+            lse_ref[0, rows] = jnp.where(half_lane(0), logs[-2], logs[-1])
+        scores = later
 
 
 def attend(qkv):
+    pair = lambda kind: pl.BlockSpec((TUBES, 128), lambda p: (0, kind * PAIRS + p))
     return pl.pallas_call(
         attend_kernel,
-        grid=(PAIRS, TUBES // TUBES),
-        in_specs=[
-            pl.BlockSpec((TUBES, 128), lambda p, i: (i, p)),
-            pl.BlockSpec((TUBES, 128), lambda p, i: (0, PAIRS + p)),
-            pl.BlockSpec((TUBES, 128), lambda p, i: (0, 2 * PAIRS + p)),
-        ],
-        out_specs=[
-            pl.BlockSpec((TUBES, 128), lambda p, i: (i, p)),
-            pl.BlockSpec((1, TUBES, 128), lambda p, i: (p, i, 0)),
-        ],
+        grid=(PAIRS,),
+        in_specs=[pair(0), pair(1), pair(2)],
+        out_specs=[pair(0), pl.BlockSpec((1, TUBES, 128), lambda p: (p, 0, 0))],
         out_shape=[
             jax.ShapeDtypeStruct((TUBES, DD), f32),
             jax.ShapeDtypeStruct((PAIRS, TUBES, 128), f32),
@@ -320,9 +335,10 @@
     h2 = (unit2 * g2 + b2).astype(bf16)
     out = x1 + bd
     active = []
-    for chunk in range(CHUNKS):
-        part = pl.ds(chunk * CHUNK, CHUNK)
-        value, slope_part = gelu_pair(nt(h2, wu_ref[part]) + bu_ref[:, part])
+    part_of = lambda chunk: pl.ds(chunk * CHUNK, CHUNK)
+    for chunk, before in ahead(CHUNKS, lambda chunk: nt(h2, wu_ref[part_of(chunk)])):
+        part = part_of(chunk)
+        value, slope_part = gelu_pair(before + bu_ref[:, part])
         slope[:, part] = slope_part
         active.append(value.astype(bf16))
         out = out + nn(active[-1], wd_ref[part])
@@ -339,10 +355,10 @@
     counted = hidden_ref[...] * scal_ref[0:1, 0:1]
     rate = hidden_ref[...] * scal_ref[1:2, 0:1]
     grad_final = jnp.zeros((TOKEN_ROWS, DD), f32)
-    for chunk in range(CHUNKS):
-        part = pl.ds(chunk * CHUNK, CHUNK)
+    for chunk, guess in ahead(CHUNKS, lambda chunk: nt(final, wh_ref[part_of(chunk)])):
+        part = part_of(chunk)
         target = (pixels[chunk] - center) * spread
-        miss = nt(final, wh_ref[part]) + bh_ref[:, part] - target
+        miss = guess + bh_ref[:, part] - target
         loss_ref[:, part] += col_sum(counted * miss * miss)
         grad_guess = (rate * miss).astype(bf16)
         gbh_ref[:, part] += col_sum(grad_guess.astype(f32))
@@ -351,10 +367,10 @@
     grad_out = norm_back(grad_final, gf, unit_f, rate_f)
     out_low = grad_out.astype(bf16)
     grad_h2 = jnp.zeros((TOKEN_ROWS, DD), f32)
-    for chunk in range(CHUNKS):
-        part = pl.ds(chunk * CHUNK, CHUNK)
+    for chunk, grad_active in ahead(CHUNKS, lambda chunk: nt(out_low, wd_ref[part_of(chunk)])):
+        part = part_of(chunk)
         grads[chunk // 2][pl.ds(DEC_D + (chunk % 2) * CHUNK, CHUNK)] += tn(active[chunk], out_low)
-        grad_before = (slope[:, part] * nt(out_low, wd_ref[part])).astype(bf16)
+        grad_before = (slope[:, part] * grad_active).astype(bf16)
         gbu_ref[:, part] += col_sum(grad_before.astype(f32))
         grads[chunk // 2][pl.ds(DEC_U + (chunk % 2) * CHUNK, CHUNK)] += tn(grad_before, h2)
         grad_h2 = grad_h2 + nn(grad_before, wu_ref[part])
@@ -610,9 +626,9 @@
     wait(3)
     out = x1 + bd
     for group in range(2):
-        for chunk in range(HALF_FF // CHUNK):
+        rows_of = lambda chunk: pl.ds(AT_U + chunk * CHUNK, CHUNK)
+        for chunk, before in ahead(HALF_FF // CHUNK, lambda chunk: nt(h2, held[group, rows_of(chunk)])):
             part = pl.ds(group * HALF_FF + chunk * CHUNK, CHUNK)
-            before = nt(h2, held[group, pl.ds(AT_U + chunk * CHUNK, CHUNK)])
             at = biases + 2 * HALF + chunk * CHUNK
             value, slope = gelu_pair(before + splits[group][:, at : at + CHUNK])
             slope_ref[:, part] = slope
@@ -804,52 +820,8 @@
     )(grad, source, vecs, h, qkv, a, x1, h2, u, slope, *starts, own, other, *pixels, *last)
 
 
-ROWS = 768
-HALF_ROWS = ROWS // 2
+HALF_ROWS = 384
 ENC_ROWS = D + 2 * LAYER_ROWS
-ENC_BLOCKS = ENC_ROWS // ROWS
-PER_LAYER = LAYER_ROWS // ROWS
-
-
-def kinds_of(inner):
-    first = jnp.where(inner < 1, 0, jnp.where(inner < 3, 1, jnp.where(inner < 4, 2, 3)))
-    first = jnp.where(inner == 2, 1, first)
-    second = jnp.where(inner < 2, 1, jnp.where(inner < 4, 2, 3))
-    return jnp.where(inner == 3, 2, first), second
-
-
-def pack_specs():
-    pixel = pl.BlockSpec((VIS, D), lambda j: (0, 0))
-    specs = []
-    for layer in range(2):
-        inner = lambda j, layer=layer: jnp.clip(j - 1 - layer * PER_LAYER, 0, PER_LAYER - 1)
-        at = RIGHT_AT // D
-        specs.append(pl.BlockSpec((VIS, ROWS), lambda j, inner=inner: (0, inner(j))))
-        for side in range(2):
-            specs.append(
-                pl.BlockSpec(
-                    (VIS, D), lambda j, inner=inner, side=side: (0, at + kinds_of(inner(j))[side])
-                )
-            )
-    embed = pl.BlockSpec((VIS, D), lambda j: (0, RIGHT_AT // D + 4))
-    return [pixel, embed] + specs
-
-
-def by_segment(refs, run):
-    step = pl.program_id(0)
-    count = len(refs) // 2
-    mine, theirs = refs[:count], refs[count:]
-
-    @pl.when(step == 0)
-    def _():
-        run((mine[0], theirs[0]), (mine[1], theirs[1]), (mine[1], theirs[1]))
-
-    for layer in range(2):
-        low = 1 + layer * PER_LAYER
-
-        @pl.when(jnp.logical_and(step >= low, step < low + PER_LAYER))
-        def _(at=2 + 3 * layer):
-            run(*((mine[at + index], theirs[at + index]) for index in range(3)))
 
 
 def error_factor_kernel(start_ref, error_ref, out_ref):
@@ -870,144 +842,17 @@
     )(start, error)
 
 
-def right_factor_kernel(basis_ref, error_ref, *refs):
-    out_ref = refs[-1]
-
-    @pl.when(pl.program_id(0) == 0)
-    def _():
-        out_ref[...] = jnp.zeros_like(out_ref)
-
-    basis = split3(basis_ref[...])
-    out_ref[...] += fold3(nn(basis, error_ref[...]))
-
-    def run(left, first, second):
-        total = jnp.zeros((3 * RANK, D), f32)
-        for clip in range(2):
-            for side, right in ((0, first), (1, second)):
-                lanes = pl.ds(side * HALF_ROWS, HALF_ROWS)
-                inner = fold3(nt(basis[:, side * HALF_ROWS : (side + 1) * HALF_ROWS],
-                                 left[clip][:, lanes]))
-                total = total + nn(split3(inner), right[clip][...])
-        out_ref[...] += fold3(total)
-
-    by_segment(refs[:-1], run)
-
-
-def right_factor(basis, error, mine, theirs):
-    return pl.pallas_call(
-        right_factor_kernel,
-        grid=(ENC_BLOCKS,),
-        in_specs=[
-            pl.BlockSpec((RANK, ROWS), lambda j: (0, j)),
-            pl.BlockSpec((ROWS, D), lambda j: (j, 0)),
-        ]
-        + pack_specs() * 2,
-        out_specs=whole((RANK, D)),
-        out_shape=jax.ShapeDtypeStruct((RANK, D), f32),
-        compiler_params=params(),
-        name="right_factor",
-    )(basis, error, *pack_args(mine), *pack_args(theirs))
-
-
-def pack_args(packs):
-    pixels, first, second = packs
-    return (pixels, first, first, first, first, second, second, second)
-
-
-def low_pairs(basis, factor):
-    basis3 = split3(basis)
-    factor3 = split3(factor)
+def low_left(basis3):
     high, middle = basis3[:RANK], basis3[RANK : 2 * RANK]
-    return (
-        jnp.concatenate([high, high, middle, jnp.zeros_like(high)], 0),
-        jnp.concatenate([factor3[: 2 * RANK], factor3[:RANK], jnp.zeros_like(factor3[:RANK])], 0),
-    )
-
-
-def residue_kernel(basis_ref, factor_ref, error_ref, *refs):
-    out_ref = refs[-1]
-    basis, factor = low_pairs(basis_ref[...], -factor_ref[...])
-
-    def run(left, first, second):
-        for side, right in ((0, first), (1, second)):
-            rows = pl.ds(side * HALF_ROWS, HALF_ROWS)
-            low = basis[:, side * HALF_ROWS : (side + 1) * HALF_ROWS]
-            lefts = jnp.concatenate([left[0][:, rows], left[1][:, rows], low], 0)
-            rights = jnp.concatenate([right[0][...], right[1][...], factor], 0)
-            out_ref[rows] = (tn(lefts, rights) + error_ref[rows].astype(f32)).astype(bf16)
-
-    by_segment(refs[:-1], run)
-
-
-def residue(basis, factor, error, mine, theirs):
-    return pl.pallas_call(
-        residue_kernel,
-        grid=(ENC_BLOCKS,),
-        in_specs=[
-            pl.BlockSpec((RANK, ROWS), lambda j: (0, j)),
-            whole((RANK, D)),
-            pl.BlockSpec((ROWS, D), lambda j: (j, 0)),
-        ]
-        + pack_specs() * 2,
-        out_specs=pl.BlockSpec((ROWS, D), lambda j: (j, 0)),
-        out_shape=jax.ShapeDtypeStruct((ENC_ROWS, D), bf16),
-        compiler_params=params(),
-        name="residue",
-    )(basis, factor, error, *pack_args(mine), *pack_args(theirs))
+    return jnp.concatenate([high, high, middle, jnp.zeros_like(high)], 0)
+
+
+def low_right(factor3):
+    high = factor3[:RANK]
+    return jnp.concatenate([factor3[: 2 * RANK], high, jnp.zeros_like(high)], 0)
 
 
 DEC_BLOCK = 1152
-
-
-def dec_right_kernel(basis_ref, own_ref, came_ref, error_ref, out_ref, comb_ref):
-    @pl.when(pl.program_id(0) == 0)
-    def _():
-        out_ref[...] = jnp.zeros_like(out_ref)
-
-    basis = split3(basis_ref[...])
-    comb = own_ref[...] + came_ref[...] + error_ref[...].astype(f32)
-    comb_ref[...] = comb
-    high = comb.astype(bf16)
-    rest = (comb - high.astype(f32)).astype(bf16)
-    out_ref[...] += fold3(nn(basis, high) + nn(basis, rest))
-
-
-def dec_right_factor(basis, own, came, error):
-    rows = pl.BlockSpec((DEC_BLOCK, DD), lambda j: (j, 0))
-    return pl.pallas_call(
-        dec_right_kernel,
-        grid=(DEC_ROWS // DEC_BLOCK,),
-        in_specs=[pl.BlockSpec((RANK, DEC_BLOCK), lambda j: (0, j)), rows, rows, rows],
-        out_specs=[whole((RANK, DD)), rows],
-        out_shape=[
-            jax.ShapeDtypeStruct((RANK, DD), f32),
-            jax.ShapeDtypeStruct((DEC_ROWS, DD), f32),
-        ],
-        compiler_params=params(),
-        name="dec_right_factor",
-    )(basis, own, came, error)
-
-
-def dec_residue_kernel(basis_ref, factor_ref, comb_ref, out_ref):
-    out_ref[...] = (
-        comb_ref[...] + tn(*low_pairs(basis_ref[...], -factor_ref[...]))
-    ).astype(bf16)
-
-
-def dec_residue(basis, factor, comb):
-    return pl.pallas_call(
-        dec_residue_kernel,
-        grid=(DEC_ROWS // DEC_BLOCK,),
-        in_specs=[
-            pl.BlockSpec((RANK, DEC_BLOCK), lambda j: (0, j)),
-            whole((RANK, DD)),
-            pl.BlockSpec((DEC_BLOCK, DD), lambda j: (j, 0)),
-        ],
-        out_specs=pl.BlockSpec((DEC_BLOCK, DD), lambda j: (j, 0)),
-        out_shape=jax.ShapeDtypeStruct((DEC_ROWS, DD), bf16),
-        compiler_params=params(),
-        name="dec_residue",
-    )(basis, factor, comb)
 
 
 def dec_left_kernel(start_ref, start_other_ref, own_ref, other_ref, out_ref):
@@ -1016,7 +861,7 @@
         grad = ref[...]
         high = grad.astype(bf16)
         rest = (grad - high.astype(f32)).astype(bf16)
-        out_ref[group] = fold3((nt(high, start) + nt(rest, start)).T)
+        out_ref[group] = fold3(nt(start, high) + nt(start, rest))
 
 
 def dec_left_factor(starts, own, other):
@@ -1046,7 +891,7 @@
     pl.semaphore_wait(barrier, workers - 1 + (partner is not None))
 
 
-def sum_workers(workers, me, lanes, local, slots, sums, sems):
+def sum_workers(workers, me, lanes, local, slots, sums, sems, work=lambda turn: None):
     def share(index):
         return pl.ds(pl.multiple_of(index * lanes, 128), lanes)
 
@@ -1067,36 +912,102 @@
         return copies
 
     copies = to_all(0, lambda peer: local.at[:, share(peer)], lambda distance: slots.at[distance])
+    work(0)
     total = local[:, share(me)]
     for distance, copy in enumerate(copies, 1):
         copy.wait_recv()
         total = total + slots[distance]
     sums[:, share(me)] = total
     more = to_all(1, lambda peer: sums.at[:, share(me)], lambda distance: sums.at[:, share(me)])
+    work(1)
     for copy in copies:
         copy.wait_send()
     for copy in more:
         copy.wait()
 
 
-def basis_kernel(
-    workers, lanes, enc_width, first_ref, second_ref, dec_ref, error_ref, dec_error_ref,
-    enc_out, dec_out,
-    send, came, local, slots, sums, sems, pair_sems,
+def orthonormal(left):
+    place = lax.broadcasted_iota(jnp.int32, (RANK, 1), 0)
+    gram = lax.dot_general(
+        left, left, (((1,), (1,)), ((), ())), precision=highest_precision,
+        preferred_element_type=f32,
+    )
+    for index in range(RANK):
+        scale = lax.rsqrt(gram[index : index + 1, index : index + 1])
+        column = gram[:, index : index + 1] * scale
+        below = jnp.where(place > index, column, 0.0)
+        pivot = left[index : index + 1] * scale
+        left = jnp.where(place == index, pivot, left - below * pivot)
+        gram = gram - below * (gram[index : index + 1] * scale)
+    return left
+
+
+def lanes_for(width, workers):
+    return pl.cdiv(width, 128 * workers) * 128
+
+
+RANGES = [(0, D)] + [
+    (D + layer * LAYER_ROWS + at, size)
+    for layer in range(2)
+    for at, size in ((AT_O, HALF), (AT_D, HALF_FF), (AT_Q, 3 * HALF), (AT_U, HALF_FF))
+]
+LOW = 4 * RANK
+LOADS = 2 * (3 + len(RANGES)) + 4 + 3
+ERROR_PARTS = 4
+
+
+def compress_kernel(
+    workers, lanes, vec_lanes,
+    first_ref, second_ref, dec_ref, error_part_ref, dec_error_part_ref, vec_ref,
+    error_ref, pix_ref, pack0_ref, pack1_ref, pix_came_ref, pack0_came_ref, pack1_came_ref,
+    dec_own_ref, dec_came_ref, dec_error_ref,
+    enc_basis, dec_basis, enc_factor, dec_factor, vec_out, turned_out, rights_out, comb_out,
+    send, came, local, slots, sums, local2, slots2, sums2, parts, dec_parts,
+    held, lefts, turned, rights, comb, dec_came, dec_held,
+    sems, sems2, pair_sems, load_sems, out_sems,
 ):
     me = lax.axis_index("dp")
     half = lax.axis_index("tensor")
     first = first_ref.shape[2]
-    second = second_ref.shape[2]
-    width = enc_width + dec_ref.shape[2]
-    spans = ((first_ref, 0, first), (second_ref, first, second), (dec_ref, enc_width, width - enc_width))
+    width = ENC_ROWS + DEC_ROWS
+    clips = ((pix_ref, pack0_ref, pack1_ref), (pix_came_ref, pack0_came_ref, pack1_came_ref))
+
+    left_loads, right_loads, error_loads, dec_loads = [], [], [], []
+
+    def load(group, source, target):
+        count = sum(len(loads) for loads in (left_loads, right_loads, error_loads, dec_loads))
+        copy = pltpu.make_async_copy(source, target, load_sems.at[count])
+        copy.start()
+        group.append(copy)
+
+    for clip, (pixels, pack0, pack1) in enumerate(clips):
+        load(left_loads, pixels, lefts.at[clip, :, pl.ds(0, D)])
+        for layer, pack in enumerate((pack0, pack1)):
+            target = lefts.at[clip, :, pl.ds(D + layer * LAYER_ROWS, LAYER_ROWS)]
+            load(left_loads, pack.at[:, pl.ds(0, LAYER_ROWS)], target)
+    size = ENC_ROWS // ERROR_PARTS
+    for index in range(ERROR_PARTS):
+        block = pl.ds(index * size, size)
+        load(error_loads, error_ref.at[block], held.at[block])
+    for clip, (_, pack0, pack1) in enumerate(clips):
+        rows = pl.ds(clip * VIS, VIS)
+        load(right_loads, pack0.at[:, pl.ds(RIGHT_AT + 4 * D, D)], rights.at[0, rows])
+        for layer, pack in enumerate((pack0, pack1)):
+            for kind in range(4):
+                target = rights.at[1 + 4 * layer + kind, rows]
+                load(right_loads, pack.at[:, pl.ds(RIGHT_AT + kind * D, D)], target)
+    load(dec_loads, dec_own_ref, comb)
+    load(dec_loads, dec_came_ref, dec_came)
+    load(dec_loads, dec_error_ref, dec_held)
+
+    spans = ((first_ref, 0, first), (second_ref, first, ENC_ROWS - first), (dec_ref, ENC_ROWS, DEC_ROWS))
     for ref, at, size in spans:
         send[:, at : at + size] = ref[1]
     if width < workers * lanes:
         tail = jnp.zeros((RANK, workers * lanes - width), f32)
         send[:, width:] = tail
     greet(workers, me, 1 - half)
-    copy = pltpu.make_async_remote_copy(
+    pair = pltpu.make_async_remote_copy(
         src_ref=send,
         dst_ref=came,
         send_sem=pair_sems.at[0],
@@ -1104,48 +1015,137 @@
         device_id={"tensor": 1 - half},
         device_id_type=MESH_ID,
     )
-    copy.start()
+    pair.start()
     for ref, at, size in spans[:2]:
-        local[:, at : at + size] = ref[0] + error_ref[:, at : at + size]
-    local[:, enc_width:width] = dec_ref[0] + dec_error_ref[...]
+        local[:, at : at + size] = ref[0] + error_part_ref[:, at : at + size]
+    local[:, ENC_ROWS:width] = dec_ref[0] + dec_error_part_ref[...]
     if width < workers * lanes:
         local[:, width:] = tail
-    copy.wait()
+    pair.wait()
     local[...] += came[...]
-    sum_workers(workers, me, lanes, local, slots, sums, sems)
-    place = lax.broadcasted_iota(jnp.int32, (RANK, 1), 0)
-    for at, out in ((0, enc_out), (enc_width, dec_out)):
-        left = sums[:, at : at + out.shape[1]]
-        gram = lax.dot_general(
-            left, left, (((1,), (1,)), ((), ())), precision=highest_precision,
-            preferred_element_type=f32,
-        )
-        for index in range(RANK):
-            scale = lax.rsqrt(gram[index : index + 1, index : index + 1])
-            column = gram[:, index : index + 1] * scale
-            below = jnp.where(place > index, column, 0.0)
-            pivot = left[index : index + 1] * scale
-            left = jnp.where(place == index, pivot, left - below * pivot)
-            gram = gram - below * (gram[index : index + 1] * scale)
-        out[...] = left
-
-
-def lanes_for(width, workers):
-    return pl.cdiv(width, 128 * workers) * 128
-
-
-def summed_basis(workers, first, second, dec, error_part, dec_error_part):
-    enc_width = first.shape[2] + second.shape[2]
-    width = enc_width + dec.shape[2]
-    lanes = lanes_for(width, workers)
+
+    blocks = ENC_ROWS // HALF_ROWS
+    dec_blocks = DEC_ROWS // HALF_ROWS
+
+    def rows_of(index):
+        return pl.ds(pl.multiple_of(index * HALF_ROWS, HALF_ROWS), HALF_ROWS)
+
+    def turn(index, _):
+        rows = rows_of(index)
+        both = jnp.concatenate([lefts[0, :, rows], lefts[1, :, rows]], 0)
+        turned[rows, 0 : 2 * VIS] = both.T
+        return 0
+
+    def combine(index, _):
+        rows = rows_of(index)
+        comb[rows] = comb[rows] + dec_came[rows] + dec_held[rows].astype(f32)
+        return 0
+
+    def meanwhile(phase):
+        if phase == 0:
+            for copy in left_loads:
+                copy.wait()
+            lax.fori_loop(0, blocks // 2, turn, 0)
+        else:
+            lax.fori_loop(blocks // 2, blocks, turn, 0)
+            for copy in dec_loads:
+                copy.wait()
+            lax.fori_loop(0, dec_blocks, combine, 0)
+
+    sum_workers(workers, me, lanes, local, slots, sums, sems, meanwhile)
+    enc = orthonormal(sums[:, :ENC_ROWS])
+    enc_basis[...] = enc
+    parts[...] = split3(enc)
+    dec = orthonormal(sums[:, ENC_ROWS:width])
+    dec_basis[...] = dec
+    dec_parts[...] = split3(dec)
+
+    for copy in error_loads + right_loads:
+        copy.wait()
+    wide_rows = 2 * HALF_ROWS
+
+    def add_error(index, total):
+        rows = pl.ds(pl.multiple_of(index * wide_rows, wide_rows), wide_rows)
+        return total + nn(parts[:, rows], held[rows])
+
+    total = lax.fori_loop(0, ENC_ROWS // wide_rows, add_error, jnp.zeros((3 * RANK, D), f32))
+    for index, (at, size) in enumerate(RANGES):
+        rows = pl.ds(at, size)
+        inner = fold3(nn(parts[:, rows], turned[rows, 0 : 2 * VIS]))
+        total = total + nn(split3(inner), rights[index, 0 : 2 * VIS])
+    local2[:, :D] = fold3(total)
+
+    def add_dec(index, total):
+        rows = rows_of(index)
+        block = comb[rows]
+        high = block.astype(bf16)
+        rest = (block - high.astype(f32)).astype(bf16)
+        return total + nn(dec_parts[:, rows], high) + nn(dec_parts[:, rows], rest)
+
+    local2[:, D : D + DD] = fold3(
+        lax.fori_loop(0, dec_blocks, add_dec, jnp.zeros((3 * RANK, DD), f32))
+    )
+    end = D + DD + vec_ref.shape[1]
+    local2[:, D + DD : end] = vec_ref[...]
+    if end < workers * vec_lanes:
+        local2[:, end:] = jnp.zeros((RANK, workers * vec_lanes - end), f32)
+
+    def turn_basis(index, _):
+        rows = rows_of(index)
+        turned[rows, 2 * VIS : 2 * VIS + LOW] = low_left(parts[:, rows]).T
+        return 0
+
+    comb_store = pltpu.make_async_copy(comb, comb_out, out_sems.at[0])
+    turned_store = pltpu.make_async_copy(turned, turned_out, out_sems.at[1])
+    right_store = pltpu.make_async_copy(
+        rights.at[:, pl.ds(0, 2 * VIS)], rights_out.at[:, pl.ds(0, 2 * VIS)], out_sems.at[2]
+    )
+    low_store = pltpu.make_async_copy(
+        rights.at[:, pl.ds(2 * VIS, LOW)], rights_out.at[:, pl.ds(2 * VIS, LOW)], out_sems.at[3]
+    )
+
+    def meanwhile2(phase):
+        if phase == 0:
+            comb_store.start()
+            right_store.start()
+            lax.fori_loop(0, blocks, turn_basis, 0)
+            turned_store.start()
+
+    sum_workers(workers, me, vec_lanes, local2, slots2, sums2, sems2, meanwhile2)
+    factor = sums2[:, :D] * (1.0 / workers)
+    enc_factor[...] = factor
+    low = low_right(split3(-factor))
+    for index in range(len(RANGES)):
+        rights[index, 2 * VIS :] = low
+    dec_mean = sums2[:, D : D + DD] * (1.0 / workers)
+    dec_factor[...] = dec_mean
+    low_store.start()
+    vec_out[...] = sums2[:, D + DD : end] * (1.0 / workers)
+    for copy in (comb_store, turned_store, right_store, low_store):
+        copy.wait()
+
+
+def compress(
+    workers, first, second, dec, error_part, dec_error_part, vec, error, mine, came, dec_own, dec_came,
+    dec_error,
+):
+    lanes = lanes_for(ENC_ROWS + DEC_ROWS, workers)
+    vec_lanes = lanes_for(D + DD + vec.shape[1], workers)
     wide = pltpu.VMEM((RANK, workers * lanes), f32)
+    wide2 = pltpu.VMEM((RANK, workers * vec_lanes), f32)
     return pl.pallas_call(
-        lambda *refs: basis_kernel(workers, lanes, enc_width, *refs),
-        in_specs=[vmem_spec()] * 5,
-        out_specs=[vmem_spec()] * 2,
+        lambda *refs: compress_kernel(workers, lanes, vec_lanes, *refs),
+        in_specs=[vmem_spec()] * 6 + [any_spec()] * 10,
+        out_specs=[vmem_spec()] * 5 + [any_spec()] * 3,
         out_shape=[
-            jax.ShapeDtypeStruct((RANK, enc_width), f32),
-            jax.ShapeDtypeStruct((RANK, width - enc_width), f32),
+            jax.ShapeDtypeStruct((RANK, ENC_ROWS), f32),
+            jax.ShapeDtypeStruct((RANK, DEC_ROWS), f32),
+            jax.ShapeDtypeStruct((RANK, D), f32),
+            jax.ShapeDtypeStruct((RANK, DD), f32),
+            jax.ShapeDtypeStruct(vec.shape, f32),
+            jax.ShapeDtypeStruct((ENC_ROWS, 2 * VIS + LOW), bf16),
+            jax.ShapeDtypeStruct((len(RANGES), 2 * VIS + LOW, D), bf16),
+            jax.ShapeDtypeStruct((DEC_ROWS, DD), f32),
         ],
         scratch_shapes=[
             wide,
@@ -1153,54 +1153,120 @@
             wide,
             pltpu.VMEM((workers, RANK, lanes), f32),
             wide,
+            wide2,
+            pltpu.VMEM((workers, RANK, vec_lanes), f32),
+            wide2,
+            pltpu.VMEM((3 * RANK, ENC_ROWS), bf16),
+            pltpu.VMEM((3 * RANK, DEC_ROWS), bf16),
+            pltpu.VMEM((ENC_ROWS, D), bf16),
+            pltpu.VMEM((2, VIS, ENC_ROWS), bf16),
+            pltpu.VMEM((ENC_ROWS, 2 * VIS + LOW), bf16),
+            pltpu.VMEM((len(RANGES), 2 * VIS + LOW, D), bf16),
+            pltpu.VMEM((DEC_ROWS, DD), f32),
+            pltpu.VMEM((DEC_ROWS, DD), f32),
+            pltpu.VMEM((DEC_ROWS, DD), bf16),
+            pltpu.SemaphoreType.DMA((4, workers)),
             pltpu.SemaphoreType.DMA((4, workers)),
             pltpu.SemaphoreType.DMA((2,)),
+            pltpu.SemaphoreType.DMA((LOADS,)),
+            pltpu.SemaphoreType.DMA((4,)),
         ],
         compiler_params=pltpu.CompilerParams(
-            collective_id=1, has_side_effects=True, vmem_limit_bytes=BIG_VMEM
+            collective_id=1, has_side_effects=True, vmem_limit_bytes=60 << 20
         ),
-        name="summed_basis",
-    )(first, second, dec, error_part, dec_error_part)
-
-
-def sum_kernel(workers, lanes, *refs):
-    count = (len(refs) - 4) // 2
-    parts, outs = refs[:count], refs[count : 2 * count]
-    local, slots, sums, sems = refs[2 * count :]
-    me = lax.axis_index("dp")
-    at = 0
-    for part in parts:
-        local[:, at : at + part.shape[1]] = part[...]
-        at += part.shape[1]
-    if at < workers * lanes:
-        local[:, at:] = jnp.zeros((RANK, workers * lanes - at), f32)
-    greet(workers, me, None)
-    sum_workers(workers, me, lanes, local, slots, sums, sems)
-    at = 0
-    for out in outs:
-        out[...] = sums[:, at : at + out.shape[1]] * (1.0 / workers)
-        at += out.shape[1]
-
-
-def mean_over_workers(workers, parts):
-    lanes = lanes_for(sum(part.shape[1] for part in parts), workers)
-    wide = pltpu.VMEM((RANK, workers * lanes), f32)
+        name="compress",
+    )(
+        first, second, dec, error_part, dec_error_part, vec, error, *mine, *came, dec_own, dec_came,
+        dec_error,
+    )
+
+
+def new_errors_kernel(
+    turned_ref, rights_ref, error_ref, comb_ref, basis_ref, factor_ref, out_ref, dec_out_ref,
+    turned, rights, held, comb, dec_held, in_sems, out_sems,
+):
+    blocks = ENC_ROWS // HALF_ROWS
+    dec_blocks = DEC_ROWS // HALF_ROWS
+
+    def rows_of(index):
+        start = index * HALF_ROWS
+        if not isinstance(index, int):
+            start = pl.multiple_of(start, HALF_ROWS)
+        return pl.ds(start, HALF_ROWS)
+
+    def loads(index):
+        rows = rows_of(index)
+        return (
+            pltpu.make_async_copy(error_ref.at[rows], held.at[rows], in_sems.at[0, index]),
+            pltpu.make_async_copy(turned_ref.at[rows], turned.at[rows], in_sems.at[1, index]),
+        )
+
+    def right_load(kind):
+        return pltpu.make_async_copy(rights_ref.at[kind], rights.at[kind], in_sems.at[2, kind])
+
+    def store(index):
+        rows = rows_of(index)
+        return pltpu.make_async_copy(held.at[rows], out_ref.at[rows], out_sems.at[index])
+
+    comb_load = pltpu.make_async_copy(comb_ref, comb, in_sems.at[2, len(RANGES)])
+    comb_load.start()
+    for kind, (at, size) in enumerate(RANGES):
+        right_load(kind).start()
+        for index in range(at // HALF_ROWS, (at + size) // HALF_ROWS):
+            for copy in loads(index):
+                copy.start()
+    comb_load.wait()
+    dec_right = low_right(split3(-factor_ref[...]))
+
+    def dec_residue(index, _):
+        rows = rows_of(index)
+        left = low_left(split3(basis_ref[:, rows]))
+        dec_held[rows] = (comb[rows] + tn(left, dec_right)).astype(bf16)
+        return 0
+
+    lax.fori_loop(0, dec_blocks, dec_residue, 0)
+    dec_store = pltpu.make_async_copy(dec_held, dec_out_ref, out_sems.at[blocks])
+    dec_store.start()
+    for kind, (at, size) in enumerate(RANGES):
+        right_load(kind).wait()
+
+        def residue(index, _, kind=kind):
+            for copy in loads(index):
+                copy.wait()
+            rows = rows_of(index)
+            value = nn(turned[rows], rights[kind]) + held[rows].astype(f32)
+            held[rows] = value.astype(bf16)
+            store(index).start()
+            return 0
+
+        lax.fori_loop(at // HALF_ROWS, (at + size) // HALF_ROWS, residue, 0)
+    for index in range(blocks):
+        store(index).wait()
+    dec_store.wait()
+
+
+def new_errors(turned, rights, error, dec_basis, dec_factor, comb):
+    blocks = ENC_ROWS // HALF_ROWS
     return pl.pallas_call(
-        lambda *refs: sum_kernel(workers, lanes, *refs),
-        in_specs=[vmem_spec()] * len(parts),
-        out_specs=[vmem_spec()] * len(parts),
-        out_shape=[jax.ShapeDtypeStruct(part.shape, f32) for part in parts],
+        new_errors_kernel,
+        in_specs=[any_spec()] * 4 + [vmem_spec()] * 2,
+        out_specs=[any_spec()] * 2,
+        out_shape=[
+            jax.ShapeDtypeStruct((ENC_ROWS, D), bf16),
+            jax.ShapeDtypeStruct((DEC_ROWS, DD), bf16),
+        ],
         scratch_shapes=[
-            wide,
-            pltpu.VMEM((workers, RANK, lanes), f32),
-            wide,
-            pltpu.SemaphoreType.DMA((4, workers)),
+            pltpu.VMEM(turned.shape, bf16),
+            pltpu.VMEM(rights.shape, bf16),
+            pltpu.VMEM(error.shape, bf16),
+            pltpu.VMEM(comb.shape, f32),
+            pltpu.VMEM(comb.shape, bf16),
+            pltpu.SemaphoreType.DMA((3, blocks)),
+            pltpu.SemaphoreType.DMA((blocks + 1,)),
         ],
-        compiler_params=pltpu.CompilerParams(
-            collective_id=2, has_side_effects=True, vmem_limit_bytes=BIG_VMEM
-        ),
-        name="mean_over_workers",
-    )(*parts)
+        compiler_params=params(),
+        name="new_errors",
+    )(turned, rights, error, comb, dec_basis, dec_factor)
 
 
 PLANE = 4
@@ -1746,10 +1812,6 @@
     mine_packs = (pix_vis, packs[0], packs[1])
     their_packs = (picked[1], came[0], came[1])
 
-    enc_basis, dec_basis = summed_basis(
-        workers, enc_lefts[0], enc_lefts[1], dec_left, enc_error_part, dec_error_part
-    )
-
     def split_half(index):
         pieces = []
         for layer in range(2):
@@ -1781,22 +1843,18 @@
     local = jnp.concatenate([split_half(0), shared_grad, loss_part[None], fill])
     vec_local = (local + swap(sent)).reshape(RANK, vec_lanes)
 
+    enc_basis, dec_basis, enc_right, dec_right, vec_mean, turned, rights, dec_comb = compress(
+        workers, enc_lefts[0], enc_lefts[1], dec_left, enc_error_part, dec_error_part, vec_local,
+        enc_error[0, 0], mine_packs, their_packs, dec_grads, dec_came, dec_error[0, 0],
+    )
+    enc_error_new, dec_error_new = new_errors(
+        turned, rights, enc_error[0, 0], dec_basis, dec_right, dec_comb
+    )
+    vec_mean = vec_mean.reshape(-1)
     enc_rows = enc_basis.shape[1] // workers
     dec_rows = dec_basis.shape[1] // workers
     enc_owned = lax.dynamic_slice_in_dim(enc_basis, worker_index * enc_rows, enc_rows, 1)
     dec_owned = lax.dynamic_slice_in_dim(dec_basis, worker_index * dec_rows, dec_rows, 1)
-    dec_right_part, dec_comb = dec_right_factor(dec_basis, dec_grads, dec_came, dec_error[0, 0])
-    enc_right, dec_right, vec_mean = mean_over_workers(
-        workers,
-        (
-            right_factor(enc_basis, enc_error[0, 0], mine_packs, their_packs),
-            dec_right_part,
-            vec_local,
-        ),
-    )
-    vec_mean = vec_mean.reshape(-1)
-    enc_error_new = residue(enc_basis, enc_right, enc_error[0, 0], mine_packs, their_packs)
-    dec_error_new = dec_residue(dec_basis, dec_right, dec_comb)
     enc_mom = momentum_keep * enc_moment[0] + jnp.einsum(
         "rx,rc->xc", enc_owned, enc_right, precision=highest_precision
     )

time: 533 us -> 494 us (0.927)
  Pallas kernels: 477 us -> 438 us
    pallas_call x7 -> x3, Pallas kernels: 136 us -> 96.7 us  [the longest x1 54.9 us: compress(): pl.pallas_call(lambda *refs: compress_kernel(workers, lanes, vec_lanes, *...]
  transfers between devices with their start and end apart: 6 -> 6, of which waited for: 1 -> 1; matrix products, arithmetic and copies ran while one was open for 4% -> 4% of each run, Pallas kernels for 48% -> 41%
where the time goes in v5:
time: 494 us; the launch traced here: 485 us
  Pallas kernels  438 us (89%)
  local copies, waits for them, and re-layouts  20.6 us (4%)
  other arithmetic  11 us (2%)
    pallas_call x1, Pallas kernels, gather_weights(): pl.pallas_call(lambda *refs: gather_kernel(parts, planes, *refs), in_spec...  150 us
    pallas_call x1, Pallas kernels, compress(): pl.pallas_call(lambda *refs: compress_kernel(workers, lanes, vec_lanes, *...  54.9 us
    pallas_call x1, Pallas kernels, decoder_tokens(): pl.pallas_call(token_kernel, grid_spec=pltpu.PrefetchScalarGridSpec(num_s...  50.8 us
    pallas_call x1, Pallas kernels, attend_back(): pl.pallas_call(attend_back_kernel, grid=(PAIRS,), in_specs=[pair(0), pair...  43.8 us
    pallas_call x2, Pallas kernels, encoder_layer_back(): pl.pallas_call(lambda *refs: encoder_back_kernel(layer, per, *refs), in_s...  40.9 us
    pallas_call x2, Pallas kernels, encoder_layer(): pl.pallas_call(lambda *refs: encoder_kernel(layer, per, *refs), in_specs=...  26.9 us
    pallas_call x1, Pallas kernels, attend(): pl.pallas_call(attend_kernel, grid=(PAIRS,), in_specs=[pair(0), pair(1),...  21.9 us
    pallas_call x1, Pallas kernels, new_errors(): pl.pallas_call(new_errors_kernel, in_specs=[any_spec()] * 4 + [vmem_spec(...  19.9 us
  transfers between devices with their start and end apart: 6, of which 1 were waited for; matrix products, arithmetic and copies ran while one was open for 4% of the time, Pallas kernels for 41%

profile of v5, /device:TPU:0, one launch (start us, length us, event | category | flops | bytes accessed | tf_op | source)
XLA Modules:
  0.0 484.5 jit_solution(17410124620124735426)
XLA Ops:
  0.7 0.5 collective-permute-start
  1.2 1.3 convert_reduce_fusion
  2.4 1.2 convert_element_type.14.refs_7_
  3.6 0.8 fusion.9
  4.4 0.7 fusion.6
  5.1 2.6 bitcast_convert_fusion.refs_0_
  7.7 0.7 slice_bitcast_fusion.2
  8.4 0.8 copy.29.refs_6_
  9.2 1.3 concatenate.24.refs_1_
  10.6 150.5 %gather_weights.1 = (bf16[16,624,768]{2,1,0:T(8,128)(2,1)}, bf16[16,624,768]{2,1,0:T(8,128)(2,1)}, bf16[1568,768]{1,0:T(8,128)(2,1)}, f32[8,9984]{1,0:T(8,128)},...) custom-call(bf16[624,768]{1,0:T(8,128)(2,1)} %bitcast_convert_fusion, ...), custom_call_target="tpu_custom_call" | custom-call | tf_op jit(solution)/shard_map/gather_weights/pallas_call | solution.py:1618
  161.1 1.9 slice_bitcast_fusion
  162.9 1.3 constant_dynamic-slice_fusion.order_ref
  164.2 0.6 reshape.86.refs_3_.refs_2_
  164.8 0.6 slice.232.vec_ref
  165.4 0.1 fusion.8
  165.5 0.7 concatenate.25.bias_ref
  166.2 13.6 %encoder_0.1 = (f32[160,768]{1,0:T(8,128)}, f32[160,768]{1,0:T(8,128)}, bf16[160,768]{1,0:T(8,128)(2,1)}, bf16[160,2304]{1,0:T(8,128)(2,1)}, bf16[160,768]{1,0:T...) custom-call(bf16[160,768]{1,0:T(8,128)(2,1)} %get-tuple-element.195., ...), custom_call_target="tpu_custom_call" | custom-call | tf_op jit(solution)/shard_map/encoder_0/pallas_call | solution.py:659
  179.9 13.2 %encoder_1.1 = (bf16[160,768]{1,0:T(8,128)(2,1)}, f32[160,384]{1,0:T(8,128)}, f32[160,768]{1,0:T(8,128)}, bf16[160,768]{1,0:T(8,128)(2,1)}, bf16[160,2304]{1,0:T...) custom-call(f32[160,768]{1,0:T(8,128)} %get-tuple-element.98.refs_0_, ...), custom_call_target="tpu_custom_call" | custom-call | tf_op jit(solution)/shard_map/encoder_1/pallas_call | solution.py:659
  193.1 9.0 %decoder_qkv.1 = (f32[1568,384]{1,0:T(8,128)}, bf16[1568,384]{1,0:T(8,128)(2,1)}, bf16[1568,1152]{1,0:T(8,128)(2,1)}, f32[1568,1]{1,0:T(8,128)}) custom-call(s32[1,160]{1,0:T(1,128)} %constant_dynamic-slice_fusion.order_ref, f32[1568,384]{1,0:T(8,128)} %get-tuple-element.92.pos_ref, f32[160,384]{1,0:T(8,128)} %get-tuple-element.100.latent_ref, ...), custom_call_target="tpu_custom_call" | custom-call | tf_op jit(solution)/shard_map/decoder_qkv/pallas_call | solution.py:177
  202.1 21.9 %attend.1 = (f32[1568,384]{1,0:T(8,128)}, f32[3,1568,128]{2,1,0:T(8,128)}) custom-call(bf16[1568,1152]{1,0:T(8,128)(2,1)} %get-tuple-element.102.q_ref.k_ref.v_ref, bf16[1568,1152]{1,0:T(8,128)(2,1)} %get-tuple-element.102.q_ref.k_ref.v_ref, bf16[1568,1152]{1,0:T(8,128)(2,1)} %get-tuple-element.102.q_ref.k_ref.v_ref), custom_call_target="tpu_custom_call" | custom-call | tf_op jit(solution)/shard_map/attend/pallas_call | solution.py:239
  224.1 0.7 fusion.7
  224.8 0.6 pad_maximum_fusion
  225.4 50.8 %decoder_tokens.1 = (bf16[1568,384]{1,0:T(8,128)(2,1)}, f32[1568,384]{1,0:T(8,128)}, f32[3456,384]{1,0:T(8,128)}, f32[3456,384]{1,0:T(8,128)}, f32[8,384]{1,0:T(...) custom-call(s32[1]{0:T(128)} %bitcast._.half_ref, f32[1568,384]{1,0:T(8,128)} %get-tuple-element.103.a_ref.o_ref, ...), custom_call_target="tpu_custom_call" | custom-call | tf_op jit(solution)/shard_map/decoder_tokens/pallas_call | solution.py:395
  276.2 43.8 %attend_back.1 = (bf16[1568,384]{1,0:T(8,128)(2,1)}, bf16[1568,384]{1,0:T(8,128)(2,1)}, bf16[1568,384]{1,0:T(8,128)(2,1)}) custom-call(bf16[1568,1152]{1,0:T(8,128)(2,1)} %get-tuple-element.102.q_ref.k_ref.v_ref, bf16[1568,1152]{1,0:T(8,128)(2,1)} %get-tuple-element.102.q_ref.k_ref.v_ref, bf16[1568,1152]{1,0:T(8,128)(2,1)} %get-tuple-element.102.q_ref.k_ref.v_ref, ...), custom_call_target="tpu_custom_call" | custom-call | tf_op jit(solution)/shard_map/attend_back/pallas_call | solution.py:286
  320.0 0.0 copy-start.5
  320.0 12.1 %decoder_qkv_back.1 = (bf16[160,384]{1,0:T(8,128)(2,1)}, f32[3456,384]{1,0:T(8,128)}, f32[3456,384]{1,0:T(8,128)}, f32[8,384]{1,0:T(8,128)}) custom-call(s32[1]{0:T(128)} %bitcast._.half_ref, s32[1,160]{1,0:T(1,128)} %constant_dynamic-slice_fusion.order_ref, ...), custom_call_target="tpu_custom_call", output_to_operand_aliasing={{1}: (11, {}), {2}: (12, {})} | custom-call | tf_op jit(solution)/shard_map/decoder_qkv_back/pallas_call | solution.py:485
  332.1 0.4 collective-permute-start.5
  332.5 0.2 collective-permute-start.1
  332.7 4.3 collective-permute-done.1.refs_11_.start_other_ref
  337.0 0.6 copy-done.6
  337.6 20.3 %encoder_back_1.1 = (f32[160,768]{1,0:T(8,128)}, bf16[160,7680]{1,0:T(8,128)(2,1)}, bf16[160,7680]{1,0:T(8,128)(2,1)}, f32[2,8,4608]{2,1,0:T(8,128)}, f32[8,768]...) custom-call(bf16[160,384]{1,0:T(8,128)(2,1)} %get-tuple-element.122.refs_0_, ...), custom_call_target="tpu_custom_call" | custom-call | tf_op jit(solution)/shard_map/encoder_back_1/pallas_call | solution.py:807
  357.9 0.0 copy-start.8
  358.0 0.0 copy-start.13
  358.0 20.6 %encoder_back_0.1 = (f32[160,768]{1,0:T(8,128)}, bf16[160,8448]{1,0:T(8,128)(2,1)}, bf16[160,8448]{1,0:T(8,128)(2,1)}, f32[2,8,5376]{2,1,0:T(8,128)}, f32[8,768]...) custom-call(f32[160,768]{1,0:T(8,128)} %get-tuple-element.131.refs_0_, f32[160,768]{1,0:T(8,128)} %get-tuple-element.132.refs_1_, ...), custom_call_target="tpu_custom_call" | custom-call | tf_op jit(solution)/shard_map/encoder_back_0/pallas_call | solution.py:807
  378.7 0.2 collective-permute-start.3
  378.9 0.4 collective-permute-start.4
  379.2 1.2 slice.289
  380.4 0.1 reduce.20
  380.5 0.6 reduce_sum.19
  381.9 0.6 fusion.10
  382.5 0.7 reshape.88
  383.2 0.8 slice_reduce_fusion.11
  384.0 0.7 slice_reduce_fusion.1
  384.8 0.8 slice_reduce_fusion.6
  385.6 0.1 concatenate.29
  385.7 0.1 collective-permute-start.2
  385.8 0.1 multiply_reduce_fusion
  385.9 0.8 concatenate.28
  386.7 7.2 %dec_left_factor.1.refs_2_ = f32[2,8,3456]{2,1,0:T(8,128)} custom-call(f32[8,1152]{1,0:T(8,128)} %bitcast.58, f32[8,1152]{1,0:T(8,128)} %copy-done.6, f32[3456,384]{1,0:T(8,128)} %get-tuple-element.142.own_ref.refs_13_, f32[3456,384]{1,0:T(8,128)} %get-tuple-element.143.other_ref), custom_call_target="tpu_custom_call" | custom-call | tf_op jit(solution)/shard_map/dec_left_factor/pallas_call | solution.py:869
  393.9 0.7 reshape.91.refs_5_
  394.6 1.5 copy-done.2
  396.0 54.9 %compress.1 = (f32[8,9984]{1,0:T(8,128)}, f32[8,3456]{1,0:T(8,128)}, f32[8,768]{1,0:T(8,128)}, f32[8,384]{1,0:T(8,128)}, f32[8,2816]{1,0:T(8,128)}, /*index=5*/b...) custom-call(f32[2,8,5376]{2,1,0:T(8,128)} %get-tuple-element.140.refs_0_, ...), custom_call_target="tpu_custom_call" | custom-call | tf_op jit(solution)/shard_map/compress/pallas_call | solution.py:1136
  451.0 1.4 maximum_bitcast_fusion
  452.3 1.3 convolution_add_fusion
  453.7 0.0 copy-start.1
  453.7 0.8 fusion.1
  454.5 3.6 bitcast_add_fusion
  458.1 0.0 copy-start.12
  458.1 1.9 fusion
  460.0 0.5 slice.296
  460.5 0.6 broadcast_in_dim.57
  461.1 0.6 broadcast_in_dim.58
  461.8 0.7 multiply_subtract_fusion
  463.1 19.9 %new_errors.1 = (bf16[9984,768]{1,0:T(8,128)(2,1)}, bf16[3456,384]{1,0:T(8,128)(2,1)}) custom-call(bf16[9984,352]{1,0:T(8,128)(2,1)} %get-tuple-element.164.turned_ref, bf16[9,352,768]{2,1,0:T(8,128)(2,1)} %get-tuple-element.165.rights_ref, bf16[9984,768]{1,0:T(8,128)(2,1)} %bitcast.48, f32[3456,384]{1,0:T(8,128)} %get-tuple-element.166.comb_ref, ...), custom_call_target="tpu_custom_call" | custom-call | tf_op jit(solution)/shard_map/new_errors/pallas_call | solution.py:1250
  (58 shorter events, 0.3 us)
Async XLA Ops:
  0.6 7.0 %copy-start.4 = (f32[1,216,384]{2,1,0:T(8,128)S(1)}, f32[1,216,384]{2,1,0:T(8,128)}, u32[]{:S(2)}) copy-start(f32[1,216,384]{2,1,0:T(8,128)} %param.18) | copy-start | bytes 995332
  0.7 164.8 %collective-permute-start = (f32[1,6528]{1,0:T(1,128)}, f32[1,6528]{1,0:T(1,128)S(1)}, u32[]{:S(2)}, u32[]{:S(2)}) collective-permute-start(f32[1,6528]{1,0:T(1,128)} %refs_3_.1), channel_id=1, source_target_pairs={{0,1},{1,0},{2,3},{3,2},{4,5},{5,4},{6,7},{7,6},{8,9},{9,8},{10,11... | collective-permute-start | bytes 78344 | tf_op jit(solution)/shard_map/ppermute | solution.py:1671
  10.6 153.6 %copy-start.9 = (f32[14976]{0:T(1024)S(1)}, f32[14976]{0:T(1024)}, u32[]{:S(2)}) copy-start(f32[14976]{0:T(1024)} %param.20) | copy-start | bytes 179716
  10.6 153.6 %slice-start = ((f32[14976]{0:T(1024)}), f32[11520]{0:T(1024)S(1)}, s32[]{:S(2)}) async-start(f32[14976]{0:T(1024)} %param.20), calls=%async_computation | async-start | bytes 98304 | tf_op jit(solution)/shard_map/slice | solution.py:1723
  165.4 0.8 copy-start.10
  320.0 12.6 %copy-start.5 = (f32[1,8,1152]{2,1,0:T(8,128)S(1)}, f32[1,8,1152]{2,1,0:T(8,128)}, u32[]{:S(2)}) copy-start(f32[1,8,1152]{2,1,0:T(8,128)} %param.27) | copy-start | bytes 110596
  332.1 62.4 %collective-permute-start.5 = (f32[3456,384]{1,0:T(8,128)}, f32[3456,384]{1,0:T(8,128)}, u32[]{:S(2)}, u32[]{:S(2)}) collective-permute-start(f32[3456,384]{1,0:T(8,128)} %get-tuple-element.143.other_ref), channel_id=1, source_target_pairs={{0,1},{1,0},{2,3},{3,2},{4,5},{5,4},{6,7},{7,6},{8,9},{9,8},{10,11... | collective-permute-start | bytes 15925256 | tf_op jit(solution)/shard_map/ppermute | solution.py:1671
  332.5 4.4 collective-permute-start.1
  337.0 0.6 copy-start.6
  357.9 22.5 %copy-start.8 = (f32[1,6528]{1,0:T(1,128)S(1)}, f32[1,6528]{1,0:T(1,128)}, u32[]{:S(2)}) copy-start(f32[1,6528]{1,0:T(1,128)} %refs_3_.1) | copy-start | bytes 78340
  357.9 22.6 %copy-start.16 = (f32[8,384]{1,0:T(8,128)S(1)}, f32[8,384]{1,0:T(8,128)}, u32[]{:S(2)}) copy-start(f32[8,384]{1,0:T(8,128)} %get-tuple-element.155) | copy-start | bytes 36868
  357.9 22.6 %copy-start.21 = (f32[1,1536]{1,0:T(1,128)S(1)}, f32[1,1536]{1,0:T(1,128)}, u32[]{:S(2)}) copy-start(f32[1,1536]{1,0:T(1,128)} %get-tuple-element.156) | copy-start | bytes 18436
  357.9 23.8 %copy-start.19 = (f32[1,1536]{1,0:T(1,128)S(1)}, f32[1,1536]{1,0:T(1,128)}, u32[]{:S(2)}) copy-start(f32[1,1536]{1,0:T(1,128)} %get-tuple-element.152) | copy-start | bytes 18436
  358.0 23.9 %copy-start.18 = (f32[1,1536]{1,0:T(1,128)S(1)}, f32[1,1536]{1,0:T(1,128)}, u32[]{:S(2)}) copy-start(f32[1,1536]{1,0:T(1,128)} %get-tuple-element.151) | copy-start | bytes 18436
  358.0 23.9 %copy-start.17 = (f32[8,384]{1,0:T(8,128)S(1)}, f32[8,384]{1,0:T(8,128)}, u32[]{:S(2)}) copy-start(f32[8,384]{1,0:T(8,128)} %get-tuple-element.150) | copy-start | bytes 36868
  358.0 25.2 %copy-start.14 = (f32[8,768]{1,0:T(8,128)S(1)}, f32[8,768]{1,0:T(8,128)}, u32[]{:S(2)}) copy-start(f32[8,768]{1,0:T(8,128)} %get-tuple-element.154) | copy-start | bytes 73732
  358.0 26.0 %copy-start.20 = (f32[2,768]{1,0:T(2,128)S(1)}, f32[2,768]{1,0:T(2,128)}, u32[]{:S(2)}) copy-start(f32[2,768]{1,0:T(2,128)} %get-tuple-element.148) | copy-start | bytes 18436
  358.0 26.8 %copy-start.15 = (f32[1,3072]{1,0:T(1,128)S(1)}, f32[1,3072]{1,0:T(1,128)}, u32[]{:S(2)}) copy-start(f32[1,3072]{1,0:T(1,128)} %get-tuple-element.149) | copy-start | bytes 36868
  358.0 27.8 %copy-start.13 = (f32[1,6528]{1,0:T(1,128)S(1)}, f32[1,6528]{1,0:T(1,128)}, u32[]{:S(2)}) copy-start(f32[1,6528]{1,0:T(1,128)} %param.23) | copy-start | bytes 78340
  378.7 15.9 %collective-permute-start.3 = (bf16[160,8448]{1,0:T(8,128)(2,1)}, bf16[160,8448]{1,0:T(8,128)(2,1)S(1)}, u32[]{:S(2)}, u32[]{:S(2)}) collective-permute-start(bf16[160,8448]{1,0:T(8,128)(2,1)} %get-tuple-element.159), channel_id=1, source_target_pairs={{0,1},{1,0},{2,3},{3,2},{4,5},{5,4},{6,7},{7,6},{8,9},{9,8},{10,11... | collective-permute-start | bytes 8110088 | tf_op jit(solution)/shard_map/ppermute | solution.py:1671
  378.9 15.7 %collective-permute-start.4 = (bf16[160,7680]{1,0:T(8,128)(2,1)}, bf16[160,7680]{1,0:T(8,128)(2,1)}, u32[]{:S(2)}, u32[]{:S(2)}) collective-permute-start(bf16[160,7680]{1,0:T(8,128)(2,1)} %get-tuple-element.160), channel_id=1, source_target_pairs={{0,1},{1,0},{2,3},{3,2},{4,5},{5,4},{6,7},{7,6},{8,9},{9,8},{10,11... | collective-permute-start | bytes 7372808 | tf_op jit(solution)/shard_map/ppermute | solution.py:1671
  385.7 8.2 %collective-permute-start.2 = (f32[22528]{0:T(1024)S(1)}, f32[22528]{0:T(1024)S(1)}, u32[]{:S(2)}, u32[]{:S(2)}) collective-permute-start(f32[22528]{0:T(1024)S(1)} %concatenate.29), channel_id=1, source_target_pairs={{0,1},{1,0},{2,3},{3,2},{4,5},{5,4},{6,7},{7,6},{8,9},{9,8},{10,11... | collective-permute-start | bytes 270344 | tf_op jit(solution)/shard_map/ppermute | solution.py:1671
  394.5 1.5 copy-start.2
  396.0 56.3 %copy-start.7 = (f32[1,216,384]{2,1,0:T(8,128)S(1)}, f32[1,216,384]{2,1,0:T(8,128)}, u32[]{:S(2)}) copy-start(f32[1,216,384]{2,1,0:T(8,128)} %param.22) | copy-start | bytes 995332
  453.7 4.4 copy-start.3
  453.7 4.4 copy-start.1
  458.1 1.9 copy-start
  458.1 1.9 copy-start.11
  458.1 3.7 copy-start.12
